TPU v7x, 32 devices: a whole 2x2x4 slice. The times are simulated.
32 devices in a mesh: wide: 8 (over z, y), grp: 4 (over x, core).
Axes of the slice: x: 2, y: 2, z: 4, core: 2. Of those that a mesh axis runs over, the one named last changes fastest.
Arguments:
- slab: float32 [64, 4, 16, 128], P(None, 'grp', 'wide'), may hold values from -400 to 400
- hblocks: float32 [4, 16, 5, 128, 128], P('grp', 'wide'), may hold values from -0.25 to 0.25
- blist: int32 [4, 16, 5], P('grp', 'wide'), may hold values from 0 to 8, as said below
- rotation: float32 [8, 8, 8], replicated, may hold values from -2 to 2
Outputs:
- rotated: float32 [64, 4, 16, 128], P('wide', 'grp')
Inputs may be any that keep to these rules, and one draw needn't show every extreme that they name: `blist`: entry 0 of every row block's list is 4 (the block itself); the other entries are distinct codes other than 4.
All inputs are finite; a program needn't handle non-finite values.
Results may differ from a plain program's by a relative error of at most 0.00012.
Values sent between devices are 32-bit elements; how exact they have to be, the bound alone decides.
No kernel may reach another device: no remote copies, remote signals or barrier semaphores. Data moves between devices by JAX's collectives and lax.ppermute only.
A program may use at most 64 MiB of HBM per device.

v0:
```python
import jax
import jax.numpy as jnp
from jax import lax
from jax.sharding import PartitionSpec as P

VEC = 8
DEG = 4


def with_halo(block, sides, width):
    for axis, dim in sides:
        count = lax.axis_size(axis)
        forward = [(i, i + 1) for i in range(count - 1)]
        backward = [(target, source) for source, target in forward]
        low = lax.ppermute(
            lax.slice_in_dim(block, block.shape[dim] - width, None, axis=dim), axis, forward
        )
        high = lax.ppermute(lax.slice_in_dim(block, 0, width, axis=dim), axis, backward)
        block = jnp.concatenate([low, block, high], axis=dim)
    return block


def combine_slots(extended, hblocks, blist):
    states = extended.shape[0]
    grid_rows, blocks_here, slot_count, block_nodes = (
        hblocks.shape[0],
        hblocks.shape[1],
        hblocks.shape[2],
        hblocks.shape[3],
    )
    flat_ext = extended.reshape(states, (grid_rows + 2) * (blocks_here + 2), block_nodes)
    row_index = jnp.arange(grid_rows, dtype=jnp.int32)[:, None]
    col_index = jnp.arange(blocks_here, dtype=jnp.int32)[None, :]
    summed = jnp.zeros((states, grid_rows * blocks_here, block_nodes), jnp.float32)
    for slot_index in range(slot_count):
        block_code = blist[:, :, slot_index]
        position = (
            (row_index + block_code // 3) * (blocks_here + 2) + col_index + block_code % 3
        ).reshape(-1)
        picked = jnp.take(flat_ext, position, axis=1)
        weights_here = hblocks[:, :, slot_index].reshape(
            grid_rows * blocks_here, block_nodes, block_nodes
        )
        summed = summed + jnp.einsum(
            "rij,srj->sri", weights_here, picked, precision=lax.Precision.HIGHEST
        )
    return summed.reshape(states, grid_rows, blocks_here, block_nodes)


def apply_rows(field_in, hblocks, blist):
    extended = with_halo(field_in, (("wide", 2), ("grp", 1)), 1)
    return combine_slots(extended, hblocks, blist)


def chebyshev(start, operator_fn):
    previous = start
    current = operator_fn(start)
    for degree_step in range(DEG - 1):
        following = 2.0 * operator_fn(current) - previous
        previous, current = (current, following)
    return current


def mixing(gram_mat, rotation):
    lower = jnp.linalg.cholesky(gram_mat)
    return lax.linalg.triangular_solve(
        lower, jnp.swapaxes(rotation, -1, -2), left_side=False, lower=True
    )


def body(slab, hblocks, blist, rotation):
    current = chebyshev(slab, lambda field_in: apply_rows(field_in, hblocks, blist))
    node_count = (
        slab.shape[1] * slab.shape[2] * slab.shape[3] * lax.axis_size("wide") * lax.axis_size("grp")
    )
    state_blocks = current.reshape(rotation.shape[0], VEC, -1)
    partial_gram = jnp.einsum(
        "bam,bcm->bac", state_blocks, state_blocks, precision=lax.Precision.HIGHEST
    )
    gram_mat = lax.psum(partial_gram, ("wide", "grp")) / node_count
    mixer = mixing(gram_mat, rotation)
    mixed_rows = jnp.einsum("bad,bdm->bam", mixer, state_blocks, precision=lax.Precision.HIGHEST)
    rotated = lax.all_to_all(
        mixed_rows.reshape(current.shape), "wide", split_axis=0, concat_axis=2, tiled=True
    )
    return rotated


def solution(mesh):
    in_specs = (
        P(None, "grp", "wide", None),
        P("grp", "wide", None, None, None),
        P("grp", "wide", None),
        P(),
    )
    out_specs = P("wide", "grp", None, None)
    return jax.shard_map(body, mesh=mesh, in_specs=in_specs, out_specs=out_specs, check_vma=False)
```

profile of v0, /device:TPU:0, one launch (start us, length us, event | category | flops | bytes accessed | tf_op | source)
XLA Modules:
  0.0 157.8 jit_solution(1213514799782078650)
XLA Ops:
  0.0 1.0 fusion.165
  1.0 4.9 %collective-permute-start = (f32[64,1,1,128]{3,0,2,1:T(8,128)S(1)}, f32[64,1,1,128]{3,0,2,1:T(8,128)S(1)}, u32[]{:S(2)}, u32[]{:S(2)}) collective-permute-start(f32[64,1,1,128]{3,0,2,1:T(8,128)S(1)} %copy.66), channel_id=1, source_target_pairs={{0,4},{4,8},{8,12},{12,16},{16,20},{20,24},{24,28},{1,5},{5,9},{9,... | collective-permute-start | bytes 98312 | tf_op jit(solution)/shard_map/ppermute | solution.py:15
  5.9 1.3 collective-permute-start.1
  8.4 3.3 %collective-permute-done.1 = f32[64,1,1,128]{3,0,2,1:T(8,128)S(1)} collective-permute-done((f32[64,1,1,128]{3,0,2,1:T(8,128)S(1)}, f32[64,1,1,128]{3,0,2,1:T(8,128)S(1)}, u32[]{:S(2)}, u32[]{:S(2)}) %collective-permute-start.1) | collective-permute-done | bytes 32800 | tf_op jit(solution)/shard_map/ppermute | solution.py:18
  11.7 1.3 collective-permute-start.2
  13.0 1.3 collective-permute-start.3
  14.4 3.6 %collective-permute-done.3 = f32[64,1,4,128]{3,0,2,1:T(8,128)S(1)} collective-permute-done((f32[64,1,4,128]{3,0,2,1:T(8,128)S(1)}, f32[64,1,4,128]{3,0,2,1:T(8,128)S(1)}, u32[]{:S(2)}, u32[]{:S(2)}) %collective-permute-start.3) | collective-permute-done | bytes 131104 | tf_op jit(solution)/shard_map/ppermute | solution.py:18
  18.0 0.6 gather_fusion
  18.6 0.6 gather_fusion.1
  19.1 0.6 gather_fusion.2
  19.7 0.6 gather_fusion.3
  20.2 0.6 gather_fusion.4
  22.9 4.3 %collective-permute-start.4 = (f32[64,1,1,128]{3,0,2,1:T(8,128)S(1)}, f32[64,1,1,128]{3,0,2,1:T(8,128)S(1)}, u32[]{:S(2)}, u32[]{:S(2)}) collective-permute-start(f32[64,1,1,128]{3,0,2,1:T(8,128)S(1)} %get-tuple-element.35), channel_id=1, source_target_pairs={{0,4},{4,8},{8,12},{12,16},{16,20},{20,24},{24,28},{1,5},{5,9},{9,... | collective-permute-start | bytes 98312 | tf_op jit(solution)/shard_map/ppermute | solution.py:15
  27.2 1.3 collective-permute-start.5
  28.8 4.2 %collective-permute-done.5 = f32[64,1,1,128]{3,0,2,1:T(8,128)S(1)} collective-permute-done((f32[64,1,1,128]{3,0,2,1:T(8,128)S(1)}, f32[64,1,1,128]{3,0,2,1:T(8,128)S(1)}, u32[]{:S(2)}, u32[]{:S(2)}) %collective-permute-start.5) | collective-permute-done | bytes 32800 | tf_op jit(solution)/shard_map/ppermute | solution.py:18
  33.0 4.0 %collective-permute-start.6 = (f32[64,1,4,128]{3,0,2,1:T(8,128)S(1)}, f32[64,1,4,128]{3,0,2,1:T(8,128)S(1)}, u32[]{:S(2)}, u32[]{:S(2)}) collective-permute-start(f32[64,1,4,128]{3,0,2,1:T(8,128)S(1)} %pad_maximum_fusion.4), channel_id=1, source_target_pairs={{0,1},{1,2},{2,3},{4,5},{5,6},{6,7},{8,9},{9,10},{10,11},{12,13},{... | collective-permute-start | bytes 393224 | tf_op jit(solution)/shard_map/ppermute | solution.py:15
  37.1 1.3 collective-permute-start.7
  38.4 2.7 %collective-permute-done.7 = f32[64,1,4,128]{3,0,2,1:T(8,128)S(1)} collective-permute-done((f32[64,1,4,128]{3,0,2,1:T(8,128)S(1)}, f32[64,1,4,128]{3,0,2,1:T(8,128)S(1)}, u32[]{:S(2)}, u32[]{:S(2)}) %collective-permute-start.7) | collective-permute-done | bytes 131104 | tf_op jit(solution)/shard_map/ppermute | solution.py:18
  41.1 0.6 gather_fusion.5
  41.7 0.6 gather_fusion.6
  42.3 0.6 gather_fusion.7
  42.8 0.6 gather_fusion.8
  43.4 0.6 gather_fusion.9
  46.0 3.4 %collective-permute-start.8 = (f32[64,1,1,128]{3,0,2,1:T(8,128)S(1)}, f32[64,1,1,128]{3,0,2,1:T(8,128)S(1)}, u32[]{:S(2)}, u32[]{:S(2)}) collective-permute-start(f32[64,1,1,128]{3,0,2,1:T(8,128)S(1)} %get-tuple-element.33), channel_id=1, source_target_pairs={{0,4},{4,8},{8,12},{12,16},{16,20},{20,24},{24,28},{1,5},{5,9},{9,... | collective-permute-start | bytes 98312 | tf_op jit(solution)/shard_map/ppermute | solution.py:15
  49.4 1.3 collective-permute-start.9
  51.0 4.2 %collective-permute-done.9 = f32[64,1,1,128]{3,0,2,1:T(8,128)S(1)} collective-permute-done((f32[64,1,1,128]{3,0,2,1:T(8,128)S(1)}, f32[64,1,1,128]{3,0,2,1:T(8,128)S(1)}, u32[]{:S(2)}, u32[]{:S(2)}) %collective-permute-start.9) | collective-permute-done | bytes 32800 | tf_op jit(solution)/shard_map/ppermute | solution.py:18
  55.3 4.0 %collective-permute-start.10 = (f32[64,1,4,128]{3,0,2,1:T(8,128)S(1)}, f32[64,1,4,128]{3,0,2,1:T(8,128)S(1)}, u32[]{:S(2)}, u32[]{:S(2)}) collective-permute-start(f32[64,1,4,128]{3,0,2,1:T(8,128)S(1)} %pad_maximum_fusion.5), channel_id=1, source_target_pairs={{0,1},{1,2},{2,3},{4,5},{5,6},{6,7},{8,9},{9,10},{10,11},{12,13},{... | collective-permute-start | bytes 393224 | tf_op jit(solution)/shard_map/ppermute | solution.py:15
  59.3 1.3 collective-permute-start.11
  60.6 2.7 %collective-permute-done.11 = f32[64,1,4,128]{3,0,2,1:T(8,128)S(1)} collective-permute-done((f32[64,1,4,128]{3,0,2,1:T(8,128)S(1)}, f32[64,1,4,128]{3,0,2,1:T(8,128)S(1)}, u32[]{:S(2)}, u32[]{:S(2)}) %collective-permute-start.11) | collective-permute-done | bytes 131104 | tf_op jit(solution)/shard_map/ppermute | solution.py:18
  63.4 0.6 gather_fusion.10
  63.9 0.6 gather_fusion.11
  64.5 0.6 gather_fusion.12
  65.6 0.6 gather_fusion.14
  68.2 4.3 %collective-permute-start.12 = (f32[64,1,1,128]{3,0,2,1:T(8,128)S(1)}, f32[64,1,1,128]{3,0,2,1:T(8,128)S(1)}, u32[]{:S(2)}, u32[]{:S(2)}) collective-permute-start(f32[64,1,1,128]{3,0,2,1:T(8,128)S(1)} %get-tuple-element.31), channel_id=1, source_target_pairs={{0,4},{4,8},{8,12},{12,16},{16,20},{20,24},{24,28},{1,5},{5,9},{9,... | collective-permute-start | bytes 98312 | tf_op jit(solution)/shard_map/ppermute | solution.py:15
  72.6 1.3 collective-permute-start.13
  74.2 4.2 %collective-permute-done.13 = f32[64,1,1,128]{3,0,2,1:T(8,128)S(1)} collective-permute-done((f32[64,1,1,128]{3,0,2,1:T(8,128)S(1)}, f32[64,1,1,128]{3,0,2,1:T(8,128)S(1)}, u32[]{:S(2)}, u32[]{:S(2)}) %collective-permute-start.13) | collective-permute-done | bytes 32800 | tf_op jit(solution)/shard_map/ppermute | solution.py:18
  78.4 4.0 %collective-permute-start.14 = (f32[64,1,4,128]{3,0,2,1:T(8,128)S(1)}, f32[64,1,4,128]{3,0,2,1:T(8,128)S(1)}, u32[]{:S(2)}, u32[]{:S(2)}) collective-permute-start(f32[64,1,4,128]{3,0,2,1:T(8,128)S(1)} %pad_maximum_fusion.6), channel_id=1, source_target_pairs={{0,1},{1,2},{2,3},{4,5},{5,6},{6,7},{8,9},{9,10},{10,11},{12,13},{... | collective-permute-start | bytes 393224 | tf_op jit(solution)/shard_map/ppermute | solution.py:15
  82.4 1.3 collective-permute-start.15
  83.8 2.7 %collective-permute-done.15 = f32[64,1,4,128]{3,0,2,1:T(8,128)S(1)} collective-permute-done((f32[64,1,4,128]{3,0,2,1:T(8,128)S(1)}, f32[64,1,4,128]{3,0,2,1:T(8,128)S(1)}, u32[]{:S(2)}, u32[]{:S(2)}) %collective-permute-start.15) | collective-permute-done | bytes 131104 | tf_op jit(solution)/shard_map/ppermute | solution.py:18
  86.5 0.6 gather_fusion.15
  87.1 0.6 gather_fusion.16
  88.2 0.6 gather_fusion.18
  88.7 0.6 gather_fusion.19
  91.7 42.5 %psum.7 = f32[8,8,8]{1,2,0:T(8,128)S(1)} all-reduce(f32[8,8,8]{1,2,0:T(8,128)S(1)} %fusion.166), channel_id=1, replica_groups=mesh['wide'=8,'grp'=4] {'wide','grp'}, use_global_device_ids=true, to_apply=%region_0.2 | all-reduce | flops 512 | bytes 4096 | tf_op jit(solution)/shard_map/psum | solution.py:80
  134.3 5.8 %custom-call.7 = f32[8,8,8]{2,1,0:T(8,128)S(1)} custom-call(f32[8,8,8]{2,1,0:T(8,128)S(1)} %fusion.96), custom_call_target="Cholesky" | custom-call | tf_op jit(solution)/shard_map/jit(cholesky)/cholesky | solution.py:65
  140.4 5.0 %custom-call.8 = f32[8,1,8,8]{2,3,1,0:T(8,128)S(1)} custom-call(f32[8,1,8,8]{3,2,1,0:T(8,128)S(1)} %select_bitcast_fusion), custom_call_target="InvertDiagBlocksLowerTriangular" | custom-call | tf_op jit(solution)/shard_map/triangular_solve | solution.py:66
  145.9 11.2 %all_to_all.18 = f32[64,1,2,128]{3,2,1,0:T(2,128)S(1)} all-to-all(f32[64,1,2,128]{3,2,1,0:T(2,128)S(1)} %bitcast.187), channel_id=1, replica_groups=mesh['wide'=8,'grp'=4] {'wide'}, dimensions={0} | all-to-all | bytes 131072 | tf_op jit(solution)/shard_map/all_to_all | solution.py:83
  157.2 0.7 copy.56
  (77 shorter events, 12.5 us)
Async XLA Ops:
  0.0 145.4 %copy-start = (f32[8,8,8]{2,1,0:T(8,128)S(1)}, f32[8,8,8]{2,1,0:T(8,128)}, u32[]{:S(2)}) copy-start(f32[8,8,8]{2,1,0:T(8,128)} %param.9) | copy-start | bytes 6148
  1.0 6.9 %collective-permute-start = (f32[64,1,1,128]{3,0,2,1:T(8,128)S(1)}, f32[64,1,1,128]{3,0,2,1:T(8,128)S(1)}, u32[]{:S(2)}, u32[]{:S(2)}) collective-permute-start(f32[64,1,1,128]{3,0,2,1:T(8,128)S(1)} %copy.66), channel_id=1, source_target_pairs={{0,4},{4,8},{8,12},{12,16},{16,20},{20,24},{24,28},{1,5},{5,9},{9,... | collective-permute-start | bytes 98312 | tf_op jit(solution)/shard_map/ppermute | solution.py:15
  5.9 1.3 copy-start.3
  5.9 5.8 %collective-permute-start.1 = (f32[64,1,1,128]{3,0,2,1:T(8,128)S(1)}, f32[64,1,1,128]{3,0,2,1:T(8,128)S(1)}, u32[]{:S(2)}, u32[]{:S(2)}) collective-permute-start(f32[64,1,1,128]{3,0,2,1:T(8,128)S(1)} %copy.67), channel_id=1, source_target_pairs={{4,0},{8,4},{12,8},{16,12},{20,16},{24,20},{28,24},{5,1},{9,5},{13... | collective-permute-start | bytes 98312 | tf_op jit(solution)/shard_map/ppermute | solution.py:18
  7.5 0.8 copy-start.2
  11.7 2.6 %collective-permute-start.2 = (f32[64,1,4,128]{3,0,2,1:T(8,128)S(1)}, f32[64,1,4,128]{3,0,2,1:T(8,128)S(1)}, u32[]{:S(2)}, u32[]{:S(2)}) collective-permute-start(f32[64,1,4,128]{3,0,2,1:T(8,128)S(1)} %constant_dynamic-update-slice_fusion), channel_id=1, source_target_pairs={{0,1},{1,2},{2,3},{4,5},{5,6},{6,7},{8,9},{9,10},{10,11},{12,13},{... | collective-permute-start | bytes 393224 | tf_op jit(solution)/shard_map/ppermute | solution.py:15
  13.0 5.0 %collective-permute-start.3 = (f32[64,1,4,128]{3,0,2,1:T(8,128)S(1)}, f32[64,1,4,128]{3,0,2,1:T(8,128)S(1)}, u32[]{:S(2)}, u32[]{:S(2)}) collective-permute-start(f32[64,1,4,128]{3,0,2,1:T(8,128)S(1)} %constant_dynamic-update-slice_fusion), channel_id=1, source_target_pairs={{1,0},{2,1},{3,2},{5,4},{6,5},{7,6},{9,8},{10,9},{11,10},{13,12},{... | collective-permute-start | bytes 393224 | tf_op jit(solution)/shard_map/ppermute | solution.py:18
  14.3 6.5 %copy-start.1 = (f32[1,2,5,128,128]{4,3,2,1,0:T(8,128)S(1)}, f32[1,2,5,128,128]{4,3,2,1,0:T(8,128)}, u32[]{:S(2)}) copy-start(f32[1,2,5,128,128]{4,3,2,1,0:T(8,128)} %param.7) | copy-start | bytes 1966084
  22.9 5.9 %collective-permute-start.4 = (f32[64,1,1,128]{3,0,2,1:T(8,128)S(1)}, f32[64,1,1,128]{3,0,2,1:T(8,128)S(1)}, u32[]{:S(2)}, u32[]{:S(2)}) collective-permute-start(f32[64,1,1,128]{3,0,2,1:T(8,128)S(1)} %get-tuple-element.35), channel_id=1, source_target_pairs={{0,4},{4,8},{8,12},{12,16},{16,20},{20,24},{24,28},{1,5},{5,9},{9,... | collective-permute-start | bytes 98312 | tf_op jit(solution)/shard_map/ppermute | solution.py:15
  27.2 5.8 %collective-permute-start.5 = (f32[64,1,1,128]{3,0,2,1:T(8,128)S(1)}, f32[64,1,1,128]{3,0,2,1:T(8,128)S(1)}, u32[]{:S(2)}, u32[]{:S(2)}) collective-permute-start(f32[64,1,1,128]{3,0,2,1:T(8,128)S(1)} %get-tuple-element.36), channel_id=1, source_target_pairs={{4,0},{8,4},{12,8},{16,12},{20,16},{24,20},{28,24},{5,1},{9,5},{13... | collective-permute-start | bytes 98312 | tf_op jit(solution)/shard_map/ppermute | solution.py:18
  33.0 5.3 %collective-permute-start.6 = (f32[64,1,4,128]{3,0,2,1:T(8,128)S(1)}, f32[64,1,4,128]{3,0,2,1:T(8,128)S(1)}, u32[]{:S(2)}, u32[]{:S(2)}) collective-permute-start(f32[64,1,4,128]{3,0,2,1:T(8,128)S(1)} %pad_maximum_fusion.4), channel_id=1, source_target_pairs={{0,1},{1,2},{2,3},{4,5},{5,6},{6,7},{8,9},{9,10},{10,11},{12,13},{... | collective-permute-start | bytes 393224 | tf_op jit(solution)/shard_map/ppermute | solution.py:15
  37.1 4.0 %collective-permute-start.7 = (f32[64,1,4,128]{3,0,2,1:T(8,128)S(1)}, f32[64,1,4,128]{3,0,2,1:T(8,128)S(1)}, u32[]{:S(2)}, u32[]{:S(2)}) collective-permute-start(f32[64,1,4,128]{3,0,2,1:T(8,128)S(1)} %pad_maximum_fusion.4), channel_id=1, source_target_pairs={{1,0},{2,1},{3,2},{5,4},{6,5},{7,6},{9,8},{10,9},{11,10},{13,12},{... | collective-permute-start | bytes 393224 | tf_op jit(solution)/shard_map/ppermute | solution.py:18
  46.0 5.0 %collective-permute-start.8 = (f32[64,1,1,128]{3,0,2,1:T(8,128)S(1)}, f32[64,1,1,128]{3,0,2,1:T(8,128)S(1)}, u32[]{:S(2)}, u32[]{:S(2)}) collective-permute-start(f32[64,1,1,128]{3,0,2,1:T(8,128)S(1)} %get-tuple-element.33), channel_id=1, source_target_pairs={{0,4},{4,8},{8,12},{12,16},{16,20},{20,24},{24,28},{1,5},{5,9},{9,... | collective-permute-start | bytes 98312 | tf_op jit(solution)/shard_map/ppermute | solution.py:15
  49.4 5.8 %collective-permute-start.9 = (f32[64,1,1,128]{3,0,2,1:T(8,128)S(1)}, f32[64,1,1,128]{3,0,2,1:T(8,128)S(1)}, u32[]{:S(2)}, u32[]{:S(2)}) collective-permute-start(f32[64,1,1,128]{3,0,2,1:T(8,128)S(1)} %get-tuple-element.34), channel_id=1, source_target_pairs={{4,0},{8,4},{12,8},{16,12},{20,16},{24,20},{28,24},{5,1},{9,5},{13... | collective-permute-start | bytes 98312 | tf_op jit(solution)/shard_map/ppermute | solution.py:18
  55.3 5.3 %collective-permute-start.10 = (f32[64,1,4,128]{3,0,2,1:T(8,128)S(1)}, f32[64,1,4,128]{3,0,2,1:T(8,128)S(1)}, u32[]{:S(2)}, u32[]{:S(2)}) collective-permute-start(f32[64,1,4,128]{3,0,2,1:T(8,128)S(1)} %pad_maximum_fusion.5), channel_id=1, source_target_pairs={{0,1},{1,2},{2,3},{4,5},{5,6},{6,7},{8,9},{9,10},{10,11},{12,13},{... | collective-permute-start | bytes 393224 | tf_op jit(solution)/shard_map/ppermute | solution.py:15
  59.3 4.0 %collective-permute-start.11 = (f32[64,1,4,128]{3,0,2,1:T(8,128)S(1)}, f32[64,1,4,128]{3,0,2,1:T(8,128)S(1)}, u32[]{:S(2)}, u32[]{:S(2)}) collective-permute-start(f32[64,1,4,128]{3,0,2,1:T(8,128)S(1)} %pad_maximum_fusion.5), channel_id=1, source_target_pairs={{1,0},{2,1},{3,2},{5,4},{6,5},{7,6},{9,8},{10,9},{11,10},{13,12},{... | collective-permute-start | bytes 393224 | tf_op jit(solution)/shard_map/ppermute | solution.py:18
  68.2 5.9 %collective-permute-start.12 = (f32[64,1,1,128]{3,0,2,1:T(8,128)S(1)}, f32[64,1,1,128]{3,0,2,1:T(8,128)S(1)}, u32[]{:S(2)}, u32[]{:S(2)}) collective-permute-start(f32[64,1,1,128]{3,0,2,1:T(8,128)S(1)} %get-tuple-element.31), channel_id=1, source_target_pairs={{0,4},{4,8},{8,12},{12,16},{16,20},{20,24},{24,28},{1,5},{5,9},{9,... | collective-permute-start | bytes 98312 | tf_op jit(solution)/shard_map/ppermute | solution.py:15
  72.6 5.8 %collective-permute-start.13 = (f32[64,1,1,128]{3,0,2,1:T(8,128)S(1)}, f32[64,1,1,128]{3,0,2,1:T(8,128)S(1)}, u32[]{:S(2)}, u32[]{:S(2)}) collective-permute-start(f32[64,1,1,128]{3,0,2,1:T(8,128)S(1)} %get-tuple-element.32), channel_id=1, source_target_pairs={{4,0},{8,4},{12,8},{16,12},{20,16},{24,20},{28,24},{5,1},{9,5},{13... | collective-permute-start | bytes 98312 | tf_op jit(solution)/shard_map/ppermute | solution.py:18
  78.4 5.4 %collective-permute-start.14 = (f32[64,1,4,128]{3,0,2,1:T(8,128)S(1)}, f32[64,1,4,128]{3,0,2,1:T(8,128)S(1)}, u32[]{:S(2)}, u32[]{:S(2)}) collective-permute-start(f32[64,1,4,128]{3,0,2,1:T(8,128)S(1)} %pad_maximum_fusion.6), channel_id=1, source_target_pairs={{0,1},{1,2},{2,3},{4,5},{5,6},{6,7},{8,9},{9,10},{10,11},{12,13},{... | collective-permute-start | bytes 393224 | tf_op jit(solution)/shard_map/ppermute | solution.py:15
  82.4 4.0 %collective-permute-start.15 = (f32[64,1,4,128]{3,0,2,1:T(8,128)S(1)}, f32[64,1,4,128]{3,0,2,1:T(8,128)S(1)}, u32[]{:S(2)}, u32[]{:S(2)}) collective-permute-start(f32[64,1,4,128]{3,0,2,1:T(8,128)S(1)} %pad_maximum_fusion.6), channel_id=1, source_target_pairs={{1,0},{2,1},{3,2},{5,4},{6,5},{7,6},{9,8},{10,9},{11,10},{13,12},{... | collective-permute-start | bytes 393224 | tf_op jit(solution)/shard_map/ppermute | solution.py:18
where the time goes:
time: 159 us; the launch traced here: 158 us
  blocking collectives  53.7 us (34%)
  starting transfers between devices  40.6 us (26%)
  waiting for transfers between devices  28.7 us (18%)
  local copies, waits for them, and re-layouts  13.4 us (8%)
  other arithmetic  11.9 us (7%)
  matrix products  8.7 us (5%)
    psum x1, blocking collectives, body(): gram_mat = lax.psum(partial_gram, ('wide', 'grp')) / node_count  42.5 us
    ppermute x8, starting transfers between devices, with_halo(): lax.ppermute(lax.slice_in_dim(block, block.shape[dim] - width, None, axis...  30.3 us
    ppermute x8, waiting for transfers between devices, with_halo(): lax.ppermute(lax.slice_in_dim(block, 0, width, axis=dim), axis, backward)  27.8 us
    all_to_all x1, blocking collectives, body(): lax.all_to_all(mixed_rows.reshape(current.shape), 'wide', split_axis=0, c...  11.2 us
    gather x20, local copies, waits for them, and re-layouts, combine_slots(): picked = jnp.take(flat_ext, position, axis=1)  11.1 us
    ppermute x8, starting transfers between devices, with_halo(): lax.ppermute(lax.slice_in_dim(block, 0, width, axis=dim), axis, backward)  10.3 us
    dot_general x20, matrix products, combine_slots(): jnp.einsum('rij,srj->sri', weights_here, picked, precision=lax.Precision....  8.04 us
    another operation x4, other arithmetic, mixing(): lower = jnp.linalg.cholesky(gram_mat)  6.03 us
  transfers between devices with their start and end apart: 16, of which 11 were waited for; matrix products, arithmetic and copies ran while one was open for 0% of the time, Pallas kernels for 0%

commit v1 on v0

v1 whole, which is shorter than its diff:
```python
import functools

import jax
import jax.numpy as jnp
from jax import lax
from jax.experimental import pallas as pl
from jax.experimental.pallas import tpu as pltpu
from jax.sharding import PartitionSpec as P

VEC = 8
DEG = 4
LIMIT = 16 * 2**20
BLOCKS = 9
VMEM = pl.BlockSpec(memory_space=pltpu.VMEM)
SMEM = pl.BlockSpec(memory_space=pltpu.SMEM)
NT = (((1,), (1,)), ((), ()))


def split(x):
    high = x.astype(jnp.bfloat16)
    low = (x - high.astype(jnp.float32)).astype(jnp.bfloat16)
    return high, low


def flag(flags_ref, n, shape):
    return jnp.broadcast_to(flags_ref[n * VEC : n * VEC + 1, :], shape) == 1


def arrange_kernel(flags_ref, codes_ref, slab_ref, out_ref):
    all_states, _, cols, size = slab_ref.shape
    slots, states = codes_ref.shape[2], all_states // 2
    odd = flag(flags_ref, 0, (all_states, size))
    second = flag(flags_ref, 2, (states, size))
    both = [slab_ref[:, 0, c, :] for c in range(cols)]
    for u in range(cols):
        value = jnp.where(odd, both[cols - 1 - u], both[u])
        low, high = value[:states], value[states:]
        rows = slice(u * states, (u + 1) * states)
        out_ref[0, rows, :] = jnp.where(second, high, low)
        out_ref[1, rows, :] = jnp.where(second, low, high)
    codes = codes_ref[0].astype(jnp.float32)
    for h in range(2):
        out_ref[h, cols * states :, :] = jnp.zeros((VEC, size), jnp.float32)
        out_ref[h, cols * states : cols * states + cols, 0:slots] = codes


def arrange(flags, blist, slab):
    all_states, _, cols, size = slab.shape
    return pl.pallas_call(
        arrange_kernel,
        in_specs=[VMEM] * 3,
        out_specs=VMEM,
        out_shape=jax.ShapeDtypeStruct((2, cols * all_states // 2 + VEC, size), jnp.float32),
        compiler_params=pltpu.CompilerParams(vmem_limit_bytes=LIMIT),
        name="arrange",
    )(flags, blist, slab)


def pick_kernel(flags_ref, own_ref, core_ref, border_ref, inner_ref):
    shape = own_ref.shape[3:]
    edge, half = flag(flags_ref, 1, shape), flag(flags_ref, 2, shape)
    for k in range(own_ref.shape[2]):
        own = jnp.where(half, own_ref[0, 1, k], own_ref[0, 0, k])
        core = jnp.where(half, core_ref[0, 1, k], core_ref[0, 0, k])
        border_ref[0, 0, k] = jnp.where(edge, own, core)
        inner_ref[0, 0, k] = jnp.where(edge, core, own)


def pick(flags, own, core):
    rows, cols, *block = own.shape
    return pl.pallas_call(
        pick_kernel,
        in_specs=[VMEM] * 3,
        out_specs=[VMEM] * 2,
        out_shape=[jax.ShapeDtypeStruct((rows, 1, *block), own.dtype)] * 2,
        compiler_params=pltpu.CompilerParams(vmem_limit_bytes=LIMIT),
        name="pick",
    )(flags, own, core)


def prepare_kernel(mode, codes_ref, *refs):
    *h_refs, out_ref = refs
    _, cols, slots, size, _ = h_refs[0].shape
    odd, edge, half, x = (codes_ref[n] for n in range(4))
    out_ref[...] = jnp.zeros_like(out_ref)

    def convert(h_ref, h_col, c, q, row):
        u = jnp.bitwise_xor(c, odd)
        for k in range(slots):
            code = codes_ref[4 + (row * 2 + c) * slots + k]
            down = (code >= 3).astype(jnp.int32) + (code >= 6).astype(jnp.int32)
            along = code - 3 * down
            down = jnp.where(x == 1, 2 - down, down)
            along = u + jnp.where(odd == 1, 2 - along, along)
            rim = (along == 0) | (along == 3)
            block = jnp.where(rim, 6 + down, 2 * down + along - 1)
            lanes = pl.ds(pl.multiple_of(block * size, size), size)
            high, low = split(h_ref[0, h_col, k])
            out_ref[q, u, 0:size, lanes] = high
            out_ref[q, u, size : 2 * size, lanes] = low

    for h, h_ref in enumerate(h_refs):
        if mode == "chip":
            for c in range(cols):
                convert(h_ref, c, c, jnp.bitwise_xor(edge, h), h)
        else:
            row = 3 - edge if mode == "border" else 2 + edge
            convert(h_ref, 0, jnp.bitwise_xor(half, h), 0, row)


def prepare(mode, codes, *h_rows):
    _, _, slots, size, _ = h_rows[0].shape
    rows = 2 if mode == "chip" else 1
    return pl.pallas_call(
        functools.partial(prepare_kernel, mode),
        in_specs=[SMEM] + [VMEM] * len(h_rows),
        out_specs=VMEM,
        out_shape=jax.ShapeDtypeStruct((rows, 2, 2 * size, BLOCKS * size), jnp.bfloat16),
        compiler_params=pltpu.CompilerParams(vmem_limit_bytes=LIMIT),
        name="prepare_" + mode,
    )(codes, *h_rows)


def fill(x_ref, fields):
    rows, states, size = fields[0].shape
    for q in range(rows):
        for n, field in enumerate(fields):
            at = (q * len(fields) + n) * size
            high, low = split(field[q])
            x_ref[0:states, at : at + size] = high
            x_ref[states : 2 * states, at : at + size] = low


def step_kernel(kind, u, count, *refs):
    h_refs, (own_0, own_1, rim_ref, *refs) = refs[:count], refs[count:]
    *refs, own_x, rim_x = refs
    before, refs = (None, refs) if kind == "first" else (refs[0], refs[1:])
    rows_in, states, size = rim_ref.shape
    h_rows = [h_ref.at[q] for h_ref in h_refs for q in range(h_ref.shape[0])]
    fill(own_x, [own_0, own_1])
    fill(rim_x, [rim_ref])
    values = []
    for q, h_row in enumerate(h_rows):
        low, high = max(q - 1, 0), min(q + 2, rows_in)
        acc = 0.0
        for x_ref, width, first in ((own_x, 2 * size, 0), (rim_x, size, 6 * size)):
            at = first + (low - q + 1) * width
            acc = acc + lax.dot_general(
                x_ref[:, low * width : high * width],
                h_row[u, :, at : at + (high - low) * width],
                NT,
                preferred_element_type=jnp.float32,
            )
        small = acc[states:, size:] + (acc[states:, :size] + acc[:states, size:])
        value = acc[:states, :size] + small
        values.append(value if kind == "first" else 2.0 * value - before[q])
    if kind in ("other", "last"):
        flat = [jnp.concatenate(part, axis=1) for part in zip(*map(split, values))]
        flat = jnp.concatenate(flat)
        gram = lax.dot_general(flat, flat, NT, preferred_element_type=jnp.float32)
        gram = gram[:states] + gram[states:]
        gram = gram[:, :states] + gram[:, states:]
    if kind != "last":
        for q, value in enumerate(values):
            refs[0][q] = value
        if kind == "other":
            refs[1][:, 0:states] = gram
        return
    other_ref, other_gram_ref, flags_ref, packed_ref, sent_ref = refs
    odd, edge = flag(flags_ref, 0, (states, size)), flag(flags_ref, 1, (states, size))
    nodes = [[other_ref[q] for q in range(len(values))], values]
    gram = gram + other_gram_ref[:, 0:states]
    for c in range(2):
        inner = jnp.where(odd, nodes[1 - c][0], nodes[c][0])
        border = jnp.where(odd, nodes[1 - c][1], nodes[c][1])
        kept, sent = jnp.where(edge, border, inner), jnp.where(edge, inner, border)
        for b in range(states // VEC):
            packed_ref[b, c * VEC : (c + 1) * VEC, :] = kept[b * VEC : (b + 1) * VEC]
            sent_ref[b, c * VEC : (c + 1) * VEC, :] = sent[b * VEC : (b + 1) * VEC]
    for b in range(states // VEC):
        rows = slice(b * VEC, (b + 1) * VEC)
        for ref in (packed_ref, sent_ref):
            ref[b, 2 * VEC :, :] = jnp.zeros((VEC, size), jnp.float32)
            ref[b, 2 * VEC :, 0:VEC] = gram[rows, rows]


def step(kind, u, name, h_ready, own, rim, *others):
    rows_in, states, size = rim.shape
    rows_out = sum(h.shape[0] for h in h_ready)
    shapes = [(rows_out, states, size)]
    if kind == "other":
        shapes.append((states, pl.cdiv(states, size) * size))
    elif kind == "last":
        blocks = states // VEC
        shapes = [(2 * blocks, 3 * VEC, size), (blocks, 3 * VEC, size)]
    operands = [*h_ready, *own, rim, *others]
    cost = pl.CostEstimate(
        flops=8 * BLOCKS * rows_out * states * size * size,
        bytes_accessed=4 * BLOCKS * rows_out * size * size,
        transcendentals=0,
    )
    outs = pl.pallas_call(
        functools.partial(step_kernel, kind, u, len(h_ready)),
        in_specs=[VMEM] * len(operands),
        out_specs=[VMEM] * len(shapes),
        out_shape=[jax.ShapeDtypeStruct(shape, jnp.float32) for shape in shapes],
        scratch_shapes=[
            pltpu.VMEM((2 * states, rows_in * width * size), jnp.bfloat16) for width in (2, 1)
        ],
        compiler_params=pltpu.CompilerParams(vmem_limit_bytes=LIMIT),
        cost_estimate=cost,
        name=name,
    )(*operands)
    return outs[0] if len(outs) == 1 else outs


def finish_kernel(cols, node_count, flags_ref, parts_ref, rot_ref, out_ref):
    wide = parts_ref.shape[0]
    gram = parts_ref[0, cols * VEC : (cols + 1) * VEC, 0:VEC]
    for w in range(1, wide):
        gram = gram + parts_ref[w, cols * VEC : (cols + 1) * VEC, 0:VEC]
    gram = gram / node_count
    row = lax.broadcasted_iota(jnp.int32, (VEC, VEC), 0)
    col = lax.broadcasted_iota(jnp.int32, (VEC, VEC), 1)
    inverse = jnp.where(row == col, 1.0, 0.0).astype(jnp.float32)
    for k in range(VEC):
        scale = 1.0 / jnp.sqrt(gram[k : k + 1, k : k + 1])
        top = gram[k : k + 1, :] * scale
        top_inverse = inverse[k : k + 1, :] * scale
        factor = gram[:, k : k + 1] * scale
        gram = gram - factor * top
        inverse = jnp.where(row == k, top_inverse, jnp.where(row > k, inverse - factor * top_inverse, inverse))
    turn = rot_ref[...]
    mixer = turn[:, 0:1] * inverse[0:1, :]
    for k in range(1, VEC):
        mixer = mixer + turn[:, k : k + 1] * inverse[k : k + 1, :]
    columns = [mixer[:, d : d + 1] for d in range(VEC)]
    mixed = []
    for w in range(wide):
        for c in range(cols):
            block = parts_ref[w, c * VEC : (c + 1) * VEC, :]
            total = columns[0] * block[0:1, :]
            for d in range(1, VEC):
                total = total + columns[d] * block[d : d + 1, :]
            mixed.append(total)
    half = flag(flags_ref, 2, mixed[0].shape)
    for at, total in enumerate(mixed):
        turned = mixed[(at + len(mixed) // 2) % len(mixed)]
        out_ref[:, 0, at, :] = jnp.where(half, turned, total)


def finish(flags, cols, node_count, parts, turn):
    wide, _, size = parts.shape
    return pl.pallas_call(
        functools.partial(finish_kernel, cols, node_count),
        in_specs=[VMEM] * 3,
        out_specs=VMEM,
        out_shape=jax.ShapeDtypeStruct((VEC, 1, wide * cols, size), jnp.float32),
        compiler_params=pltpu.CompilerParams(vmem_limit_bytes=LIMIT),
        name="finish",
    )(flags, parts, turn)


def after(x, token):
    return lax.optimization_barrier((x, token))[0]


def body(slab, hblocks, blist, rotation):
    wide, grp = lax.axis_size("wide"), lax.axis_size("grp")
    _, _, cols, size = slab.shape
    slots = hblocks.shape[2]
    near = [(i, i ^ 1) for i in range(wide)]
    far = [(i, ((i + 1) ^ 1) - 1) for i in range(1, wide - 1)]
    mine, odd = lax.axis_index("grp"), lax.axis_index("wide") % 2
    x = mine // 2
    edge = half = x ^ (mine % 2)
    place = jnp.stack([odd, edge, half, x]).astype(jnp.int32)
    flags = jnp.broadcast_to(jnp.repeat(place, VEC)[:, None], (4 * VEC, size))

    def across(value):
        return lax.ppermute(value, "grp", [(i, i ^ 3) for i in range(grp)])

    def core(value):
        return lax.ppermute(value, "grp", [(i, i ^ 1) for i in range(grp)])

    def over_far(value):
        return lax.ppermute(value, "wide", far)

    def over_near(value):
        return lax.ppermute(value, "wide", near)

    own = arrange(flags, blist, slab)
    own_core = core(own[1])
    h_core = core(hblocks)
    border, inside = pick(flags, hblocks, h_core)
    own_across = across(after(jnp.stack([own[0], own_core]), border))
    rows = [own[0], own_core, own_across[0], own_across[1]]
    codes = jnp.stack([row[-VEC : cols - VEC, :slots] for row in rows]).astype(jnp.int32).reshape(-1)
    codes = jnp.concatenate([place, codes])
    states = (own.shape[1] - VEC) // cols
    zero = []
    for u in range(cols):
        parts = [row[u * states : (u + 1) * states] for row in rows]
        border_mine = jnp.stack([parts[m] for m in (1, 0, 2, 3)])
        border_core = jnp.stack([parts[m] for m in (0, 1, 3, 2)])
        zero.append(jnp.where(edge == 1, border_mine, border_core))

    zero[1] = after(zero[1], zero[0])
    far_rim, near_rim = over_far(zero[0]), over_near(zero[1])
    border = across(after(border, own_core))
    inside = across(after(inside, zero[1]))
    h_two = [prepare("chip", codes, hblocks, h_core)]
    border_core = core(after(border, (far_rim, near_rim, h_two)))
    h_three = h_two + [prepare("border", codes, border, border_core)]

    one = [step("first", 0, "one_0", h_three, zero, far_rim)]
    rim = after(near_rim, one[0])
    one.append(step("first", 1, "one_1", h_three, zero, rim))
    rims = over_far(one[0]), over_near(one[1])
    two, sent, before = [], (), []
    for u in range(cols):
        rim = after(rims[u], (sent, inside))
        two.append(step("next", u, f"two_{u}", h_two, one, rim, zero[u]))
        sent = jnp.concatenate([two[u], one[u][:1]])
        other = across(sent)
        two[u] = jnp.concatenate([two[u], other[1:2], other[0:1]])
        before.append(jnp.concatenate([one[u], other[2:]]))
    inside_core = core(after(inside, two[0]))
    h_four = h_three + [prepare("inner", codes, inside, inside_core)]
    rims = over_far(two[0]), over_near(two[1])
    three = [step("next", 0, "three_0", h_four, two, rims[0], before[0])]
    rim = after(rims[1], three[0])
    three.append(step("next", 1, "three_1", h_four, two, rim, before[1]))
    rims = over_far(three[0]), over_near(three[1])
    four = step("other", 0, "four_0", h_four, three, rims[0], two[0])
    packed, sent = step("last", 1, "four_1", h_four, three, rims[1], two[1], *four, flags)

    packed = lax.dynamic_update_slice(packed, core(sent), (sent.shape[0], 0, 0))
    owners = wide // 2
    groups = [
        [((i + owners * (g // 2 ^ g % 2)) % wide) * grp + g for i in range(wide)] for g in range(grp)
    ]
    packed = lax.all_to_all(
        packed,
        ("wide", "grp"),
        split_axis=0,
        concat_axis=0,
        tiled=True,
        axis_index_groups=groups,
    )
    turn = lax.dynamic_index_in_dim(rotation, lax.axis_index("wide"), 0, keepdims=False)
    node_count = grp * wide * cols * size
    return finish(flags, cols, node_count, packed, turn.T)


def solution(mesh):
    in_specs = (
        P(None, "grp", "wide", None),
        P("grp", "wide", None, None, None),
        P("grp", "wide", None),
        P(),
    )
    out_specs = P("wide", "grp", None, None)
    return jax.shard_map(body, mesh=mesh, in_specs=in_specs, out_specs=out_specs, check_vma=False)
```

time: 159 us -> 66 us (0.42)
  blocking collectives: 53.7 us -> 0 us
  other arithmetic: 11.9 us -> 0.15 us
  local copies, waits for them, and re-layouts: 13.4 us -> 2.68 us
  waiting for transfers between devices: 28.7 us -> 18.4 us
  Pallas kernels: 0 us -> 9.94 us
  matrix products: 8.7 us -> 0 us
  starting transfers between devices: 40.6 us -> 34.3 us
    psum x1 -> x0, blocking collectives: 42.5 us -> none  [body(): gram_mat = lax.psum(partial_gram, ('wide', 'grp')) / node_count]
    ppermute x16 -> x18, waiting for transfers between devices: 28.7 us -> 11.4 us  [the longest x5 5.2 us: across(): return lax.ppermute(value, 'grp', [(i, i ^ 3) for i in range(grp)])]
    ppermute x16 -> x18, starting transfers between devices: 40.6 us -> 29 us  [the longest x4 19.1 us: over_near(): return lax.ppermute(value, 'wide', near)]
    all_to_all x1 -> x0, blocking collectives: 11.2 us -> none  [body(): lax.all_to_all(mixed_rows.reshape(current.shape), 'wide', split_axis=0, c...]
    gather x20 -> x0, local copies, waits for them, and re-layouts: 11.1 us -> none  [combine_slots(): picked = jnp.take(flat_ext, position, axis=1)]
    another operation x7 -> x2, other arithmetic: 11.1 us -> 0.09 us  [the longest x1 0.08 us: body(): place = jnp.stack([odd, edge, half, x]).astype(jnp.int32)]
    pallas_call x0 -> x14, Pallas kernels: none -> 9.94 us  [the longest x8 5.98 us: step(): pl.pallas_call(functools.partial(step_kernel, kind, u, len(h_ready)), in_...]
    dot_general x22 -> x0, matrix products: 8.42 us -> none  [the longest x20 8.04 us: combine_slots(): jnp.einsum('rij,srj->sri', weights_here, picked, precision=lax.Precision....]
  transfers between devices with their start and end apart: 16 -> 19, of which waited for: 11 -> 10; matrix products, arithmetic and copies ran while one was open for 0% -> 1% of each run, Pallas kernels for 0% -> 10%
where the time goes in v1:
time: 66 us; the launch traced here: 65.7 us
  starting transfers between devices  34.3 us (52%)
  waiting for transfers between devices  18.4 us (28%)
  Pallas kernels  9.94 us (15%)
  local copies, waits for them, and re-layouts  2.68 us (4%)
    ppermute x4, starting transfers between devices, over_near(): return lax.ppermute(value, 'wide', near)  19.1 us
    all_to_all x1, waiting for transfers between devices, body(): lax.all_to_all(packed, ('wide', 'grp'), split_axis=0, concat_axis=0, tile...  7.03 us
    ppermute x5, starting transfers between devices, across(): return lax.ppermute(value, 'grp', [(i, i ^ 3) for i in range(grp)])  6.39 us
    pallas_call x8, Pallas kernels, step(): pl.pallas_call(functools.partial(step_kernel, kind, u, len(h_ready)), in_...  5.98 us
    all_to_all x1, starting transfers between devices, body(): lax.all_to_all(packed, ('wide', 'grp'), split_axis=0, concat_axis=0, tile...  5.33 us
    ppermute x5, waiting for transfers between devices, across(): return lax.ppermute(value, 'grp', [(i, i ^ 3) for i in range(grp)])  5.2 us
    ppermute x4, waiting for transfers between devices, over_near(): return lax.ppermute(value, 'wide', near)  3.76 us
    ppermute x4, starting transfers between devices, over_far(): return lax.ppermute(value, 'wide', far)  2.66 us
  transfers between devices with their start and end apart: 19, of which 10 were waited for; matrix products, arithmetic and copies ran while one was open for 1% of the time, Pallas kernels for 10%

profile of v1, /device:TPU:0, one launch (start us, length us, event | category | flops | bytes accessed | tf_op | source)
XLA Modules:
  0.0 65.7 jit_solution(10767674821572260011)
XLA Ops:
  0.0 0.5 collective-permute-start.1
  0.5 0.1 pad_add_fusion
  0.5 0.1 broadcast_in_dim.10
  0.6 0.1 broadcast_in_dim.11
  0.7 0.1 broadcast_in_dim.12.flags_ref.refs_9_
  0.8 0.8 %copy-done.2 = f32[64,1,2,128]{3,2,1,0:T(2,128)S(1)} copy-done((f32[64,1,2,128]{3,2,1,0:T(2,128)S(1)}, f32[64,1,2,128]{3,2,1,0:T(2,128)}, u32[]{:S(2)}) %copy-start.2) | copy-done | bytes 65560
  1.6 0.7 %copy-done.3 = s32[1,2,5]{2,1,0:T(2,128)S(1)} copy-done((s32[1,2,5]{2,1,0:T(2,128)S(1)}, s32[1,2,5]{2,1,0:T(2,128)}, u32[]{:S(2)}) %copy-start.3) | copy-done | bytes 64
  2.4 0.1 collective-permute-start
  2.5 1.1 %collective-permute-done = f32[72,128]{1,0:T(8,128)S(1)} collective-permute-done((f32[72,128]{1,0:T(8,128)S(1)}, f32[72,128]{1,0:T(8,128)S(1)}, u32[]{:S(2)}, u32[]{:S(2)}) %collective-permute-start) | collective-permute-done | bytes 36896 | tf_op jit(solution)/shard_map/ppermute | solution.py:284
  3.7 0.1 pick.1
  3.8 2.7 %collective-permute-start.2 = (f32[2,72,128]{2,1,0:T(8,128)S(1)}, f32[2,72,128]{2,1,0:T(8,128)S(1)}, u32[]{:S(2)}, u32[]{:S(2)}) collective-permute-start(f32[2,72,128]{2,1,0:T(8,128)S(1)} %pad_maximum_fusion), channel_id=1, source_target_pairs={{0,3},{1,2},{2,1},{3,0},{4,7},{5,6},{6,5},{7,4},{8,11},{9,10},{10,... | collective-permute-start | bytes 221192 | tf_op jit(solution)/shard_map/ppermute | solution.py:281
  6.4 0.1 collective-permute-start.3
  6.5 2.5 %collective-permute-done.2 = f32[2,72,128]{2,1,0:T(8,128)S(1)} collective-permute-done((f32[2,72,128]{2,1,0:T(8,128)S(1)}, f32[2,72,128]{2,1,0:T(8,128)S(1)}, u32[]{:S(2)}, u32[]{:S(2)}) %collective-permute-start.2) | collective-permute-done | bytes 73760 | tf_op jit(solution)/shard_map/ppermute | solution.py:281
  9.0 0.7 %collective-permute-start.4 = (f32[4,32,128]{2,1,0:T(8,128)S(1)}, f32[4,32,128]{2,1,0:T(8,128)S(1)}, u32[]{:S(2)}, u32[]{:S(2)}) collective-permute-start(f32[4,32,128]{2,1,0:T(8,128)S(1)} %maximum_select_fusion.refs_2_.refs_4_), channel_id=1, source_target_pairs={{4,8},{8,4},{12,16},{16,12},{20,24},{24,20},{5,9},{9,5},{13,17},{1... | collective-permute-start | bytes 196616 | tf_op jit(solution)/shard_map/ppermute | solution.py:287
  9.7 4.4 %collective-permute-start.5 = (f32[4,32,128]{2,1,0:T(8,128)S(1)}, f32[4,32,128]{2,1,0:T(8,128)S(1)}, u32[]{:S(2)}, u32[]{:S(2)}) collective-permute-start(f32[4,32,128]{2,1,0:T(8,128)S(1)} %maximum_select_fusion.1.refs_3_.refs_4_), channel_id=1, source_target_pairs={{0,4},{4,0},{8,12},{12,8},{16,20},{20,16},{24,28},{28,24},{1,5},{5... | collective-permute-start | bytes 196616 | tf_op jit(solution)/shard_map/ppermute | solution.py:290
  14.2 0.1 convert_element_type.8
  14.3 0.1 concatenate.22.codes_ref
  14.3 0.9 %prepare_chip.1.refs_0_ = bf16[2,2,256,1152]{3,2,1,0:T(8,128)(2,1)S(1)} custom-call(s32[44]{0:T(128)S(1)} %concatenate.22.codes_ref, f32[1,2,5,128,128]{4,3,2,1,0:T(8,128)S(1)} %copy-done.1, f32[1,2,5,128,128]{4,3,2,1,0:T(8,128)S(1)} %collective-permute-done.1.core_ref.refs_1_), custom_call_target="tpu_custom_call" | custom-call | tf_op jit(solution)/shard_map/prepare_chip/pallas_call | solution.py:114
  15.3 1.8 %collective-permute-done.5.refs_4_ = f32[4,32,128]{2,1,0:T(8,128)S(1)} collective-permute-done((f32[4,32,128]{2,1,0:T(8,128)S(1)}, f32[4,32,128]{2,1,0:T(8,128)S(1)}, u32[]{:S(2)}, u32[]{:S(2)}) %collective-permute-start.5) | collective-permute-done | bytes 65568 | tf_op jit(solution)/shard_map/ppermute | solution.py:290
  17.1 1.8 %collective-permute-start.7 = (f32[1,1,5,128,128]{4,3,2,1,0:T(8,128)S(1)}, f32[1,1,5,128,128]{4,3,2,1,0:T(8,128)S(1)}, u32[]{:S(2)}, u32[]{:S(2)}) collective-permute-start(f32[1,1,5,128,128]{4,3,2,1,0:T(8,128)S(1)} %get-tuple-element.27), channel_id=1, source_target_pairs={{0,3},{1,2},{2,1},{3,0},{4,7},{5,6},{6,5},{7,4},{8,11},{9,10},{10,... | collective-permute-start | bytes 983048 | tf_op jit(solution)/shard_map/ppermute | solution.py:281
  19.0 0.7 %prepare_border.1.refs_1_ = bf16[1,2,256,1152]{3,2,1,0:T(8,128)(2,1)S(1)} custom-call(s32[44]{0:T(128)S(1)} %concatenate.22.codes_ref, f32[1,1,5,128,128]{4,3,2,1,0:T(8,128)S(1)} %collective-permute-done.3.refs_0_, f32[1,1,5,128,128]{4,3,2,1,0:T(8,128)S(1)} %collective-permute-done.6.refs_1_), custom_call_target="tpu_custom_call" | custom-call | tf_op jit(solution)/shard_map/prepare_border/pallas_call | solution.py:114
  19.7 0.6 one_0.1.refs_1_
  20.3 0.7 %collective-permute-start.8 = (f32[3,32,128]{2,1,0:T(8,128)S(1)}, f32[3,32,128]{2,1,0:T(8,128)S(1)}, u32[]{:S(2)}, u32[]{:S(2)}) collective-permute-start(f32[3,32,128]{2,1,0:T(8,128)S(1)} %one_0.1.refs_1_), channel_id=1, source_target_pairs={{4,8},{8,4},{12,16},{16,12},{20,24},{24,20},{5,9},{9,5},{13,17},{1... | collective-permute-start | bytes 147464 | tf_op jit(solution)/shard_map/ppermute | solution.py:287
  21.0 0.6 one_1.1.refs_2_
  21.5 5.3 %collective-permute-start.11 = (f32[3,32,128]{2,1,0:T(8,128)S(1)}, f32[3,32,128]{2,1,0:T(8,128)S(1)}, u32[]{:S(2)}, u32[]{:S(2)}) collective-permute-start(f32[3,32,128]{2,1,0:T(8,128)S(1)} %one_1.1.refs_2_), channel_id=1, source_target_pairs={{0,4},{4,0},{8,12},{12,8},{16,20},{20,16},{24,28},{28,24},{1,5},{5... | collective-permute-start | bytes 147464 | tf_op jit(solution)/shard_map/ppermute | solution.py:290
  26.9 0.4 two_0.1
  27.3 1.6 %collective-permute-start.9 = (f32[3,32,128]{2,1,0:T(8,128)S(1)}, f32[3,32,128]{2,1,0:T(8,128)S(1)}, u32[]{:S(2)}, u32[]{:S(2)}) collective-permute-start(f32[3,32,128]{2,1,0:T(8,128)S(1)} %pad_maximum_fusion.5), channel_id=1, source_target_pairs={{0,3},{1,2},{2,1},{3,0},{4,7},{5,6},{6,5},{7,4},{8,11},{9,10},{10,... | collective-permute-start | bytes 147464 | tf_op jit(solution)/shard_map/ppermute | solution.py:281
  28.9 0.4 two_1.1
  29.4 0.3 collective-permute-start.12
  29.6 1.5 %collective-permute-done.9 = f32[3,32,128]{2,1,0:T(8,128)S(1)} collective-permute-done((f32[3,32,128]{2,1,0:T(8,128)S(1)}, f32[3,32,128]{2,1,0:T(8,128)S(1)}, u32[]{:S(2)}, u32[]{:S(2)}) %collective-permute-start.9) | collective-permute-done | bytes 49184 | tf_op jit(solution)/shard_map/ppermute | solution.py:281
  31.2 0.7 %collective-permute-start.13 = (f32[4,32,128]{2,1,0:T(8,128)S(1)}, f32[4,32,128]{2,1,0:T(8,128)S(1)}, u32[]{:S(2)}, u32[]{:S(2)}) collective-permute-start(f32[4,32,128]{2,1,0:T(8,128)S(1)} %pad_maximum_fusion.1.refs_3_.refs_6_), channel_id=1, source_target_pairs={{4,8},{8,4},{12,16},{16,12},{20,24},{24,20},{5,9},{9,5},{13,17},{1... | collective-permute-start | bytes 196616 | tf_op jit(solution)/shard_map/ppermute | solution.py:287
  31.8 0.2 collective-permute-start.10
  32.0 1.2 %collective-permute-done.12 = f32[3,32,128]{2,1,0:T(8,128)S(1)} collective-permute-done((f32[3,32,128]{2,1,0:T(8,128)S(1)}, f32[3,32,128]{2,1,0:T(8,128)S(1)}, u32[]{:S(2)}, u32[]{:S(2)}) %collective-permute-start.12) | collective-permute-done | bytes 49184 | tf_op jit(solution)/shard_map/ppermute | solution.py:281
  33.2 4.4 %collective-permute-start.14 = (f32[4,32,128]{2,1,0:T(8,128)S(1)}, f32[4,32,128]{2,1,0:T(8,128)S(1)}, u32[]{:S(2)}, u32[]{:S(2)}) collective-permute-start(f32[4,32,128]{2,1,0:T(8,128)S(1)} %pad_maximum_fusion.2.refs_4_.refs_6_), channel_id=1, source_target_pairs={{0,4},{4,0},{8,12},{12,8},{16,20},{20,16},{24,28},{28,24},{1,5},{5... | collective-permute-start | bytes 196616 | tf_op jit(solution)/shard_map/ppermute | solution.py:290
  37.6 0.7 %prepare_inner.1.refs_2_ = bf16[1,2,256,1152]{3,2,1,0:T(8,128)(2,1)S(1)} custom-call(s32[44]{0:T(128)S(1)} %concatenate.22.codes_ref, f32[1,1,5,128,128]{4,3,2,1,0:T(8,128)S(1)} %collective-permute-done.7.refs_0_, f32[1,1,5,128,128]{4,3,2,1,0:T(8,128)S(1)} %collective-permute-done.10.refs_1_), custom_call_target="tpu_custom_call" | custom-call | tf_op jit(solution)/shard_map/prepare_inner/pallas_call | solution.py:114
  38.4 0.7 %three_0.1.refs_3_ = f32[4,32,128]{2,1,0:T(8,128)S(1)} custom-call(bf16[2,2,256,1152]{3,2,1,0:T(8,128)(2,1)S(1)} %prepare_chip.1.refs_0_, bf16[1,2,256,1152]{3,2,1,0:T(8,128)(2,1)S(1)} %prepare_border.1.refs_1_, bf16[1,2,256,1152]{3,2,1,0:T(8,128)(2,1)S(1)} %prepare_inner.1.refs_2_, f32[4,32,128]{2,1,0:T(8,128)S(1)} %pad_maximum_fusion.1.refs_3_.refs_6_, ...), custom_call_target="tpu_custom_call" | custom-call | flops 150994944 | bytes 2359296 | tf_op jit(solution)/shard_map/three_0/pallas_call | solution.py:202
  39.1 0.7 %collective-permute-start.16 = (f32[4,32,128]{2,1,0:T(8,128)S(1)}, f32[4,32,128]{2,1,0:T(8,128)S(1)}, u32[]{:S(2)}, u32[]{:S(2)}) collective-permute-start(f32[4,32,128]{2,1,0:T(8,128)S(1)} %three_0.1.refs_3_), channel_id=1, source_target_pairs={{4,8},{8,4},{12,16},{16,12},{20,24},{24,20},{5,9},{9,5},{13,17},{1... | collective-permute-start | bytes 196616 | tf_op jit(solution)/shard_map/ppermute | solution.py:287
  39.8 0.6 collective-permute-done.14.refs_5_
  40.4 0.7 %three_1.1.refs_4_ = f32[4,32,128]{2,1,0:T(8,128)S(1)} custom-call(bf16[2,2,256,1152]{3,2,1,0:T(8,128)(2,1)S(1)} %prepare_chip.1.refs_0_, bf16[1,2,256,1152]{3,2,1,0:T(8,128)(2,1)S(1)} %prepare_border.1.refs_1_, bf16[1,2,256,1152]{3,2,1,0:T(8,128)(2,1)S(1)} %prepare_inner.1.refs_2_, f32[4,32,128]{2,1,0:T(8,128)S(1)} %pad_maximum_fusion.1.refs_3_.refs_6_, ...), custom_call_target="tpu_custom_call" | custom-call | flops 150994944 | bytes 2359296 | tf_op jit(solution)/shard_map/three_1/pallas_call | solution.py:202
  41.1 5.0 %collective-permute-start.15 = (f32[4,32,128]{2,1,0:T(8,128)S(1)}, f32[4,32,128]{2,1,0:T(8,128)S(1)}, u32[]{:S(2)}, u32[]{:S(2)}) collective-permute-start(f32[4,32,128]{2,1,0:T(8,128)S(1)} %three_1.1.refs_4_), channel_id=1, source_target_pairs={{0,4},{4,0},{8,12},{12,8},{16,20},{20,16},{24,28},{28,24},{1,5},{5... | collective-permute-start | bytes 196616 | tf_op jit(solution)/shard_map/ppermute | solution.py:290
  46.1 0.9 %four_0.1 = (f32[4,32,128]{2,1,0:T(8,128)S(1)}, f32[32,128]{1,0:T(8,128)S(1)}) custom-call(bf16[2,2,256,1152]{3,2,1,0:T(8,128)(2,1)S(1)} %prepare_chip.1.refs_0_, bf16[1,2,256,1152]{3,2,1,0:T(8,128)(2,1)S(1)} %prepare_border.1.refs_1_, bf16[1,2,256,1152]{3,2,1,0:T(8,128)(2,1)S(1)} %prepare_inner.1.refs_2_, f32[4,32,128]{2,1,0:T(8,128)S(1)} %three_0.1.refs_3_, ...), custom_call_target="tpu_custom_call" | custom-call | flops 150994944 | bytes 2359296 | tf_op jit(solution)/shard_map/four_0/pallas_call | solution.py:202
  47.0 1.3 %collective-permute-done.15.refs_5_ = f32[4,32,128]{2,1,0:T(8,128)S(1)} collective-permute-done((f32[4,32,128]{2,1,0:T(8,128)S(1)}, f32[4,32,128]{2,1,0:T(8,128)S(1)}, u32[]{:S(2)}, u32[]{:S(2)}) %collective-permute-start.15) | collective-permute-done | bytes 65568 | tf_op jit(solution)/shard_map/ppermute | solution.py:290
  48.3 1.6 %four_1.1 = (f32[8,24,128]{2,1,0:T(8,128)}, f32[4,24,128]{2,1,0:T(8,128)S(1)}) custom-call(bf16[2,2,256,1152]{3,2,1,0:T(8,128)(2,1)S(1)} %prepare_chip.1.refs_0_, bf16[1,2,256,1152]{3,2,1,0:T(8,128)(2,1)S(1)} %prepare_border.1.refs_1_, bf16[1,2,256,1152]{3,2,1,0:T(8,128)(2,1)S(1)} %prepare_inner.1.refs_2_, f32[4,32,128]{2,1,0:T(8,128)S(1)} %three_0.1.refs_3_, ...), custom_call_target="tpu_custom_call" | custom-call | flops 150994944 | bytes 2359296 | tf_op jit(solution)/shard_map/four_1/pallas_call | solution.py:202
  49.9 1.2 %collective-permute-done.17 = f32[4,24,128]{2,1,0:T(8,128)S(1)} collective-permute-done((f32[4,24,128]{2,1,0:T(8,128)S(1)}, f32[4,24,128]{2,1,0:T(8,128)S(1)}, u32[]{:S(2)}, u32[]{:S(2)}) %collective-permute-start.17) | collective-permute-done | bytes 49184 | tf_op jit(solution)/shard_map/ppermute | solution.py:284
  51.2 0.6 constant_dynamic-update-slice_fusion
  51.8 5.3 %all-to-all-start = ((f32[8,24,128]{2,1,0:T(8,128)}), f32[8,24,128]{2,1,0:T(8,128)S(1)}, u32[]{:S(2)}, u32[]{:S(2)}) async-start(f32[8,24,128]{2,1,0:T(8,128)} %constant_dynamic-update-slice_fusion), calls=%async_computation | async-start | bytes 196608 | tf_op jit(solution)/shard_map/all_to_all | solution.py:343
  57.2 7.0 %all-to-all-done.parts_ref = f32[8,24,128]{2,1,0:T(8,128)S(1)} async-done(((f32[8,24,128]{2,1,0:T(8,128)}), f32[8,24,128]{2,1,0:T(8,128)S(1)}, u32[]{:S(2)}, u32[]{:S(2)}) %all-to-all-start) | async-done | bytes 98336 | tf_op jit(solution)/shard_map/all_to_all | solution.py:343
  64.2 1.5 %finish.1 = f32[8,1,16,128]{3,2,1,0:T(8,128)} custom-call(s32[32,128]{1,0:T(8,128)S(1)} %broadcast_in_dim.12.flags_ref.refs_9_, f32[8,24,128]{2,1,0:T(8,128)S(1)} %all-to-all-done.parts_ref, f32[8,8]{1,0:T(8,128)S(1)} %bitcast.27), custom_call_target="tpu_custom_call" | custom-call | tf_op jit(solution)/shard_map/finish/pallas_call | solution.py:254
  (44 shorter events, 0.4 us)
Async XLA Ops:
  0.0 57.1 %copy-start = (f32[8,8,8]{2,1,0:T(8,128)S(1)}, f32[8,8,8]{2,1,0:T(8,128)}, u32[]{:S(2)}) copy-start(f32[8,8,8]{2,1,0:T(8,128)} %param.7) | copy-start | bytes 6148
  0.0 3.7 %copy-start.1 = (f32[1,2,5,128,128]{4,3,2,1,0:T(8,128)S(1)}, f32[1,2,5,128,128]{4,3,2,1,0:T(8,128)}, u32[]{:S(2)}) copy-start(f32[1,2,5,128,128]{4,3,2,1,0:T(8,128)} %refs_0_.1) | copy-start | bytes 1966084
  0.0 3.6 %collective-permute-start.1 = (f32[1,2,5,128,128]{4,3,2,1,0:T(8,128)}, f32[1,2,5,128,128]{4,3,2,1,0:T(8,128)S(1)}, u32[]{:S(2)}, u32[]{:S(2)}) collective-permute-start(f32[1,2,5,128,128]{4,3,2,1,0:T(8,128)} %refs_0_.1), channel_id=1, source_target_pairs={{0,1},{1,0},{2,3},{3,2},{4,5},{5,4},{6,7},{7,6},{8,9},{9,8},{10,11... | collective-permute-start | bytes 1966088 | tf_op jit(solution)/shard_map/ppermute | solution.py:284
  0.8 0.8 %copy-start.2 = (f32[64,1,2,128]{3,2,1,0:T(2,128)S(1)}, f32[64,1,2,128]{3,2,1,0:T(2,128)}, u32[]{:S(2)}) copy-start(f32[64,1,2,128]{3,2,1,0:T(2,128)} %slab_ref.1) | copy-start | bytes 196612
  1.6 0.7 %copy-start.3 = (s32[1,2,5]{2,1,0:T(2,128)S(1)}, s32[1,2,5]{2,1,0:T(2,128)}, u32[]{:S(2)}) copy-start(s32[1,2,5]{2,1,0:T(2,128)} %codes_ref.1) | copy-start | bytes 124
  2.4 1.3 %collective-permute-start = (f32[72,128]{1,0:T(8,128)S(1)}, f32[72,128]{1,0:T(8,128)S(1)}, u32[]{:S(2)}, u32[]{:S(2)}) collective-permute-start(f32[72,128]{1,0:T(8,128)S(1)} %get-tuple-element.46), channel_id=1, source_target_pairs={{0,1},{1,0},{2,3},{3,2},{4,5},{5,4},{6,7},{7,6},{8,9},{9,8},{10,11... | collective-permute-start | bytes 110600 | tf_op jit(solution)/shard_map/ppermute | solution.py:284
  3.8 5.3 %collective-permute-start.2 = (f32[2,72,128]{2,1,0:T(8,128)S(1)}, f32[2,72,128]{2,1,0:T(8,128)S(1)}, u32[]{:S(2)}, u32[]{:S(2)}) collective-permute-start(f32[2,72,128]{2,1,0:T(8,128)S(1)} %pad_maximum_fusion), channel_id=1, source_target_pairs={{0,3},{1,2},{2,1},{3,0},{4,7},{5,6},{6,5},{7,4},{8,11},{9,10},{10,... | collective-permute-start | bytes 221192 | tf_op jit(solution)/shard_map/ppermute | solution.py:281
  6.4 10.7 %collective-permute-start.3 = (f32[1,1,5,128,128]{4,3,2,1,0:T(8,128)S(1)}, f32[1,1,5,128,128]{4,3,2,1,0:T(8,128)S(1)}, u32[]{:S(2)}, u32[]{:S(2)}) collective-permute-start(f32[1,1,5,128,128]{4,3,2,1,0:T(8,128)S(1)} %get-tuple-element.23), channel_id=1, source_target_pairs={{0,3},{1,2},{2,1},{3,0},{4,7},{5,6},{6,5},{7,4},{8,11},{9,10},{10,... | collective-permute-start | bytes 983048 | tf_op jit(solution)/shard_map/ppermute | solution.py:281
  9.0 8.0 %collective-permute-start.4 = (f32[4,32,128]{2,1,0:T(8,128)S(1)}, f32[4,32,128]{2,1,0:T(8,128)S(1)}, u32[]{:S(2)}, u32[]{:S(2)}) collective-permute-start(f32[4,32,128]{2,1,0:T(8,128)S(1)} %maximum_select_fusion.refs_2_.refs_4_), channel_id=1, source_target_pairs={{4,8},{8,4},{12,16},{16,12},{20,24},{24,20},{5,9},{9,5},{13,17},{1... | collective-permute-start | bytes 196616 | tf_op jit(solution)/shard_map/ppermute | solution.py:287
  9.7 7.3 %collective-permute-start.5 = (f32[4,32,128]{2,1,0:T(8,128)S(1)}, f32[4,32,128]{2,1,0:T(8,128)S(1)}, u32[]{:S(2)}, u32[]{:S(2)}) collective-permute-start(f32[4,32,128]{2,1,0:T(8,128)S(1)} %maximum_select_fusion.1.refs_3_.refs_4_), channel_id=1, source_target_pairs={{0,4},{4,0},{8,12},{12,8},{16,20},{20,16},{24,28},{28,24},{1,5},{5... | collective-permute-start | bytes 196616 | tf_op jit(solution)/shard_map/ppermute | solution.py:290
  17.1 1.9 %collective-permute-start.6 = (f32[1,1,5,128,128]{4,3,2,1,0:T(8,128)S(1)}, f32[1,1,5,128,128]{4,3,2,1,0:T(8,128)S(1)}, u32[]{:S(2)}, u32[]{:S(2)}) collective-permute-start(f32[1,1,5,128,128]{4,3,2,1,0:T(8,128)S(1)} %collective-permute-done.3.refs_0_), channel_id=1, source_target_pairs={{0,1},{1,0},{2,3},{3,2},{4,5},{5,4},{6,7},{7,6},{8,9},{9,8},{10,11... | collective-permute-start | bytes 983048 | tf_op jit(solution)/shard_map/ppermute | solution.py:284
  17.1 9.7 %collective-permute-start.7 = (f32[1,1,5,128,128]{4,3,2,1,0:T(8,128)S(1)}, f32[1,1,5,128,128]{4,3,2,1,0:T(8,128)S(1)}, u32[]{:S(2)}, u32[]{:S(2)}) collective-permute-start(f32[1,1,5,128,128]{4,3,2,1,0:T(8,128)S(1)} %get-tuple-element.27), channel_id=1, source_target_pairs={{0,3},{1,2},{2,1},{3,0},{4,7},{5,6},{6,5},{7,4},{8,11},{9,10},{10,... | collective-permute-start | bytes 983048 | tf_op jit(solution)/shard_map/ppermute | solution.py:281
  20.3 6.6 %collective-permute-start.8 = (f32[3,32,128]{2,1,0:T(8,128)S(1)}, f32[3,32,128]{2,1,0:T(8,128)S(1)}, u32[]{:S(2)}, u32[]{:S(2)}) collective-permute-start(f32[3,32,128]{2,1,0:T(8,128)S(1)} %one_0.1.refs_1_), channel_id=1, source_target_pairs={{4,8},{8,4},{12,16},{16,12},{20,24},{24,20},{5,9},{9,5},{13,17},{1... | collective-permute-start | bytes 147464 | tf_op jit(solution)/shard_map/ppermute | solution.py:287
  21.5 7.4 %collective-permute-start.11 = (f32[3,32,128]{2,1,0:T(8,128)S(1)}, f32[3,32,128]{2,1,0:T(8,128)S(1)}, u32[]{:S(2)}, u32[]{:S(2)}) collective-permute-start(f32[3,32,128]{2,1,0:T(8,128)S(1)} %one_1.1.refs_2_), channel_id=1, source_target_pairs={{0,4},{4,0},{8,12},{12,8},{16,20},{20,16},{24,28},{28,24},{1,5},{5... | collective-permute-start | bytes 147464 | tf_op jit(solution)/shard_map/ppermute | solution.py:290
  27.3 3.8 %collective-permute-start.9 = (f32[3,32,128]{2,1,0:T(8,128)S(1)}, f32[3,32,128]{2,1,0:T(8,128)S(1)}, u32[]{:S(2)}, u32[]{:S(2)}) collective-permute-start(f32[3,32,128]{2,1,0:T(8,128)S(1)} %pad_maximum_fusion.5), channel_id=1, source_target_pairs={{0,3},{1,2},{2,1},{3,0},{4,7},{5,6},{6,5},{7,4},{8,11},{9,10},{10,... | collective-permute-start | bytes 147464 | tf_op jit(solution)/shard_map/ppermute | solution.py:281
  29.4 3.8 %collective-permute-start.12 = (f32[3,32,128]{2,1,0:T(8,128)S(1)}, f32[3,32,128]{2,1,0:T(8,128)S(1)}, u32[]{:S(2)}, u32[]{:S(2)}) collective-permute-start(f32[3,32,128]{2,1,0:T(8,128)S(1)} %pad_maximum_fusion.6), channel_id=1, source_target_pairs={{0,3},{1,2},{2,1},{3,0},{4,7},{5,6},{6,5},{7,4},{8,11},{9,10},{10,... | collective-permute-start | bytes 147464 | tf_op jit(solution)/shard_map/ppermute | solution.py:281
  31.2 7.2 %collective-permute-start.13 = (f32[4,32,128]{2,1,0:T(8,128)S(1)}, f32[4,32,128]{2,1,0:T(8,128)S(1)}, u32[]{:S(2)}, u32[]{:S(2)}) collective-permute-start(f32[4,32,128]{2,1,0:T(8,128)S(1)} %pad_maximum_fusion.1.refs_3_.refs_6_), channel_id=1, source_target_pairs={{4,8},{8,4},{12,16},{16,12},{20,24},{24,20},{5,9},{9,5},{13,17},{1... | collective-permute-start | bytes 196616 | tf_op jit(solution)/shard_map/ppermute | solution.py:287
  31.8 5.8 %collective-permute-start.10 = (f32[1,1,5,128,128]{4,3,2,1,0:T(8,128)S(1)}, f32[1,1,5,128,128]{4,3,2,1,0:T(8,128)S(1)}, u32[]{:S(2)}, u32[]{:S(2)}) collective-permute-start(f32[1,1,5,128,128]{4,3,2,1,0:T(8,128)S(1)} %collective-permute-done.7.refs_0_), channel_id=1, source_target_pairs={{0,1},{1,0},{2,3},{3,2},{4,5},{5,4},{6,7},{7,6},{8,9},{9,8},{10,11... | collective-permute-start | bytes 983048 | tf_op jit(solution)/shard_map/ppermute | solution.py:284
  33.2 7.2 %collective-permute-start.14 = (f32[4,32,128]{2,1,0:T(8,128)S(1)}, f32[4,32,128]{2,1,0:T(8,128)S(1)}, u32[]{:S(2)}, u32[]{:S(2)}) collective-permute-start(f32[4,32,128]{2,1,0:T(8,128)S(1)} %pad_maximum_fusion.2.refs_4_.refs_6_), channel_id=1, source_target_pairs={{0,4},{4,0},{8,12},{12,8},{16,20},{20,16},{24,28},{28,24},{1,5},{5... | collective-permute-start | bytes 196616 | tf_op jit(solution)/shard_map/ppermute | solution.py:290
  39.1 7.0 %collective-permute-start.16 = (f32[4,32,128]{2,1,0:T(8,128)S(1)}, f32[4,32,128]{2,1,0:T(8,128)S(1)}, u32[]{:S(2)}, u32[]{:S(2)}) collective-permute-start(f32[4,32,128]{2,1,0:T(8,128)S(1)} %three_0.1.refs_3_), channel_id=1, source_target_pairs={{4,8},{8,4},{12,16},{16,12},{20,24},{24,20},{5,9},{9,5},{13,17},{1... | collective-permute-start | bytes 196616 | tf_op jit(solution)/shard_map/ppermute | solution.py:287
  41.1 7.2 %collective-permute-start.15 = (f32[4,32,128]{2,1,0:T(8,128)S(1)}, f32[4,32,128]{2,1,0:T(8,128)S(1)}, u32[]{:S(2)}, u32[]{:S(2)}) collective-permute-start(f32[4,32,128]{2,1,0:T(8,128)S(1)} %three_1.1.refs_4_), channel_id=1, source_target_pairs={{0,4},{4,0},{8,12},{12,8},{16,20},{20,16},{24,28},{28,24},{1,5},{5... | collective-permute-start | bytes 196616 | tf_op jit(solution)/shard_map/ppermute | solution.py:290
  49.9 1.2 %collective-permute-start.17 = (f32[4,24,128]{2,1,0:T(8,128)S(1)}, f32[4,24,128]{2,1,0:T(8,128)S(1)}, u32[]{:S(2)}, u32[]{:S(2)}) collective-permute-start(f32[4,24,128]{2,1,0:T(8,128)S(1)} %get-tuple-element.36), channel_id=1, source_target_pairs={{0,1},{1,0},{2,3},{3,2},{4,5},{5,4},{6,7},{7,6},{8,9},{9,8},{10,11... | collective-permute-start | bytes 147464 | tf_op jit(solution)/shard_map/ppermute | solution.py:284
  51.8 12.5 %all-to-all-start = ((f32[8,24,128]{2,1,0:T(8,128)}), f32[8,24,128]{2,1,0:T(8,128)S(1)}, u32[]{:S(2)}, u32[]{:S(2)}) async-start(f32[8,24,128]{2,1,0:T(8,128)} %constant_dynamic-update-slice_fusion), calls=%async_computation | async-start | bytes 196608 | tf_op jit(solution)/shard_map/all_to_all | solution.py:343

commit v2 on v1

--- a/solution.py
+++ b/solution.py
@@ -166,22 +166,24 @@
         if kind == "other":
             refs[1][:, 0:states] = gram
         return
-    other_ref, other_gram_ref, flags_ref, packed_ref, sent_ref = refs
+    other_ref, other_gram_ref, flags_ref, kept_ref, sent_ref = refs
     odd, edge = flag(flags_ref, 0, (states, size)), flag(flags_ref, 1, (states, size))
     nodes = [[other_ref[q] for q in range(len(values))], values]
     gram = gram + other_gram_ref[:, 0:states]
+    blocks = states // VEC
     for c in range(2):
         inner = jnp.where(odd, nodes[1 - c][0], nodes[c][0])
         border = jnp.where(odd, nodes[1 - c][1], nodes[c][1])
         kept, sent = jnp.where(edge, border, inner), jnp.where(edge, inner, border)
-        for b in range(states // VEC):
-            packed_ref[b, c * VEC : (c + 1) * VEC, :] = kept[b * VEC : (b + 1) * VEC]
-            sent_ref[b, c * VEC : (c + 1) * VEC, :] = sent[b * VEC : (b + 1) * VEC]
-    for b in range(states // VEC):
+        for b in range(blocks):
+            rows = slice(b * VEC, (b + 1) * VEC)
+            kept_ref[blocks - 1 - b, c * VEC : (c + 1) * VEC, :] = kept[rows]
+            sent_ref[blocks - 1 - b, c * VEC : (c + 1) * VEC, :] = sent[rows]
+    for b in range(blocks):
         rows = slice(b * VEC, (b + 1) * VEC)
-        for ref in (packed_ref, sent_ref):
-            ref[b, 2 * VEC :, :] = jnp.zeros((VEC, size), jnp.float32)
-            ref[b, 2 * VEC :, 0:VEC] = gram[rows, rows]
+        for ref in (kept_ref, sent_ref):
+            ref[blocks - 1 - b, 2 * VEC :, :] = jnp.zeros((VEC, size), jnp.float32)
+            ref[blocks - 1 - b, 2 * VEC :, 0:VEC] = gram[rows, rows]
 
 
 def step(kind, u, name, h_ready, own, rim, *others):
@@ -192,7 +194,7 @@
         shapes.append((states, pl.cdiv(states, size) * size))
     elif kind == "last":
         blocks = states // VEC
-        shapes = [(2 * blocks, 3 * VEC, size), (blocks, 3 * VEC, size)]
+        shapes = [(blocks, 3 * VEC, size)] * 2
     operands = [*h_ready, *own, rim, *others]
     cost = pl.CostEstimate(
         flops=8 * BLOCKS * rows_out * states * size * size,
@@ -244,9 +246,11 @@
                 total = total + columns[d] * block[d : d + 1, :]
             mixed.append(total)
     half = flag(flags_ref, 2, mixed[0].shape)
-    for at, total in enumerate(mixed):
-        turned = mixed[(at + len(mixed) // 2) % len(mixed)]
-        out_ref[:, 0, at, :] = jnp.where(half, turned, total)
+    for w in range(wide):
+        for c in range(cols):
+            first = mixed[(wide - 1 - w) * cols + c]
+            second = mixed[(wide - 1 - w + wide // 2) % wide * cols + c]
+            out_ref[:, 0, w * cols + c, :] = jnp.where(half, second, first)
 
 
 def finish(flags, cols, node_count, parts, turn):
@@ -308,9 +312,9 @@
     zero[1] = after(zero[1], zero[0])
     far_rim, near_rim = over_far(zero[0]), over_near(zero[1])
     border = across(after(border, own_core))
-    inside = across(after(inside, zero[1]))
+    inside = across(after(inside, near_rim))
     h_two = [prepare("chip", codes, hblocks, h_core)]
-    border_core = core(after(border, (far_rim, near_rim, h_two)))
+    border_core = core(after(border, (far_rim, h_two)))
     h_three = h_two + [prepare("border", codes, border, border_core)]
 
     one = [step("first", 0, "one_0", h_three, zero, far_rim)]
@@ -333,12 +337,13 @@
     three.append(step("next", 1, "three_1", h_four, two, rim, before[1]))
     rims = over_far(three[0]), over_near(three[1])
     four = step("other", 0, "four_0", h_four, three, rims[0], two[0])
-    packed, sent = step("last", 1, "four_1", h_four, three, rims[1], two[1], *four, flags)
-
-    packed = lax.dynamic_update_slice(packed, core(sent), (sent.shape[0], 0, 0))
+    kept, sent = step("last", 1, "four_1", h_four, three, rims[1], two[1], *four, flags)
+
+    packed = jnp.concatenate([core(sent), kept])
     owners = wide // 2
     groups = [
-        [((i + owners * (g // 2 ^ g % 2)) % wide) * grp + g for i in range(wide)] for g in range(grp)
+        [((wide - 1 - i + owners * (g // 2 ^ g % 2)) % wide) * grp + g for i in range(wide)]
+        for g in range(grp)
     ]
     packed = lax.all_to_all(
         packed,

time: 66 us -> 63.5 us (0.962)
  waiting for transfers between devices: 18.4 us -> 15.5 us
  starting transfers between devices: 34.3 us -> 35.2 us
  Pallas kernels: 9.94 us -> 9.28 us
    all_to_all x1, waiting for transfers between devices: 7.03 us -> 4.07 us  [body(): lax.all_to_all(packed, ('wide', 'grp'), split_axis=0, concat_axis=0, tile...]
    all_to_all x1, starting transfers between devices: 5.33 us -> 6.8 us  [body(): lax.all_to_all(packed, ('wide', 'grp'), split_axis=0, concat_axis=0, tile...]
    ppermute x5, waiting for transfers between devices: 5.2 us -> 6.62 us  [across(): return lax.ppermute(value, 'grp', [(i, i ^ 3) for i in range(grp)])]
    ppermute x4, waiting for transfers between devices: 3.76 us -> 2.44 us  [over_near(): return lax.ppermute(value, 'wide', near)]
  transfers between devices with their start and end apart: 19 -> 19, of which waited for: 10 -> 11; matrix products, arithmetic and copies ran while one was open for 1% -> 1% of each run, Pallas kernels for 10% -> 11%
where the time goes in v2:
time: 63.5 us; the launch traced here: 63.1 us
  starting transfers between devices  35.2 us (55%)
  waiting for transfers between devices  15.5 us (24%)
  Pallas kernels  9.28 us (15%)
  local copies, waits for them, and re-layouts  2.06 us (3%)
  other arithmetic  0.8 us (1%)
    ppermute x4, starting transfers between devices, over_near(): return lax.ppermute(value, 'wide', near)  18.6 us
    all_to_all x1, starting transfers between devices, body(): lax.all_to_all(packed, ('wide', 'grp'), split_axis=0, concat_axis=0, tile...  6.8 us
    ppermute x5, waiting for transfers between devices, across(): return lax.ppermute(value, 'grp', [(i, i ^ 3) for i in range(grp)])  6.62 us
    ppermute x5, starting transfers between devices, across(): return lax.ppermute(value, 'grp', [(i, i ^ 3) for i in range(grp)])  6.07 us
    pallas_call x8, Pallas kernels, step(): pl.pallas_call(functools.partial(step_kernel, kind, u, len(h_ready)), in_...  5.32 us
    all_to_all x1, waiting for transfers between devices, body(): lax.all_to_all(packed, ('wide', 'grp'), split_axis=0, concat_axis=0, tile...  4.07 us
    ppermute x4, starting transfers between devices, over_far(): return lax.ppermute(value, 'wide', far)  2.66 us
    ppermute x4, waiting for transfers between devices, over_near(): return lax.ppermute(value, 'wide', near)  2.44 us
  transfers between devices with their start and end apart: 19, of which 11 were waited for; matrix products, arithmetic and copies ran while one was open for 1% of the time, Pallas kernels for 11%

profile of v2, /device:TPU:0, one launch (start us, length us, event | category | flops | bytes accessed | tf_op | source)
XLA Modules:
  0.0 63.1 jit_solution(12857483855624931901)
XLA Ops:
  0.0 0.5 collective-permute-start.1
  0.5 0.1 pad_add_fusion
  0.6 0.1 broadcast_in_dim.11
  0.8 0.8 %copy-done.2 = f32[64,1,2,128]{3,2,1,0:T(2,128)S(1)} copy-done((f32[64,1,2,128]{3,2,1,0:T(2,128)S(1)}, f32[64,1,2,128]{3,2,1,0:T(2,128)}, u32[]{:S(2)}) %copy-start.2) | copy-done | bytes 65560
  1.6 0.7 %copy-done.3 = s32[1,2,5]{2,1,0:T(2,128)S(1)} copy-done((s32[1,2,5]{2,1,0:T(2,128)S(1)}, s32[1,2,5]{2,1,0:T(2,128)}, u32[]{:S(2)}) %copy-start.3) | copy-done | bytes 64
  2.4 0.1 collective-permute-start
  2.5 1.1 %collective-permute-done = f32[72,128]{1,0:T(8,128)S(1)} collective-permute-done((f32[72,128]{1,0:T(8,128)S(1)}, f32[72,128]{1,0:T(8,128)S(1)}, u32[]{:S(2)}, u32[]{:S(2)}) %collective-permute-start) | collective-permute-done | bytes 36896 | tf_op jit(solution)/shard_map/ppermute | solution.py:288
  3.7 0.1 pick.1
  3.8 2.7 %collective-permute-start.2 = (f32[2,72,128]{2,1,0:T(8,128)S(1)}, f32[2,72,128]{2,1,0:T(8,128)S(1)}, u32[]{:S(2)}, u32[]{:S(2)}) collective-permute-start(f32[2,72,128]{2,1,0:T(8,128)S(1)} %pad_maximum_fusion.1), channel_id=1, source_target_pairs={{0,3},{1,2},{2,1},{3,0},{4,7},{5,6},{6,5},{7,4},{8,11},{9,10},{10,... | collective-permute-start | bytes 221192 | tf_op jit(solution)/shard_map/ppermute | solution.py:285
  6.4 0.1 collective-permute-start.3
  6.5 2.5 %collective-permute-done.2 = f32[2,72,128]{2,1,0:T(8,128)S(1)} collective-permute-done((f32[2,72,128]{2,1,0:T(8,128)S(1)}, f32[2,72,128]{2,1,0:T(8,128)S(1)}, u32[]{:S(2)}, u32[]{:S(2)}) %collective-permute-start.2) | collective-permute-done | bytes 73760 | tf_op jit(solution)/shard_map/ppermute | solution.py:285
  9.0 0.7 %collective-permute-start.4 = (f32[4,32,128]{2,1,0:T(8,128)S(1)}, f32[4,32,128]{2,1,0:T(8,128)S(1)}, u32[]{:S(2)}, u32[]{:S(2)}) collective-permute-start(f32[4,32,128]{2,1,0:T(8,128)S(1)} %maximum_select_fusion.refs_2_.refs_4_), channel_id=1, source_target_pairs={{4,8},{8,4},{12,16},{16,12},{20,24},{24,20},{5,9},{9,5},{13,17},{1... | collective-permute-start | bytes 196616 | tf_op jit(solution)/shard_map/ppermute | solution.py:291
  9.7 4.4 %collective-permute-start.6 = (f32[4,32,128]{2,1,0:T(8,128)S(1)}, f32[4,32,128]{2,1,0:T(8,128)S(1)}, u32[]{:S(2)}, u32[]{:S(2)}) collective-permute-start(f32[4,32,128]{2,1,0:T(8,128)S(1)} %maximum_select_fusion.1.refs_3_.refs_4_), channel_id=1, source_target_pairs={{0,4},{4,0},{8,12},{12,8},{16,20},{20,16},{24,28},{28,24},{1,5},{5... | collective-permute-start | bytes 196616 | tf_op jit(solution)/shard_map/ppermute | solution.py:294
  14.2 0.1 convert_element_type.8
  14.3 0.1 concatenate.25.codes_ref
  14.3 0.9 %prepare_chip.1.refs_0_ = bf16[2,2,256,1152]{3,2,1,0:T(8,128)(2,1)S(1)} custom-call(s32[44]{0:T(128)S(1)} %concatenate.25.codes_ref, f32[1,2,5,128,128]{4,3,2,1,0:T(8,128)S(1)} %copy-done.1, f32[1,2,5,128,128]{4,3,2,1,0:T(8,128)S(1)} %collective-permute-done.1.core_ref.refs_1_), custom_call_target="tpu_custom_call" | custom-call | tf_op jit(solution)/shard_map/prepare_chip/pallas_call | solution.py:114
  15.3 0.8 %collective-permute-done.3.refs_0_ = f32[1,1,5,128,128]{4,3,2,1,0:T(8,128)S(1)} collective-permute-done((f32[1,1,5,128,128]{4,3,2,1,0:T(8,128)S(1)}, f32[1,1,5,128,128]{4,3,2,1,0:T(8,128)S(1)}, u32[]{:S(2)}, u32[]{:S(2)}) %collective-permute-start.3) | collective-permute-done | bytes 327712 | tf_op jit(solution)/shard_map/ppermute | solution.py:285
  16.1 0.5 collective-permute-start.5
  16.5 0.5 collective-permute-done.6.refs_4_
  17.1 1.4 %collective-permute-start.7 = (f32[1,1,5,128,128]{4,3,2,1,0:T(8,128)S(1)}, f32[1,1,5,128,128]{4,3,2,1,0:T(8,128)S(1)}, u32[]{:S(2)}, u32[]{:S(2)}) collective-permute-start(f32[1,1,5,128,128]{4,3,2,1,0:T(8,128)S(1)} %get-tuple-element.27), channel_id=1, source_target_pairs={{0,3},{1,2},{2,1},{3,0},{4,7},{5,6},{6,5},{7,4},{8,11},{9,10},{10,... | collective-permute-start | bytes 983048 | tf_op jit(solution)/shard_map/ppermute | solution.py:285
  18.5 0.7 %prepare_border.1.refs_1_ = bf16[1,2,256,1152]{3,2,1,0:T(8,128)(2,1)S(1)} custom-call(s32[44]{0:T(128)S(1)} %concatenate.25.codes_ref, f32[1,1,5,128,128]{4,3,2,1,0:T(8,128)S(1)} %collective-permute-done.3.refs_0_, f32[1,1,5,128,128]{4,3,2,1,0:T(8,128)S(1)} %collective-permute-done.5.refs_1_), custom_call_target="tpu_custom_call" | custom-call | tf_op jit(solution)/shard_map/prepare_border/pallas_call | solution.py:114
  19.2 0.6 one_0.1.refs_1_
  19.8 0.7 %collective-permute-start.8 = (f32[3,32,128]{2,1,0:T(8,128)S(1)}, f32[3,32,128]{2,1,0:T(8,128)S(1)}, u32[]{:S(2)}, u32[]{:S(2)}) collective-permute-start(f32[3,32,128]{2,1,0:T(8,128)S(1)} %one_0.1.refs_1_), channel_id=1, source_target_pairs={{4,8},{8,4},{12,16},{16,12},{20,24},{24,20},{5,9},{9,5},{13,17},{1... | collective-permute-start | bytes 147464 | tf_op jit(solution)/shard_map/ppermute | solution.py:291
  20.5 0.6 one_1.1.refs_2_
  21.1 5.3 %collective-permute-start.11 = (f32[3,32,128]{2,1,0:T(8,128)S(1)}, f32[3,32,128]{2,1,0:T(8,128)S(1)}, u32[]{:S(2)}, u32[]{:S(2)}) collective-permute-start(f32[3,32,128]{2,1,0:T(8,128)S(1)} %one_1.1.refs_2_), channel_id=1, source_target_pairs={{0,4},{4,0},{8,12},{12,8},{16,20},{20,16},{24,28},{28,24},{1,5},{5... | collective-permute-start | bytes 147464 | tf_op jit(solution)/shard_map/ppermute | solution.py:294
  26.4 0.4 collective-permute-done.7.refs_0_
  26.8 0.4 two_0.1
  27.3 1.8 %collective-permute-start.9 = (f32[3,32,128]{2,1,0:T(8,128)S(1)}, f32[3,32,128]{2,1,0:T(8,128)S(1)}, u32[]{:S(2)}, u32[]{:S(2)}) collective-permute-start(f32[3,32,128]{2,1,0:T(8,128)S(1)} %pad_maximum_fusion.6), channel_id=1, source_target_pairs={{0,3},{1,2},{2,1},{3,0},{4,7},{5,6},{6,5},{7,4},{8,11},{9,10},{10,... | collective-permute-start | bytes 147464 | tf_op jit(solution)/shard_map/ppermute | solution.py:285
  29.1 0.4 two_1.1
  29.5 0.1 collective-permute-start.12
  29.6 1.6 %collective-permute-done.9 = f32[3,32,128]{2,1,0:T(8,128)S(1)} collective-permute-done((f32[3,32,128]{2,1,0:T(8,128)S(1)}, f32[3,32,128]{2,1,0:T(8,128)S(1)}, u32[]{:S(2)}, u32[]{:S(2)}) %collective-permute-start.9) | collective-permute-done | bytes 49184 | tf_op jit(solution)/shard_map/ppermute | solution.py:285
  31.2 0.7 %collective-permute-start.13 = (f32[4,32,128]{2,1,0:T(8,128)S(1)}, f32[4,32,128]{2,1,0:T(8,128)S(1)}, u32[]{:S(2)}, u32[]{:S(2)}) collective-permute-start(f32[4,32,128]{2,1,0:T(8,128)S(1)} %pad_maximum_fusion.2.refs_3_.refs_6_), channel_id=1, source_target_pairs={{4,8},{8,4},{12,16},{16,12},{20,24},{24,20},{5,9},{9,5},{13,17},{1... | collective-permute-start | bytes 196616 | tf_op jit(solution)/shard_map/ppermute | solution.py:291
  32.0 1.3 %collective-permute-done.12 = f32[3,32,128]{2,1,0:T(8,128)S(1)} collective-permute-done((f32[3,32,128]{2,1,0:T(8,128)S(1)}, f32[3,32,128]{2,1,0:T(8,128)S(1)}, u32[]{:S(2)}, u32[]{:S(2)}) %collective-permute-start.12) | collective-permute-done | bytes 49184 | tf_op jit(solution)/shard_map/ppermute | solution.py:285
  33.3 3.9 %collective-permute-start.14 = (f32[4,32,128]{2,1,0:T(8,128)S(1)}, f32[4,32,128]{2,1,0:T(8,128)S(1)}, u32[]{:S(2)}, u32[]{:S(2)}) collective-permute-start(f32[4,32,128]{2,1,0:T(8,128)S(1)} %pad_maximum_fusion.3.refs_4_.refs_6_), channel_id=1, source_target_pairs={{0,4},{4,0},{8,12},{12,8},{16,20},{20,16},{24,28},{28,24},{1,5},{5... | collective-permute-start | bytes 196616 | tf_op jit(solution)/shard_map/ppermute | solution.py:294
  37.2 0.7 %prepare_inner.1.refs_2_ = bf16[1,2,256,1152]{3,2,1,0:T(8,128)(2,1)S(1)} custom-call(s32[44]{0:T(128)S(1)} %concatenate.25.codes_ref, f32[1,1,5,128,128]{4,3,2,1,0:T(8,128)S(1)} %collective-permute-done.7.refs_0_, f32[1,1,5,128,128]{4,3,2,1,0:T(8,128)S(1)} %collective-permute-done.10.refs_1_), custom_call_target="tpu_custom_call" | custom-call | tf_op jit(solution)/shard_map/prepare_inner/pallas_call | solution.py:114
  37.9 0.7 %three_0.1.refs_3_ = f32[4,32,128]{2,1,0:T(8,128)S(1)} custom-call(bf16[2,2,256,1152]{3,2,1,0:T(8,128)(2,1)S(1)} %prepare_chip.1.refs_0_, bf16[1,2,256,1152]{3,2,1,0:T(8,128)(2,1)S(1)} %prepare_border.1.refs_1_, bf16[1,2,256,1152]{3,2,1,0:T(8,128)(2,1)S(1)} %prepare_inner.1.refs_2_, f32[4,32,128]{2,1,0:T(8,128)S(1)} %pad_maximum_fusion.2.refs_3_.refs_6_, ...), custom_call_target="tpu_custom_call" | custom-call | flops 150994944 | bytes 2359296 | tf_op jit(solution)/shard_map/three_0/pallas_call | solution.py:204
  38.6 0.7 %collective-permute-start.16 = (f32[4,32,128]{2,1,0:T(8,128)S(1)}, f32[4,32,128]{2,1,0:T(8,128)S(1)}, u32[]{:S(2)}, u32[]{:S(2)}) collective-permute-start(f32[4,32,128]{2,1,0:T(8,128)S(1)} %three_0.1.refs_3_), channel_id=1, source_target_pairs={{4,8},{8,4},{12,16},{16,12},{20,24},{24,20},{5,9},{9,5},{13,17},{1... | collective-permute-start | bytes 196616 | tf_op jit(solution)/shard_map/ppermute | solution.py:291
  39.3 0.6 collective-permute-done.14.refs_5_
  39.9 0.7 %three_1.1.refs_4_ = f32[4,32,128]{2,1,0:T(8,128)S(1)} custom-call(bf16[2,2,256,1152]{3,2,1,0:T(8,128)(2,1)S(1)} %prepare_chip.1.refs_0_, bf16[1,2,256,1152]{3,2,1,0:T(8,128)(2,1)S(1)} %prepare_border.1.refs_1_, bf16[1,2,256,1152]{3,2,1,0:T(8,128)(2,1)S(1)} %prepare_inner.1.refs_2_, f32[4,32,128]{2,1,0:T(8,128)S(1)} %pad_maximum_fusion.2.refs_3_.refs_6_, ...), custom_call_target="tpu_custom_call" | custom-call | flops 150994944 | bytes 2359296 | tf_op jit(solution)/shard_map/three_1/pallas_call | solution.py:204
  40.6 5.0 %collective-permute-start.15 = (f32[4,32,128]{2,1,0:T(8,128)S(1)}, f32[4,32,128]{2,1,0:T(8,128)S(1)}, u32[]{:S(2)}, u32[]{:S(2)}) collective-permute-start(f32[4,32,128]{2,1,0:T(8,128)S(1)} %three_1.1.refs_4_), channel_id=1, source_target_pairs={{0,4},{4,0},{8,12},{12,8},{16,20},{20,16},{24,28},{28,24},{1,5},{5... | collective-permute-start | bytes 196616 | tf_op jit(solution)/shard_map/ppermute | solution.py:294
  45.6 0.9 %four_0.1 = (f32[4,32,128]{2,1,0:T(8,128)S(1)}, f32[32,128]{1,0:T(8,128)S(1)}) custom-call(bf16[2,2,256,1152]{3,2,1,0:T(8,128)(2,1)S(1)} %prepare_chip.1.refs_0_, bf16[1,2,256,1152]{3,2,1,0:T(8,128)(2,1)S(1)} %prepare_border.1.refs_1_, bf16[1,2,256,1152]{3,2,1,0:T(8,128)(2,1)S(1)} %prepare_inner.1.refs_2_, f32[4,32,128]{2,1,0:T(8,128)S(1)} %three_0.1.refs_3_, ...), custom_call_target="tpu_custom_call" | custom-call | flops 150994944 | bytes 2359296 | tf_op jit(solution)/shard_map/four_0/pallas_call | solution.py:204
  46.5 1.3 %collective-permute-done.15.refs_5_ = f32[4,32,128]{2,1,0:T(8,128)S(1)} collective-permute-done((f32[4,32,128]{2,1,0:T(8,128)S(1)}, f32[4,32,128]{2,1,0:T(8,128)S(1)}, u32[]{:S(2)}, u32[]{:S(2)}) %collective-permute-start.15) | collective-permute-done | bytes 65568 | tf_op jit(solution)/shard_map/ppermute | solution.py:294
  47.8 1.0 %four_1.1 = (f32[4,24,128]{2,1,0:T(8,128)S(1)}, f32[4,24,128]{2,1,0:T(8,128)S(1)}) custom-call(bf16[2,2,256,1152]{3,2,1,0:T(8,128)(2,1)S(1)} %prepare_chip.1.refs_0_, bf16[1,2,256,1152]{3,2,1,0:T(8,128)(2,1)S(1)} %prepare_border.1.refs_1_, bf16[1,2,256,1152]{3,2,1,0:T(8,128)(2,1)S(1)} %prepare_inner.1.refs_2_, f32[4,32,128]{2,1,0:T(8,128)S(1)} %three_0.1.refs_3_, ...), custom_call_target="tpu_custom_call" | custom-call | flops 150994944 | bytes 2359296 | tf_op jit(solution)/shard_map/four_1/pallas_call | solution.py:204
  48.9 1.2 %collective-permute-done.17 = f32[4,24,128]{2,1,0:T(8,128)S(1)} collective-permute-done((f32[4,24,128]{2,1,0:T(8,128)S(1)}, f32[4,24,128]{2,1,0:T(8,128)S(1)}, u32[]{:S(2)}, u32[]{:S(2)}) %collective-permute-start.17) | collective-permute-done | bytes 49184 | tf_op jit(solution)/shard_map/ppermute | solution.py:288
  50.1 0.6 %pad_maximum_fusion = f32[8,24,128]{2,1,0:T(8,128)} fusion(f32[4,24,128]{2,1,0:T(8,128)S(1)} %get-tuple-element.36, f32[4,24,128]{2,1,0:T(8,128)S(1)} %collective-permute-done.17), kind=kLoop, calls=%fused_computation | loop fusion | flops 24576 | bytes 196608 | tf_op jit(solution)/shard_map/concatenate | solution.py:342
  50.7 6.8 %all-to-all-start = ((f32[8,24,128]{2,1,0:T(8,128)}), f32[8,24,128]{2,1,0:T(8,128)S(1)}, u32[]{:S(2)}, u32[]{:S(2)}) async-start(f32[8,24,128]{2,1,0:T(8,128)} %pad_maximum_fusion), calls=%async_computation | async-start | bytes 196608 | tf_op jit(solution)/shard_map/all_to_all | solution.py:348
  57.6 4.1 %all-to-all-done.parts_ref = f32[8,24,128]{2,1,0:T(8,128)S(1)} async-done(((f32[8,24,128]{2,1,0:T(8,128)}), f32[8,24,128]{2,1,0:T(8,128)S(1)}, u32[]{:S(2)}, u32[]{:S(2)}) %all-to-all-start) | async-done | bytes 98336 | tf_op jit(solution)/shard_map/all_to_all | solution.py:348
  61.7 1.5 %finish.1 = f32[8,1,16,128]{3,2,1,0:T(8,128)} custom-call(s32[32,128]{1,0:T(8,128)S(1)} %broadcast_in_dim.12.flags_ref.refs_9_, f32[8,24,128]{2,1,0:T(8,128)S(1)} %all-to-all-done.parts_ref, f32[8,8]{1,0:T(8,128)S(1)} %bitcast.27), custom_call_target="tpu_custom_call" | custom-call | tf_op jit(solution)/shard_map/finish/pallas_call | solution.py:258
  (44 shorter events, 0.5 us)
Async XLA Ops:
  0.0 57.5 %copy-start = (f32[8,8,8]{2,1,0:T(8,128)S(1)}, f32[8,8,8]{2,1,0:T(8,128)}, u32[]{:S(2)}) copy-start(f32[8,8,8]{2,1,0:T(8,128)} %param.7) | copy-start | bytes 6148
  0.0 3.7 %copy-start.1 = (f32[1,2,5,128,128]{4,3,2,1,0:T(8,128)S(1)}, f32[1,2,5,128,128]{4,3,2,1,0:T(8,128)}, u32[]{:S(2)}) copy-start(f32[1,2,5,128,128]{4,3,2,1,0:T(8,128)} %refs_0_.1) | copy-start | bytes 1966084
  0.0 3.6 %collective-permute-start.1 = (f32[1,2,5,128,128]{4,3,2,1,0:T(8,128)}, f32[1,2,5,128,128]{4,3,2,1,0:T(8,128)S(1)}, u32[]{:S(2)}, u32[]{:S(2)}) collective-permute-start(f32[1,2,5,128,128]{4,3,2,1,0:T(8,128)} %refs_0_.1), channel_id=1, source_target_pairs={{0,1},{1,0},{2,3},{3,2},{4,5},{5,4},{6,7},{7,6},{8,9},{9,8},{10,11... | collective-permute-start | bytes 1966088 | tf_op jit(solution)/shard_map/ppermute | solution.py:288
  0.8 0.8 %copy-start.2 = (f32[64,1,2,128]{3,2,1,0:T(2,128)S(1)}, f32[64,1,2,128]{3,2,1,0:T(2,128)}, u32[]{:S(2)}) copy-start(f32[64,1,2,128]{3,2,1,0:T(2,128)} %slab_ref.1) | copy-start | bytes 196612
  1.6 0.7 %copy-start.3 = (s32[1,2,5]{2,1,0:T(2,128)S(1)}, s32[1,2,5]{2,1,0:T(2,128)}, u32[]{:S(2)}) copy-start(s32[1,2,5]{2,1,0:T(2,128)} %codes_ref.1) | copy-start | bytes 124
  2.4 1.3 %collective-permute-start = (f32[72,128]{1,0:T(8,128)S(1)}, f32[72,128]{1,0:T(8,128)S(1)}, u32[]{:S(2)}, u32[]{:S(2)}) collective-permute-start(f32[72,128]{1,0:T(8,128)S(1)} %get-tuple-element.46), channel_id=1, source_target_pairs={{0,1},{1,0},{2,3},{3,2},{4,5},{5,4},{6,7},{7,6},{8,9},{9,8},{10,11... | collective-permute-start | bytes 110600 | tf_op jit(solution)/shard_map/ppermute | solution.py:288
  3.8 5.3 %collective-permute-start.2 = (f32[2,72,128]{2,1,0:T(8,128)S(1)}, f32[2,72,128]{2,1,0:T(8,128)S(1)}, u32[]{:S(2)}, u32[]{:S(2)}) collective-permute-start(f32[2,72,128]{2,1,0:T(8,128)S(1)} %pad_maximum_fusion.1), channel_id=1, source_target_pairs={{0,3},{1,2},{2,1},{3,0},{4,7},{5,6},{6,5},{7,4},{8,11},{9,10},{10,... | collective-permute-start | bytes 221192 | tf_op jit(solution)/shard_map/ppermute | solution.py:285
  6.4 9.7 %collective-permute-start.3 = (f32[1,1,5,128,128]{4,3,2,1,0:T(8,128)S(1)}, f32[1,1,5,128,128]{4,3,2,1,0:T(8,128)S(1)}, u32[]{:S(2)}, u32[]{:S(2)}) collective-permute-start(f32[1,1,5,128,128]{4,3,2,1,0:T(8,128)S(1)} %get-tuple-element.23), channel_id=1, source_target_pairs={{0,3},{1,2},{2,1},{3,0},{4,7},{5,6},{6,5},{7,4},{8,11},{9,10},{10,... | collective-permute-start | bytes 983048 | tf_op jit(solution)/shard_map/ppermute | solution.py:285
  9.0 6.2 %collective-permute-start.4 = (f32[4,32,128]{2,1,0:T(8,128)S(1)}, f32[4,32,128]{2,1,0:T(8,128)S(1)}, u32[]{:S(2)}, u32[]{:S(2)}) collective-permute-start(f32[4,32,128]{2,1,0:T(8,128)S(1)} %maximum_select_fusion.refs_2_.refs_4_), channel_id=1, source_target_pairs={{4,8},{8,4},{12,16},{16,12},{20,24},{24,20},{5,9},{9,5},{13,17},{1... | collective-permute-start | bytes 196616 | tf_op jit(solution)/shard_map/ppermute | solution.py:291
  9.7 7.3 %collective-permute-start.6 = (f32[4,32,128]{2,1,0:T(8,128)S(1)}, f32[4,32,128]{2,1,0:T(8,128)S(1)}, u32[]{:S(2)}, u32[]{:S(2)}) collective-permute-start(f32[4,32,128]{2,1,0:T(8,128)S(1)} %maximum_select_fusion.1.refs_3_.refs_4_), channel_id=1, source_target_pairs={{0,4},{4,0},{8,12},{12,8},{16,20},{20,16},{24,28},{28,24},{1,5},{5... | collective-permute-start | bytes 196616 | tf_op jit(solution)/shard_map/ppermute | solution.py:294
  16.1 2.4 %collective-permute-start.5 = (f32[1,1,5,128,128]{4,3,2,1,0:T(8,128)S(1)}, f32[1,1,5,128,128]{4,3,2,1,0:T(8,128)S(1)}, u32[]{:S(2)}, u32[]{:S(2)}) collective-permute-start(f32[1,1,5,128,128]{4,3,2,1,0:T(8,128)S(1)} %collective-permute-done.3.refs_0_), channel_id=1, source_target_pairs={{0,1},{1,0},{2,3},{3,2},{4,5},{5,4},{6,7},{7,6},{8,9},{9,8},{10,11... | collective-permute-start | bytes 983048 | tf_op jit(solution)/shard_map/ppermute | solution.py:288
  17.1 9.7 %collective-permute-start.7 = (f32[1,1,5,128,128]{4,3,2,1,0:T(8,128)S(1)}, f32[1,1,5,128,128]{4,3,2,1,0:T(8,128)S(1)}, u32[]{:S(2)}, u32[]{:S(2)}) collective-permute-start(f32[1,1,5,128,128]{4,3,2,1,0:T(8,128)S(1)} %get-tuple-element.27), channel_id=1, source_target_pairs={{0,3},{1,2},{2,1},{3,0},{4,7},{5,6},{6,5},{7,4},{8,11},{9,10},{10,... | collective-permute-start | bytes 983048 | tf_op jit(solution)/shard_map/ppermute | solution.py:285
  19.8 7.0 %collective-permute-start.8 = (f32[3,32,128]{2,1,0:T(8,128)S(1)}, f32[3,32,128]{2,1,0:T(8,128)S(1)}, u32[]{:S(2)}, u32[]{:S(2)}) collective-permute-start(f32[3,32,128]{2,1,0:T(8,128)S(1)} %one_0.1.refs_1_), channel_id=1, source_target_pairs={{4,8},{8,4},{12,16},{16,12},{20,24},{24,20},{5,9},{9,5},{13,17},{1... | collective-permute-start | bytes 147464 | tf_op jit(solution)/shard_map/ppermute | solution.py:291
  21.1 8.0 %collective-permute-start.11 = (f32[3,32,128]{2,1,0:T(8,128)S(1)}, f32[3,32,128]{2,1,0:T(8,128)S(1)}, u32[]{:S(2)}, u32[]{:S(2)}) collective-permute-start(f32[3,32,128]{2,1,0:T(8,128)S(1)} %one_1.1.refs_2_), channel_id=1, source_target_pairs={{0,4},{4,0},{8,12},{12,8},{16,20},{20,16},{24,28},{28,24},{1,5},{5... | collective-permute-start | bytes 147464 | tf_op jit(solution)/shard_map/ppermute | solution.py:294
  27.3 3.9 %collective-permute-start.9 = (f32[3,32,128]{2,1,0:T(8,128)S(1)}, f32[3,32,128]{2,1,0:T(8,128)S(1)}, u32[]{:S(2)}, u32[]{:S(2)}) collective-permute-start(f32[3,32,128]{2,1,0:T(8,128)S(1)} %pad_maximum_fusion.6), channel_id=1, source_target_pairs={{0,3},{1,2},{2,1},{3,0},{4,7},{5,6},{6,5},{7,4},{8,11},{9,10},{10,... | collective-permute-start | bytes 147464 | tf_op jit(solution)/shard_map/ppermute | solution.py:285
  29.5 3.8 %collective-permute-start.12 = (f32[3,32,128]{2,1,0:T(8,128)S(1)}, f32[3,32,128]{2,1,0:T(8,128)S(1)}, u32[]{:S(2)}, u32[]{:S(2)}) collective-permute-start(f32[3,32,128]{2,1,0:T(8,128)S(1)} %pad_maximum_fusion.7), channel_id=1, source_target_pairs={{0,3},{1,2},{2,1},{3,0},{4,7},{5,6},{6,5},{7,4},{8,11},{9,10},{10,... | collective-permute-start | bytes 147464 | tf_op jit(solution)/shard_map/ppermute | solution.py:285
  31.2 6.7 %collective-permute-start.13 = (f32[4,32,128]{2,1,0:T(8,128)S(1)}, f32[4,32,128]{2,1,0:T(8,128)S(1)}, u32[]{:S(2)}, u32[]{:S(2)}) collective-permute-start(f32[4,32,128]{2,1,0:T(8,128)S(1)} %pad_maximum_fusion.2.refs_3_.refs_6_), channel_id=1, source_target_pairs={{4,8},{8,4},{12,16},{16,12},{20,24},{24,20},{5,9},{9,5},{13,17},{1... | collective-permute-start | bytes 196616 | tf_op jit(solution)/shard_map/ppermute | solution.py:291
  31.9 5.3 %collective-permute-start.10 = (f32[1,1,5,128,128]{4,3,2,1,0:T(8,128)S(1)}, f32[1,1,5,128,128]{4,3,2,1,0:T(8,128)S(1)}, u32[]{:S(2)}, u32[]{:S(2)}) collective-permute-start(f32[1,1,5,128,128]{4,3,2,1,0:T(8,128)S(1)} %collective-permute-done.7.refs_0_), channel_id=1, source_target_pairs={{0,1},{1,0},{2,3},{3,2},{4,5},{5,4},{6,7},{7,6},{8,9},{9,8},{10,11... | collective-permute-start | bytes 983048 | tf_op jit(solution)/shard_map/ppermute | solution.py:288
  33.3 6.6 %collective-permute-start.14 = (f32[4,32,128]{2,1,0:T(8,128)S(1)}, f32[4,32,128]{2,1,0:T(8,128)S(1)}, u32[]{:S(2)}, u32[]{:S(2)}) collective-permute-start(f32[4,32,128]{2,1,0:T(8,128)S(1)} %pad_maximum_fusion.3.refs_4_.refs_6_), channel_id=1, source_target_pairs={{0,4},{4,0},{8,12},{12,8},{16,20},{20,16},{24,28},{28,24},{1,5},{5... | collective-permute-start | bytes 196616 | tf_op jit(solution)/shard_map/ppermute | solution.py:294
  38.6 7.0 %collective-permute-start.16 = (f32[4,32,128]{2,1,0:T(8,128)S(1)}, f32[4,32,128]{2,1,0:T(8,128)S(1)}, u32[]{:S(2)}, u32[]{:S(2)}) collective-permute-start(f32[4,32,128]{2,1,0:T(8,128)S(1)} %three_0.1.refs_3_), channel_id=1, source_target_pairs={{4,8},{8,4},{12,16},{16,12},{20,24},{24,20},{5,9},{9,5},{13,17},{1... | collective-permute-start | bytes 196616 | tf_op jit(solution)/shard_map/ppermute | solution.py:291
  40.6 7.2 %collective-permute-start.15 = (f32[4,32,128]{2,1,0:T(8,128)S(1)}, f32[4,32,128]{2,1,0:T(8,128)S(1)}, u32[]{:S(2)}, u32[]{:S(2)}) collective-permute-start(f32[4,32,128]{2,1,0:T(8,128)S(1)} %three_1.1.refs_4_), channel_id=1, source_target_pairs={{0,4},{4,0},{8,12},{12,8},{16,20},{20,16},{24,28},{28,24},{1,5},{5... | collective-permute-start | bytes 196616 | tf_op jit(solution)/shard_map/ppermute | solution.py:294
  48.8 1.3 %collective-permute-start.17 = (f32[4,24,128]{2,1,0:T(8,128)S(1)}, f32[4,24,128]{2,1,0:T(8,128)S(1)}, u32[]{:S(2)}, u32[]{:S(2)}) collective-permute-start(f32[4,24,128]{2,1,0:T(8,128)S(1)} %get-tuple-element.35), channel_id=1, source_target_pairs={{0,1},{1,0},{2,3},{3,2},{4,5},{5,4},{6,7},{7,6},{8,9},{9,8},{10,11... | collective-permute-start | bytes 147464 | tf_op jit(solution)/shard_map/ppermute | solution.py:288
  50.7 10.9 %all-to-all-start = ((f32[8,24,128]{2,1,0:T(8,128)}), f32[8,24,128]{2,1,0:T(8,128)S(1)}, u32[]{:S(2)}, u32[]{:S(2)}) async-start(f32[8,24,128]{2,1,0:T(8,128)} %pad_maximum_fusion), calls=%async_computation | async-start | bytes 196608 | tf_op jit(solution)/shard_map/all_to_all | solution.py:348

commit v3 on v2

--- a/solution.py
+++ b/solution.py
@@ -224,14 +224,13 @@
     gram = gram / node_count
     row = lax.broadcasted_iota(jnp.int32, (VEC, VEC), 0)
     col = lax.broadcasted_iota(jnp.int32, (VEC, VEC), 1)
-    inverse = jnp.where(row == col, 1.0, 0.0).astype(jnp.float32)
-    for k in range(VEC):
-        scale = 1.0 / jnp.sqrt(gram[k : k + 1, k : k + 1])
-        top = gram[k : k + 1, :] * scale
-        top_inverse = inverse[k : k + 1, :] * scale
-        factor = gram[:, k : k + 1] * scale
-        gram = gram - factor * top
-        inverse = jnp.where(row == k, top_inverse, jnp.where(row > k, inverse - factor * top_inverse, inverse))
+    both = jnp.concatenate([gram, jnp.where(row == col, 1.0, 0.0).astype(jnp.float32)], axis=1)
+    below = lax.broadcasted_iota(jnp.int32, both.shape, 0)
+    for k in range(VEC - 1):
+        factor = both[:, k : k + 1] * (1.0 / both[k : k + 1, k : k + 1])
+        both = jnp.where(below > k, both - factor * both[k : k + 1, :], both)
+    pivots = jnp.sum(jnp.where(row == col, both[:, :VEC], 0.0), axis=1, keepdims=True)
+    inverse = both[:, VEC:] * (1.0 / jnp.sqrt(pivots))
     turn = rot_ref[...]
     mixer = turn[:, 0:1] * inverse[0:1, :]
     for k in range(1, VEC):
@@ -309,11 +308,11 @@
         border_core = jnp.stack([parts[m] for m in (0, 1, 3, 2)])
         zero.append(jnp.where(edge == 1, border_mine, border_core))
 
-    zero[1] = after(zero[1], zero[0])
+    zero[0] = after(zero[0], zero[1])
     far_rim, near_rim = over_far(zero[0]), over_near(zero[1])
     border = across(after(border, own_core))
-    inside = across(after(inside, near_rim))
-    h_two = [prepare("chip", codes, hblocks, h_core)]
+    inside = across(after(inside, border))
+    h_two = [prepare("chip", after(codes, near_rim), hblocks, h_core)]
     border_core = core(after(border, (far_rim, h_two)))
     h_three = h_two + [prepare("border", codes, border, border_core)]
 

time: 63.5 us -> 64 us (level)
  waiting for transfers between devices: 15.5 us -> 18 us
  starting transfers between devices: 35.2 us -> 33.2 us
    ppermute x4, waiting for transfers between devices: 2.44 us -> 4.84 us  [over_near(): return lax.ppermute(value, 'wide', near)]
    ppermute x4, starting transfers between devices: 18.6 us -> 17.7 us  [over_near(): return lax.ppermute(value, 'wide', near)]
    ppermute x5, starting transfers between devices: 6.07 us -> 5.23 us  [across(): return lax.ppermute(value, 'grp', [(i, i ^ 3) for i in range(grp)])]
where the time goes in v3:
time: 64 us; the launch traced here: 63.6 us
  starting transfers between devices  33.2 us (52%)
  waiting for transfers between devices  18 us (28%)
  Pallas kernels  9.3 us (15%)
  local copies, waits for them, and re-layouts  2.06 us (3%)
  other arithmetic  0.79 us (1%)
    ppermute x4, starting transfers between devices, over_near(): return lax.ppermute(value, 'wide', near)  17.7 us
    all_to_all x1, starting transfers between devices, body(): lax.all_to_all(packed, ('wide', 'grp'), split_axis=0, concat_axis=0, tile...  6.72 us
    ppermute x5, waiting for transfers between devices, across(): return lax.ppermute(value, 'grp', [(i, i ^ 3) for i in range(grp)])  6.69 us
    pallas_call x8, Pallas kernels, step(): pl.pallas_call(functools.partial(step_kernel, kind, u, len(h_ready)), in_...  5.33 us
    ppermute x5, starting transfers between devices, across(): return lax.ppermute(value, 'grp', [(i, i ^ 3) for i in range(grp)])  5.23 us
    ppermute x4, waiting for transfers between devices, over_near(): return lax.ppermute(value, 'wide', near)  4.84 us
    all_to_all x1, waiting for transfers between devices, body(): lax.all_to_all(packed, ('wide', 'grp'), split_axis=0, concat_axis=0, tile...  4.09 us
    ppermute x4, starting transfers between devices, over_far(): return lax.ppermute(value, 'wide', far)  2.66 us
  transfers between devices with their start and end apart: 19, of which 11 were waited for; matrix products, arithmetic and copies ran while one was open for 1% of the time, Pallas kernels for 11%

profile of v3, /device:TPU:0, one launch (start us, length us, event | category | flops | bytes accessed | tf_op | source)
XLA Modules:
  0.0 63.6 jit_solution(528794612380650210)
XLA Ops:
  0.0 0.5 collective-permute-start.1
  0.5 0.1 pad_add_fusion
  0.6 0.1 broadcast_in_dim.11
  0.8 0.8 %copy-done.2 = f32[64,1,2,128]{3,2,1,0:T(2,128)S(1)} copy-done((f32[64,1,2,128]{3,2,1,0:T(2,128)S(1)}, f32[64,1,2,128]{3,2,1,0:T(2,128)}, u32[]{:S(2)}) %copy-start.2) | copy-done | bytes 65560
  1.6 0.7 %copy-done.3 = s32[1,2,5]{2,1,0:T(2,128)S(1)} copy-done((s32[1,2,5]{2,1,0:T(2,128)S(1)}, s32[1,2,5]{2,1,0:T(2,128)}, u32[]{:S(2)}) %copy-start.3) | copy-done | bytes 64
  2.4 0.1 collective-permute-start
  2.5 1.1 %collective-permute-done = f32[72,128]{1,0:T(8,128)S(1)} collective-permute-done((f32[72,128]{1,0:T(8,128)S(1)}, f32[72,128]{1,0:T(8,128)S(1)}, u32[]{:S(2)}, u32[]{:S(2)}) %collective-permute-start) | collective-permute-done | bytes 36896 | tf_op jit(solution)/shard_map/ppermute | solution.py:287
  3.8 2.7 %collective-permute-start.2 = (f32[2,72,128]{2,1,0:T(8,128)S(1)}, f32[2,72,128]{2,1,0:T(8,128)S(1)}, u32[]{:S(2)}, u32[]{:S(2)}) collective-permute-start(f32[2,72,128]{2,1,0:T(8,128)S(1)} %pad_maximum_fusion.1), channel_id=1, source_target_pairs={{0,3},{1,2},{2,1},{3,0},{4,7},{5,6},{6,5},{7,4},{8,11},{9,10},{10,... | collective-permute-start | bytes 221192 | tf_op jit(solution)/shard_map/ppermute | solution.py:284
  6.4 0.1 collective-permute-start.4
  6.5 2.5 %collective-permute-done.2 = f32[2,72,128]{2,1,0:T(8,128)S(1)} collective-permute-done((f32[2,72,128]{2,1,0:T(8,128)S(1)}, f32[2,72,128]{2,1,0:T(8,128)S(1)}, u32[]{:S(2)}, u32[]{:S(2)}) %collective-permute-start.2) | collective-permute-done | bytes 73760 | tf_op jit(solution)/shard_map/ppermute | solution.py:284
  9.0 1.6 %collective-permute-start.3 = (f32[4,32,128]{2,1,0:T(8,128)S(1)}, f32[4,32,128]{2,1,0:T(8,128)S(1)}, u32[]{:S(2)}, u32[]{:S(2)}) collective-permute-start(f32[4,32,128]{2,1,0:T(8,128)S(1)} %maximum_select_fusion.refs_3_.refs_4_), channel_id=1, source_target_pairs={{0,4},{4,0},{8,12},{12,8},{16,20},{20,16},{24,28},{28,24},{1,5},{5... | collective-permute-start | bytes 196616 | tf_op jit(solution)/shard_map/ppermute | solution.py:293
  10.7 0.7 %collective-permute-start.5 = (f32[4,32,128]{2,1,0:T(8,128)S(1)}, f32[4,32,128]{2,1,0:T(8,128)S(1)}, u32[]{:S(2)}, u32[]{:S(2)}) collective-permute-start(f32[4,32,128]{2,1,0:T(8,128)S(1)} %maximum_select_fusion.1.refs_2_.refs_4_), channel_id=1, source_target_pairs={{4,8},{8,4},{12,16},{16,12},{20,24},{24,20},{5,9},{9,5},{13,17},{1... | collective-permute-start | bytes 196616 | tf_op jit(solution)/shard_map/ppermute | solution.py:290
  11.4 0.1 convert_element_type.8
  11.5 0.1 concatenate.25.codes_ref
  11.6 2.1 %collective-permute-done.3.refs_4_ = f32[4,32,128]{2,1,0:T(8,128)S(1)} collective-permute-done((f32[4,32,128]{2,1,0:T(8,128)S(1)}, f32[4,32,128]{2,1,0:T(8,128)S(1)}, u32[]{:S(2)}, u32[]{:S(2)}) %collective-permute-start.3) | collective-permute-done | bytes 65568 | tf_op jit(solution)/shard_map/ppermute | solution.py:293
  13.7 0.9 %prepare_chip.1.refs_0_ = bf16[2,2,256,1152]{3,2,1,0:T(8,128)(2,1)S(1)} custom-call(s32[44]{0:T(128)S(1)} %concatenate.25.codes_ref, f32[1,2,5,128,128]{4,3,2,1,0:T(8,128)S(1)} %copy-done.1, f32[1,2,5,128,128]{4,3,2,1,0:T(8,128)S(1)} %collective-permute-done.1.core_ref.refs_1_), custom_call_target="tpu_custom_call" | custom-call | tf_op jit(solution)/shard_map/prepare_chip/pallas_call | solution.py:114
  14.6 1.5 %collective-permute-done.4.refs_0_ = f32[1,1,5,128,128]{4,3,2,1,0:T(8,128)S(1)} collective-permute-done((f32[1,1,5,128,128]{4,3,2,1,0:T(8,128)S(1)}, f32[1,1,5,128,128]{4,3,2,1,0:T(8,128)S(1)}, u32[]{:S(2)}, u32[]{:S(2)}) %collective-permute-start.4) | collective-permute-done | bytes 327712 | tf_op jit(solution)/shard_map/ppermute | solution.py:284
  16.1 0.2 collective-permute-start.6
  16.3 1.5 %collective-permute-start.7 = (f32[1,1,5,128,128]{4,3,2,1,0:T(8,128)S(1)}, f32[1,1,5,128,128]{4,3,2,1,0:T(8,128)S(1)}, u32[]{:S(2)}, u32[]{:S(2)}) collective-permute-start(f32[1,1,5,128,128]{4,3,2,1,0:T(8,128)S(1)} %get-tuple-element.29), channel_id=1, source_target_pairs={{0,3},{1,2},{2,1},{3,0},{4,7},{5,6},{6,5},{7,4},{8,11},{9,10},{10,... | collective-permute-start | bytes 983048 | tf_op jit(solution)/shard_map/ppermute | solution.py:284
  17.7 0.7 %prepare_border.1.refs_1_ = bf16[1,2,256,1152]{3,2,1,0:T(8,128)(2,1)S(1)} custom-call(s32[44]{0:T(128)S(1)} %concatenate.25.codes_ref, f32[1,1,5,128,128]{4,3,2,1,0:T(8,128)S(1)} %collective-permute-done.4.refs_0_, f32[1,1,5,128,128]{4,3,2,1,0:T(8,128)S(1)} %collective-permute-done.6.refs_1_), custom_call_target="tpu_custom_call" | custom-call | tf_op jit(solution)/shard_map/prepare_border/pallas_call | solution.py:114
  18.4 0.6 one_0.1.refs_1_
  19.0 0.7 %collective-permute-start.8 = (f32[3,32,128]{2,1,0:T(8,128)S(1)}, f32[3,32,128]{2,1,0:T(8,128)S(1)}, u32[]{:S(2)}, u32[]{:S(2)}) collective-permute-start(f32[3,32,128]{2,1,0:T(8,128)S(1)} %one_0.1.refs_1_), channel_id=1, source_target_pairs={{4,8},{8,4},{12,16},{16,12},{20,24},{24,20},{5,9},{9,5},{13,17},{1... | collective-permute-start | bytes 147464 | tf_op jit(solution)/shard_map/ppermute | solution.py:290
  19.7 0.6 one_1.1.refs_2_
  20.3 6.5 %collective-permute-start.11 = (f32[3,32,128]{2,1,0:T(8,128)S(1)}, f32[3,32,128]{2,1,0:T(8,128)S(1)}, u32[]{:S(2)}, u32[]{:S(2)}) collective-permute-start(f32[3,32,128]{2,1,0:T(8,128)S(1)} %one_1.1.refs_2_), channel_id=1, source_target_pairs={{0,4},{4,0},{8,12},{12,8},{16,20},{20,16},{24,28},{28,24},{1,5},{5... | collective-permute-start | bytes 147464 | tf_op jit(solution)/shard_map/ppermute | solution.py:293
  26.8 0.4 two_0.1
  27.3 0.8 %collective-permute-start.9 = (f32[3,32,128]{2,1,0:T(8,128)S(1)}, f32[3,32,128]{2,1,0:T(8,128)S(1)}, u32[]{:S(2)}, u32[]{:S(2)}) collective-permute-start(f32[3,32,128]{2,1,0:T(8,128)S(1)} %pad_maximum_fusion.6), channel_id=1, source_target_pairs={{0,3},{1,2},{2,1},{3,0},{4,7},{5,6},{6,5},{7,4},{8,11},{9,10},{10,... | collective-permute-start | bytes 147464 | tf_op jit(solution)/shard_map/ppermute | solution.py:284
  28.0 0.9 %collective-permute-done.11.refs_3_ = f32[3,32,128]{2,1,0:T(8,128)S(1)} collective-permute-done((f32[3,32,128]{2,1,0:T(8,128)S(1)}, f32[3,32,128]{2,1,0:T(8,128)S(1)}, u32[]{:S(2)}, u32[]{:S(2)}) %collective-permute-start.11) | collective-permute-done | bytes 49184 | tf_op jit(solution)/shard_map/ppermute | solution.py:293
  28.9 0.4 two_1.1
  29.3 0.3 collective-permute-start.12
  29.6 1.7 %collective-permute-done.9 = f32[3,32,128]{2,1,0:T(8,128)S(1)} collective-permute-done((f32[3,32,128]{2,1,0:T(8,128)S(1)}, f32[3,32,128]{2,1,0:T(8,128)S(1)}, u32[]{:S(2)}, u32[]{:S(2)}) %collective-permute-start.9) | collective-permute-done | bytes 49184 | tf_op jit(solution)/shard_map/ppermute | solution.py:284
  31.3 0.7 %collective-permute-start.13 = (f32[4,32,128]{2,1,0:T(8,128)S(1)}, f32[4,32,128]{2,1,0:T(8,128)S(1)}, u32[]{:S(2)}, u32[]{:S(2)}) collective-permute-start(f32[4,32,128]{2,1,0:T(8,128)S(1)} %pad_maximum_fusion.2.refs_3_.refs_6_), channel_id=1, source_target_pairs={{4,8},{8,4},{12,16},{16,12},{20,24},{24,20},{5,9},{9,5},{13,17},{1... | collective-permute-start | bytes 196616 | tf_op jit(solution)/shard_map/ppermute | solution.py:290
  32.0 0.2 collective-permute-start.10
  32.2 1.0 %collective-permute-done.12 = f32[3,32,128]{2,1,0:T(8,128)S(1)} collective-permute-done((f32[3,32,128]{2,1,0:T(8,128)S(1)}, f32[3,32,128]{2,1,0:T(8,128)S(1)}, u32[]{:S(2)}, u32[]{:S(2)}) %collective-permute-start.12) | collective-permute-done | bytes 49184 | tf_op jit(solution)/shard_map/ppermute | solution.py:284
  33.2 4.5 %collective-permute-start.14 = (f32[4,32,128]{2,1,0:T(8,128)S(1)}, f32[4,32,128]{2,1,0:T(8,128)S(1)}, u32[]{:S(2)}, u32[]{:S(2)}) collective-permute-start(f32[4,32,128]{2,1,0:T(8,128)S(1)} %pad_maximum_fusion.3.refs_4_.refs_6_), channel_id=1, source_target_pairs={{0,4},{4,0},{8,12},{12,8},{16,20},{20,16},{24,28},{28,24},{1,5},{5... | collective-permute-start | bytes 196616 | tf_op jit(solution)/shard_map/ppermute | solution.py:293
  37.7 0.7 %prepare_inner.1.refs_2_ = bf16[1,2,256,1152]{3,2,1,0:T(8,128)(2,1)S(1)} custom-call(s32[44]{0:T(128)S(1)} %concatenate.25.codes_ref, f32[1,1,5,128,128]{4,3,2,1,0:T(8,128)S(1)} %collective-permute-done.7.refs_0_, f32[1,1,5,128,128]{4,3,2,1,0:T(8,128)S(1)} %collective-permute-done.10.refs_1_), custom_call_target="tpu_custom_call" | custom-call | tf_op jit(solution)/shard_map/prepare_inner/pallas_call | solution.py:114
  38.5 0.7 %three_0.1.refs_3_ = f32[4,32,128]{2,1,0:T(8,128)S(1)} custom-call(bf16[2,2,256,1152]{3,2,1,0:T(8,128)(2,1)S(1)} %prepare_chip.1.refs_0_, bf16[1,2,256,1152]{3,2,1,0:T(8,128)(2,1)S(1)} %prepare_border.1.refs_1_, bf16[1,2,256,1152]{3,2,1,0:T(8,128)(2,1)S(1)} %prepare_inner.1.refs_2_, f32[4,32,128]{2,1,0:T(8,128)S(1)} %pad_maximum_fusion.2.refs_3_.refs_6_, ...), custom_call_target="tpu_custom_call" | custom-call | flops 150994944 | bytes 2359296 | tf_op jit(solution)/shard_map/three_0/pallas_call | solution.py:204
  39.2 0.7 %collective-permute-start.16 = (f32[4,32,128]{2,1,0:T(8,128)S(1)}, f32[4,32,128]{2,1,0:T(8,128)S(1)}, u32[]{:S(2)}, u32[]{:S(2)}) collective-permute-start(f32[4,32,128]{2,1,0:T(8,128)S(1)} %three_0.1.refs_3_), channel_id=1, source_target_pairs={{4,8},{8,4},{12,16},{16,12},{20,24},{24,20},{5,9},{9,5},{13,17},{1... | collective-permute-start | bytes 196616 | tf_op jit(solution)/shard_map/ppermute | solution.py:290
  39.8 0.6 collective-permute-done.14.refs_5_
  40.4 0.7 %three_1.1.refs_4_ = f32[4,32,128]{2,1,0:T(8,128)S(1)} custom-call(bf16[2,2,256,1152]{3,2,1,0:T(8,128)(2,1)S(1)} %prepare_chip.1.refs_0_, bf16[1,2,256,1152]{3,2,1,0:T(8,128)(2,1)S(1)} %prepare_border.1.refs_1_, bf16[1,2,256,1152]{3,2,1,0:T(8,128)(2,1)S(1)} %prepare_inner.1.refs_2_, f32[4,32,128]{2,1,0:T(8,128)S(1)} %pad_maximum_fusion.2.refs_3_.refs_6_, ...), custom_call_target="tpu_custom_call" | custom-call | flops 150994944 | bytes 2359296 | tf_op jit(solution)/shard_map/three_1/pallas_call | solution.py:204
  41.1 5.0 %collective-permute-start.15 = (f32[4,32,128]{2,1,0:T(8,128)S(1)}, f32[4,32,128]{2,1,0:T(8,128)S(1)}, u32[]{:S(2)}, u32[]{:S(2)}) collective-permute-start(f32[4,32,128]{2,1,0:T(8,128)S(1)} %three_1.1.refs_4_), channel_id=1, source_target_pairs={{0,4},{4,0},{8,12},{12,8},{16,20},{20,16},{24,28},{28,24},{1,5},{5... | collective-permute-start | bytes 196616 | tf_op jit(solution)/shard_map/ppermute | solution.py:293
  46.1 0.9 %four_0.1 = (f32[4,32,128]{2,1,0:T(8,128)S(1)}, f32[32,128]{1,0:T(8,128)S(1)}) custom-call(bf16[2,2,256,1152]{3,2,1,0:T(8,128)(2,1)S(1)} %prepare_chip.1.refs_0_, bf16[1,2,256,1152]{3,2,1,0:T(8,128)(2,1)S(1)} %prepare_border.1.refs_1_, bf16[1,2,256,1152]{3,2,1,0:T(8,128)(2,1)S(1)} %prepare_inner.1.refs_2_, f32[4,32,128]{2,1,0:T(8,128)S(1)} %three_0.1.refs_3_, ...), custom_call_target="tpu_custom_call" | custom-call | flops 150994944 | bytes 2359296 | tf_op jit(solution)/shard_map/four_0/pallas_call | solution.py:204
  47.1 1.3 %collective-permute-done.15.refs_5_ = f32[4,32,128]{2,1,0:T(8,128)S(1)} collective-permute-done((f32[4,32,128]{2,1,0:T(8,128)S(1)}, f32[4,32,128]{2,1,0:T(8,128)S(1)}, u32[]{:S(2)}, u32[]{:S(2)}) %collective-permute-start.15) | collective-permute-done | bytes 65568 | tf_op jit(solution)/shard_map/ppermute | solution.py:293
  48.4 1.0 %four_1.1 = (f32[4,24,128]{2,1,0:T(8,128)S(1)}, f32[4,24,128]{2,1,0:T(8,128)S(1)}) custom-call(bf16[2,2,256,1152]{3,2,1,0:T(8,128)(2,1)S(1)} %prepare_chip.1.refs_0_, bf16[1,2,256,1152]{3,2,1,0:T(8,128)(2,1)S(1)} %prepare_border.1.refs_1_, bf16[1,2,256,1152]{3,2,1,0:T(8,128)(2,1)S(1)} %prepare_inner.1.refs_2_, f32[4,32,128]{2,1,0:T(8,128)S(1)} %three_0.1.refs_3_, ...), custom_call_target="tpu_custom_call" | custom-call | flops 150994944 | bytes 2359296 | tf_op jit(solution)/shard_map/four_1/pallas_call | solution.py:204
  49.4 1.2 %collective-permute-done.17 = f32[4,24,128]{2,1,0:T(8,128)S(1)} collective-permute-done((f32[4,24,128]{2,1,0:T(8,128)S(1)}, f32[4,24,128]{2,1,0:T(8,128)S(1)}, u32[]{:S(2)}, u32[]{:S(2)}) %collective-permute-start.17) | collective-permute-done | bytes 49184 | tf_op jit(solution)/shard_map/ppermute | solution.py:287
  50.6 0.6 %pad_maximum_fusion = f32[8,24,128]{2,1,0:T(8,128)} fusion(f32[4,24,128]{2,1,0:T(8,128)S(1)} %get-tuple-element.38, f32[4,24,128]{2,1,0:T(8,128)S(1)} %collective-permute-done.17), kind=kLoop, calls=%fused_computation | loop fusion | flops 24576 | bytes 196608 | tf_op jit(solution)/shard_map/concatenate | solution.py:341
  51.3 6.7 %all-to-all-start = ((f32[8,24,128]{2,1,0:T(8,128)}), f32[8,24,128]{2,1,0:T(8,128)S(1)}, u32[]{:S(2)}, u32[]{:S(2)}) async-start(f32[8,24,128]{2,1,0:T(8,128)} %pad_maximum_fusion), calls=%async_computation | async-start | bytes 196608 | tf_op jit(solution)/shard_map/all_to_all | solution.py:347
  58.1 4.1 %all-to-all-done.parts_ref = f32[8,24,128]{2,1,0:T(8,128)S(1)} async-done(((f32[8,24,128]{2,1,0:T(8,128)}), f32[8,24,128]{2,1,0:T(8,128)S(1)}, u32[]{:S(2)}, u32[]{:S(2)}) %all-to-all-start) | async-done | bytes 98336 | tf_op jit(solution)/shard_map/all_to_all | solution.py:347
  62.2 1.5 %finish.1 = f32[8,1,16,128]{3,2,1,0:T(8,128)} custom-call(s32[32,128]{1,0:T(8,128)S(1)} %broadcast_in_dim.12.flags_ref.refs_9_, f32[8,24,128]{2,1,0:T(8,128)S(1)} %all-to-all-done.parts_ref, f32[8,8]{1,0:T(8,128)S(1)} %bitcast.27), custom_call_target="tpu_custom_call" | custom-call | tf_op jit(solution)/shard_map/finish/pallas_call | solution.py:257
  (44 shorter events, 0.5 us)
Async XLA Ops:
  0.0 58.0 %copy-start = (f32[8,8,8]{2,1,0:T(8,128)S(1)}, f32[8,8,8]{2,1,0:T(8,128)}, u32[]{:S(2)}) copy-start(f32[8,8,8]{2,1,0:T(8,128)} %param.7) | copy-start | bytes 6148
  0.0 3.7 %copy-start.1 = (f32[1,2,5,128,128]{4,3,2,1,0:T(8,128)S(1)}, f32[1,2,5,128,128]{4,3,2,1,0:T(8,128)}, u32[]{:S(2)}) copy-start(f32[1,2,5,128,128]{4,3,2,1,0:T(8,128)} %refs_0_.1) | copy-start | bytes 1966084
  0.0 3.6 %collective-permute-start.1 = (f32[1,2,5,128,128]{4,3,2,1,0:T(8,128)}, f32[1,2,5,128,128]{4,3,2,1,0:T(8,128)S(1)}, u32[]{:S(2)}, u32[]{:S(2)}) collective-permute-start(f32[1,2,5,128,128]{4,3,2,1,0:T(8,128)} %refs_0_.1), channel_id=1, source_target_pairs={{0,1},{1,0},{2,3},{3,2},{4,5},{5,4},{6,7},{7,6},{8,9},{9,8},{10,11... | collective-permute-start | bytes 1966088 | tf_op jit(solution)/shard_map/ppermute | solution.py:287
  0.8 0.8 %copy-start.2 = (f32[64,1,2,128]{3,2,1,0:T(2,128)S(1)}, f32[64,1,2,128]{3,2,1,0:T(2,128)}, u32[]{:S(2)}) copy-start(f32[64,1,2,128]{3,2,1,0:T(2,128)} %slab_ref.1) | copy-start | bytes 196612
  1.6 0.7 %copy-start.3 = (s32[1,2,5]{2,1,0:T(2,128)S(1)}, s32[1,2,5]{2,1,0:T(2,128)}, u32[]{:S(2)}) copy-start(s32[1,2,5]{2,1,0:T(2,128)} %codes_ref.1) | copy-start | bytes 124
  2.4 1.3 %collective-permute-start = (f32[72,128]{1,0:T(8,128)S(1)}, f32[72,128]{1,0:T(8,128)S(1)}, u32[]{:S(2)}, u32[]{:S(2)}) collective-permute-start(f32[72,128]{1,0:T(8,128)S(1)} %get-tuple-element.48), channel_id=1, source_target_pairs={{0,1},{1,0},{2,3},{3,2},{4,5},{5,4},{6,7},{7,6},{8,9},{9,8},{10,11... | collective-permute-start | bytes 110600 | tf_op jit(solution)/shard_map/ppermute | solution.py:287
  3.8 5.3 %collective-permute-start.2 = (f32[2,72,128]{2,1,0:T(8,128)S(1)}, f32[2,72,128]{2,1,0:T(8,128)S(1)}, u32[]{:S(2)}, u32[]{:S(2)}) collective-permute-start(f32[2,72,128]{2,1,0:T(8,128)S(1)} %pad_maximum_fusion.1), channel_id=1, source_target_pairs={{0,3},{1,2},{2,1},{3,0},{4,7},{5,6},{6,5},{7,4},{8,11},{9,10},{10,... | collective-permute-start | bytes 221192 | tf_op jit(solution)/shard_map/ppermute | solution.py:284
  6.4 9.7 %collective-permute-start.4 = (f32[1,1,5,128,128]{4,3,2,1,0:T(8,128)S(1)}, f32[1,1,5,128,128]{4,3,2,1,0:T(8,128)S(1)}, u32[]{:S(2)}, u32[]{:S(2)}) collective-permute-start(f32[1,1,5,128,128]{4,3,2,1,0:T(8,128)S(1)} %get-tuple-element.25), channel_id=1, source_target_pairs={{0,3},{1,2},{2,1},{3,0},{4,7},{5,6},{6,5},{7,4},{8,11},{9,10},{10,... | collective-permute-start | bytes 983048 | tf_op jit(solution)/shard_map/ppermute | solution.py:284
  9.0 4.6 %collective-permute-start.3 = (f32[4,32,128]{2,1,0:T(8,128)S(1)}, f32[4,32,128]{2,1,0:T(8,128)S(1)}, u32[]{:S(2)}, u32[]{:S(2)}) collective-permute-start(f32[4,32,128]{2,1,0:T(8,128)S(1)} %maximum_select_fusion.refs_3_.refs_4_), channel_id=1, source_target_pairs={{0,4},{4,0},{8,12},{12,8},{16,20},{20,16},{24,28},{28,24},{1,5},{5... | collective-permute-start | bytes 196616 | tf_op jit(solution)/shard_map/ppermute | solution.py:293
  10.7 3.9 %collective-permute-start.5 = (f32[4,32,128]{2,1,0:T(8,128)S(1)}, f32[4,32,128]{2,1,0:T(8,128)S(1)}, u32[]{:S(2)}, u32[]{:S(2)}) collective-permute-start(f32[4,32,128]{2,1,0:T(8,128)S(1)} %maximum_select_fusion.1.refs_2_.refs_4_), channel_id=1, source_target_pairs={{4,8},{8,4},{12,16},{16,12},{20,24},{24,20},{5,9},{9,5},{13,17},{1... | collective-permute-start | bytes 196616 | tf_op jit(solution)/shard_map/ppermute | solution.py:290
  16.1 1.6 %collective-permute-start.6 = (f32[1,1,5,128,128]{4,3,2,1,0:T(8,128)S(1)}, f32[1,1,5,128,128]{4,3,2,1,0:T(8,128)S(1)}, u32[]{:S(2)}, u32[]{:S(2)}) collective-permute-start(f32[1,1,5,128,128]{4,3,2,1,0:T(8,128)S(1)} %collective-permute-done.4.refs_0_), channel_id=1, source_target_pairs={{0,1},{1,0},{2,3},{3,2},{4,5},{5,4},{6,7},{7,6},{8,9},{9,8},{10,11... | collective-permute-start | bytes 983048 | tf_op jit(solution)/shard_map/ppermute | solution.py:287
  16.3 10.6 %collective-permute-start.7 = (f32[1,1,5,128,128]{4,3,2,1,0:T(8,128)S(1)}, f32[1,1,5,128,128]{4,3,2,1,0:T(8,128)S(1)}, u32[]{:S(2)}, u32[]{:S(2)}) collective-permute-start(f32[1,1,5,128,128]{4,3,2,1,0:T(8,128)S(1)} %get-tuple-element.29), channel_id=1, source_target_pairs={{0,3},{1,2},{2,1},{3,0},{4,7},{5,6},{6,5},{7,4},{8,11},{9,10},{10,... | collective-permute-start | bytes 983048 | tf_op jit(solution)/shard_map/ppermute | solution.py:284
  19.0 7.8 %collective-permute-start.8 = (f32[3,32,128]{2,1,0:T(8,128)S(1)}, f32[3,32,128]{2,1,0:T(8,128)S(1)}, u32[]{:S(2)}, u32[]{:S(2)}) collective-permute-start(f32[3,32,128]{2,1,0:T(8,128)S(1)} %one_0.1.refs_1_), channel_id=1, source_target_pairs={{4,8},{8,4},{12,16},{16,12},{20,24},{24,20},{5,9},{9,5},{13,17},{1... | collective-permute-start | bytes 147464 | tf_op jit(solution)/shard_map/ppermute | solution.py:290
  20.3 8.6 %collective-permute-start.11 = (f32[3,32,128]{2,1,0:T(8,128)S(1)}, f32[3,32,128]{2,1,0:T(8,128)S(1)}, u32[]{:S(2)}, u32[]{:S(2)}) collective-permute-start(f32[3,32,128]{2,1,0:T(8,128)S(1)} %one_1.1.refs_2_), channel_id=1, source_target_pairs={{0,4},{4,0},{8,12},{12,8},{16,20},{20,16},{24,28},{28,24},{1,5},{5... | collective-permute-start | bytes 147464 | tf_op jit(solution)/shard_map/ppermute | solution.py:293
  27.3 4.0 %collective-permute-start.9 = (f32[3,32,128]{2,1,0:T(8,128)S(1)}, f32[3,32,128]{2,1,0:T(8,128)S(1)}, u32[]{:S(2)}, u32[]{:S(2)}) collective-permute-start(f32[3,32,128]{2,1,0:T(8,128)S(1)} %pad_maximum_fusion.6), channel_id=1, source_target_pairs={{0,3},{1,2},{2,1},{3,0},{4,7},{5,6},{6,5},{7,4},{8,11},{9,10},{10,... | collective-permute-start | bytes 147464 | tf_op jit(solution)/shard_map/ppermute | solution.py:284
  29.3 3.8 %collective-permute-start.12 = (f32[3,32,128]{2,1,0:T(8,128)S(1)}, f32[3,32,128]{2,1,0:T(8,128)S(1)}, u32[]{:S(2)}, u32[]{:S(2)}) collective-permute-start(f32[3,32,128]{2,1,0:T(8,128)S(1)} %pad_maximum_fusion.7), channel_id=1, source_target_pairs={{0,3},{1,2},{2,1},{3,0},{4,7},{5,6},{6,5},{7,4},{8,11},{9,10},{10,... | collective-permute-start | bytes 147464 | tf_op jit(solution)/shard_map/ppermute | solution.py:284
  31.3 7.1 %collective-permute-start.13 = (f32[4,32,128]{2,1,0:T(8,128)S(1)}, f32[4,32,128]{2,1,0:T(8,128)S(1)}, u32[]{:S(2)}, u32[]{:S(2)}) collective-permute-start(f32[4,32,128]{2,1,0:T(8,128)S(1)} %pad_maximum_fusion.2.refs_3_.refs_6_), channel_id=1, source_target_pairs={{4,8},{8,4},{12,16},{16,12},{20,24},{24,20},{5,9},{9,5},{13,17},{1... | collective-permute-start | bytes 196616 | tf_op jit(solution)/shard_map/ppermute | solution.py:290
  32.0 5.7 %collective-permute-start.10 = (f32[1,1,5,128,128]{4,3,2,1,0:T(8,128)S(1)}, f32[1,1,5,128,128]{4,3,2,1,0:T(8,128)S(1)}, u32[]{:S(2)}, u32[]{:S(2)}) collective-permute-start(f32[1,1,5,128,128]{4,3,2,1,0:T(8,128)S(1)} %collective-permute-done.7.refs_0_), channel_id=1, source_target_pairs={{0,1},{1,0},{2,3},{3,2},{4,5},{5,4},{6,7},{7,6},{8,9},{9,8},{10,11... | collective-permute-start | bytes 983048 | tf_op jit(solution)/shard_map/ppermute | solution.py:287
  33.2 7.2 %collective-permute-start.14 = (f32[4,32,128]{2,1,0:T(8,128)S(1)}, f32[4,32,128]{2,1,0:T(8,128)S(1)}, u32[]{:S(2)}, u32[]{:S(2)}) collective-permute-start(f32[4,32,128]{2,1,0:T(8,128)S(1)} %pad_maximum_fusion.3.refs_4_.refs_6_), channel_id=1, source_target_pairs={{0,4},{4,0},{8,12},{12,8},{16,20},{20,16},{24,28},{28,24},{1,5},{5... | collective-permute-start | bytes 196616 | tf_op jit(solution)/shard_map/ppermute | solution.py:293
  39.2 7.0 %collective-permute-start.16 = (f32[4,32,128]{2,1,0:T(8,128)S(1)}, f32[4,32,128]{2,1,0:T(8,128)S(1)}, u32[]{:S(2)}, u32[]{:S(2)}) collective-permute-start(f32[4,32,128]{2,1,0:T(8,128)S(1)} %three_0.1.refs_3_), channel_id=1, source_target_pairs={{4,8},{8,4},{12,16},{16,12},{20,24},{24,20},{5,9},{9,5},{13,17},{1... | collective-permute-start | bytes 196616 | tf_op jit(solution)/shard_map/ppermute | solution.py:290
  41.1 7.2 %collective-permute-start.15 = (f32[4,32,128]{2,1,0:T(8,128)S(1)}, f32[4,32,128]{2,1,0:T(8,128)S(1)}, u32[]{:S(2)}, u32[]{:S(2)}) collective-permute-start(f32[4,32,128]{2,1,0:T(8,128)S(1)} %three_1.1.refs_4_), channel_id=1, source_target_pairs={{0,4},{4,0},{8,12},{12,8},{16,20},{20,16},{24,28},{28,24},{1,5},{5... | collective-permute-start | bytes 196616 | tf_op jit(solution)/shard_map/ppermute | solution.py:293
  49.4 1.3 %collective-permute-start.17 = (f32[4,24,128]{2,1,0:T(8,128)S(1)}, f32[4,24,128]{2,1,0:T(8,128)S(1)}, u32[]{:S(2)}, u32[]{:S(2)}) collective-permute-start(f32[4,24,128]{2,1,0:T(8,128)S(1)} %get-tuple-element.37), channel_id=1, source_target_pairs={{0,1},{1,0},{2,3},{3,2},{4,5},{5,4},{6,7},{7,6},{8,9},{9,8},{10,11... | collective-permute-start | bytes 147464 | tf_op jit(solution)/shard_map/ppermute | solution.py:287
  51.3 10.9 %all-to-all-start = ((f32[8,24,128]{2,1,0:T(8,128)}), f32[8,24,128]{2,1,0:T(8,128)S(1)}, u32[]{:S(2)}, u32[]{:S(2)}) async-start(f32[8,24,128]{2,1,0:T(8,128)} %pad_maximum_fusion), calls=%async_computation | async-start | bytes 196608 | tf_op jit(solution)/shard_map/all_to_all | solution.py:347

commit v4 on v2

--- a/solution.py
+++ b/solution.py
@@ -177,13 +177,13 @@
         kept, sent = jnp.where(edge, border, inner), jnp.where(edge, inner, border)
         for b in range(blocks):
             rows = slice(b * VEC, (b + 1) * VEC)
-            kept_ref[blocks - 1 - b, c * VEC : (c + 1) * VEC, :] = kept[rows]
+            kept_ref[-b % blocks, c * VEC : (c + 1) * VEC, :] = kept[rows]
             sent_ref[blocks - 1 - b, c * VEC : (c + 1) * VEC, :] = sent[rows]
     for b in range(blocks):
         rows = slice(b * VEC, (b + 1) * VEC)
-        for ref in (kept_ref, sent_ref):
-            ref[blocks - 1 - b, 2 * VEC :, :] = jnp.zeros((VEC, size), jnp.float32)
-            ref[blocks - 1 - b, 2 * VEC :, 0:VEC] = gram[rows, rows]
+        for ref, at in ((kept_ref, -b % blocks), (sent_ref, blocks - 1 - b)):
+            ref[at, 2 * VEC :, :] = jnp.zeros((VEC, size), jnp.float32)
+            ref[at, 2 * VEC :, 0:VEC] = gram[rows, rows]
 
 
 def step(kind, u, name, h_ready, own, rim, *others):
@@ -248,8 +248,8 @@
     half = flag(flags_ref, 2, mixed[0].shape)
     for w in range(wide):
         for c in range(cols):
-            first = mixed[(wide - 1 - w) * cols + c]
-            second = mixed[(wide - 1 - w + wide // 2) % wide * cols + c]
+            first = mixed[-w % wide * cols + c]
+            second = mixed[(wide // 2 - w) % wide * cols + c]
             out_ref[:, 0, w * cols + c, :] = jnp.where(half, second, first)
 
 
@@ -339,10 +339,10 @@
     four = step("other", 0, "four_0", h_four, three, rims[0], two[0])
     kept, sent = step("last", 1, "four_1", h_four, three, rims[1], two[1], *four, flags)
 
-    packed = jnp.concatenate([core(sent), kept])
+    packed = jnp.concatenate([kept[:1], core(sent), kept[1:]])
     owners = wide // 2
     groups = [
-        [((wide - 1 - i + owners * (g // 2 ^ g % 2)) % wide) * grp + g for i in range(wide)]
+        [((wide - i + owners * (g // 2 ^ g % 2)) % wide) * grp + g for i in range(wide)]
         for g in range(grp)
     ]
     packed = lax.all_to_all(

time: 63.5 us -> 64.4 us (1.014)
  waiting for transfers between devices: 15.5 us -> 17.9 us
  starting transfers between devices: 35.2 us -> 33.8 us
    all_to_all x1, waiting for transfers between devices: 4.07 us -> 6.5 us  [body(): lax.all_to_all(packed, ('wide', 'grp'), split_axis=0, concat_axis=0, tile...]
    all_to_all x1, starting transfers between devices: 6.8 us -> 5.34 us  [body(): lax.all_to_all(packed, ('wide', 'grp'), split_axis=0, concat_axis=0, tile...]
where the time goes in v4:
time: 64.4 us; the launch traced here: 64.1 us
  starting transfers between devices  33.8 us (52%)
  waiting for transfers between devices  17.9 us (28%)
  Pallas kernels  9.28 us (14%)
  local copies, waits for them, and re-layouts  2.07 us (3%)
  other arithmetic  0.8 us (1%)
    ppermute x4, starting transfers between devices, over_near(): return lax.ppermute(value, 'wide', near)  18.6 us
    ppermute x5, waiting for transfers between devices, across(): return lax.ppermute(value, 'grp', [(i, i ^ 3) for i in range(grp)])  6.62 us
    all_to_all x1, waiting for transfers between devices, body(): lax.all_to_all(packed, ('wide', 'grp'), split_axis=0, concat_axis=0, tile...  6.5 us
    ppermute x5, starting transfers between devices, across(): return lax.ppermute(value, 'grp', [(i, i ^ 3) for i in range(grp)])  6.07 us
    all_to_all x1, starting transfers between devices, body(): lax.all_to_all(packed, ('wide', 'grp'), split_axis=0, concat_axis=0, tile...  5.34 us
    pallas_call x8, Pallas kernels, step(): pl.pallas_call(functools.partial(step_kernel, kind, u, len(h_ready)), in_...  5.32 us
    ppermute x4, starting transfers between devices, over_far(): return lax.ppermute(value, 'wide', far)  2.66 us
    ppermute x4, waiting for transfers between devices, over_near(): return lax.ppermute(value, 'wide', near)  2.44 us
  transfers between devices with their start and end apart: 19, of which 11 were waited for; matrix products, arithmetic and copies ran while one was open for 1% of the time, Pallas kernels for 11%

profile of v4, /device:TPU:0, one launch (start us, length us, event | category | flops | bytes accessed | tf_op | source)
XLA Modules:
  0.0 64.1 jit_solution(17323929267729166396)
XLA Ops:
  0.0 0.5 collective-permute-start.1
  0.5 0.1 pad_add_fusion
  0.6 0.1 broadcast_in_dim.11
  0.8 0.8 %copy-done.2 = f32[64,1,2,128]{3,2,1,0:T(2,128)S(1)} copy-done((f32[64,1,2,128]{3,2,1,0:T(2,128)S(1)}, f32[64,1,2,128]{3,2,1,0:T(2,128)}, u32[]{:S(2)}) %copy-start.2) | copy-done | bytes 65560
  1.6 0.7 %copy-done.3 = s32[1,2,5]{2,1,0:T(2,128)S(1)} copy-done((s32[1,2,5]{2,1,0:T(2,128)S(1)}, s32[1,2,5]{2,1,0:T(2,128)}, u32[]{:S(2)}) %copy-start.3) | copy-done | bytes 64
  2.4 0.1 collective-permute-start
  2.5 1.1 %collective-permute-done = f32[72,128]{1,0:T(8,128)S(1)} collective-permute-done((f32[72,128]{1,0:T(8,128)S(1)}, f32[72,128]{1,0:T(8,128)S(1)}, u32[]{:S(2)}, u32[]{:S(2)}) %collective-permute-start) | collective-permute-done | bytes 36896 | tf_op jit(solution)/shard_map/ppermute | solution.py:288
  3.7 0.1 pick.1
  3.8 2.7 %collective-permute-start.2 = (f32[2,72,128]{2,1,0:T(8,128)S(1)}, f32[2,72,128]{2,1,0:T(8,128)S(1)}, u32[]{:S(2)}, u32[]{:S(2)}) collective-permute-start(f32[2,72,128]{2,1,0:T(8,128)S(1)} %pad_maximum_fusion.1), channel_id=1, source_target_pairs={{0,3},{1,2},{2,1},{3,0},{4,7},{5,6},{6,5},{7,4},{8,11},{9,10},{10,... | collective-permute-start | bytes 221192 | tf_op jit(solution)/shard_map/ppermute | solution.py:285
  6.4 0.1 collective-permute-start.3
  6.5 2.5 %collective-permute-done.2 = f32[2,72,128]{2,1,0:T(8,128)S(1)} collective-permute-done((f32[2,72,128]{2,1,0:T(8,128)S(1)}, f32[2,72,128]{2,1,0:T(8,128)S(1)}, u32[]{:S(2)}, u32[]{:S(2)}) %collective-permute-start.2) | collective-permute-done | bytes 73760 | tf_op jit(solution)/shard_map/ppermute | solution.py:285
  9.0 0.7 %collective-permute-start.4 = (f32[4,32,128]{2,1,0:T(8,128)S(1)}, f32[4,32,128]{2,1,0:T(8,128)S(1)}, u32[]{:S(2)}, u32[]{:S(2)}) collective-permute-start(f32[4,32,128]{2,1,0:T(8,128)S(1)} %maximum_select_fusion.refs_2_.refs_4_), channel_id=1, source_target_pairs={{4,8},{8,4},{12,16},{16,12},{20,24},{24,20},{5,9},{9,5},{13,17},{1... | collective-permute-start | bytes 196616 | tf_op jit(solution)/shard_map/ppermute | solution.py:291
  9.7 4.4 %collective-permute-start.6 = (f32[4,32,128]{2,1,0:T(8,128)S(1)}, f32[4,32,128]{2,1,0:T(8,128)S(1)}, u32[]{:S(2)}, u32[]{:S(2)}) collective-permute-start(f32[4,32,128]{2,1,0:T(8,128)S(1)} %maximum_select_fusion.1.refs_3_.refs_4_), channel_id=1, source_target_pairs={{0,4},{4,0},{8,12},{12,8},{16,20},{20,16},{24,28},{28,24},{1,5},{5... | collective-permute-start | bytes 196616 | tf_op jit(solution)/shard_map/ppermute | solution.py:294
  14.2 0.1 convert_element_type.8
  14.3 0.1 concatenate.25.codes_ref
  14.3 0.9 %prepare_chip.1.refs_0_ = bf16[2,2,256,1152]{3,2,1,0:T(8,128)(2,1)S(1)} custom-call(s32[44]{0:T(128)S(1)} %concatenate.25.codes_ref, f32[1,2,5,128,128]{4,3,2,1,0:T(8,128)S(1)} %copy-done.1, f32[1,2,5,128,128]{4,3,2,1,0:T(8,128)S(1)} %collective-permute-done.1.core_ref.refs_1_), custom_call_target="tpu_custom_call" | custom-call | tf_op jit(solution)/shard_map/prepare_chip/pallas_call | solution.py:114
  15.3 0.8 %collective-permute-done.3.refs_0_ = f32[1,1,5,128,128]{4,3,2,1,0:T(8,128)S(1)} collective-permute-done((f32[1,1,5,128,128]{4,3,2,1,0:T(8,128)S(1)}, f32[1,1,5,128,128]{4,3,2,1,0:T(8,128)S(1)}, u32[]{:S(2)}, u32[]{:S(2)}) %collective-permute-start.3) | collective-permute-done | bytes 327712 | tf_op jit(solution)/shard_map/ppermute | solution.py:285
  16.1 0.5 collective-permute-start.5
  16.5 0.5 collective-permute-done.6.refs_4_
  17.1 1.4 %collective-permute-start.7 = (f32[1,1,5,128,128]{4,3,2,1,0:T(8,128)S(1)}, f32[1,1,5,128,128]{4,3,2,1,0:T(8,128)S(1)}, u32[]{:S(2)}, u32[]{:S(2)}) collective-permute-start(f32[1,1,5,128,128]{4,3,2,1,0:T(8,128)S(1)} %get-tuple-element.27), channel_id=1, source_target_pairs={{0,3},{1,2},{2,1},{3,0},{4,7},{5,6},{6,5},{7,4},{8,11},{9,10},{10,... | collective-permute-start | bytes 983048 | tf_op jit(solution)/shard_map/ppermute | solution.py:285
  18.5 0.7 %prepare_border.1.refs_1_ = bf16[1,2,256,1152]{3,2,1,0:T(8,128)(2,1)S(1)} custom-call(s32[44]{0:T(128)S(1)} %concatenate.25.codes_ref, f32[1,1,5,128,128]{4,3,2,1,0:T(8,128)S(1)} %collective-permute-done.3.refs_0_, f32[1,1,5,128,128]{4,3,2,1,0:T(8,128)S(1)} %collective-permute-done.5.refs_1_), custom_call_target="tpu_custom_call" | custom-call | tf_op jit(solution)/shard_map/prepare_border/pallas_call | solution.py:114
  19.2 0.6 one_0.1.refs_1_
  19.8 0.7 %collective-permute-start.8 = (f32[3,32,128]{2,1,0:T(8,128)S(1)}, f32[3,32,128]{2,1,0:T(8,128)S(1)}, u32[]{:S(2)}, u32[]{:S(2)}) collective-permute-start(f32[3,32,128]{2,1,0:T(8,128)S(1)} %one_0.1.refs_1_), channel_id=1, source_target_pairs={{4,8},{8,4},{12,16},{16,12},{20,24},{24,20},{5,9},{9,5},{13,17},{1... | collective-permute-start | bytes 147464 | tf_op jit(solution)/shard_map/ppermute | solution.py:291
  20.5 0.6 one_1.1.refs_2_
  21.1 5.3 %collective-permute-start.11 = (f32[3,32,128]{2,1,0:T(8,128)S(1)}, f32[3,32,128]{2,1,0:T(8,128)S(1)}, u32[]{:S(2)}, u32[]{:S(2)}) collective-permute-start(f32[3,32,128]{2,1,0:T(8,128)S(1)} %one_1.1.refs_2_), channel_id=1, source_target_pairs={{0,4},{4,0},{8,12},{12,8},{16,20},{20,16},{24,28},{28,24},{1,5},{5... | collective-permute-start | bytes 147464 | tf_op jit(solution)/shard_map/ppermute | solution.py:294
  26.4 0.4 collective-permute-done.7.refs_0_
  26.8 0.4 two_0.1
  27.3 1.8 %collective-permute-start.9 = (f32[3,32,128]{2,1,0:T(8,128)S(1)}, f32[3,32,128]{2,1,0:T(8,128)S(1)}, u32[]{:S(2)}, u32[]{:S(2)}) collective-permute-start(f32[3,32,128]{2,1,0:T(8,128)S(1)} %pad_maximum_fusion.6), channel_id=1, source_target_pairs={{0,3},{1,2},{2,1},{3,0},{4,7},{5,6},{6,5},{7,4},{8,11},{9,10},{10,... | collective-permute-start | bytes 147464 | tf_op jit(solution)/shard_map/ppermute | solution.py:285
  29.1 0.4 two_1.1
  29.5 0.1 collective-permute-start.12
  29.6 1.6 %collective-permute-done.9 = f32[3,32,128]{2,1,0:T(8,128)S(1)} collective-permute-done((f32[3,32,128]{2,1,0:T(8,128)S(1)}, f32[3,32,128]{2,1,0:T(8,128)S(1)}, u32[]{:S(2)}, u32[]{:S(2)}) %collective-permute-start.9) | collective-permute-done | bytes 49184 | tf_op jit(solution)/shard_map/ppermute | solution.py:285
  31.2 0.7 %collective-permute-start.13 = (f32[4,32,128]{2,1,0:T(8,128)S(1)}, f32[4,32,128]{2,1,0:T(8,128)S(1)}, u32[]{:S(2)}, u32[]{:S(2)}) collective-permute-start(f32[4,32,128]{2,1,0:T(8,128)S(1)} %pad_maximum_fusion.2.refs_3_.refs_6_), channel_id=1, source_target_pairs={{4,8},{8,4},{12,16},{16,12},{20,24},{24,20},{5,9},{9,5},{13,17},{1... | collective-permute-start | bytes 196616 | tf_op jit(solution)/shard_map/ppermute | solution.py:291
  32.0 1.3 %collective-permute-done.12 = f32[3,32,128]{2,1,0:T(8,128)S(1)} collective-permute-done((f32[3,32,128]{2,1,0:T(8,128)S(1)}, f32[3,32,128]{2,1,0:T(8,128)S(1)}, u32[]{:S(2)}, u32[]{:S(2)}) %collective-permute-start.12) | collective-permute-done | bytes 49184 | tf_op jit(solution)/shard_map/ppermute | solution.py:285
  33.3 3.9 %collective-permute-start.14 = (f32[4,32,128]{2,1,0:T(8,128)S(1)}, f32[4,32,128]{2,1,0:T(8,128)S(1)}, u32[]{:S(2)}, u32[]{:S(2)}) collective-permute-start(f32[4,32,128]{2,1,0:T(8,128)S(1)} %pad_maximum_fusion.3.refs_4_.refs_6_), channel_id=1, source_target_pairs={{0,4},{4,0},{8,12},{12,8},{16,20},{20,16},{24,28},{28,24},{1,5},{5... | collective-permute-start | bytes 196616 | tf_op jit(solution)/shard_map/ppermute | solution.py:294
  37.2 0.7 %prepare_inner.1.refs_2_ = bf16[1,2,256,1152]{3,2,1,0:T(8,128)(2,1)S(1)} custom-call(s32[44]{0:T(128)S(1)} %concatenate.25.codes_ref, f32[1,1,5,128,128]{4,3,2,1,0:T(8,128)S(1)} %collective-permute-done.7.refs_0_, f32[1,1,5,128,128]{4,3,2,1,0:T(8,128)S(1)} %collective-permute-done.10.refs_1_), custom_call_target="tpu_custom_call" | custom-call | tf_op jit(solution)/shard_map/prepare_inner/pallas_call | solution.py:114
  37.9 0.7 %three_0.1.refs_3_ = f32[4,32,128]{2,1,0:T(8,128)S(1)} custom-call(bf16[2,2,256,1152]{3,2,1,0:T(8,128)(2,1)S(1)} %prepare_chip.1.refs_0_, bf16[1,2,256,1152]{3,2,1,0:T(8,128)(2,1)S(1)} %prepare_border.1.refs_1_, bf16[1,2,256,1152]{3,2,1,0:T(8,128)(2,1)S(1)} %prepare_inner.1.refs_2_, f32[4,32,128]{2,1,0:T(8,128)S(1)} %pad_maximum_fusion.2.refs_3_.refs_6_, ...), custom_call_target="tpu_custom_call" | custom-call | flops 150994944 | bytes 2359296 | tf_op jit(solution)/shard_map/three_0/pallas_call | solution.py:204
  38.6 0.7 %collective-permute-start.16 = (f32[4,32,128]{2,1,0:T(8,128)S(1)}, f32[4,32,128]{2,1,0:T(8,128)S(1)}, u32[]{:S(2)}, u32[]{:S(2)}) collective-permute-start(f32[4,32,128]{2,1,0:T(8,128)S(1)} %three_0.1.refs_3_), channel_id=1, source_target_pairs={{4,8},{8,4},{12,16},{16,12},{20,24},{24,20},{5,9},{9,5},{13,17},{1... | collective-permute-start | bytes 196616 | tf_op jit(solution)/shard_map/ppermute | solution.py:291
  39.3 0.6 collective-permute-done.14.refs_5_
  39.9 0.7 %three_1.1.refs_4_ = f32[4,32,128]{2,1,0:T(8,128)S(1)} custom-call(bf16[2,2,256,1152]{3,2,1,0:T(8,128)(2,1)S(1)} %prepare_chip.1.refs_0_, bf16[1,2,256,1152]{3,2,1,0:T(8,128)(2,1)S(1)} %prepare_border.1.refs_1_, bf16[1,2,256,1152]{3,2,1,0:T(8,128)(2,1)S(1)} %prepare_inner.1.refs_2_, f32[4,32,128]{2,1,0:T(8,128)S(1)} %pad_maximum_fusion.2.refs_3_.refs_6_, ...), custom_call_target="tpu_custom_call" | custom-call | flops 150994944 | bytes 2359296 | tf_op jit(solution)/shard_map/three_1/pallas_call | solution.py:204
  40.6 5.0 %collective-permute-start.15 = (f32[4,32,128]{2,1,0:T(8,128)S(1)}, f32[4,32,128]{2,1,0:T(8,128)S(1)}, u32[]{:S(2)}, u32[]{:S(2)}) collective-permute-start(f32[4,32,128]{2,1,0:T(8,128)S(1)} %three_1.1.refs_4_), channel_id=1, source_target_pairs={{0,4},{4,0},{8,12},{12,8},{16,20},{20,16},{24,28},{28,24},{1,5},{5... | collective-permute-start | bytes 196616 | tf_op jit(solution)/shard_map/ppermute | solution.py:294
  45.6 0.9 %four_0.1 = (f32[4,32,128]{2,1,0:T(8,128)S(1)}, f32[32,128]{1,0:T(8,128)S(1)}) custom-call(bf16[2,2,256,1152]{3,2,1,0:T(8,128)(2,1)S(1)} %prepare_chip.1.refs_0_, bf16[1,2,256,1152]{3,2,1,0:T(8,128)(2,1)S(1)} %prepare_border.1.refs_1_, bf16[1,2,256,1152]{3,2,1,0:T(8,128)(2,1)S(1)} %prepare_inner.1.refs_2_, f32[4,32,128]{2,1,0:T(8,128)S(1)} %three_0.1.refs_3_, ...), custom_call_target="tpu_custom_call" | custom-call | flops 150994944 | bytes 2359296 | tf_op jit(solution)/shard_map/four_0/pallas_call | solution.py:204
  46.5 1.3 %collective-permute-done.15.refs_5_ = f32[4,32,128]{2,1,0:T(8,128)S(1)} collective-permute-done((f32[4,32,128]{2,1,0:T(8,128)S(1)}, f32[4,32,128]{2,1,0:T(8,128)S(1)}, u32[]{:S(2)}, u32[]{:S(2)}) %collective-permute-start.15) | collective-permute-done | bytes 65568 | tf_op jit(solution)/shard_map/ppermute | solution.py:294
  47.8 1.0 %four_1.1 = (f32[4,24,128]{2,1,0:T(8,128)S(1)}, f32[4,24,128]{2,1,0:T(8,128)S(1)}) custom-call(bf16[2,2,256,1152]{3,2,1,0:T(8,128)(2,1)S(1)} %prepare_chip.1.refs_0_, bf16[1,2,256,1152]{3,2,1,0:T(8,128)(2,1)S(1)} %prepare_border.1.refs_1_, bf16[1,2,256,1152]{3,2,1,0:T(8,128)(2,1)S(1)} %prepare_inner.1.refs_2_, f32[4,32,128]{2,1,0:T(8,128)S(1)} %three_0.1.refs_3_, ...), custom_call_target="tpu_custom_call" | custom-call | flops 150994944 | bytes 2359296 | tf_op jit(solution)/shard_map/four_1/pallas_call | solution.py:204
  48.9 1.2 %collective-permute-done.17 = f32[4,24,128]{2,1,0:T(8,128)S(1)} collective-permute-done((f32[4,24,128]{2,1,0:T(8,128)S(1)}, f32[4,24,128]{2,1,0:T(8,128)S(1)}, u32[]{:S(2)}, u32[]{:S(2)}) %collective-permute-start.17) | collective-permute-done | bytes 49184 | tf_op jit(solution)/shard_map/ppermute | solution.py:288
  50.1 0.6 %pad_maximum_fusion = f32[8,24,128]{2,1,0:T(8,128)} fusion(f32[3,24,128]{2,1,0:T(8,128)S(1)} %slice.124, f32[4,24,128]{2,1,0:T(8,128)S(1)} %collective-permute-done.17, f32[1,24,128]{2,1,0:T(8,128)S(1)} %slice.123), kind=kLoop, calls=%fused_computation | loop fusion | flops 49152 | bytes 196608 | tf_op jit(solution)/shard_map/concatenate | solution.py:342
  50.7 5.3 %all-to-all-start = ((f32[8,24,128]{2,1,0:T(8,128)}), f32[8,24,128]{2,1,0:T(8,128)S(1)}, u32[]{:S(2)}, u32[]{:S(2)}) async-start(f32[8,24,128]{2,1,0:T(8,128)} %pad_maximum_fusion), calls=%async_computation | async-start | bytes 196608 | tf_op jit(solution)/shard_map/all_to_all | solution.py:348
  56.2 6.5 %all-to-all-done.parts_ref = f32[8,24,128]{2,1,0:T(8,128)S(1)} async-done(((f32[8,24,128]{2,1,0:T(8,128)}), f32[8,24,128]{2,1,0:T(8,128)S(1)}, u32[]{:S(2)}, u32[]{:S(2)}) %all-to-all-start) | async-done | bytes 98336 | tf_op jit(solution)/shard_map/all_to_all | solution.py:348
  62.7 1.5 %finish.1 = f32[8,1,16,128]{3,2,1,0:T(8,128)} custom-call(s32[32,128]{1,0:T(8,128)S(1)} %broadcast_in_dim.12.flags_ref.refs_9_, f32[8,24,128]{2,1,0:T(8,128)S(1)} %all-to-all-done.parts_ref, f32[8,8]{1,0:T(8,128)S(1)} %bitcast.27), custom_call_target="tpu_custom_call" | custom-call | tf_op jit(solution)/shard_map/finish/pallas_call | solution.py:258
  (46 shorter events, 0.5 us)
Async XLA Ops:
  0.0 56.1 %copy-start = (f32[8,8,8]{2,1,0:T(8,128)S(1)}, f32[8,8,8]{2,1,0:T(8,128)}, u32[]{:S(2)}) copy-start(f32[8,8,8]{2,1,0:T(8,128)} %param.7) | copy-start | bytes 6148
  0.0 3.7 %copy-start.1 = (f32[1,2,5,128,128]{4,3,2,1,0:T(8,128)S(1)}, f32[1,2,5,128,128]{4,3,2,1,0:T(8,128)}, u32[]{:S(2)}) copy-start(f32[1,2,5,128,128]{4,3,2,1,0:T(8,128)} %refs_0_.1) | copy-start | bytes 1966084
  0.0 3.6 %collective-permute-start.1 = (f32[1,2,5,128,128]{4,3,2,1,0:T(8,128)}, f32[1,2,5,128,128]{4,3,2,1,0:T(8,128)S(1)}, u32[]{:S(2)}, u32[]{:S(2)}) collective-permute-start(f32[1,2,5,128,128]{4,3,2,1,0:T(8,128)} %refs_0_.1), channel_id=1, source_target_pairs={{0,1},{1,0},{2,3},{3,2},{4,5},{5,4},{6,7},{7,6},{8,9},{9,8},{10,11... | collective-permute-start | bytes 1966088 | tf_op jit(solution)/shard_map/ppermute | solution.py:288
  0.8 0.8 %copy-start.2 = (f32[64,1,2,128]{3,2,1,0:T(2,128)S(1)}, f32[64,1,2,128]{3,2,1,0:T(2,128)}, u32[]{:S(2)}) copy-start(f32[64,1,2,128]{3,2,1,0:T(2,128)} %slab_ref.1) | copy-start | bytes 196612
  1.6 0.7 %copy-start.3 = (s32[1,2,5]{2,1,0:T(2,128)S(1)}, s32[1,2,5]{2,1,0:T(2,128)}, u32[]{:S(2)}) copy-start(s32[1,2,5]{2,1,0:T(2,128)} %codes_ref.1) | copy-start | bytes 124
  2.4 1.3 %collective-permute-start = (f32[72,128]{1,0:T(8,128)S(1)}, f32[72,128]{1,0:T(8,128)S(1)}, u32[]{:S(2)}, u32[]{:S(2)}) collective-permute-start(f32[72,128]{1,0:T(8,128)S(1)} %get-tuple-element.46), channel_id=1, source_target_pairs={{0,1},{1,0},{2,3},{3,2},{4,5},{5,4},{6,7},{7,6},{8,9},{9,8},{10,11... | collective-permute-start | bytes 110600 | tf_op jit(solution)/shard_map/ppermute | solution.py:288
  3.8 5.3 %collective-permute-start.2 = (f32[2,72,128]{2,1,0:T(8,128)S(1)}, f32[2,72,128]{2,1,0:T(8,128)S(1)}, u32[]{:S(2)}, u32[]{:S(2)}) collective-permute-start(f32[2,72,128]{2,1,0:T(8,128)S(1)} %pad_maximum_fusion.1), channel_id=1, source_target_pairs={{0,3},{1,2},{2,1},{3,0},{4,7},{5,6},{6,5},{7,4},{8,11},{9,10},{10,... | collective-permute-start | bytes 221192 | tf_op jit(solution)/shard_map/ppermute | solution.py:285
  6.4 9.7 %collective-permute-start.3 = (f32[1,1,5,128,128]{4,3,2,1,0:T(8,128)S(1)}, f32[1,1,5,128,128]{4,3,2,1,0:T(8,128)S(1)}, u32[]{:S(2)}, u32[]{:S(2)}) collective-permute-start(f32[1,1,5,128,128]{4,3,2,1,0:T(8,128)S(1)} %get-tuple-element.23), channel_id=1, source_target_pairs={{0,3},{1,2},{2,1},{3,0},{4,7},{5,6},{6,5},{7,4},{8,11},{9,10},{10,... | collective-permute-start | bytes 983048 | tf_op jit(solution)/shard_map/ppermute | solution.py:285
  9.0 6.2 %collective-permute-start.4 = (f32[4,32,128]{2,1,0:T(8,128)S(1)}, f32[4,32,128]{2,1,0:T(8,128)S(1)}, u32[]{:S(2)}, u32[]{:S(2)}) collective-permute-start(f32[4,32,128]{2,1,0:T(8,128)S(1)} %maximum_select_fusion.refs_2_.refs_4_), channel_id=1, source_target_pairs={{4,8},{8,4},{12,16},{16,12},{20,24},{24,20},{5,9},{9,5},{13,17},{1... | collective-permute-start | bytes 196616 | tf_op jit(solution)/shard_map/ppermute | solution.py:291
  9.7 7.3 %collective-permute-start.6 = (f32[4,32,128]{2,1,0:T(8,128)S(1)}, f32[4,32,128]{2,1,0:T(8,128)S(1)}, u32[]{:S(2)}, u32[]{:S(2)}) collective-permute-start(f32[4,32,128]{2,1,0:T(8,128)S(1)} %maximum_select_fusion.1.refs_3_.refs_4_), channel_id=1, source_target_pairs={{0,4},{4,0},{8,12},{12,8},{16,20},{20,16},{24,28},{28,24},{1,5},{5... | collective-permute-start | bytes 196616 | tf_op jit(solution)/shard_map/ppermute | solution.py:294
  16.1 2.4 %collective-permute-start.5 = (f32[1,1,5,128,128]{4,3,2,1,0:T(8,128)S(1)}, f32[1,1,5,128,128]{4,3,2,1,0:T(8,128)S(1)}, u32[]{:S(2)}, u32[]{:S(2)}) collective-permute-start(f32[1,1,5,128,128]{4,3,2,1,0:T(8,128)S(1)} %collective-permute-done.3.refs_0_), channel_id=1, source_target_pairs={{0,1},{1,0},{2,3},{3,2},{4,5},{5,4},{6,7},{7,6},{8,9},{9,8},{10,11... | collective-permute-start | bytes 983048 | tf_op jit(solution)/shard_map/ppermute | solution.py:288
  17.1 9.7 %collective-permute-start.7 = (f32[1,1,5,128,128]{4,3,2,1,0:T(8,128)S(1)}, f32[1,1,5,128,128]{4,3,2,1,0:T(8,128)S(1)}, u32[]{:S(2)}, u32[]{:S(2)}) collective-permute-start(f32[1,1,5,128,128]{4,3,2,1,0:T(8,128)S(1)} %get-tuple-element.27), channel_id=1, source_target_pairs={{0,3},{1,2},{2,1},{3,0},{4,7},{5,6},{6,5},{7,4},{8,11},{9,10},{10,... | collective-permute-start | bytes 983048 | tf_op jit(solution)/shard_map/ppermute | solution.py:285
  19.8 7.0 %collective-permute-start.8 = (f32[3,32,128]{2,1,0:T(8,128)S(1)}, f32[3,32,128]{2,1,0:T(8,128)S(1)}, u32[]{:S(2)}, u32[]{:S(2)}) collective-permute-start(f32[3,32,128]{2,1,0:T(8,128)S(1)} %one_0.1.refs_1_), channel_id=1, source_target_pairs={{4,8},{8,4},{12,16},{16,12},{20,24},{24,20},{5,9},{9,5},{13,17},{1... | collective-permute-start | bytes 147464 | tf_op jit(solution)/shard_map/ppermute | solution.py:291
  21.1 8.0 %collective-permute-start.11 = (f32[3,32,128]{2,1,0:T(8,128)S(1)}, f32[3,32,128]{2,1,0:T(8,128)S(1)}, u32[]{:S(2)}, u32[]{:S(2)}) collective-permute-start(f32[3,32,128]{2,1,0:T(8,128)S(1)} %one_1.1.refs_2_), channel_id=1, source_target_pairs={{0,4},{4,0},{8,12},{12,8},{16,20},{20,16},{24,28},{28,24},{1,5},{5... | collective-permute-start | bytes 147464 | tf_op jit(solution)/shard_map/ppermute | solution.py:294
  27.3 3.9 %collective-permute-start.9 = (f32[3,32,128]{2,1,0:T(8,128)S(1)}, f32[3,32,128]{2,1,0:T(8,128)S(1)}, u32[]{:S(2)}, u32[]{:S(2)}) collective-permute-start(f32[3,32,128]{2,1,0:T(8,128)S(1)} %pad_maximum_fusion.6), channel_id=1, source_target_pairs={{0,3},{1,2},{2,1},{3,0},{4,7},{5,6},{6,5},{7,4},{8,11},{9,10},{10,... | collective-permute-start | bytes 147464 | tf_op jit(solution)/shard_map/ppermute | solution.py:285
  29.5 3.8 %collective-permute-start.12 = (f32[3,32,128]{2,1,0:T(8,128)S(1)}, f32[3,32,128]{2,1,0:T(8,128)S(1)}, u32[]{:S(2)}, u32[]{:S(2)}) collective-permute-start(f32[3,32,128]{2,1,0:T(8,128)S(1)} %pad_maximum_fusion.7), channel_id=1, source_target_pairs={{0,3},{1,2},{2,1},{3,0},{4,7},{5,6},{6,5},{7,4},{8,11},{9,10},{10,... | collective-permute-start | bytes 147464 | tf_op jit(solution)/shard_map/ppermute | solution.py:285
  31.2 6.7 %collective-permute-start.13 = (f32[4,32,128]{2,1,0:T(8,128)S(1)}, f32[4,32,128]{2,1,0:T(8,128)S(1)}, u32[]{:S(2)}, u32[]{:S(2)}) collective-permute-start(f32[4,32,128]{2,1,0:T(8,128)S(1)} %pad_maximum_fusion.2.refs_3_.refs_6_), channel_id=1, source_target_pairs={{4,8},{8,4},{12,16},{16,12},{20,24},{24,20},{5,9},{9,5},{13,17},{1... | collective-permute-start | bytes 196616 | tf_op jit(solution)/shard_map/ppermute | solution.py:291
  31.9 5.3 %collective-permute-start.10 = (f32[1,1,5,128,128]{4,3,2,1,0:T(8,128)S(1)}, f32[1,1,5,128,128]{4,3,2,1,0:T(8,128)S(1)}, u32[]{:S(2)}, u32[]{:S(2)}) collective-permute-start(f32[1,1,5,128,128]{4,3,2,1,0:T(8,128)S(1)} %collective-permute-done.7.refs_0_), channel_id=1, source_target_pairs={{0,1},{1,0},{2,3},{3,2},{4,5},{5,4},{6,7},{7,6},{8,9},{9,8},{10,11... | collective-permute-start | bytes 983048 | tf_op jit(solution)/shard_map/ppermute | solution.py:288
  33.3 6.6 %collective-permute-start.14 = (f32[4,32,128]{2,1,0:T(8,128)S(1)}, f32[4,32,128]{2,1,0:T(8,128)S(1)}, u32[]{:S(2)}, u32[]{:S(2)}) collective-permute-start(f32[4,32,128]{2,1,0:T(8,128)S(1)} %pad_maximum_fusion.3.refs_4_.refs_6_), channel_id=1, source_target_pairs={{0,4},{4,0},{8,12},{12,8},{16,20},{20,16},{24,28},{28,24},{1,5},{5... | collective-permute-start | bytes 196616 | tf_op jit(solution)/shard_map/ppermute | solution.py:294
  38.6 7.0 %collective-permute-start.16 = (f32[4,32,128]{2,1,0:T(8,128)S(1)}, f32[4,32,128]{2,1,0:T(8,128)S(1)}, u32[]{:S(2)}, u32[]{:S(2)}) collective-permute-start(f32[4,32,128]{2,1,0:T(8,128)S(1)} %three_0.1.refs_3_), channel_id=1, source_target_pairs={{4,8},{8,4},{12,16},{16,12},{20,24},{24,20},{5,9},{9,5},{13,17},{1... | collective-permute-start | bytes 196616 | tf_op jit(solution)/shard_map/ppermute | solution.py:291
  40.6 7.2 %collective-permute-start.15 = (f32[4,32,128]{2,1,0:T(8,128)S(1)}, f32[4,32,128]{2,1,0:T(8,128)S(1)}, u32[]{:S(2)}, u32[]{:S(2)}) collective-permute-start(f32[4,32,128]{2,1,0:T(8,128)S(1)} %three_1.1.refs_4_), channel_id=1, source_target_pairs={{0,4},{4,0},{8,12},{12,8},{16,20},{20,16},{24,28},{28,24},{1,5},{5... | collective-permute-start | bytes 196616 | tf_op jit(solution)/shard_map/ppermute | solution.py:294
  48.8 1.3 %collective-permute-start.17 = (f32[4,24,128]{2,1,0:T(8,128)S(1)}, f32[4,24,128]{2,1,0:T(8,128)S(1)}, u32[]{:S(2)}, u32[]{:S(2)}) collective-permute-start(f32[4,24,128]{2,1,0:T(8,128)S(1)} %get-tuple-element.36), channel_id=1, source_target_pairs={{0,1},{1,0},{2,3},{3,2},{4,5},{5,4},{6,7},{7,6},{8,9},{9,8},{10,11... | collective-permute-start | bytes 147464 | tf_op jit(solution)/shard_map/ppermute | solution.py:288
  50.7 11.9 %all-to-all-start = ((f32[8,24,128]{2,1,0:T(8,128)}), f32[8,24,128]{2,1,0:T(8,128)S(1)}, u32[]{:S(2)}, u32[]{:S(2)}) async-start(f32[8,24,128]{2,1,0:T(8,128)} %pad_maximum_fusion), calls=%async_computation | async-start | bytes 196608 | tf_op jit(solution)/shard_map/all_to_all | solution.py:348

commit v5 on v2

--- a/solution.py
+++ b/solution.py
@@ -232,7 +232,11 @@
         factor = gram[:, k : k + 1] * scale
         gram = gram - factor * top
         inverse = jnp.where(row == k, top_inverse, jnp.where(row > k, inverse - factor * top_inverse, inverse))
-    turn = rot_ref[...]
+    number = jnp.broadcast_to(flags_ref[3 * VEC : 3 * VEC + 1, 0:VEC], (VEC, VEC))
+    turn = rot_ref[0]
+    for w in range(1, wide):
+        turn = jnp.where(number == w, rot_ref[w], turn)
+    turn = turn.T
     mixer = turn[:, 0:1] * inverse[0:1, :]
     for k in range(1, VEC):
         mixer = mixer + turn[:, k : k + 1] * inverse[k : k + 1, :]
@@ -253,7 +257,7 @@
             out_ref[:, 0, w * cols + c, :] = jnp.where(half, second, first)
 
 
-def finish(flags, cols, node_count, parts, turn):
+def finish(flags, cols, node_count, parts, rotation):
     wide, _, size = parts.shape
     return pl.pallas_call(
         functools.partial(finish_kernel, cols, node_count),
@@ -262,7 +266,7 @@
         out_shape=jax.ShapeDtypeStruct((VEC, 1, wide * cols, size), jnp.float32),
         compiler_params=pltpu.CompilerParams(vmem_limit_bytes=LIMIT),
         name="finish",
-    )(flags, parts, turn)
+    )(flags, parts, rotation)
 
 
 def after(x, token):
@@ -279,7 +283,8 @@
     x = mine // 2
     edge = half = x ^ (mine % 2)
     place = jnp.stack([odd, edge, half, x]).astype(jnp.int32)
-    flags = jnp.broadcast_to(jnp.repeat(place, VEC)[:, None], (4 * VEC, size))
+    flags = jnp.stack([odd, edge, half, lax.axis_index("wide")]).astype(jnp.int32)
+    flags = jnp.broadcast_to(jnp.repeat(flags, VEC)[:, None], (4 * VEC, size))
 
     def across(value):
         return lax.ppermute(value, "grp", [(i, i ^ 3) for i in range(grp)])
@@ -353,9 +358,8 @@
         tiled=True,
         axis_index_groups=groups,
     )
-    turn = lax.dynamic_index_in_dim(rotation, lax.axis_index("wide"), 0, keepdims=False)
     node_count = grp * wide * cols * size
-    return finish(flags, cols, node_count, packed, turn.T)
+    return finish(flags, cols, node_count, packed, rotation)
 
 
 def solution(mesh):

time: 63.5 us -> 62.6 us (0.986)
  blocking collectives: 0 us -> 10.7 us
  starting transfers between devices: 35.2 us -> 28.4 us
  waiting for transfers between devices: 15.5 us -> 11.4 us
  other arithmetic: 0.8 us -> 0.16 us
    all_to_all x0 -> x1, blocking collectives: none -> 10.7 us  [body(): lax.all_to_all(packed, ('wide', 'grp'), split_axis=0, concat_axis=0, tile...]
    all_to_all x1 -> x0, starting transfers between devices: 6.8 us -> none  [body(): lax.all_to_all(packed, ('wide', 'grp'), split_axis=0, concat_axis=0, tile...]
    all_to_all x1 -> x0, waiting for transfers between devices: 4.07 us -> none  [body(): lax.all_to_all(packed, ('wide', 'grp'), split_axis=0, concat_axis=0, tile...]
    concatenate x1, other arithmetic: 0.64 us -> 0.01 us  [body(): packed = jnp.concatenate([core(sent), kept])]
  transfers between devices with their start and end apart: 19 -> 18, of which waited for: 11 -> 10; matrix products, arithmetic and copies ran while one was open for 1% -> 1% of each run, Pallas kernels for 11% -> 11%
where the time goes in v5:
time: 62.6 us; the launch traced here: 62.3 us
  starting transfers between devices  28.4 us (45%)
  waiting for transfers between devices  11.4 us (18%)
  blocking collectives  10.7 us (17%)
  Pallas kernels  9.29 us (15%)
  local copies, waits for them, and re-layouts  1.99 us (3%)
    ppermute x4, starting transfers between devices, over_near(): return lax.ppermute(value, 'wide', near)  18.6 us
    all_to_all x1, blocking collectives, body(): lax.all_to_all(packed, ('wide', 'grp'), split_axis=0, concat_axis=0, tile...  10.7 us
    ppermute x5, waiting for transfers between devices, across(): return lax.ppermute(value, 'grp', [(i, i ^ 3) for i in range(grp)])  6.62 us
    ppermute x5, starting transfers between devices, across(): return lax.ppermute(value, 'grp', [(i, i ^ 3) for i in range(grp)])  6.07 us
    pallas_call x8, Pallas kernels, step(): pl.pallas_call(functools.partial(step_kernel, kind, u, len(h_ready)), in_...  5.33 us
    ppermute x4, starting transfers between devices, over_far(): return lax.ppermute(value, 'wide', far)  2.66 us
    ppermute x4, waiting for transfers between devices, over_near(): return lax.ppermute(value, 'wide', near)  2.44 us
    ppermute x5, waiting for transfers between devices, core(): return lax.ppermute(value, 'grp', [(i, i ^ 1) for i in range(grp)])  2.38 us
  transfers between devices with their start and end apart: 18, of which 10 were waited for; matrix products, arithmetic and copies ran while one was open for 1% of the time, Pallas kernels for 11%

profile of v5, /device:TPU:0, one launch (start us, length us, event | category | flops | bytes accessed | tf_op | source)
XLA Modules:
  0.0 62.3 jit_solution(9573738943460598643)
XLA Ops:
  0.0 0.5 collective-permute-start.1
  0.5 0.1 pad_add_fusion
  0.5 0.1 broadcast_in_dim.10
  0.6 0.1 broadcast_in_dim.11
  0.7 0.1 broadcast_in_dim.12.flags_ref.refs_9_
  0.8 0.8 %copy-done.1 = f32[64,1,2,128]{3,2,1,0:T(2,128)S(1)} copy-done((f32[64,1,2,128]{3,2,1,0:T(2,128)S(1)}, f32[64,1,2,128]{3,2,1,0:T(2,128)}, u32[]{:S(2)}) %copy-start.1) | copy-done | bytes 65560
  1.6 0.7 %copy-done.3 = s32[1,2,5]{2,1,0:T(2,128)S(1)} copy-done((s32[1,2,5]{2,1,0:T(2,128)S(1)}, s32[1,2,5]{2,1,0:T(2,128)}, u32[]{:S(2)}) %copy-start.3) | copy-done | bytes 64
  2.4 0.1 collective-permute-start
  2.5 1.1 %collective-permute-done = f32[72,128]{1,0:T(8,128)S(1)} collective-permute-done((f32[72,128]{1,0:T(8,128)S(1)}, f32[72,128]{1,0:T(8,128)S(1)}, u32[]{:S(2)}, u32[]{:S(2)}) %collective-permute-start) | collective-permute-done | bytes 36896 | tf_op jit(solution)/shard_map/ppermute | solution.py:293
  3.7 0.1 pick.1
  3.7 2.7 %collective-permute-start.2 = (f32[2,72,128]{2,1,0:T(8,128)S(1)}, f32[2,72,128]{2,1,0:T(8,128)S(1)}, u32[]{:S(2)}, u32[]{:S(2)}) collective-permute-start(f32[2,72,128]{2,1,0:T(8,128)S(1)} %pad_maximum_fusion.1), channel_id=1, source_target_pairs={{0,3},{1,2},{2,1},{3,0},{4,7},{5,6},{6,5},{7,4},{8,11},{9,10},{10,... | collective-permute-start | bytes 221192 | tf_op jit(solution)/shard_map/ppermute | solution.py:290
  6.4 0.1 collective-permute-start.3
  6.5 2.5 %collective-permute-done.2 = f32[2,72,128]{2,1,0:T(8,128)S(1)} collective-permute-done((f32[2,72,128]{2,1,0:T(8,128)S(1)}, f32[2,72,128]{2,1,0:T(8,128)S(1)}, u32[]{:S(2)}, u32[]{:S(2)}) %collective-permute-start.2) | collective-permute-done | bytes 73760 | tf_op jit(solution)/shard_map/ppermute | solution.py:290
  9.0 0.7 %collective-permute-start.4 = (f32[4,32,128]{2,1,0:T(8,128)S(1)}, f32[4,32,128]{2,1,0:T(8,128)S(1)}, u32[]{:S(2)}, u32[]{:S(2)}) collective-permute-start(f32[4,32,128]{2,1,0:T(8,128)S(1)} %maximum_select_fusion.refs_2_.refs_4_), channel_id=1, source_target_pairs={{4,8},{8,4},{12,16},{16,12},{20,24},{24,20},{5,9},{9,5},{13,17},{1... | collective-permute-start | bytes 196616 | tf_op jit(solution)/shard_map/ppermute | solution.py:296
  9.7 4.4 %collective-permute-start.6 = (f32[4,32,128]{2,1,0:T(8,128)S(1)}, f32[4,32,128]{2,1,0:T(8,128)S(1)}, u32[]{:S(2)}, u32[]{:S(2)}) collective-permute-start(f32[4,32,128]{2,1,0:T(8,128)S(1)} %maximum_select_fusion.1.refs_3_.refs_4_), channel_id=1, source_target_pairs={{0,4},{4,0},{8,12},{12,8},{16,20},{20,16},{24,28},{28,24},{1,5},{5... | collective-permute-start | bytes 196616 | tf_op jit(solution)/shard_map/ppermute | solution.py:299
  14.2 0.1 convert_element_type.8
  14.3 0.1 concatenate.24.codes_ref
  14.3 0.9 %prepare_chip.1.refs_0_ = bf16[2,2,256,1152]{3,2,1,0:T(8,128)(2,1)S(1)} custom-call(s32[44]{0:T(128)S(1)} %concatenate.24.codes_ref, f32[1,2,5,128,128]{4,3,2,1,0:T(8,128)S(1)} %copy-done, f32[1,2,5,128,128]{4,3,2,1,0:T(8,128)S(1)} %collective-permute-done.1.core_ref.refs_1_), custom_call_target="tpu_custom_call" | custom-call | tf_op jit(solution)/shard_map/prepare_chip/pallas_call | solution.py:114
  15.3 0.8 %collective-permute-done.3.refs_0_ = f32[1,1,5,128,128]{4,3,2,1,0:T(8,128)S(1)} collective-permute-done((f32[1,1,5,128,128]{4,3,2,1,0:T(8,128)S(1)}, f32[1,1,5,128,128]{4,3,2,1,0:T(8,128)S(1)}, u32[]{:S(2)}, u32[]{:S(2)}) %collective-permute-start.3) | collective-permute-done | bytes 327712 | tf_op jit(solution)/shard_map/ppermute | solution.py:290
  16.1 0.5 collective-permute-start.5
  16.5 0.5 collective-permute-done.6.refs_4_
  17.1 1.4 %collective-permute-start.7 = (f32[1,1,5,128,128]{4,3,2,1,0:T(8,128)S(1)}, f32[1,1,5,128,128]{4,3,2,1,0:T(8,128)S(1)}, u32[]{:S(2)}, u32[]{:S(2)}) collective-permute-start(f32[1,1,5,128,128]{4,3,2,1,0:T(8,128)S(1)} %get-tuple-element.27), channel_id=1, source_target_pairs={{0,3},{1,2},{2,1},{3,0},{4,7},{5,6},{6,5},{7,4},{8,11},{9,10},{10,... | collective-permute-start | bytes 983048 | tf_op jit(solution)/shard_map/ppermute | solution.py:290
  18.5 0.7 %prepare_border.1.refs_1_ = bf16[1,2,256,1152]{3,2,1,0:T(8,128)(2,1)S(1)} custom-call(s32[44]{0:T(128)S(1)} %concatenate.24.codes_ref, f32[1,1,5,128,128]{4,3,2,1,0:T(8,128)S(1)} %collective-permute-done.3.refs_0_, f32[1,1,5,128,128]{4,3,2,1,0:T(8,128)S(1)} %collective-permute-done.5.refs_1_), custom_call_target="tpu_custom_call" | custom-call | tf_op jit(solution)/shard_map/prepare_border/pallas_call | solution.py:114
  19.2 0.6 one_0.1.refs_1_
  19.8 0.7 %collective-permute-start.8 = (f32[3,32,128]{2,1,0:T(8,128)S(1)}, f32[3,32,128]{2,1,0:T(8,128)S(1)}, u32[]{:S(2)}, u32[]{:S(2)}) collective-permute-start(f32[3,32,128]{2,1,0:T(8,128)S(1)} %one_0.1.refs_1_), channel_id=1, source_target_pairs={{4,8},{8,4},{12,16},{16,12},{20,24},{24,20},{5,9},{9,5},{13,17},{1... | collective-permute-start | bytes 147464 | tf_op jit(solution)/shard_map/ppermute | solution.py:296
  20.5 0.6 one_1.1.refs_2_
  21.1 5.3 %collective-permute-start.11 = (f32[3,32,128]{2,1,0:T(8,128)S(1)}, f32[3,32,128]{2,1,0:T(8,128)S(1)}, u32[]{:S(2)}, u32[]{:S(2)}) collective-permute-start(f32[3,32,128]{2,1,0:T(8,128)S(1)} %one_1.1.refs_2_), channel_id=1, source_target_pairs={{0,4},{4,0},{8,12},{12,8},{16,20},{20,16},{24,28},{28,24},{1,5},{5... | collective-permute-start | bytes 147464 | tf_op jit(solution)/shard_map/ppermute | solution.py:299
  26.4 0.4 collective-permute-done.7.refs_0_
  26.8 0.4 two_0.1
  27.3 1.8 %collective-permute-start.9 = (f32[3,32,128]{2,1,0:T(8,128)S(1)}, f32[3,32,128]{2,1,0:T(8,128)S(1)}, u32[]{:S(2)}, u32[]{:S(2)}) collective-permute-start(f32[3,32,128]{2,1,0:T(8,128)S(1)} %pad_maximum_fusion.6), channel_id=1, source_target_pairs={{0,3},{1,2},{2,1},{3,0},{4,7},{5,6},{6,5},{7,4},{8,11},{9,10},{10,... | collective-permute-start | bytes 147464 | tf_op jit(solution)/shard_map/ppermute | solution.py:290
  29.1 0.4 two_1.1
  29.5 0.1 collective-permute-start.12
  29.6 1.6 %collective-permute-done.9 = f32[3,32,128]{2,1,0:T(8,128)S(1)} collective-permute-done((f32[3,32,128]{2,1,0:T(8,128)S(1)}, f32[3,32,128]{2,1,0:T(8,128)S(1)}, u32[]{:S(2)}, u32[]{:S(2)}) %collective-permute-start.9) | collective-permute-done | bytes 49184 | tf_op jit(solution)/shard_map/ppermute | solution.py:290
  31.2 0.7 %collective-permute-start.13 = (f32[4,32,128]{2,1,0:T(8,128)S(1)}, f32[4,32,128]{2,1,0:T(8,128)S(1)}, u32[]{:S(2)}, u32[]{:S(2)}) collective-permute-start(f32[4,32,128]{2,1,0:T(8,128)S(1)} %pad_maximum_fusion.2.refs_3_.refs_6_), channel_id=1, source_target_pairs={{4,8},{8,4},{12,16},{16,12},{20,24},{24,20},{5,9},{9,5},{13,17},{1... | collective-permute-start | bytes 196616 | tf_op jit(solution)/shard_map/ppermute | solution.py:296
  32.0 1.3 %collective-permute-done.12 = f32[3,32,128]{2,1,0:T(8,128)S(1)} collective-permute-done((f32[3,32,128]{2,1,0:T(8,128)S(1)}, f32[3,32,128]{2,1,0:T(8,128)S(1)}, u32[]{:S(2)}, u32[]{:S(2)}) %collective-permute-start.12) | collective-permute-done | bytes 49184 | tf_op jit(solution)/shard_map/ppermute | solution.py:290
  33.3 3.9 %collective-permute-start.14 = (f32[4,32,128]{2,1,0:T(8,128)S(1)}, f32[4,32,128]{2,1,0:T(8,128)S(1)}, u32[]{:S(2)}, u32[]{:S(2)}) collective-permute-start(f32[4,32,128]{2,1,0:T(8,128)S(1)} %pad_maximum_fusion.3.refs_4_.refs_6_), channel_id=1, source_target_pairs={{0,4},{4,0},{8,12},{12,8},{16,20},{20,16},{24,28},{28,24},{1,5},{5... | collective-permute-start | bytes 196616 | tf_op jit(solution)/shard_map/ppermute | solution.py:299
  37.2 0.7 %prepare_inner.1.refs_2_ = bf16[1,2,256,1152]{3,2,1,0:T(8,128)(2,1)S(1)} custom-call(s32[44]{0:T(128)S(1)} %concatenate.24.codes_ref, f32[1,1,5,128,128]{4,3,2,1,0:T(8,128)S(1)} %collective-permute-done.7.refs_0_, f32[1,1,5,128,128]{4,3,2,1,0:T(8,128)S(1)} %collective-permute-done.10.refs_1_), custom_call_target="tpu_custom_call" | custom-call | tf_op jit(solution)/shard_map/prepare_inner/pallas_call | solution.py:114
  37.9 0.7 %three_0.1.refs_3_ = f32[4,32,128]{2,1,0:T(8,128)S(1)} custom-call(bf16[2,2,256,1152]{3,2,1,0:T(8,128)(2,1)S(1)} %prepare_chip.1.refs_0_, bf16[1,2,256,1152]{3,2,1,0:T(8,128)(2,1)S(1)} %prepare_border.1.refs_1_, bf16[1,2,256,1152]{3,2,1,0:T(8,128)(2,1)S(1)} %prepare_inner.1.refs_2_, f32[4,32,128]{2,1,0:T(8,128)S(1)} %pad_maximum_fusion.2.refs_3_.refs_6_, ...), custom_call_target="tpu_custom_call" | custom-call | flops 150994944 | bytes 2359296 | tf_op jit(solution)/shard_map/three_0/pallas_call | solution.py:204
  38.6 0.7 %collective-permute-start.16 = (f32[4,32,128]{2,1,0:T(8,128)S(1)}, f32[4,32,128]{2,1,0:T(8,128)S(1)}, u32[]{:S(2)}, u32[]{:S(2)}) collective-permute-start(f32[4,32,128]{2,1,0:T(8,128)S(1)} %three_0.1.refs_3_), channel_id=1, source_target_pairs={{4,8},{8,4},{12,16},{16,12},{20,24},{24,20},{5,9},{9,5},{13,17},{1... | collective-permute-start | bytes 196616 | tf_op jit(solution)/shard_map/ppermute | solution.py:296
  39.3 0.6 collective-permute-done.14.refs_5_
  39.9 0.7 %three_1.1.refs_4_ = f32[4,32,128]{2,1,0:T(8,128)S(1)} custom-call(bf16[2,2,256,1152]{3,2,1,0:T(8,128)(2,1)S(1)} %prepare_chip.1.refs_0_, bf16[1,2,256,1152]{3,2,1,0:T(8,128)(2,1)S(1)} %prepare_border.1.refs_1_, bf16[1,2,256,1152]{3,2,1,0:T(8,128)(2,1)S(1)} %prepare_inner.1.refs_2_, f32[4,32,128]{2,1,0:T(8,128)S(1)} %pad_maximum_fusion.2.refs_3_.refs_6_, ...), custom_call_target="tpu_custom_call" | custom-call | flops 150994944 | bytes 2359296 | tf_op jit(solution)/shard_map/three_1/pallas_call | solution.py:204
  40.6 5.0 %collective-permute-start.15 = (f32[4,32,128]{2,1,0:T(8,128)S(1)}, f32[4,32,128]{2,1,0:T(8,128)S(1)}, u32[]{:S(2)}, u32[]{:S(2)}) collective-permute-start(f32[4,32,128]{2,1,0:T(8,128)S(1)} %three_1.1.refs_4_), channel_id=1, source_target_pairs={{0,4},{4,0},{8,12},{12,8},{16,20},{20,16},{24,28},{28,24},{1,5},{5... | collective-permute-start | bytes 196616 | tf_op jit(solution)/shard_map/ppermute | solution.py:299
  45.6 0.9 %four_0.1 = (f32[4,32,128]{2,1,0:T(8,128)S(1)}, f32[32,128]{1,0:T(8,128)S(1)}) custom-call(bf16[2,2,256,1152]{3,2,1,0:T(8,128)(2,1)S(1)} %prepare_chip.1.refs_0_, bf16[1,2,256,1152]{3,2,1,0:T(8,128)(2,1)S(1)} %prepare_border.1.refs_1_, bf16[1,2,256,1152]{3,2,1,0:T(8,128)(2,1)S(1)} %prepare_inner.1.refs_2_, f32[4,32,128]{2,1,0:T(8,128)S(1)} %three_0.1.refs_3_, ...), custom_call_target="tpu_custom_call" | custom-call | flops 150994944 | bytes 2359296 | tf_op jit(solution)/shard_map/four_0/pallas_call | solution.py:204
  46.5 1.3 %collective-permute-done.15.refs_5_ = f32[4,32,128]{2,1,0:T(8,128)S(1)} collective-permute-done((f32[4,32,128]{2,1,0:T(8,128)S(1)}, f32[4,32,128]{2,1,0:T(8,128)S(1)}, u32[]{:S(2)}, u32[]{:S(2)}) %collective-permute-start.15) | collective-permute-done | bytes 65568 | tf_op jit(solution)/shard_map/ppermute | solution.py:299
  47.8 1.0 %four_1.1 = (f32[4,24,128]{2,1,0:T(8,128)S(1)}, f32[4,24,128]{2,1,0:T(8,128)S(1)}) custom-call(bf16[2,2,256,1152]{3,2,1,0:T(8,128)(2,1)S(1)} %prepare_chip.1.refs_0_, bf16[1,2,256,1152]{3,2,1,0:T(8,128)(2,1)S(1)} %prepare_border.1.refs_1_, bf16[1,2,256,1152]{3,2,1,0:T(8,128)(2,1)S(1)} %prepare_inner.1.refs_2_, f32[4,32,128]{2,1,0:T(8,128)S(1)} %three_0.1.refs_3_, ...), custom_call_target="tpu_custom_call" | custom-call | flops 150994944 | bytes 2359296 | tf_op jit(solution)/shard_map/four_1/pallas_call | solution.py:204
  48.9 1.2 %collective-permute-done.17 = f32[4,24,128]{2,1,0:T(8,128)S(1)} collective-permute-done((f32[4,24,128]{2,1,0:T(8,128)S(1)}, f32[4,24,128]{2,1,0:T(8,128)S(1)}, u32[]{:S(2)}, u32[]{:S(2)}) %collective-permute-start.17) | collective-permute-done | bytes 49184 | tf_op jit(solution)/shard_map/ppermute | solution.py:293
  50.1 10.7 %all_to_all.5.parts_ref = f32[8,24,128]{2,1,0:T(8,128)S(1)} all-to-all(f32[8,24,128]{2,1,0:T(8,128)S(1)} %pad_maximum_fusion), channel_id=1, replica_groups={{28,24,20,16,12,8,4,0},{13,9,5,1,29,25,21,17},{14,10,6,2,30,26,22,18},{..., dimensions={0} | all-to-all | bytes 196608 | tf_op jit(solution)/shard_map/all_to_all | solution.py:353
  60.8 1.5 %finish.1 = f32[8,1,16,128]{3,2,1,0:T(8,128)} custom-call(s32[32,128]{1,0:T(8,128)S(1)} %broadcast_in_dim.12.flags_ref.refs_9_, f32[8,24,128]{2,1,0:T(8,128)S(1)} %all_to_all.5.parts_ref, f32[8,8,8]{2,1,0:T(8,128)S(1)} %copy-done.2), custom_call_target="tpu_custom_call" | custom-call | tf_op jit(solution)/shard_map/finish/pallas_call | solution.py:262
  (41 shorter events, 0.3 us)
Async XLA Ops:
  0.0 3.7 %copy-start = (f32[1,2,5,128,128]{4,3,2,1,0:T(8,128)S(1)}, f32[1,2,5,128,128]{4,3,2,1,0:T(8,128)}, u32[]{:S(2)}) copy-start(f32[1,2,5,128,128]{4,3,2,1,0:T(8,128)} %refs_0_.1) | copy-start | bytes 1966084
  0.0 3.6 %collective-permute-start.1 = (f32[1,2,5,128,128]{4,3,2,1,0:T(8,128)}, f32[1,2,5,128,128]{4,3,2,1,0:T(8,128)S(1)}, u32[]{:S(2)}, u32[]{:S(2)}) collective-permute-start(f32[1,2,5,128,128]{4,3,2,1,0:T(8,128)} %refs_0_.1), channel_id=1, source_target_pairs={{0,1},{1,0},{2,3},{3,2},{4,5},{5,4},{6,7},{7,6},{8,9},{9,8},{10,11... | collective-permute-start | bytes 1966088 | tf_op jit(solution)/shard_map/ppermute | solution.py:293
  0.8 0.8 %copy-start.1 = (f32[64,1,2,128]{3,2,1,0:T(2,128)S(1)}, f32[64,1,2,128]{3,2,1,0:T(2,128)}, u32[]{:S(2)}) copy-start(f32[64,1,2,128]{3,2,1,0:T(2,128)} %slab_ref.1) | copy-start | bytes 196612
  1.6 0.7 %copy-start.3 = (s32[1,2,5]{2,1,0:T(2,128)S(1)}, s32[1,2,5]{2,1,0:T(2,128)}, u32[]{:S(2)}) copy-start(s32[1,2,5]{2,1,0:T(2,128)} %codes_ref.1) | copy-start | bytes 124
  2.4 1.3 %collective-permute-start = (f32[72,128]{1,0:T(8,128)S(1)}, f32[72,128]{1,0:T(8,128)S(1)}, u32[]{:S(2)}, u32[]{:S(2)}) collective-permute-start(f32[72,128]{1,0:T(8,128)S(1)} %get-tuple-element.46), channel_id=1, source_target_pairs={{0,1},{1,0},{2,3},{3,2},{4,5},{5,4},{6,7},{7,6},{8,9},{9,8},{10,11... | collective-permute-start | bytes 110600 | tf_op jit(solution)/shard_map/ppermute | solution.py:293
  3.7 5.3 %collective-permute-start.2 = (f32[2,72,128]{2,1,0:T(8,128)S(1)}, f32[2,72,128]{2,1,0:T(8,128)S(1)}, u32[]{:S(2)}, u32[]{:S(2)}) collective-permute-start(f32[2,72,128]{2,1,0:T(8,128)S(1)} %pad_maximum_fusion.1), channel_id=1, source_target_pairs={{0,3},{1,2},{2,1},{3,0},{4,7},{5,6},{6,5},{7,4},{8,11},{9,10},{10,... | collective-permute-start | bytes 221192 | tf_op jit(solution)/shard_map/ppermute | solution.py:290
  6.4 9.7 %collective-permute-start.3 = (f32[1,1,5,128,128]{4,3,2,1,0:T(8,128)S(1)}, f32[1,1,5,128,128]{4,3,2,1,0:T(8,128)S(1)}, u32[]{:S(2)}, u32[]{:S(2)}) collective-permute-start(f32[1,1,5,128,128]{4,3,2,1,0:T(8,128)S(1)} %get-tuple-element.23), channel_id=1, source_target_pairs={{0,3},{1,2},{2,1},{3,0},{4,7},{5,6},{6,5},{7,4},{8,11},{9,10},{10,... | collective-permute-start | bytes 983048 | tf_op jit(solution)/shard_map/ppermute | solution.py:290
  9.0 6.2 %collective-permute-start.4 = (f32[4,32,128]{2,1,0:T(8,128)S(1)}, f32[4,32,128]{2,1,0:T(8,128)S(1)}, u32[]{:S(2)}, u32[]{:S(2)}) collective-permute-start(f32[4,32,128]{2,1,0:T(8,128)S(1)} %maximum_select_fusion.refs_2_.refs_4_), channel_id=1, source_target_pairs={{4,8},{8,4},{12,16},{16,12},{20,24},{24,20},{5,9},{9,5},{13,17},{1... | collective-permute-start | bytes 196616 | tf_op jit(solution)/shard_map/ppermute | solution.py:296
  9.7 7.3 %collective-permute-start.6 = (f32[4,32,128]{2,1,0:T(8,128)S(1)}, f32[4,32,128]{2,1,0:T(8,128)S(1)}, u32[]{:S(2)}, u32[]{:S(2)}) collective-permute-start(f32[4,32,128]{2,1,0:T(8,128)S(1)} %maximum_select_fusion.1.refs_3_.refs_4_), channel_id=1, source_target_pairs={{0,4},{4,0},{8,12},{12,8},{16,20},{20,16},{24,28},{28,24},{1,5},{5... | collective-permute-start | bytes 196616 | tf_op jit(solution)/shard_map/ppermute | solution.py:299
  16.1 2.4 %collective-permute-start.5 = (f32[1,1,5,128,128]{4,3,2,1,0:T(8,128)S(1)}, f32[1,1,5,128,128]{4,3,2,1,0:T(8,128)S(1)}, u32[]{:S(2)}, u32[]{:S(2)}) collective-permute-start(f32[1,1,5,128,128]{4,3,2,1,0:T(8,128)S(1)} %collective-permute-done.3.refs_0_), channel_id=1, source_target_pairs={{0,1},{1,0},{2,3},{3,2},{4,5},{5,4},{6,7},{7,6},{8,9},{9,8},{10,11... | collective-permute-start | bytes 983048 | tf_op jit(solution)/shard_map/ppermute | solution.py:293
  17.1 9.7 %collective-permute-start.7 = (f32[1,1,5,128,128]{4,3,2,1,0:T(8,128)S(1)}, f32[1,1,5,128,128]{4,3,2,1,0:T(8,128)S(1)}, u32[]{:S(2)}, u32[]{:S(2)}) collective-permute-start(f32[1,1,5,128,128]{4,3,2,1,0:T(8,128)S(1)} %get-tuple-element.27), channel_id=1, source_target_pairs={{0,3},{1,2},{2,1},{3,0},{4,7},{5,6},{6,5},{7,4},{8,11},{9,10},{10,... | collective-permute-start | bytes 983048 | tf_op jit(solution)/shard_map/ppermute | solution.py:290
  19.8 7.0 %collective-permute-start.8 = (f32[3,32,128]{2,1,0:T(8,128)S(1)}, f32[3,32,128]{2,1,0:T(8,128)S(1)}, u32[]{:S(2)}, u32[]{:S(2)}) collective-permute-start(f32[3,32,128]{2,1,0:T(8,128)S(1)} %one_0.1.refs_1_), channel_id=1, source_target_pairs={{4,8},{8,4},{12,16},{16,12},{20,24},{24,20},{5,9},{9,5},{13,17},{1... | collective-permute-start | bytes 147464 | tf_op jit(solution)/shard_map/ppermute | solution.py:296
  21.1 8.0 %collective-permute-start.11 = (f32[3,32,128]{2,1,0:T(8,128)S(1)}, f32[3,32,128]{2,1,0:T(8,128)S(1)}, u32[]{:S(2)}, u32[]{:S(2)}) collective-permute-start(f32[3,32,128]{2,1,0:T(8,128)S(1)} %one_1.1.refs_2_), channel_id=1, source_target_pairs={{0,4},{4,0},{8,12},{12,8},{16,20},{20,16},{24,28},{28,24},{1,5},{5... | collective-permute-start | bytes 147464 | tf_op jit(solution)/shard_map/ppermute | solution.py:299
  27.3 3.9 %collective-permute-start.9 = (f32[3,32,128]{2,1,0:T(8,128)S(1)}, f32[3,32,128]{2,1,0:T(8,128)S(1)}, u32[]{:S(2)}, u32[]{:S(2)}) collective-permute-start(f32[3,32,128]{2,1,0:T(8,128)S(1)} %pad_maximum_fusion.6), channel_id=1, source_target_pairs={{0,3},{1,2},{2,1},{3,0},{4,7},{5,6},{6,5},{7,4},{8,11},{9,10},{10,... | collective-permute-start | bytes 147464 | tf_op jit(solution)/shard_map/ppermute | solution.py:290
  29.5 3.8 %collective-permute-start.12 = (f32[3,32,128]{2,1,0:T(8,128)S(1)}, f32[3,32,128]{2,1,0:T(8,128)S(1)}, u32[]{:S(2)}, u32[]{:S(2)}) collective-permute-start(f32[3,32,128]{2,1,0:T(8,128)S(1)} %pad_maximum_fusion.7), channel_id=1, source_target_pairs={{0,3},{1,2},{2,1},{3,0},{4,7},{5,6},{6,5},{7,4},{8,11},{9,10},{10,... | collective-permute-start | bytes 147464 | tf_op jit(solution)/shard_map/ppermute | solution.py:290
  31.2 6.7 %collective-permute-start.13 = (f32[4,32,128]{2,1,0:T(8,128)S(1)}, f32[4,32,128]{2,1,0:T(8,128)S(1)}, u32[]{:S(2)}, u32[]{:S(2)}) collective-permute-start(f32[4,32,128]{2,1,0:T(8,128)S(1)} %pad_maximum_fusion.2.refs_3_.refs_6_), channel_id=1, source_target_pairs={{4,8},{8,4},{12,16},{16,12},{20,24},{24,20},{5,9},{9,5},{13,17},{1... | collective-permute-start | bytes 196616 | tf_op jit(solution)/shard_map/ppermute | solution.py:296
  31.9 5.3 %collective-permute-start.10 = (f32[1,1,5,128,128]{4,3,2,1,0:T(8,128)S(1)}, f32[1,1,5,128,128]{4,3,2,1,0:T(8,128)S(1)}, u32[]{:S(2)}, u32[]{:S(2)}) collective-permute-start(f32[1,1,5,128,128]{4,3,2,1,0:T(8,128)S(1)} %collective-permute-done.7.refs_0_), channel_id=1, source_target_pairs={{0,1},{1,0},{2,3},{3,2},{4,5},{5,4},{6,7},{7,6},{8,9},{9,8},{10,11... | collective-permute-start | bytes 983048 | tf_op jit(solution)/shard_map/ppermute | solution.py:293
  33.3 6.6 %collective-permute-start.14 = (f32[4,32,128]{2,1,0:T(8,128)S(1)}, f32[4,32,128]{2,1,0:T(8,128)S(1)}, u32[]{:S(2)}, u32[]{:S(2)}) collective-permute-start(f32[4,32,128]{2,1,0:T(8,128)S(1)} %pad_maximum_fusion.3.refs_4_.refs_6_), channel_id=1, source_target_pairs={{0,4},{4,0},{8,12},{12,8},{16,20},{20,16},{24,28},{28,24},{1,5},{5... | collective-permute-start | bytes 196616 | tf_op jit(solution)/shard_map/ppermute | solution.py:299
  38.6 7.0 %collective-permute-start.16 = (f32[4,32,128]{2,1,0:T(8,128)S(1)}, f32[4,32,128]{2,1,0:T(8,128)S(1)}, u32[]{:S(2)}, u32[]{:S(2)}) collective-permute-start(f32[4,32,128]{2,1,0:T(8,128)S(1)} %three_0.1.refs_3_), channel_id=1, source_target_pairs={{4,8},{8,4},{12,16},{16,12},{20,24},{24,20},{5,9},{9,5},{13,17},{1... | collective-permute-start | bytes 196616 | tf_op jit(solution)/shard_map/ppermute | solution.py:296
  40.6 7.2 %collective-permute-start.15 = (f32[4,32,128]{2,1,0:T(8,128)S(1)}, f32[4,32,128]{2,1,0:T(8,128)S(1)}, u32[]{:S(2)}, u32[]{:S(2)}) collective-permute-start(f32[4,32,128]{2,1,0:T(8,128)S(1)} %three_1.1.refs_4_), channel_id=1, source_target_pairs={{0,4},{4,0},{8,12},{12,8},{16,20},{20,16},{24,28},{28,24},{1,5},{5... | collective-permute-start | bytes 196616 | tf_op jit(solution)/shard_map/ppermute | solution.py:299
  47.8 13.0 %copy-start.2 = (f32[8,8,8]{2,1,0:T(8,128)S(1)}, f32[8,8,8]{2,1,0:T(8,128)}, u32[]{:S(2)}) copy-start(f32[8,8,8]{2,1,0:T(8,128)} %rot_ref.1) | copy-start | bytes 6148
  48.8 1.3 %collective-permute-start.17 = (f32[4,24,128]{2,1,0:T(8,128)S(1)}, f32[4,24,128]{2,1,0:T(8,128)S(1)}, u32[]{:S(2)}, u32[]{:S(2)}) collective-permute-start(f32[4,24,128]{2,1,0:T(8,128)S(1)} %get-tuple-element.35), channel_id=1, source_target_pairs={{0,1},{1,0},{2,3},{3,2},{4,5},{5,4},{6,7},{7,6},{8,9},{9,8},{10,11... | collective-permute-start | bytes 147464 | tf_op jit(solution)/shard_map/ppermute | solution.py:293

commit v6 on v5

--- a/solution.py
+++ b/solution.py
@@ -249,12 +249,9 @@
             for d in range(1, VEC):
                 total = total + columns[d] * block[d : d + 1, :]
             mixed.append(total)
-    half = flag(flags_ref, 2, mixed[0].shape)
     for w in range(wide):
         for c in range(cols):
-            first = mixed[(wide - 1 - w) * cols + c]
-            second = mixed[(wide - 1 - w + wide // 2) % wide * cols + c]
-            out_ref[:, 0, w * cols + c, :] = jnp.where(half, second, first)
+            out_ref[:, 0, w * cols + c, :] = mixed[(wide - 1 - w) * cols + c]
 
 
 def finish(flags, cols, node_count, parts, rotation):
@@ -344,12 +341,9 @@
     four = step("other", 0, "four_0", h_four, three, rims[0], two[0])
     kept, sent = step("last", 1, "four_1", h_four, three, rims[1], two[1], *four, flags)
 
-    packed = jnp.concatenate([core(sent), kept])
-    owners = wide // 2
-    groups = [
-        [((wide - 1 - i + owners * (g // 2 ^ g % 2)) % wide) * grp + g for i in range(wide)]
-        for g in range(grp)
-    ]
+    sent = core(sent)
+    packed = jnp.where(half == 1, jnp.concatenate([kept, sent]), jnp.concatenate([sent, kept]))
+    groups = [[(wide - 1 - i) * grp + g for i in range(wide)] for g in range(grp)]
     packed = lax.all_to_all(
         packed,
         ("wide", "grp"),

time: 62.6 us -> 61.8 us (0.987)
  blocking collectives: 10.7 us -> 9.94 us
    all_to_all x1, blocking collectives: 10.7 us -> 9.94 us  [body(): lax.all_to_all(packed, ('wide', 'grp'), split_axis=0, concat_axis=0, tile...]
where the time goes in v6:
time: 61.8 us; the launch traced here: 61.5 us
  starting transfers between devices  28.4 us (46%)
  waiting for transfers between devices  11.4 us (18%)
  blocking collectives  9.94 us (16%)
  Pallas kernels  9.29 us (15%)
  local copies, waits for them, and re-layouts  1.99 us (3%)
    ppermute x4, starting transfers between devices, over_near(): return lax.ppermute(value, 'wide', near)  18.6 us
    all_to_all x1, blocking collectives, body(): lax.all_to_all(packed, ('wide', 'grp'), split_axis=0, concat_axis=0, tile...  9.94 us
    ppermute x5, waiting for transfers between devices, across(): return lax.ppermute(value, 'grp', [(i, i ^ 3) for i in range(grp)])  6.62 us
    ppermute x5, starting transfers between devices, across(): return lax.ppermute(value, 'grp', [(i, i ^ 3) for i in range(grp)])  6.07 us
    pallas_call x8, Pallas kernels, step(): pl.pallas_call(functools.partial(step_kernel, kind, u, len(h_ready)), in_...  5.33 us
    ppermute x4, starting transfers between devices, over_far(): return lax.ppermute(value, 'wide', far)  2.66 us
    ppermute x4, waiting for transfers between devices, over_near(): return lax.ppermute(value, 'wide', near)  2.44 us
    ppermute x5, waiting for transfers between devices, core(): return lax.ppermute(value, 'grp', [(i, i ^ 1) for i in range(grp)])  2.38 us
  transfers between devices with their start and end apart: 18, of which 10 were waited for; matrix products, arithmetic and copies ran while one was open for 1% of the time, Pallas kernels for 11%

profile of v6, /device:TPU:0, one launch (start us, length us, event | category | flops | bytes accessed | tf_op | source)
XLA Modules:
  0.0 61.5 jit_solution(9027104825237503732)
XLA Ops:
  0.0 0.5 collective-permute-start.1
  0.5 0.1 pad_add_fusion
  0.5 0.1 broadcast_in_dim.10
  0.6 0.1 broadcast_in_dim.11
  0.7 0.1 broadcast_in_dim.12.flags_ref.refs_9_
  0.8 0.8 %copy-done.1 = f32[64,1,2,128]{3,2,1,0:T(2,128)S(1)} copy-done((f32[64,1,2,128]{3,2,1,0:T(2,128)S(1)}, f32[64,1,2,128]{3,2,1,0:T(2,128)}, u32[]{:S(2)}) %copy-start.1) | copy-done | bytes 65560
  1.6 0.7 %copy-done.3 = s32[1,2,5]{2,1,0:T(2,128)S(1)} copy-done((s32[1,2,5]{2,1,0:T(2,128)S(1)}, s32[1,2,5]{2,1,0:T(2,128)}, u32[]{:S(2)}) %copy-start.3) | copy-done | bytes 64
  2.4 0.1 collective-permute-start
  2.5 1.1 %collective-permute-done = f32[72,128]{1,0:T(8,128)S(1)} collective-permute-done((f32[72,128]{1,0:T(8,128)S(1)}, f32[72,128]{1,0:T(8,128)S(1)}, u32[]{:S(2)}, u32[]{:S(2)}) %collective-permute-start) | collective-permute-done | bytes 36896 | tf_op jit(solution)/shard_map/ppermute | solution.py:290
  3.7 0.1 pick.1
  3.7 2.7 %collective-permute-start.2 = (f32[2,72,128]{2,1,0:T(8,128)S(1)}, f32[2,72,128]{2,1,0:T(8,128)S(1)}, u32[]{:S(2)}, u32[]{:S(2)}) collective-permute-start(f32[2,72,128]{2,1,0:T(8,128)S(1)} %pad_maximum_fusion), channel_id=1, source_target_pairs={{0,3},{1,2},{2,1},{3,0},{4,7},{5,6},{6,5},{7,4},{8,11},{9,10},{10,... | collective-permute-start | bytes 221192 | tf_op jit(solution)/shard_map/ppermute | solution.py:287
  6.4 0.1 collective-permute-start.3
  6.5 2.5 %collective-permute-done.2 = f32[2,72,128]{2,1,0:T(8,128)S(1)} collective-permute-done((f32[2,72,128]{2,1,0:T(8,128)S(1)}, f32[2,72,128]{2,1,0:T(8,128)S(1)}, u32[]{:S(2)}, u32[]{:S(2)}) %collective-permute-start.2) | collective-permute-done | bytes 73760 | tf_op jit(solution)/shard_map/ppermute | solution.py:287
  9.0 0.7 %collective-permute-start.4 = (f32[4,32,128]{2,1,0:T(8,128)S(1)}, f32[4,32,128]{2,1,0:T(8,128)S(1)}, u32[]{:S(2)}, u32[]{:S(2)}) collective-permute-start(f32[4,32,128]{2,1,0:T(8,128)S(1)} %maximum_select_fusion.1.refs_2_.refs_4_), channel_id=1, source_target_pairs={{4,8},{8,4},{12,16},{16,12},{20,24},{24,20},{5,9},{9,5},{13,17},{1... | collective-permute-start | bytes 196616 | tf_op jit(solution)/shard_map/ppermute | solution.py:293
  9.7 4.4 %collective-permute-start.6 = (f32[4,32,128]{2,1,0:T(8,128)S(1)}, f32[4,32,128]{2,1,0:T(8,128)S(1)}, u32[]{:S(2)}, u32[]{:S(2)}) collective-permute-start(f32[4,32,128]{2,1,0:T(8,128)S(1)} %maximum_select_fusion.2.refs_3_.refs_4_), channel_id=1, source_target_pairs={{0,4},{4,0},{8,12},{12,8},{16,20},{20,16},{24,28},{28,24},{1,5},{5... | collective-permute-start | bytes 196616 | tf_op jit(solution)/shard_map/ppermute | solution.py:296
  14.2 0.1 convert_element_type.8
  14.3 0.1 concatenate.27.codes_ref
  14.3 0.9 %prepare_chip.1.refs_0_ = bf16[2,2,256,1152]{3,2,1,0:T(8,128)(2,1)S(1)} custom-call(s32[44]{0:T(128)S(1)} %concatenate.27.codes_ref, f32[1,2,5,128,128]{4,3,2,1,0:T(8,128)S(1)} %copy-done, f32[1,2,5,128,128]{4,3,2,1,0:T(8,128)S(1)} %collective-permute-done.1.core_ref.refs_1_), custom_call_target="tpu_custom_call" | custom-call | tf_op jit(solution)/shard_map/prepare_chip/pallas_call | solution.py:114
  15.3 0.8 %collective-permute-done.3.refs_0_ = f32[1,1,5,128,128]{4,3,2,1,0:T(8,128)S(1)} collective-permute-done((f32[1,1,5,128,128]{4,3,2,1,0:T(8,128)S(1)}, f32[1,1,5,128,128]{4,3,2,1,0:T(8,128)S(1)}, u32[]{:S(2)}, u32[]{:S(2)}) %collective-permute-start.3) | collective-permute-done | bytes 327712 | tf_op jit(solution)/shard_map/ppermute | solution.py:287
  16.1 0.5 collective-permute-start.5
  16.5 0.5 collective-permute-done.6.refs_4_
  17.1 1.4 %collective-permute-start.7 = (f32[1,1,5,128,128]{4,3,2,1,0:T(8,128)S(1)}, f32[1,1,5,128,128]{4,3,2,1,0:T(8,128)S(1)}, u32[]{:S(2)}, u32[]{:S(2)}) collective-permute-start(f32[1,1,5,128,128]{4,3,2,1,0:T(8,128)S(1)} %get-tuple-element.27), channel_id=1, source_target_pairs={{0,3},{1,2},{2,1},{3,0},{4,7},{5,6},{6,5},{7,4},{8,11},{9,10},{10,... | collective-permute-start | bytes 983048 | tf_op jit(solution)/shard_map/ppermute | solution.py:287
  18.5 0.7 %prepare_border.1.refs_1_ = bf16[1,2,256,1152]{3,2,1,0:T(8,128)(2,1)S(1)} custom-call(s32[44]{0:T(128)S(1)} %concatenate.27.codes_ref, f32[1,1,5,128,128]{4,3,2,1,0:T(8,128)S(1)} %collective-permute-done.3.refs_0_, f32[1,1,5,128,128]{4,3,2,1,0:T(8,128)S(1)} %collective-permute-done.5.refs_1_), custom_call_target="tpu_custom_call" | custom-call | tf_op jit(solution)/shard_map/prepare_border/pallas_call | solution.py:114
  19.2 0.6 one_0.1.refs_1_
  19.8 0.7 %collective-permute-start.8 = (f32[3,32,128]{2,1,0:T(8,128)S(1)}, f32[3,32,128]{2,1,0:T(8,128)S(1)}, u32[]{:S(2)}, u32[]{:S(2)}) collective-permute-start(f32[3,32,128]{2,1,0:T(8,128)S(1)} %one_0.1.refs_1_), channel_id=1, source_target_pairs={{4,8},{8,4},{12,16},{16,12},{20,24},{24,20},{5,9},{9,5},{13,17},{1... | collective-permute-start | bytes 147464 | tf_op jit(solution)/shard_map/ppermute | solution.py:293
  20.5 0.6 one_1.1.refs_2_
  21.1 5.3 %collective-permute-start.11 = (f32[3,32,128]{2,1,0:T(8,128)S(1)}, f32[3,32,128]{2,1,0:T(8,128)S(1)}, u32[]{:S(2)}, u32[]{:S(2)}) collective-permute-start(f32[3,32,128]{2,1,0:T(8,128)S(1)} %one_1.1.refs_2_), channel_id=1, source_target_pairs={{0,4},{4,0},{8,12},{12,8},{16,20},{20,16},{24,28},{28,24},{1,5},{5... | collective-permute-start | bytes 147464 | tf_op jit(solution)/shard_map/ppermute | solution.py:296
  26.4 0.4 collective-permute-done.7.refs_0_
  26.8 0.4 two_0.1
  27.3 1.8 %collective-permute-start.9 = (f32[3,32,128]{2,1,0:T(8,128)S(1)}, f32[3,32,128]{2,1,0:T(8,128)S(1)}, u32[]{:S(2)}, u32[]{:S(2)}) collective-permute-start(f32[3,32,128]{2,1,0:T(8,128)S(1)} %pad_maximum_fusion.5), channel_id=1, source_target_pairs={{0,3},{1,2},{2,1},{3,0},{4,7},{5,6},{6,5},{7,4},{8,11},{9,10},{10,... | collective-permute-start | bytes 147464 | tf_op jit(solution)/shard_map/ppermute | solution.py:287
  29.1 0.4 two_1.1
  29.5 0.1 collective-permute-start.12
  29.6 1.6 %collective-permute-done.9 = f32[3,32,128]{2,1,0:T(8,128)S(1)} collective-permute-done((f32[3,32,128]{2,1,0:T(8,128)S(1)}, f32[3,32,128]{2,1,0:T(8,128)S(1)}, u32[]{:S(2)}, u32[]{:S(2)}) %collective-permute-start.9) | collective-permute-done | bytes 49184 | tf_op jit(solution)/shard_map/ppermute | solution.py:287
  31.2 0.7 %collective-permute-start.13 = (f32[4,32,128]{2,1,0:T(8,128)S(1)}, f32[4,32,128]{2,1,0:T(8,128)S(1)}, u32[]{:S(2)}, u32[]{:S(2)}) collective-permute-start(f32[4,32,128]{2,1,0:T(8,128)S(1)} %pad_maximum_fusion.1.refs_3_.refs_6_), channel_id=1, source_target_pairs={{4,8},{8,4},{12,16},{16,12},{20,24},{24,20},{5,9},{9,5},{13,17},{1... | collective-permute-start | bytes 196616 | tf_op jit(solution)/shard_map/ppermute | solution.py:293
  32.0 1.3 %collective-permute-done.12 = f32[3,32,128]{2,1,0:T(8,128)S(1)} collective-permute-done((f32[3,32,128]{2,1,0:T(8,128)S(1)}, f32[3,32,128]{2,1,0:T(8,128)S(1)}, u32[]{:S(2)}, u32[]{:S(2)}) %collective-permute-start.12) | collective-permute-done | bytes 49184 | tf_op jit(solution)/shard_map/ppermute | solution.py:287
  33.3 3.9 %collective-permute-start.14 = (f32[4,32,128]{2,1,0:T(8,128)S(1)}, f32[4,32,128]{2,1,0:T(8,128)S(1)}, u32[]{:S(2)}, u32[]{:S(2)}) collective-permute-start(f32[4,32,128]{2,1,0:T(8,128)S(1)} %pad_maximum_fusion.2.refs_4_.refs_6_), channel_id=1, source_target_pairs={{0,4},{4,0},{8,12},{12,8},{16,20},{20,16},{24,28},{28,24},{1,5},{5... | collective-permute-start | bytes 196616 | tf_op jit(solution)/shard_map/ppermute | solution.py:296
  37.2 0.7 %prepare_inner.1.refs_2_ = bf16[1,2,256,1152]{3,2,1,0:T(8,128)(2,1)S(1)} custom-call(s32[44]{0:T(128)S(1)} %concatenate.27.codes_ref, f32[1,1,5,128,128]{4,3,2,1,0:T(8,128)S(1)} %collective-permute-done.7.refs_0_, f32[1,1,5,128,128]{4,3,2,1,0:T(8,128)S(1)} %collective-permute-done.10.refs_1_), custom_call_target="tpu_custom_call" | custom-call | tf_op jit(solution)/shard_map/prepare_inner/pallas_call | solution.py:114
  37.9 0.7 %three_0.1.refs_3_ = f32[4,32,128]{2,1,0:T(8,128)S(1)} custom-call(bf16[2,2,256,1152]{3,2,1,0:T(8,128)(2,1)S(1)} %prepare_chip.1.refs_0_, bf16[1,2,256,1152]{3,2,1,0:T(8,128)(2,1)S(1)} %prepare_border.1.refs_1_, bf16[1,2,256,1152]{3,2,1,0:T(8,128)(2,1)S(1)} %prepare_inner.1.refs_2_, f32[4,32,128]{2,1,0:T(8,128)S(1)} %pad_maximum_fusion.1.refs_3_.refs_6_, ...), custom_call_target="tpu_custom_call" | custom-call | flops 150994944 | bytes 2359296 | tf_op jit(solution)/shard_map/three_0/pallas_call | solution.py:204
  38.6 0.7 %collective-permute-start.16 = (f32[4,32,128]{2,1,0:T(8,128)S(1)}, f32[4,32,128]{2,1,0:T(8,128)S(1)}, u32[]{:S(2)}, u32[]{:S(2)}) collective-permute-start(f32[4,32,128]{2,1,0:T(8,128)S(1)} %three_0.1.refs_3_), channel_id=1, source_target_pairs={{4,8},{8,4},{12,16},{16,12},{20,24},{24,20},{5,9},{9,5},{13,17},{1... | collective-permute-start | bytes 196616 | tf_op jit(solution)/shard_map/ppermute | solution.py:293
  39.3 0.6 collective-permute-done.14.refs_5_
  39.9 0.7 %three_1.1.refs_4_ = f32[4,32,128]{2,1,0:T(8,128)S(1)} custom-call(bf16[2,2,256,1152]{3,2,1,0:T(8,128)(2,1)S(1)} %prepare_chip.1.refs_0_, bf16[1,2,256,1152]{3,2,1,0:T(8,128)(2,1)S(1)} %prepare_border.1.refs_1_, bf16[1,2,256,1152]{3,2,1,0:T(8,128)(2,1)S(1)} %prepare_inner.1.refs_2_, f32[4,32,128]{2,1,0:T(8,128)S(1)} %pad_maximum_fusion.1.refs_3_.refs_6_, ...), custom_call_target="tpu_custom_call" | custom-call | flops 150994944 | bytes 2359296 | tf_op jit(solution)/shard_map/three_1/pallas_call | solution.py:204
  40.6 5.0 %collective-permute-start.15 = (f32[4,32,128]{2,1,0:T(8,128)S(1)}, f32[4,32,128]{2,1,0:T(8,128)S(1)}, u32[]{:S(2)}, u32[]{:S(2)}) collective-permute-start(f32[4,32,128]{2,1,0:T(8,128)S(1)} %three_1.1.refs_4_), channel_id=1, source_target_pairs={{0,4},{4,0},{8,12},{12,8},{16,20},{20,16},{24,28},{28,24},{1,5},{5... | collective-permute-start | bytes 196616 | tf_op jit(solution)/shard_map/ppermute | solution.py:296
  45.6 0.9 %four_0.1 = (f32[4,32,128]{2,1,0:T(8,128)S(1)}, f32[32,128]{1,0:T(8,128)S(1)}) custom-call(bf16[2,2,256,1152]{3,2,1,0:T(8,128)(2,1)S(1)} %prepare_chip.1.refs_0_, bf16[1,2,256,1152]{3,2,1,0:T(8,128)(2,1)S(1)} %prepare_border.1.refs_1_, bf16[1,2,256,1152]{3,2,1,0:T(8,128)(2,1)S(1)} %prepare_inner.1.refs_2_, f32[4,32,128]{2,1,0:T(8,128)S(1)} %three_0.1.refs_3_, ...), custom_call_target="tpu_custom_call" | custom-call | flops 150994944 | bytes 2359296 | tf_op jit(solution)/shard_map/four_0/pallas_call | solution.py:204
  46.5 1.3 %collective-permute-done.15.refs_5_ = f32[4,32,128]{2,1,0:T(8,128)S(1)} collective-permute-done((f32[4,32,128]{2,1,0:T(8,128)S(1)}, f32[4,32,128]{2,1,0:T(8,128)S(1)}, u32[]{:S(2)}, u32[]{:S(2)}) %collective-permute-start.15) | collective-permute-done | bytes 65568 | tf_op jit(solution)/shard_map/ppermute | solution.py:296
  47.8 1.0 %four_1.1 = (f32[4,24,128]{2,1,0:T(8,128)S(1)}, f32[4,24,128]{2,1,0:T(8,128)S(1)}) custom-call(bf16[2,2,256,1152]{3,2,1,0:T(8,128)(2,1)S(1)} %prepare_chip.1.refs_0_, bf16[1,2,256,1152]{3,2,1,0:T(8,128)(2,1)S(1)} %prepare_border.1.refs_1_, bf16[1,2,256,1152]{3,2,1,0:T(8,128)(2,1)S(1)} %prepare_inner.1.refs_2_, f32[4,32,128]{2,1,0:T(8,128)S(1)} %three_0.1.refs_3_, ...), custom_call_target="tpu_custom_call" | custom-call | flops 150994944 | bytes 2359296 | tf_op jit(solution)/shard_map/four_1/pallas_call | solution.py:204
  48.9 1.2 %collective-permute-done.17 = f32[4,24,128]{2,1,0:T(8,128)S(1)} collective-permute-done((f32[4,24,128]{2,1,0:T(8,128)S(1)}, f32[4,24,128]{2,1,0:T(8,128)S(1)}, u32[]{:S(2)}, u32[]{:S(2)}) %collective-permute-start.17) | collective-permute-done | bytes 49184 | tf_op jit(solution)/shard_map/ppermute | solution.py:290
  50.1 9.9 %all_to_all.5.parts_ref = f32[8,24,128]{2,1,0:T(8,128)S(1)} all-to-all(f32[8,24,128]{2,1,0:T(8,128)S(1)} %maximum_select_fusion), channel_id=1, replica_groups={{28,24,20,16,12,8,4,0},{29,25,21,17,13,9,5,1},{30,26,22,18,14,10,6,2},{..., dimensions={0} | all-to-all | bytes 196608 | tf_op jit(solution)/shard_map/all_to_all | solution.py:347
  60.0 1.5 %finish.1 = f32[8,1,16,128]{3,2,1,0:T(8,128)} custom-call(s32[32,128]{1,0:T(8,128)S(1)} %broadcast_in_dim.12.flags_ref.refs_9_, f32[8,24,128]{2,1,0:T(8,128)S(1)} %all_to_all.5.parts_ref, f32[8,8,8]{2,1,0:T(8,128)S(1)} %copy-done.2), custom_call_target="tpu_custom_call" | custom-call | tf_op jit(solution)/shard_map/finish/pallas_call | solution.py:259
  (41 shorter events, 0.3 us)
Async XLA Ops:
  0.0 3.7 %copy-start = (f32[1,2,5,128,128]{4,3,2,1,0:T(8,128)S(1)}, f32[1,2,5,128,128]{4,3,2,1,0:T(8,128)}, u32[]{:S(2)}) copy-start(f32[1,2,5,128,128]{4,3,2,1,0:T(8,128)} %refs_0_.1) | copy-start | bytes 1966084
  0.0 3.6 %collective-permute-start.1 = (f32[1,2,5,128,128]{4,3,2,1,0:T(8,128)}, f32[1,2,5,128,128]{4,3,2,1,0:T(8,128)S(1)}, u32[]{:S(2)}, u32[]{:S(2)}) collective-permute-start(f32[1,2,5,128,128]{4,3,2,1,0:T(8,128)} %refs_0_.1), channel_id=1, source_target_pairs={{0,1},{1,0},{2,3},{3,2},{4,5},{5,4},{6,7},{7,6},{8,9},{9,8},{10,11... | collective-permute-start | bytes 1966088 | tf_op jit(solution)/shard_map/ppermute | solution.py:290
  0.8 0.8 %copy-start.1 = (f32[64,1,2,128]{3,2,1,0:T(2,128)S(1)}, f32[64,1,2,128]{3,2,1,0:T(2,128)}, u32[]{:S(2)}) copy-start(f32[64,1,2,128]{3,2,1,0:T(2,128)} %slab_ref.1) | copy-start | bytes 196612
  1.6 0.7 %copy-start.3 = (s32[1,2,5]{2,1,0:T(2,128)S(1)}, s32[1,2,5]{2,1,0:T(2,128)}, u32[]{:S(2)}) copy-start(s32[1,2,5]{2,1,0:T(2,128)} %codes_ref.1) | copy-start | bytes 124
  2.4 1.3 %collective-permute-start = (f32[72,128]{1,0:T(8,128)S(1)}, f32[72,128]{1,0:T(8,128)S(1)}, u32[]{:S(2)}, u32[]{:S(2)}) collective-permute-start(f32[72,128]{1,0:T(8,128)S(1)} %get-tuple-element.46), channel_id=1, source_target_pairs={{0,1},{1,0},{2,3},{3,2},{4,5},{5,4},{6,7},{7,6},{8,9},{9,8},{10,11... | collective-permute-start | bytes 110600 | tf_op jit(solution)/shard_map/ppermute | solution.py:290
  3.7 5.3 %collective-permute-start.2 = (f32[2,72,128]{2,1,0:T(8,128)S(1)}, f32[2,72,128]{2,1,0:T(8,128)S(1)}, u32[]{:S(2)}, u32[]{:S(2)}) collective-permute-start(f32[2,72,128]{2,1,0:T(8,128)S(1)} %pad_maximum_fusion), channel_id=1, source_target_pairs={{0,3},{1,2},{2,1},{3,0},{4,7},{5,6},{6,5},{7,4},{8,11},{9,10},{10,... | collective-permute-start | bytes 221192 | tf_op jit(solution)/shard_map/ppermute | solution.py:287
  6.4 9.7 %collective-permute-start.3 = (f32[1,1,5,128,128]{4,3,2,1,0:T(8,128)S(1)}, f32[1,1,5,128,128]{4,3,2,1,0:T(8,128)S(1)}, u32[]{:S(2)}, u32[]{:S(2)}) collective-permute-start(f32[1,1,5,128,128]{4,3,2,1,0:T(8,128)S(1)} %get-tuple-element.23), channel_id=1, source_target_pairs={{0,3},{1,2},{2,1},{3,0},{4,7},{5,6},{6,5},{7,4},{8,11},{9,10},{10,... | collective-permute-start | bytes 983048 | tf_op jit(solution)/shard_map/ppermute | solution.py:287
  9.0 6.2 %collective-permute-start.4 = (f32[4,32,128]{2,1,0:T(8,128)S(1)}, f32[4,32,128]{2,1,0:T(8,128)S(1)}, u32[]{:S(2)}, u32[]{:S(2)}) collective-permute-start(f32[4,32,128]{2,1,0:T(8,128)S(1)} %maximum_select_fusion.1.refs_2_.refs_4_), channel_id=1, source_target_pairs={{4,8},{8,4},{12,16},{16,12},{20,24},{24,20},{5,9},{9,5},{13,17},{1... | collective-permute-start | bytes 196616 | tf_op jit(solution)/shard_map/ppermute | solution.py:293
  9.7 7.3 %collective-permute-start.6 = (f32[4,32,128]{2,1,0:T(8,128)S(1)}, f32[4,32,128]{2,1,0:T(8,128)S(1)}, u32[]{:S(2)}, u32[]{:S(2)}) collective-permute-start(f32[4,32,128]{2,1,0:T(8,128)S(1)} %maximum_select_fusion.2.refs_3_.refs_4_), channel_id=1, source_target_pairs={{0,4},{4,0},{8,12},{12,8},{16,20},{20,16},{24,28},{28,24},{1,5},{5... | collective-permute-start | bytes 196616 | tf_op jit(solution)/shard_map/ppermute | solution.py:296
  16.1 2.4 %collective-permute-start.5 = (f32[1,1,5,128,128]{4,3,2,1,0:T(8,128)S(1)}, f32[1,1,5,128,128]{4,3,2,1,0:T(8,128)S(1)}, u32[]{:S(2)}, u32[]{:S(2)}) collective-permute-start(f32[1,1,5,128,128]{4,3,2,1,0:T(8,128)S(1)} %collective-permute-done.3.refs_0_), channel_id=1, source_target_pairs={{0,1},{1,0},{2,3},{3,2},{4,5},{5,4},{6,7},{7,6},{8,9},{9,8},{10,11... | collective-permute-start | bytes 983048 | tf_op jit(solution)/shard_map/ppermute | solution.py:290
  17.1 9.7 %collective-permute-start.7 = (f32[1,1,5,128,128]{4,3,2,1,0:T(8,128)S(1)}, f32[1,1,5,128,128]{4,3,2,1,0:T(8,128)S(1)}, u32[]{:S(2)}, u32[]{:S(2)}) collective-permute-start(f32[1,1,5,128,128]{4,3,2,1,0:T(8,128)S(1)} %get-tuple-element.27), channel_id=1, source_target_pairs={{0,3},{1,2},{2,1},{3,0},{4,7},{5,6},{6,5},{7,4},{8,11},{9,10},{10,... | collective-permute-start | bytes 983048 | tf_op jit(solution)/shard_map/ppermute | solution.py:287
  19.8 7.0 %collective-permute-start.8 = (f32[3,32,128]{2,1,0:T(8,128)S(1)}, f32[3,32,128]{2,1,0:T(8,128)S(1)}, u32[]{:S(2)}, u32[]{:S(2)}) collective-permute-start(f32[3,32,128]{2,1,0:T(8,128)S(1)} %one_0.1.refs_1_), channel_id=1, source_target_pairs={{4,8},{8,4},{12,16},{16,12},{20,24},{24,20},{5,9},{9,5},{13,17},{1... | collective-permute-start | bytes 147464 | tf_op jit(solution)/shard_map/ppermute | solution.py:293
  21.1 8.0 %collective-permute-start.11 = (f32[3,32,128]{2,1,0:T(8,128)S(1)}, f32[3,32,128]{2,1,0:T(8,128)S(1)}, u32[]{:S(2)}, u32[]{:S(2)}) collective-permute-start(f32[3,32,128]{2,1,0:T(8,128)S(1)} %one_1.1.refs_2_), channel_id=1, source_target_pairs={{0,4},{4,0},{8,12},{12,8},{16,20},{20,16},{24,28},{28,24},{1,5},{5... | collective-permute-start | bytes 147464 | tf_op jit(solution)/shard_map/ppermute | solution.py:296
  27.3 3.9 %collective-permute-start.9 = (f32[3,32,128]{2,1,0:T(8,128)S(1)}, f32[3,32,128]{2,1,0:T(8,128)S(1)}, u32[]{:S(2)}, u32[]{:S(2)}) collective-permute-start(f32[3,32,128]{2,1,0:T(8,128)S(1)} %pad_maximum_fusion.5), channel_id=1, source_target_pairs={{0,3},{1,2},{2,1},{3,0},{4,7},{5,6},{6,5},{7,4},{8,11},{9,10},{10,... | collective-permute-start | bytes 147464 | tf_op jit(solution)/shard_map/ppermute | solution.py:287
  29.5 3.8 %collective-permute-start.12 = (f32[3,32,128]{2,1,0:T(8,128)S(1)}, f32[3,32,128]{2,1,0:T(8,128)S(1)}, u32[]{:S(2)}, u32[]{:S(2)}) collective-permute-start(f32[3,32,128]{2,1,0:T(8,128)S(1)} %pad_maximum_fusion.6), channel_id=1, source_target_pairs={{0,3},{1,2},{2,1},{3,0},{4,7},{5,6},{6,5},{7,4},{8,11},{9,10},{10,... | collective-permute-start | bytes 147464 | tf_op jit(solution)/shard_map/ppermute | solution.py:287
  31.2 6.7 %collective-permute-start.13 = (f32[4,32,128]{2,1,0:T(8,128)S(1)}, f32[4,32,128]{2,1,0:T(8,128)S(1)}, u32[]{:S(2)}, u32[]{:S(2)}) collective-permute-start(f32[4,32,128]{2,1,0:T(8,128)S(1)} %pad_maximum_fusion.1.refs_3_.refs_6_), channel_id=1, source_target_pairs={{4,8},{8,4},{12,16},{16,12},{20,24},{24,20},{5,9},{9,5},{13,17},{1... | collective-permute-start | bytes 196616 | tf_op jit(solution)/shard_map/ppermute | solution.py:293
  31.9 5.3 %collective-permute-start.10 = (f32[1,1,5,128,128]{4,3,2,1,0:T(8,128)S(1)}, f32[1,1,5,128,128]{4,3,2,1,0:T(8,128)S(1)}, u32[]{:S(2)}, u32[]{:S(2)}) collective-permute-start(f32[1,1,5,128,128]{4,3,2,1,0:T(8,128)S(1)} %collective-permute-done.7.refs_0_), channel_id=1, source_target_pairs={{0,1},{1,0},{2,3},{3,2},{4,5},{5,4},{6,7},{7,6},{8,9},{9,8},{10,11... | collective-permute-start | bytes 983048 | tf_op jit(solution)/shard_map/ppermute | solution.py:290
  33.3 6.6 %collective-permute-start.14 = (f32[4,32,128]{2,1,0:T(8,128)S(1)}, f32[4,32,128]{2,1,0:T(8,128)S(1)}, u32[]{:S(2)}, u32[]{:S(2)}) collective-permute-start(f32[4,32,128]{2,1,0:T(8,128)S(1)} %pad_maximum_fusion.2.refs_4_.refs_6_), channel_id=1, source_target_pairs={{0,4},{4,0},{8,12},{12,8},{16,20},{20,16},{24,28},{28,24},{1,5},{5... | collective-permute-start | bytes 196616 | tf_op jit(solution)/shard_map/ppermute | solution.py:296
  38.6 7.0 %collective-permute-start.16 = (f32[4,32,128]{2,1,0:T(8,128)S(1)}, f32[4,32,128]{2,1,0:T(8,128)S(1)}, u32[]{:S(2)}, u32[]{:S(2)}) collective-permute-start(f32[4,32,128]{2,1,0:T(8,128)S(1)} %three_0.1.refs_3_), channel_id=1, source_target_pairs={{4,8},{8,4},{12,16},{16,12},{20,24},{24,20},{5,9},{9,5},{13,17},{1... | collective-permute-start | bytes 196616 | tf_op jit(solution)/shard_map/ppermute | solution.py:293
  40.6 7.2 %collective-permute-start.15 = (f32[4,32,128]{2,1,0:T(8,128)S(1)}, f32[4,32,128]{2,1,0:T(8,128)S(1)}, u32[]{:S(2)}, u32[]{:S(2)}) collective-permute-start(f32[4,32,128]{2,1,0:T(8,128)S(1)} %three_1.1.refs_4_), channel_id=1, source_target_pairs={{0,4},{4,0},{8,12},{12,8},{16,20},{20,16},{24,28},{28,24},{1,5},{5... | collective-permute-start | bytes 196616 | tf_op jit(solution)/shard_map/ppermute | solution.py:296
  47.8 12.2 %copy-start.2 = (f32[8,8,8]{2,1,0:T(8,128)S(1)}, f32[8,8,8]{2,1,0:T(8,128)}, u32[]{:S(2)}) copy-start(f32[8,8,8]{2,1,0:T(8,128)} %rot_ref.1) | copy-start | bytes 6148
  48.8 1.3 %collective-permute-start.17 = (f32[4,24,128]{2,1,0:T(8,128)S(1)}, f32[4,24,128]{2,1,0:T(8,128)S(1)}, u32[]{:S(2)}, u32[]{:S(2)}) collective-permute-start(f32[4,24,128]{2,1,0:T(8,128)S(1)} %get-tuple-element.36), channel_id=1, source_target_pairs={{0,1},{1,0},{2,3},{3,2},{4,5},{5,4},{6,7},{7,6},{8,9},{9,8},{10,11... | collective-permute-start | bytes 147464 | tf_op jit(solution)/shard_map/ppermute | solution.py:290

commit v7 on v6

--- a/solution.py
+++ b/solution.py
@@ -131,29 +131,74 @@
             x_ref[states : 2 * states, at : at + size] = low
 
 
-def step_kernel(kind, u, count, *refs):
-    h_refs, (own_0, own_1, rim_ref, *refs) = refs[:count], refs[count:]
-    *refs, own_x, rim_x = refs
-    before, refs = (None, refs) if kind == "first" else (refs[0], refs[1:])
-    rows_in, states, size = rim_ref.shape
+def products(h_refs, u, x_ref, width, first, rows_in):
+    states, size = x_ref.shape[0] // 2, h_refs[0].shape[2] // 2
+    width, first = width * size, first * size
     h_rows = [h_ref.at[q] for h_ref in h_refs for q in range(h_ref.shape[0])]
-    fill(own_x, [own_0, own_1])
-    fill(rim_x, [rim_ref])
-    values = []
+    sums = []
     for q, h_row in enumerate(h_rows):
         low, high = max(q - 1, 0), min(q + 2, rows_in)
-        acc = 0.0
-        for x_ref, width, first in ((own_x, 2 * size, 0), (rim_x, size, 6 * size)):
-            at = first + (low - q + 1) * width
-            acc = acc + lax.dot_general(
-                x_ref[:, low * width : high * width],
-                h_row[u, :, at : at + (high - low) * width],
-                NT,
-                preferred_element_type=jnp.float32,
-            )
+        at = first + (low - q + 1) * width
+        acc = lax.dot_general(
+            x_ref[:, low * width : high * width],
+            h_row[u, :, at : at + (high - low) * width],
+            NT,
+            preferred_element_type=jnp.float32,
+        )
         small = acc[states:, size:] + (acc[states:, :size] + acc[:states, size:])
-        value = acc[:states, :size] + small
-        values.append(value if kind == "first" else 2.0 * value - before[q])
+        sums.append(acc[:states, :size] + small)
+    return sums
+
+
+def inner_kernel(u, count, *refs):
+    h_refs, (own_0, own_1, before, out_ref, x_ref) = refs[:count], refs[count:]
+    fill(x_ref, [own_0, own_1])
+    for q, value in enumerate(products(h_refs, u, x_ref, 2, 0, own_0.shape[0])):
+        out_ref[q] = 2.0 * value - before[q]
+
+
+def inner(u, name, h_ready, own, before):
+    rows_in, states, size = own[0].shape
+    rows_out = sum(h.shape[0] for h in h_ready)
+    operands = [*h_ready, *own, before]
+    return pl.pallas_call(
+        functools.partial(inner_kernel, u, len(h_ready)),
+        in_specs=[VMEM] * len(operands),
+        out_specs=VMEM,
+        out_shape=jax.ShapeDtypeStruct((rows_out, states, size), jnp.float32),
+        scratch_shapes=[pltpu.VMEM((2 * states, rows_in * 2 * size), jnp.bfloat16)],
+        compiler_params=pltpu.CompilerParams(vmem_limit_bytes=LIMIT),
+        cost_estimate=cost_of(rows_out, 6, states, size),
+        name=name,
+    )(*operands)
+
+
+def cost_of(rows, blocks, states, size):
+    return pl.CostEstimate(
+        flops=8 * blocks * rows * states * size * size,
+        bytes_accessed=4 * blocks * rows * size * size,
+        transcendentals=0,
+    )
+
+
+def step_kernel(kind, u, count, *refs):
+    h_refs, refs = refs[:count], refs[count:]
+    if kind in ("first", "whole"):
+        own_0, own_1, rim_ref, *refs, own_x, rim_x = refs
+    else:
+        rim_ref, acc_ref, *refs, rim_x = refs
+    rows_in, states, size = rim_ref.shape
+    fill(rim_x, [rim_ref])
+    values = products(h_refs, u, rim_x, 1, 6, rows_in)
+    if kind in ("first", "whole"):
+        fill(own_x, [own_0, own_1])
+        own = products(h_refs, u, own_x, 2, 0, rows_in)
+        values = [value + own[q] for q, value in enumerate(values)]
+        if kind == "whole":
+            before, *refs = refs
+            values = [2.0 * value - before[q] for q, value in enumerate(values)]
+    else:
+        values = [acc_ref[q] + 2.0 * value for q, value in enumerate(values)]
     if kind in ("other", "last"):
         flat = [jnp.concatenate(part, axis=1) for part in zip(*map(split, values))]
         flat = jnp.concatenate(flat)
@@ -186,31 +231,27 @@
             ref[blocks - 1 - b, 2 * VEC :, 0:VEC] = gram[rows, rows]
 
 
-def step(kind, u, name, h_ready, own, rim, *others):
-    rows_in, states, size = rim.shape
+def step(kind, u, name, h_ready, *operands):
+    merged = kind in ("first", "whole")
+    rows_in, states, size = operands[0].shape
     rows_out = sum(h.shape[0] for h in h_ready)
     shapes = [(rows_out, states, size)]
     if kind == "other":
         shapes.append((states, pl.cdiv(states, size) * size))
     elif kind == "last":
-        blocks = states // VEC
-        shapes = [(blocks, 3 * VEC, size)] * 2
-    operands = [*h_ready, *own, rim, *others]
-    cost = pl.CostEstimate(
-        flops=8 * BLOCKS * rows_out * states * size * size,
-        bytes_accessed=4 * BLOCKS * rows_out * size * size,
-        transcendentals=0,
-    )
+        shapes = [(states // VEC, 3 * VEC, size)] * 2
+    operands = [*h_ready, *operands]
     outs = pl.pallas_call(
         functools.partial(step_kernel, kind, u, len(h_ready)),
         in_specs=[VMEM] * len(operands),
         out_specs=[VMEM] * len(shapes),
         out_shape=[jax.ShapeDtypeStruct(shape, jnp.float32) for shape in shapes],
         scratch_shapes=[
-            pltpu.VMEM((2 * states, rows_in * width * size), jnp.bfloat16) for width in (2, 1)
+            pltpu.VMEM((2 * states, rows_in * width * size), jnp.bfloat16)
+            for width in ((2, 1) if merged else (1,))
         ],
         compiler_params=pltpu.CompilerParams(vmem_limit_bytes=LIMIT),
-        cost_estimate=cost,
+        cost_estimate=cost_of(rows_out, BLOCKS if merged else 3, states, size),
         name=name,
     )(*operands)
     return outs[0] if len(outs) == 1 else outs
@@ -319,14 +360,15 @@
     border_core = core(after(border, (far_rim, h_two)))
     h_three = h_two + [prepare("border", codes, border, border_core)]
 
-    one = [step("first", 0, "one_0", h_three, zero, far_rim)]
+    one = [step("first", 0, "one_0", h_three, *zero, far_rim)]
     rim = after(near_rim, one[0])
-    one.append(step("first", 1, "one_1", h_three, zero, rim))
+    one.append(step("first", 1, "one_1", h_three, *zero, rim))
     rims = over_far(one[0]), over_near(one[1])
+    acc = [inner(u, f"two_inner_{u}", h_two, one, zero[u]) for u in range(cols)]
     two, sent, before = [], (), []
     for u in range(cols):
         rim = after(rims[u], (sent, inside))
-        two.append(step("next", u, f"two_{u}", h_two, one, rim, zero[u]))
+        two.append(step("next", u, f"two_{u}", h_two, rim, acc[u]))
         sent = jnp.concatenate([two[u], one[u][:1]])
         other = across(sent)
         two[u] = jnp.concatenate([two[u], other[1:2], other[0:1]])
@@ -334,12 +376,14 @@
     inside_core = core(after(inside, two[0]))
     h_four = h_three + [prepare("inner", codes, inside, inside_core)]
     rims = over_far(two[0]), over_near(two[1])
-    three = [step("next", 0, "three_0", h_four, two, rims[0], before[0])]
+    acc = inner(0, "three_inner_0", h_four, two, before[0])
+    three = [step("next", 0, "three_0", h_four, rims[0], acc)]
     rim = after(rims[1], three[0])
-    three.append(step("next", 1, "three_1", h_four, two, rim, before[1]))
+    three.append(step("whole", 1, "three_1", h_four, *two, rim, before[1]))
     rims = over_far(three[0]), over_near(three[1])
-    four = step("other", 0, "four_0", h_four, three, rims[0], two[0])
-    kept, sent = step("last", 1, "four_1", h_four, three, rims[1], two[1], *four, flags)
+    acc = [inner(u, f"four_inner_{u}", h_four, three, two[u]) for u in range(cols)]
+    four = step("other", 0, "four_0", h_four, rims[0], acc[0])
+    kept, sent = step("last", 1, "four_1", h_four, rims[1], acc[1], *four, flags)
 
     sent = core(sent)
     packed = jnp.where(half == 1, jnp.concatenate([kept, sent]), jnp.concatenate([sent, kept]))

time: 61.8 us -> 60.8 us (0.984)
  waiting for transfers between devices: 11.4 us -> 9.83 us
  Pallas kernels: 9.29 us -> 9.94 us
    pallas_call x0 -> x5, Pallas kernels: none -> 2.29 us  [inner(): pl.pallas_call(functools.partial(inner_kernel, u, len(h_ready)), in_specs...]
    pallas_call x8, Pallas kernels: 5.33 us -> 3.69 us  [step(): pl.pallas_call(functools.partial(step_kernel, kind, u, len(h_ready)), in_...]
    ppermute x5, waiting for transfers between devices: 6.62 us -> 5.78 us  [across(): return lax.ppermute(value, 'grp', [(i, i ^ 3) for i in range(grp)])]
    ppermute x4, waiting for transfers between devices: 2.44 us -> 1.66 us  [over_near(): return lax.ppermute(value, 'wide', near)]
  transfers between devices with their start and end apart: 18 -> 18, of which waited for: 10 -> 9; matrix products, arithmetic and copies ran while one was open for 1% -> 1% of each run, Pallas kernels for 11% -> 13%
where the time goes in v7:
time: 60.8 us; the launch traced here: 60.5 us
  starting transfers between devices  28.4 us (47%)
  Pallas kernels  9.94 us (16%)
  blocking collectives  9.93 us (16%)
  waiting for transfers between devices  9.83 us (16%)
  local copies, waits for them, and re-layouts  1.99 us (3%)
    ppermute x4, starting transfers between devices, over_near(): return lax.ppermute(value, 'wide', near)  18.4 us
    all_to_all x1, blocking collectives, body(): lax.all_to_all(packed, ('wide', 'grp'), split_axis=0, concat_axis=0, tile...  9.93 us
    ppermute x5, starting transfers between devices, across(): return lax.ppermute(value, 'grp', [(i, i ^ 3) for i in range(grp)])  6.05 us
    ppermute x5, waiting for transfers between devices, across(): return lax.ppermute(value, 'grp', [(i, i ^ 3) for i in range(grp)])  5.78 us
    pallas_call x8, Pallas kernels, step(): pl.pallas_call(functools.partial(step_kernel, kind, u, len(h_ready)), in_...  3.69 us
    ppermute x4, starting transfers between devices, over_far(): return lax.ppermute(value, 'wide', far)  2.66 us
    ppermute x5, waiting for transfers between devices, core(): return lax.ppermute(value, 'grp', [(i, i ^ 1) for i in range(grp)])  2.38 us
    pallas_call x3, Pallas kernels, prepare(): pl.pallas_call(functools.partial(prepare_kernel, mode), in_specs=[SMEM] +...  2.37 us
  transfers between devices with their start and end apart: 18, of which 9 were waited for; matrix products, arithmetic and copies ran while one was open for 1% of the time, Pallas kernels for 13%

profile of v7, /device:TPU:0, one launch (start us, length us, event | category | flops | bytes accessed | tf_op | source)
XLA Modules:
  0.0 60.5 jit_solution(10716894713771756117)
XLA Ops:
  0.0 0.5 collective-permute-start.1
  0.6 0.1 broadcast_in_dim.11
  0.8 0.8 %copy-done.1 = f32[64,1,2,128]{3,2,1,0:T(2,128)S(1)} copy-done((f32[64,1,2,128]{3,2,1,0:T(2,128)S(1)}, f32[64,1,2,128]{3,2,1,0:T(2,128)}, u32[]{:S(2)}) %copy-start.1) | copy-done | bytes 65560
  1.6 0.7 %copy-done.3 = s32[1,2,5]{2,1,0:T(2,128)S(1)} copy-done((s32[1,2,5]{2,1,0:T(2,128)S(1)}, s32[1,2,5]{2,1,0:T(2,128)}, u32[]{:S(2)}) %copy-start.3) | copy-done | bytes 64
  2.4 0.1 collective-permute-start
  2.5 1.1 %collective-permute-done = f32[72,128]{1,0:T(8,128)S(1)} collective-permute-done((f32[72,128]{1,0:T(8,128)S(1)}, f32[72,128]{1,0:T(8,128)S(1)}, u32[]{:S(2)}, u32[]{:S(2)}) %collective-permute-start) | collective-permute-done | bytes 36896 | tf_op jit(solution)/shard_map/ppermute | solution.py:331
  3.7 2.7 %collective-permute-start.2 = (f32[2,72,128]{2,1,0:T(8,128)S(1)}, f32[2,72,128]{2,1,0:T(8,128)S(1)}, u32[]{:S(2)}, u32[]{:S(2)}) collective-permute-start(f32[2,72,128]{2,1,0:T(8,128)S(1)} %pad_maximum_fusion), channel_id=1, source_target_pairs={{0,3},{1,2},{2,1},{3,0},{4,7},{5,6},{6,5},{7,4},{8,11},{9,10},{10,... | collective-permute-start | bytes 221192 | tf_op jit(solution)/shard_map/ppermute | solution.py:328
  6.4 0.1 collective-permute-start.3
  6.5 2.5 %collective-permute-done.2 = f32[2,72,128]{2,1,0:T(8,128)S(1)} collective-permute-done((f32[2,72,128]{2,1,0:T(8,128)S(1)}, f32[2,72,128]{2,1,0:T(8,128)S(1)}, u32[]{:S(2)}, u32[]{:S(2)}) %collective-permute-start.2) | collective-permute-done | bytes 73760 | tf_op jit(solution)/shard_map/ppermute | solution.py:328
  9.0 0.7 %collective-permute-start.4 = (f32[4,32,128]{2,1,0:T(8,128)S(1)}, f32[4,32,128]{2,1,0:T(8,128)S(1)}, u32[]{:S(2)}, u32[]{:S(2)}) collective-permute-start(f32[4,32,128]{2,1,0:T(8,128)S(1)} %maximum_select_fusion.1.refs_2_.refs_3_), channel_id=1, source_target_pairs={{4,8},{8,4},{12,16},{16,12},{20,24},{24,20},{5,9},{9,5},{13,17},{1... | collective-permute-start | bytes 196616 | tf_op jit(solution)/shard_map/ppermute | solution.py:334
  9.7 4.4 %collective-permute-start.6 = (f32[4,32,128]{2,1,0:T(8,128)S(1)}, f32[4,32,128]{2,1,0:T(8,128)S(1)}, u32[]{:S(2)}, u32[]{:S(2)}) collective-permute-start(f32[4,32,128]{2,1,0:T(8,128)S(1)} %maximum_select_fusion.2.refs_3_), channel_id=1, source_target_pairs={{0,4},{4,0},{8,12},{12,8},{16,20},{20,16},{24,28},{28,24},{1,5},{5... | collective-permute-start | bytes 196616 | tf_op jit(solution)/shard_map/ppermute | solution.py:337
  14.3 0.1 concatenate.27.codes_ref
  14.3 0.9 %prepare_chip.1.refs_0_ = bf16[2,2,256,1152]{3,2,1,0:T(8,128)(2,1)S(1)} custom-call(s32[44]{0:T(128)S(1)} %concatenate.27.codes_ref, f32[1,2,5,128,128]{4,3,2,1,0:T(8,128)S(1)} %copy-done, f32[1,2,5,128,128]{4,3,2,1,0:T(8,128)S(1)} %collective-permute-done.1.core_ref.refs_1_), custom_call_target="tpu_custom_call" | custom-call | tf_op jit(solution)/shard_map/prepare_chip/pallas_call | solution.py:114
  15.3 0.8 %collective-permute-done.3.refs_0_ = f32[1,1,5,128,128]{4,3,2,1,0:T(8,128)S(1)} collective-permute-done((f32[1,1,5,128,128]{4,3,2,1,0:T(8,128)S(1)}, f32[1,1,5,128,128]{4,3,2,1,0:T(8,128)S(1)}, u32[]{:S(2)}, u32[]{:S(2)}) %collective-permute-start.3) | collective-permute-done | bytes 327712 | tf_op jit(solution)/shard_map/ppermute | solution.py:328
  16.1 0.5 collective-permute-start.5
  16.5 0.5 collective-permute-done.6.refs_4_
  17.1 1.4 %collective-permute-start.7 = (f32[1,1,5,128,128]{4,3,2,1,0:T(8,128)S(1)}, f32[1,1,5,128,128]{4,3,2,1,0:T(8,128)S(1)}, u32[]{:S(2)}, u32[]{:S(2)}) collective-permute-start(f32[1,1,5,128,128]{4,3,2,1,0:T(8,128)S(1)} %get-tuple-element.27), channel_id=1, source_target_pairs={{0,3},{1,2},{2,1},{3,0},{4,7},{5,6},{6,5},{7,4},{8,11},{9,10},{10,... | collective-permute-start | bytes 983048 | tf_op jit(solution)/shard_map/ppermute | solution.py:328
  18.5 0.7 %prepare_border.1.refs_1_ = bf16[1,2,256,1152]{3,2,1,0:T(8,128)(2,1)S(1)} custom-call(s32[44]{0:T(128)S(1)} %concatenate.27.codes_ref, f32[1,1,5,128,128]{4,3,2,1,0:T(8,128)S(1)} %collective-permute-done.3.refs_0_, f32[1,1,5,128,128]{4,3,2,1,0:T(8,128)S(1)} %collective-permute-done.5.refs_1_), custom_call_target="tpu_custom_call" | custom-call | tf_op jit(solution)/shard_map/prepare_border/pallas_call | solution.py:114
  19.2 0.6 one_0.1.refs_1_
  19.8 0.7 %collective-permute-start.8 = (f32[3,32,128]{2,1,0:T(8,128)S(1)}, f32[3,32,128]{2,1,0:T(8,128)S(1)}, u32[]{:S(2)}, u32[]{:S(2)}) collective-permute-start(f32[3,32,128]{2,1,0:T(8,128)S(1)} %one_0.1.refs_1_), channel_id=1, source_target_pairs={{4,8},{8,4},{12,16},{16,12},{20,24},{24,20},{5,9},{9,5},{13,17},{1... | collective-permute-start | bytes 147464 | tf_op jit(solution)/shard_map/ppermute | solution.py:334
  20.5 0.6 one_1.1.refs_2_
  21.1 5.3 %collective-permute-start.11 = (f32[3,32,128]{2,1,0:T(8,128)S(1)}, f32[3,32,128]{2,1,0:T(8,128)S(1)}, u32[]{:S(2)}, u32[]{:S(2)}) collective-permute-start(f32[3,32,128]{2,1,0:T(8,128)S(1)} %one_1.1.refs_2_), channel_id=1, source_target_pairs={{0,4},{4,0},{8,12},{12,8},{16,20},{20,16},{24,28},{28,24},{1,5},{5... | collective-permute-start | bytes 147464 | tf_op jit(solution)/shard_map/ppermute | solution.py:337
  26.4 0.4 two_inner_1.1.refs_2_
  26.8 0.4 two_inner_0.1.refs_2_
  27.2 0.2 two_0.1
  27.4 1.4 %collective-permute-start.9 = (f32[3,32,128]{2,1,0:T(8,128)S(1)}, f32[3,32,128]{2,1,0:T(8,128)S(1)}, u32[]{:S(2)}, u32[]{:S(2)}) collective-permute-start(f32[3,32,128]{2,1,0:T(8,128)S(1)} %pad_maximum_fusion.5), channel_id=1, source_target_pairs={{0,3},{1,2},{2,1},{3,0},{4,7},{5,6},{6,5},{7,4},{8,11},{9,10},{10,... | collective-permute-start | bytes 147464 | tf_op jit(solution)/shard_map/ppermute | solution.py:328
  28.9 0.2 two_1.1
  29.1 0.4 collective-permute-start.12
  29.6 1.9 %collective-permute-done.9 = f32[3,32,128]{2,1,0:T(8,128)S(1)} collective-permute-done((f32[3,32,128]{2,1,0:T(8,128)S(1)}, f32[3,32,128]{2,1,0:T(8,128)S(1)}, u32[]{:S(2)}, u32[]{:S(2)}) %collective-permute-start.9) | collective-permute-done | bytes 49184 | tf_op jit(solution)/shard_map/ppermute | solution.py:328
  31.5 0.7 %collective-permute-start.14 = (f32[4,32,128]{2,1,0:T(8,128)S(1)}, f32[4,32,128]{2,1,0:T(8,128)S(1)}, u32[]{:S(2)}, u32[]{:S(2)}) collective-permute-start(f32[4,32,128]{2,1,0:T(8,128)S(1)} %pad_maximum_fusion.1.refs_3_.refs_5_), channel_id=1, source_target_pairs={{4,8},{8,4},{12,16},{16,12},{20,24},{24,20},{5,9},{9,5},{13,17},{1... | collective-permute-start | bytes 196616 | tf_op jit(solution)/shard_map/ppermute | solution.py:334
  32.2 0.2 collective-permute-start.10
  32.4 0.5 collective-permute-done.12
  32.9 4.0 %collective-permute-start.13 = (f32[4,32,128]{2,1,0:T(8,128)S(1)}, f32[4,32,128]{2,1,0:T(8,128)S(1)}, u32[]{:S(2)}, u32[]{:S(2)}) collective-permute-start(f32[4,32,128]{2,1,0:T(8,128)S(1)} %pad_maximum_fusion.2.refs_4_.refs_5_), channel_id=1, source_target_pairs={{0,4},{4,0},{8,12},{12,8},{16,20},{20,16},{24,28},{28,24},{1,5},{5... | collective-permute-start | bytes 196616 | tf_op jit(solution)/shard_map/ppermute | solution.py:337
  37.0 0.7 %prepare_inner.1.refs_2_ = bf16[1,2,256,1152]{3,2,1,0:T(8,128)(2,1)S(1)} custom-call(s32[44]{0:T(128)S(1)} %concatenate.27.codes_ref, f32[1,1,5,128,128]{4,3,2,1,0:T(8,128)S(1)} %collective-permute-done.7.refs_0_, f32[1,1,5,128,128]{4,3,2,1,0:T(8,128)S(1)} %collective-permute-done.10.refs_1_), custom_call_target="tpu_custom_call" | custom-call | tf_op jit(solution)/shard_map/prepare_inner/pallas_call | solution.py:114
  37.7 0.5 three_inner_0.1.refs_4_
  38.3 0.3 three_0.1.refs_3_
  38.6 0.7 %collective-permute-start.16 = (f32[4,32,128]{2,1,0:T(8,128)S(1)}, f32[4,32,128]{2,1,0:T(8,128)S(1)}, u32[]{:S(2)}, u32[]{:S(2)}) collective-permute-start(f32[4,32,128]{2,1,0:T(8,128)S(1)} %three_0.1.refs_3_), channel_id=1, source_target_pairs={{4,8},{8,4},{12,16},{16,12},{20,24},{24,20},{5,9},{9,5},{13,17},{1... | collective-permute-start | bytes 196616 | tf_op jit(solution)/shard_map/ppermute | solution.py:334
  39.3 0.4 collective-permute-done.13.refs_5_
  39.7 0.7 %three_1.1.refs_4_ = f32[4,32,128]{2,1,0:T(8,128)S(1)} custom-call(bf16[2,2,256,1152]{3,2,1,0:T(8,128)(2,1)S(1)} %prepare_chip.1.refs_0_, bf16[1,2,256,1152]{3,2,1,0:T(8,128)(2,1)S(1)} %prepare_border.1.refs_1_, bf16[1,2,256,1152]{3,2,1,0:T(8,128)(2,1)S(1)} %prepare_inner.1.refs_2_, f32[4,32,128]{2,1,0:T(8,128)S(1)} %pad_maximum_fusion.1.refs_3_.refs_5_, ...), custom_call_target="tpu_custom_call" | custom-call | flops 150994944 | bytes 2359296 | tf_op jit(solution)/shard_map/three_1/pallas_call | solution.py:244
  40.4 4.6 %collective-permute-start.15 = (f32[4,32,128]{2,1,0:T(8,128)S(1)}, f32[4,32,128]{2,1,0:T(8,128)S(1)}, u32[]{:S(2)}, u32[]{:S(2)}) collective-permute-start(f32[4,32,128]{2,1,0:T(8,128)S(1)} %three_1.1.refs_4_), channel_id=1, source_target_pairs={{0,4},{4,0},{8,12},{12,8},{16,20},{20,16},{24,28},{28,24},{1,5},{5... | collective-permute-start | bytes 196616 | tf_op jit(solution)/shard_map/ppermute | solution.py:337
  45.0 0.5 four_inner_0.1.refs_4_
  45.5 0.5 four_inner_1.1.refs_4_
  46.1 0.5 four_0.1
  46.6 0.7 %collective-permute-done.15.refs_3_ = f32[4,32,128]{2,1,0:T(8,128)S(1)} collective-permute-done((f32[4,32,128]{2,1,0:T(8,128)S(1)}, f32[4,32,128]{2,1,0:T(8,128)S(1)}, u32[]{:S(2)}, u32[]{:S(2)}) %collective-permute-start.15) | collective-permute-done | bytes 65568 | tf_op jit(solution)/shard_map/ppermute | solution.py:337
  47.3 0.5 four_1.1
  47.9 1.2 %collective-permute-done.17 = f32[4,24,128]{2,1,0:T(8,128)S(1)} collective-permute-done((f32[4,24,128]{2,1,0:T(8,128)S(1)}, f32[4,24,128]{2,1,0:T(8,128)S(1)}, u32[]{:S(2)}, u32[]{:S(2)}) %collective-permute-start.17) | collective-permute-done | bytes 49184 | tf_op jit(solution)/shard_map/ppermute | solution.py:331
  49.1 9.9 %all_to_all.5.parts_ref = f32[8,24,128]{2,1,0:T(8,128)S(1)} all-to-all(f32[8,24,128]{2,1,0:T(8,128)S(1)} %maximum_select_fusion), channel_id=1, replica_groups={{28,24,20,16,12,8,4,0},{29,25,21,17,13,9,5,1},{30,26,22,18,14,10,6,2},{..., dimensions={0} | all-to-all | bytes 196608 | tf_op jit(solution)/shard_map/all_to_all | solution.py:391
  59.0 1.5 %finish.1 = f32[8,1,16,128]{3,2,1,0:T(8,128)} custom-call(s32[32,128]{1,0:T(8,128)S(1)} %broadcast_in_dim.12.flags_ref.refs_7_, f32[8,24,128]{2,1,0:T(8,128)S(1)} %all_to_all.5.parts_ref, f32[8,8,8]{2,1,0:T(8,128)S(1)} %copy-done.2), custom_call_target="tpu_custom_call" | custom-call | tf_op jit(solution)/shard_map/finish/pallas_call | solution.py:300
  (46 shorter events, 0.7 us)
Async XLA Ops:
  0.0 3.7 %copy-start = (f32[1,2,5,128,128]{4,3,2,1,0:T(8,128)S(1)}, f32[1,2,5,128,128]{4,3,2,1,0:T(8,128)}, u32[]{:S(2)}) copy-start(f32[1,2,5,128,128]{4,3,2,1,0:T(8,128)} %refs_0_.1) | copy-start | bytes 1966084
  0.0 3.6 %collective-permute-start.1 = (f32[1,2,5,128,128]{4,3,2,1,0:T(8,128)}, f32[1,2,5,128,128]{4,3,2,1,0:T(8,128)S(1)}, u32[]{:S(2)}, u32[]{:S(2)}) collective-permute-start(f32[1,2,5,128,128]{4,3,2,1,0:T(8,128)} %refs_0_.1), channel_id=1, source_target_pairs={{0,1},{1,0},{2,3},{3,2},{4,5},{5,4},{6,7},{7,6},{8,9},{9,8},{10,11... | collective-permute-start | bytes 1966088 | tf_op jit(solution)/shard_map/ppermute | solution.py:331
  0.8 0.8 %copy-start.1 = (f32[64,1,2,128]{3,2,1,0:T(2,128)S(1)}, f32[64,1,2,128]{3,2,1,0:T(2,128)}, u32[]{:S(2)}) copy-start(f32[64,1,2,128]{3,2,1,0:T(2,128)} %slab_ref.1) | copy-start | bytes 196612
  1.6 0.7 %copy-start.3 = (s32[1,2,5]{2,1,0:T(2,128)S(1)}, s32[1,2,5]{2,1,0:T(2,128)}, u32[]{:S(2)}) copy-start(s32[1,2,5]{2,1,0:T(2,128)} %codes_ref.1) | copy-start | bytes 124
  2.4 1.3 %collective-permute-start = (f32[72,128]{1,0:T(8,128)S(1)}, f32[72,128]{1,0:T(8,128)S(1)}, u32[]{:S(2)}, u32[]{:S(2)}) collective-permute-start(f32[72,128]{1,0:T(8,128)S(1)} %get-tuple-element.46), channel_id=1, source_target_pairs={{0,1},{1,0},{2,3},{3,2},{4,5},{5,4},{6,7},{7,6},{8,9},{9,8},{10,11... | collective-permute-start | bytes 110600 | tf_op jit(solution)/shard_map/ppermute | solution.py:331
  3.7 5.3 %collective-permute-start.2 = (f32[2,72,128]{2,1,0:T(8,128)S(1)}, f32[2,72,128]{2,1,0:T(8,128)S(1)}, u32[]{:S(2)}, u32[]{:S(2)}) collective-permute-start(f32[2,72,128]{2,1,0:T(8,128)S(1)} %pad_maximum_fusion), channel_id=1, source_target_pairs={{0,3},{1,2},{2,1},{3,0},{4,7},{5,6},{6,5},{7,4},{8,11},{9,10},{10,... | collective-permute-start | bytes 221192 | tf_op jit(solution)/shard_map/ppermute | solution.py:328
  6.4 9.7 %collective-permute-start.3 = (f32[1,1,5,128,128]{4,3,2,1,0:T(8,128)S(1)}, f32[1,1,5,128,128]{4,3,2,1,0:T(8,128)S(1)}, u32[]{:S(2)}, u32[]{:S(2)}) collective-permute-start(f32[1,1,5,128,128]{4,3,2,1,0:T(8,128)S(1)} %get-tuple-element.23), channel_id=1, source_target_pairs={{0,3},{1,2},{2,1},{3,0},{4,7},{5,6},{6,5},{7,4},{8,11},{9,10},{10,... | collective-permute-start | bytes 983048 | tf_op jit(solution)/shard_map/ppermute | solution.py:328
  9.0 6.2 %collective-permute-start.4 = (f32[4,32,128]{2,1,0:T(8,128)S(1)}, f32[4,32,128]{2,1,0:T(8,128)S(1)}, u32[]{:S(2)}, u32[]{:S(2)}) collective-permute-start(f32[4,32,128]{2,1,0:T(8,128)S(1)} %maximum_select_fusion.1.refs_2_.refs_3_), channel_id=1, source_target_pairs={{4,8},{8,4},{12,16},{16,12},{20,24},{24,20},{5,9},{9,5},{13,17},{1... | collective-permute-start | bytes 196616 | tf_op jit(solution)/shard_map/ppermute | solution.py:334
  9.7 7.3 %collective-permute-start.6 = (f32[4,32,128]{2,1,0:T(8,128)S(1)}, f32[4,32,128]{2,1,0:T(8,128)S(1)}, u32[]{:S(2)}, u32[]{:S(2)}) collective-permute-start(f32[4,32,128]{2,1,0:T(8,128)S(1)} %maximum_select_fusion.2.refs_3_), channel_id=1, source_target_pairs={{0,4},{4,0},{8,12},{12,8},{16,20},{20,16},{24,28},{28,24},{1,5},{5... | collective-permute-start | bytes 196616 | tf_op jit(solution)/shard_map/ppermute | solution.py:337
  16.1 2.4 %collective-permute-start.5 = (f32[1,1,5,128,128]{4,3,2,1,0:T(8,128)S(1)}, f32[1,1,5,128,128]{4,3,2,1,0:T(8,128)S(1)}, u32[]{:S(2)}, u32[]{:S(2)}) collective-permute-start(f32[1,1,5,128,128]{4,3,2,1,0:T(8,128)S(1)} %collective-permute-done.3.refs_0_), channel_id=1, source_target_pairs={{0,1},{1,0},{2,3},{3,2},{4,5},{5,4},{6,7},{7,6},{8,9},{9,8},{10,11... | collective-permute-start | bytes 983048 | tf_op jit(solution)/shard_map/ppermute | solution.py:331
  17.1 10.1 %collective-permute-start.7 = (f32[1,1,5,128,128]{4,3,2,1,0:T(8,128)S(1)}, f32[1,1,5,128,128]{4,3,2,1,0:T(8,128)S(1)}, u32[]{:S(2)}, u32[]{:S(2)}) collective-permute-start(f32[1,1,5,128,128]{4,3,2,1,0:T(8,128)S(1)} %get-tuple-element.27), channel_id=1, source_target_pairs={{0,3},{1,2},{2,1},{3,0},{4,7},{5,6},{6,5},{7,4},{8,11},{9,10},{10,... | collective-permute-start | bytes 983048 | tf_op jit(solution)/shard_map/ppermute | solution.py:328
  19.8 7.3 %collective-permute-start.8 = (f32[3,32,128]{2,1,0:T(8,128)S(1)}, f32[3,32,128]{2,1,0:T(8,128)S(1)}, u32[]{:S(2)}, u32[]{:S(2)}) collective-permute-start(f32[3,32,128]{2,1,0:T(8,128)S(1)} %one_0.1.refs_1_), channel_id=1, source_target_pairs={{4,8},{8,4},{12,16},{16,12},{20,24},{24,20},{5,9},{9,5},{13,17},{1... | collective-permute-start | bytes 147464 | tf_op jit(solution)/shard_map/ppermute | solution.py:334
  21.1 7.7 %collective-permute-start.11 = (f32[3,32,128]{2,1,0:T(8,128)S(1)}, f32[3,32,128]{2,1,0:T(8,128)S(1)}, u32[]{:S(2)}, u32[]{:S(2)}) collective-permute-start(f32[3,32,128]{2,1,0:T(8,128)S(1)} %one_1.1.refs_2_), channel_id=1, source_target_pairs={{0,4},{4,0},{8,12},{12,8},{16,20},{20,16},{24,28},{28,24},{1,5},{5... | collective-permute-start | bytes 147464 | tf_op jit(solution)/shard_map/ppermute | solution.py:337
  27.4 4.1 %collective-permute-start.9 = (f32[3,32,128]{2,1,0:T(8,128)S(1)}, f32[3,32,128]{2,1,0:T(8,128)S(1)}, u32[]{:S(2)}, u32[]{:S(2)}) collective-permute-start(f32[3,32,128]{2,1,0:T(8,128)S(1)} %pad_maximum_fusion.5), channel_id=1, source_target_pairs={{0,3},{1,2},{2,1},{3,0},{4,7},{5,6},{6,5},{7,4},{8,11},{9,10},{10,... | collective-permute-start | bytes 147464 | tf_op jit(solution)/shard_map/ppermute | solution.py:328
  29.1 3.8 %collective-permute-start.12 = (f32[3,32,128]{2,1,0:T(8,128)S(1)}, f32[3,32,128]{2,1,0:T(8,128)S(1)}, u32[]{:S(2)}, u32[]{:S(2)}) collective-permute-start(f32[3,32,128]{2,1,0:T(8,128)S(1)} %pad_maximum_fusion.6), channel_id=1, source_target_pairs={{0,3},{1,2},{2,1},{3,0},{4,7},{5,6},{6,5},{7,4},{8,11},{9,10},{10,... | collective-permute-start | bytes 147464 | tf_op jit(solution)/shard_map/ppermute | solution.py:328
  31.5 6.8 %collective-permute-start.14 = (f32[4,32,128]{2,1,0:T(8,128)S(1)}, f32[4,32,128]{2,1,0:T(8,128)S(1)}, u32[]{:S(2)}, u32[]{:S(2)}) collective-permute-start(f32[4,32,128]{2,1,0:T(8,128)S(1)} %pad_maximum_fusion.1.refs_3_.refs_5_), channel_id=1, source_target_pairs={{4,8},{8,4},{12,16},{16,12},{20,24},{24,20},{5,9},{9,5},{13,17},{1... | collective-permute-start | bytes 196616 | tf_op jit(solution)/shard_map/ppermute | solution.py:334
  32.2 4.8 %collective-permute-start.10 = (f32[1,1,5,128,128]{4,3,2,1,0:T(8,128)S(1)}, f32[1,1,5,128,128]{4,3,2,1,0:T(8,128)S(1)}, u32[]{:S(2)}, u32[]{:S(2)}) collective-permute-start(f32[1,1,5,128,128]{4,3,2,1,0:T(8,128)S(1)} %collective-permute-done.7.refs_0_), channel_id=1, source_target_pairs={{0,1},{1,0},{2,3},{3,2},{4,5},{5,4},{6,7},{7,6},{8,9},{9,8},{10,11... | collective-permute-start | bytes 983048 | tf_op jit(solution)/shard_map/ppermute | solution.py:331
  32.9 6.8 %collective-permute-start.13 = (f32[4,32,128]{2,1,0:T(8,128)S(1)}, f32[4,32,128]{2,1,0:T(8,128)S(1)}, u32[]{:S(2)}, u32[]{:S(2)}) collective-permute-start(f32[4,32,128]{2,1,0:T(8,128)S(1)} %pad_maximum_fusion.2.refs_4_.refs_5_), channel_id=1, source_target_pairs={{0,4},{4,0},{8,12},{12,8},{16,20},{20,16},{24,28},{28,24},{1,5},{5... | collective-permute-start | bytes 196616 | tf_op jit(solution)/shard_map/ppermute | solution.py:337
  38.6 7.5 %collective-permute-start.16 = (f32[4,32,128]{2,1,0:T(8,128)S(1)}, f32[4,32,128]{2,1,0:T(8,128)S(1)}, u32[]{:S(2)}, u32[]{:S(2)}) collective-permute-start(f32[4,32,128]{2,1,0:T(8,128)S(1)} %three_0.1.refs_3_), channel_id=1, source_target_pairs={{4,8},{8,4},{12,16},{16,12},{20,24},{24,20},{5,9},{9,5},{13,17},{1... | collective-permute-start | bytes 196616 | tf_op jit(solution)/shard_map/ppermute | solution.py:334
  40.4 6.8 %collective-permute-start.15 = (f32[4,32,128]{2,1,0:T(8,128)S(1)}, f32[4,32,128]{2,1,0:T(8,128)S(1)}, u32[]{:S(2)}, u32[]{:S(2)}) collective-permute-start(f32[4,32,128]{2,1,0:T(8,128)S(1)} %three_1.1.refs_4_), channel_id=1, source_target_pairs={{0,4},{4,0},{8,12},{12,8},{16,20},{20,16},{24,28},{28,24},{1,5},{5... | collective-permute-start | bytes 196616 | tf_op jit(solution)/shard_map/ppermute | solution.py:337
  47.2 11.8 %copy-start.2 = (f32[8,8,8]{2,1,0:T(8,128)S(1)}, f32[8,8,8]{2,1,0:T(8,128)}, u32[]{:S(2)}) copy-start(f32[8,8,8]{2,1,0:T(8,128)} %rot_ref.1) | copy-start | bytes 6148
  47.8 1.3 %collective-permute-start.17 = (f32[4,24,128]{2,1,0:T(8,128)S(1)}, f32[4,24,128]{2,1,0:T(8,128)S(1)}, u32[]{:S(2)}, u32[]{:S(2)}) collective-permute-start(f32[4,24,128]{2,1,0:T(8,128)S(1)} %get-tuple-element.36), channel_id=1, source_target_pairs={{0,1},{1,0},{2,3},{3,2},{4,5},{5,4},{6,7},{7,6},{8,9},{9,8},{10,11... | collective-permute-start | bytes 147464 | tf_op jit(solution)/shard_map/ppermute | solution.py:331

commit v8 on v7

--- a/solution.py
+++ b/solution.py
@@ -183,20 +183,17 @@
 
 def step_kernel(kind, u, count, *refs):
     h_refs, refs = refs[:count], refs[count:]
-    if kind in ("first", "whole"):
+    if kind == "first":
         own_0, own_1, rim_ref, *refs, own_x, rim_x = refs
     else:
         rim_ref, acc_ref, *refs, rim_x = refs
     rows_in, states, size = rim_ref.shape
     fill(rim_x, [rim_ref])
     values = products(h_refs, u, rim_x, 1, 6, rows_in)
-    if kind in ("first", "whole"):
+    if kind == "first":
         fill(own_x, [own_0, own_1])
         own = products(h_refs, u, own_x, 2, 0, rows_in)
         values = [value + own[q] for q, value in enumerate(values)]
-        if kind == "whole":
-            before, *refs = refs
-            values = [2.0 * value - before[q] for q, value in enumerate(values)]
     else:
         values = [acc_ref[q] + 2.0 * value for q, value in enumerate(values)]
     if kind in ("other", "last"):
@@ -232,7 +229,7 @@
 
 
 def step(kind, u, name, h_ready, *operands):
-    merged = kind in ("first", "whole")
+    merged = kind == "first"
     rows_in, states, size = operands[0].shape
     rows_out = sum(h.shape[0] for h in h_ready)
     shapes = [(rows_out, states, size)]
@@ -376,10 +373,11 @@
     inside_core = core(after(inside, two[0]))
     h_four = h_three + [prepare("inner", codes, inside, inside_core)]
     rims = over_far(two[0]), over_near(two[1])
-    acc = inner(0, "three_inner_0", h_four, two, before[0])
-    three = [step("next", 0, "three_0", h_four, rims[0], acc)]
+    acc = [inner(0, "three_inner_0", h_four, two, before[0])]
+    acc.append(inner(1, "three_inner_1", h_four, two, after(before[1], acc[0])))
+    three = [step("next", 0, "three_0", h_four, after(rims[0], acc[1]), acc[0])]
     rim = after(rims[1], three[0])
-    three.append(step("whole", 1, "three_1", h_four, *two, rim, before[1]))
+    three.append(step("next", 1, "three_1", h_four, rim, acc[1]))
     rims = over_far(three[0]), over_near(three[1])
     acc = [inner(u, f"four_inner_{u}", h_four, three, two[u]) for u in range(cols)]
     four = step("other", 0, "four_0", h_four, rims[0], acc[0])

time: 60.8 us -> 60.5 us (level)
    pallas_call x5 -> x6, Pallas kernels: 2.29 us -> 2.82 us  [inner(): pl.pallas_call(functools.partial(inner_kernel, u, len(h_ready)), in_specs...]
  transfers between devices with their start and end apart: 18 -> 18, of which waited for: 9 -> 8; matrix products, arithmetic and copies ran while one was open for 1% -> 1% of each run, Pallas kernels for 13% -> 13%
where the time goes in v8:
time: 60.5 us; the launch traced here: 60.2 us
  starting transfers between devices  28.2 us (47%)
  Pallas kernels  10.1 us (17%)
  blocking collectives  10 us (17%)
  waiting for transfers between devices  9.4 us (16%)
  local copies, waits for them, and re-layouts  1.99 us (3%)
    ppermute x4, starting transfers between devices, over_near(): return lax.ppermute(value, 'wide', near)  18.2 us
    all_to_all x1, blocking collectives, body(): lax.all_to_all(packed, ('wide', 'grp'), split_axis=0, concat_axis=0, tile...  10 us
    ppermute x5, starting transfers between devices, across(): return lax.ppermute(value, 'grp', [(i, i ^ 3) for i in range(grp)])  6.05 us
    ppermute x5, waiting for transfers between devices, across(): return lax.ppermute(value, 'grp', [(i, i ^ 3) for i in range(grp)])  5.78 us
    pallas_call x8, Pallas kernels, step(): pl.pallas_call(functools.partial(step_kernel, kind, u, len(h_ready)), in_...  3.29 us
    pallas_call x6, Pallas kernels, inner(): pl.pallas_call(functools.partial(inner_kernel, u, len(h_ready)), in_specs...  2.82 us
    ppermute x4, starting transfers between devices, over_far(): return lax.ppermute(value, 'wide', far)  2.66 us
    ppermute x5, waiting for transfers between devices, core(): return lax.ppermute(value, 'grp', [(i, i ^ 1) for i in range(grp)])  2.38 us
  transfers between devices with their start and end apart: 18, of which 8 were waited for; matrix products, arithmetic and copies ran while one was open for 1% of the time, Pallas kernels for 13%

profile of v8, /device:TPU:0, one launch (start us, length us, event | category | flops | bytes accessed | tf_op | source)
XLA Modules:
  0.0 60.2 jit_solution(13844140872595142317)
XLA Ops:
  0.0 0.5 collective-permute-start.1
  0.6 0.1 broadcast_in_dim.11
  0.8 0.8 %copy-done.1 = f32[64,1,2,128]{3,2,1,0:T(2,128)S(1)} copy-done((f32[64,1,2,128]{3,2,1,0:T(2,128)S(1)}, f32[64,1,2,128]{3,2,1,0:T(2,128)}, u32[]{:S(2)}) %copy-start.1) | copy-done | bytes 65560
  1.6 0.7 %copy-done.3 = s32[1,2,5]{2,1,0:T(2,128)S(1)} copy-done((s32[1,2,5]{2,1,0:T(2,128)S(1)}, s32[1,2,5]{2,1,0:T(2,128)}, u32[]{:S(2)}) %copy-start.3) | copy-done | bytes 64
  2.4 0.1 collective-permute-start
  2.5 1.1 %collective-permute-done = f32[72,128]{1,0:T(8,128)S(1)} collective-permute-done((f32[72,128]{1,0:T(8,128)S(1)}, f32[72,128]{1,0:T(8,128)S(1)}, u32[]{:S(2)}, u32[]{:S(2)}) %collective-permute-start) | collective-permute-done | bytes 36896 | tf_op jit(solution)/shard_map/ppermute | solution.py:328
  3.7 2.7 %collective-permute-start.2 = (f32[2,72,128]{2,1,0:T(8,128)S(1)}, f32[2,72,128]{2,1,0:T(8,128)S(1)}, u32[]{:S(2)}, u32[]{:S(2)}) collective-permute-start(f32[2,72,128]{2,1,0:T(8,128)S(1)} %pad_maximum_fusion), channel_id=1, source_target_pairs={{0,3},{1,2},{2,1},{3,0},{4,7},{5,6},{6,5},{7,4},{8,11},{9,10},{10,... | collective-permute-start | bytes 221192 | tf_op jit(solution)/shard_map/ppermute | solution.py:325
  6.4 0.1 collective-permute-start.3
  6.5 2.5 %collective-permute-done.2 = f32[2,72,128]{2,1,0:T(8,128)S(1)} collective-permute-done((f32[2,72,128]{2,1,0:T(8,128)S(1)}, f32[2,72,128]{2,1,0:T(8,128)S(1)}, u32[]{:S(2)}, u32[]{:S(2)}) %collective-permute-start.2) | collective-permute-done | bytes 73760 | tf_op jit(solution)/shard_map/ppermute | solution.py:325
  9.0 0.7 %collective-permute-start.4 = (f32[4,32,128]{2,1,0:T(8,128)S(1)}, f32[4,32,128]{2,1,0:T(8,128)S(1)}, u32[]{:S(2)}, u32[]{:S(2)}) collective-permute-start(f32[4,32,128]{2,1,0:T(8,128)S(1)} %maximum_select_fusion.1.refs_2_.refs_3_), channel_id=1, source_target_pairs={{4,8},{8,4},{12,16},{16,12},{20,24},{24,20},{5,9},{9,5},{13,17},{1... | collective-permute-start | bytes 196616 | tf_op jit(solution)/shard_map/ppermute | solution.py:331
  9.7 4.4 %collective-permute-start.6 = (f32[4,32,128]{2,1,0:T(8,128)S(1)}, f32[4,32,128]{2,1,0:T(8,128)S(1)}, u32[]{:S(2)}, u32[]{:S(2)}) collective-permute-start(f32[4,32,128]{2,1,0:T(8,128)S(1)} %maximum_select_fusion.2.refs_3_), channel_id=1, source_target_pairs={{0,4},{4,0},{8,12},{12,8},{16,20},{20,16},{24,28},{28,24},{1,5},{5... | collective-permute-start | bytes 196616 | tf_op jit(solution)/shard_map/ppermute | solution.py:334
  14.3 0.1 concatenate.27.codes_ref
  14.3 0.9 %prepare_chip.1.refs_0_ = bf16[2,2,256,1152]{3,2,1,0:T(8,128)(2,1)S(1)} custom-call(s32[44]{0:T(128)S(1)} %concatenate.27.codes_ref, f32[1,2,5,128,128]{4,3,2,1,0:T(8,128)S(1)} %copy-done, f32[1,2,5,128,128]{4,3,2,1,0:T(8,128)S(1)} %collective-permute-done.1.core_ref.refs_1_), custom_call_target="tpu_custom_call" | custom-call | tf_op jit(solution)/shard_map/prepare_chip/pallas_call | solution.py:114
  15.3 0.8 %collective-permute-done.3.refs_0_ = f32[1,1,5,128,128]{4,3,2,1,0:T(8,128)S(1)} collective-permute-done((f32[1,1,5,128,128]{4,3,2,1,0:T(8,128)S(1)}, f32[1,1,5,128,128]{4,3,2,1,0:T(8,128)S(1)}, u32[]{:S(2)}, u32[]{:S(2)}) %collective-permute-start.3) | collective-permute-done | bytes 327712 | tf_op jit(solution)/shard_map/ppermute | solution.py:325
  16.1 0.5 collective-permute-start.5
  16.5 0.5 collective-permute-done.6.refs_4_
  17.1 1.4 %collective-permute-start.7 = (f32[1,1,5,128,128]{4,3,2,1,0:T(8,128)S(1)}, f32[1,1,5,128,128]{4,3,2,1,0:T(8,128)S(1)}, u32[]{:S(2)}, u32[]{:S(2)}) collective-permute-start(f32[1,1,5,128,128]{4,3,2,1,0:T(8,128)S(1)} %get-tuple-element.29), channel_id=1, source_target_pairs={{0,3},{1,2},{2,1},{3,0},{4,7},{5,6},{6,5},{7,4},{8,11},{9,10},{10,... | collective-permute-start | bytes 983048 | tf_op jit(solution)/shard_map/ppermute | solution.py:325
  18.5 0.7 %prepare_border.1.refs_1_ = bf16[1,2,256,1152]{3,2,1,0:T(8,128)(2,1)S(1)} custom-call(s32[44]{0:T(128)S(1)} %concatenate.27.codes_ref, f32[1,1,5,128,128]{4,3,2,1,0:T(8,128)S(1)} %collective-permute-done.3.refs_0_, f32[1,1,5,128,128]{4,3,2,1,0:T(8,128)S(1)} %collective-permute-done.5.refs_1_), custom_call_target="tpu_custom_call" | custom-call | tf_op jit(solution)/shard_map/prepare_border/pallas_call | solution.py:114
  19.2 0.6 one_0.1.refs_1_
  19.8 0.7 %collective-permute-start.8 = (f32[3,32,128]{2,1,0:T(8,128)S(1)}, f32[3,32,128]{2,1,0:T(8,128)S(1)}, u32[]{:S(2)}, u32[]{:S(2)}) collective-permute-start(f32[3,32,128]{2,1,0:T(8,128)S(1)} %one_0.1.refs_1_), channel_id=1, source_target_pairs={{4,8},{8,4},{12,16},{16,12},{20,24},{24,20},{5,9},{9,5},{13,17},{1... | collective-permute-start | bytes 147464 | tf_op jit(solution)/shard_map/ppermute | solution.py:331
  20.5 0.6 one_1.1.refs_2_
  21.1 5.3 %collective-permute-start.11 = (f32[3,32,128]{2,1,0:T(8,128)S(1)}, f32[3,32,128]{2,1,0:T(8,128)S(1)}, u32[]{:S(2)}, u32[]{:S(2)}) collective-permute-start(f32[3,32,128]{2,1,0:T(8,128)S(1)} %one_1.1.refs_2_), channel_id=1, source_target_pairs={{0,4},{4,0},{8,12},{12,8},{16,20},{20,16},{24,28},{28,24},{1,5},{5... | collective-permute-start | bytes 147464 | tf_op jit(solution)/shard_map/ppermute | solution.py:334
  26.4 0.3 two_inner_0.1.refs_2_
  26.8 0.4 two_inner_1.1.refs_2_
  27.2 0.2 two_0.1
  27.4 1.4 %collective-permute-start.9 = (f32[3,32,128]{2,1,0:T(8,128)S(1)}, f32[3,32,128]{2,1,0:T(8,128)S(1)}, u32[]{:S(2)}, u32[]{:S(2)}) collective-permute-start(f32[3,32,128]{2,1,0:T(8,128)S(1)} %pad_maximum_fusion.5), channel_id=1, source_target_pairs={{0,3},{1,2},{2,1},{3,0},{4,7},{5,6},{6,5},{7,4},{8,11},{9,10},{10,... | collective-permute-start | bytes 147464 | tf_op jit(solution)/shard_map/ppermute | solution.py:325
  28.9 0.2 two_1.1
  29.1 0.4 collective-permute-start.12
  29.6 1.9 %collective-permute-done.9 = f32[3,32,128]{2,1,0:T(8,128)S(1)} collective-permute-done((f32[3,32,128]{2,1,0:T(8,128)S(1)}, f32[3,32,128]{2,1,0:T(8,128)S(1)}, u32[]{:S(2)}, u32[]{:S(2)}) %collective-permute-start.9) | collective-permute-done | bytes 49184 | tf_op jit(solution)/shard_map/ppermute | solution.py:325
  31.5 0.7 %collective-permute-start.14 = (f32[4,32,128]{2,1,0:T(8,128)S(1)}, f32[4,32,128]{2,1,0:T(8,128)S(1)}, u32[]{:S(2)}, u32[]{:S(2)}) collective-permute-start(f32[4,32,128]{2,1,0:T(8,128)S(1)} %pad_maximum_fusion.1.refs_3_.refs_5_), channel_id=1, source_target_pairs={{4,8},{8,4},{12,16},{16,12},{20,24},{24,20},{5,9},{9,5},{13,17},{1... | collective-permute-start | bytes 196616 | tf_op jit(solution)/shard_map/ppermute | solution.py:331
  32.2 0.2 collective-permute-start.10
  32.4 0.5 collective-permute-done.12
  32.9 4.0 %collective-permute-start.13 = (f32[4,32,128]{2,1,0:T(8,128)S(1)}, f32[4,32,128]{2,1,0:T(8,128)S(1)}, u32[]{:S(2)}, u32[]{:S(2)}) collective-permute-start(f32[4,32,128]{2,1,0:T(8,128)S(1)} %pad_maximum_fusion.2.refs_4_.refs_5_), channel_id=1, source_target_pairs={{0,4},{4,0},{8,12},{12,8},{16,20},{20,16},{24,28},{28,24},{1,5},{5... | collective-permute-start | bytes 196616 | tf_op jit(solution)/shard_map/ppermute | solution.py:334
  37.0 0.7 %prepare_inner.1.refs_2_ = bf16[1,2,256,1152]{3,2,1,0:T(8,128)(2,1)S(1)} custom-call(s32[44]{0:T(128)S(1)} %concatenate.27.codes_ref, f32[1,1,5,128,128]{4,3,2,1,0:T(8,128)S(1)} %collective-permute-done.7.refs_0_, f32[1,1,5,128,128]{4,3,2,1,0:T(8,128)S(1)} %collective-permute-done.10.refs_1_), custom_call_target="tpu_custom_call" | custom-call | tf_op jit(solution)/shard_map/prepare_inner/pallas_call | solution.py:114
  37.7 0.5 three_inner_0.1.refs_4_
  38.2 0.5 three_inner_1.1.refs_4_
  38.8 0.3 three_0.1.refs_3_
  39.1 0.7 %collective-permute-start.16 = (f32[4,32,128]{2,1,0:T(8,128)S(1)}, f32[4,32,128]{2,1,0:T(8,128)S(1)}, u32[]{:S(2)}, u32[]{:S(2)}) collective-permute-start(f32[4,32,128]{2,1,0:T(8,128)S(1)} %three_0.1.refs_3_), channel_id=1, source_target_pairs={{4,8},{8,4},{12,16},{16,12},{20,24},{24,20},{5,9},{9,5},{13,17},{1... | collective-permute-start | bytes 196616 | tf_op jit(solution)/shard_map/ppermute | solution.py:331
  39.8 0.3 three_1.1.refs_4_
  40.1 4.5 %collective-permute-start.15 = (f32[4,32,128]{2,1,0:T(8,128)S(1)}, f32[4,32,128]{2,1,0:T(8,128)S(1)}, u32[]{:S(2)}, u32[]{:S(2)}) collective-permute-start(f32[4,32,128]{2,1,0:T(8,128)S(1)} %three_1.1.refs_4_), channel_id=1, source_target_pairs={{0,4},{4,0},{8,12},{12,8},{16,20},{20,16},{24,28},{28,24},{1,5},{5... | collective-permute-start | bytes 196616 | tf_op jit(solution)/shard_map/ppermute | solution.py:334
  44.6 0.5 four_inner_0.1.refs_4_
  45.1 0.5 four_inner_1.1.refs_4_
  45.7 0.5 four_0.1
  46.2 0.7 %collective-permute-done.15.refs_3_ = f32[4,32,128]{2,1,0:T(8,128)S(1)} collective-permute-done((f32[4,32,128]{2,1,0:T(8,128)S(1)}, f32[4,32,128]{2,1,0:T(8,128)S(1)}, u32[]{:S(2)}, u32[]{:S(2)}) %collective-permute-start.15) | collective-permute-done | bytes 65568 | tf_op jit(solution)/shard_map/ppermute | solution.py:334
  46.9 0.5 four_1.1
  47.5 1.2 %collective-permute-done.17 = f32[4,24,128]{2,1,0:T(8,128)S(1)} collective-permute-done((f32[4,24,128]{2,1,0:T(8,128)S(1)}, f32[4,24,128]{2,1,0:T(8,128)S(1)}, u32[]{:S(2)}, u32[]{:S(2)}) %collective-permute-start.17) | collective-permute-done | bytes 49184 | tf_op jit(solution)/shard_map/ppermute | solution.py:328
  48.7 10.0 %all_to_all.5.parts_ref = f32[8,24,128]{2,1,0:T(8,128)S(1)} all-to-all(f32[8,24,128]{2,1,0:T(8,128)S(1)} %maximum_select_fusion), channel_id=1, replica_groups={{28,24,20,16,12,8,4,0},{29,25,21,17,13,9,5,1},{30,26,22,18,14,10,6,2},{..., dimensions={0} | all-to-all | bytes 196608 | tf_op jit(solution)/shard_map/all_to_all | solution.py:389
  58.8 1.5 %finish.1 = f32[8,1,16,128]{3,2,1,0:T(8,128)} custom-call(s32[32,128]{1,0:T(8,128)S(1)} %broadcast_in_dim.12.flags_ref.refs_7_, f32[8,24,128]{2,1,0:T(8,128)S(1)} %all_to_all.5.parts_ref, f32[8,8,8]{2,1,0:T(8,128)S(1)} %copy-done.2), custom_call_target="tpu_custom_call" | custom-call | tf_op jit(solution)/shard_map/finish/pallas_call | solution.py:297
  (47 shorter events, 0.7 us)
Async XLA Ops:
  0.0 3.7 %copy-start = (f32[1,2,5,128,128]{4,3,2,1,0:T(8,128)S(1)}, f32[1,2,5,128,128]{4,3,2,1,0:T(8,128)}, u32[]{:S(2)}) copy-start(f32[1,2,5,128,128]{4,3,2,1,0:T(8,128)} %refs_0_.1) | copy-start | bytes 1966084
  0.0 3.6 %collective-permute-start.1 = (f32[1,2,5,128,128]{4,3,2,1,0:T(8,128)}, f32[1,2,5,128,128]{4,3,2,1,0:T(8,128)S(1)}, u32[]{:S(2)}, u32[]{:S(2)}) collective-permute-start(f32[1,2,5,128,128]{4,3,2,1,0:T(8,128)} %refs_0_.1), channel_id=1, source_target_pairs={{0,1},{1,0},{2,3},{3,2},{4,5},{5,4},{6,7},{7,6},{8,9},{9,8},{10,11... | collective-permute-start | bytes 1966088 | tf_op jit(solution)/shard_map/ppermute | solution.py:328
  0.8 0.8 %copy-start.1 = (f32[64,1,2,128]{3,2,1,0:T(2,128)S(1)}, f32[64,1,2,128]{3,2,1,0:T(2,128)}, u32[]{:S(2)}) copy-start(f32[64,1,2,128]{3,2,1,0:T(2,128)} %slab_ref.1) | copy-start | bytes 196612
  1.6 0.7 %copy-start.3 = (s32[1,2,5]{2,1,0:T(2,128)S(1)}, s32[1,2,5]{2,1,0:T(2,128)}, u32[]{:S(2)}) copy-start(s32[1,2,5]{2,1,0:T(2,128)} %codes_ref.1) | copy-start | bytes 124
  2.4 1.3 %collective-permute-start = (f32[72,128]{1,0:T(8,128)S(1)}, f32[72,128]{1,0:T(8,128)S(1)}, u32[]{:S(2)}, u32[]{:S(2)}) collective-permute-start(f32[72,128]{1,0:T(8,128)S(1)} %get-tuple-element.50), channel_id=1, source_target_pairs={{0,1},{1,0},{2,3},{3,2},{4,5},{5,4},{6,7},{7,6},{8,9},{9,8},{10,11... | collective-permute-start | bytes 110600 | tf_op jit(solution)/shard_map/ppermute | solution.py:328
  3.7 5.3 %collective-permute-start.2 = (f32[2,72,128]{2,1,0:T(8,128)S(1)}, f32[2,72,128]{2,1,0:T(8,128)S(1)}, u32[]{:S(2)}, u32[]{:S(2)}) collective-permute-start(f32[2,72,128]{2,1,0:T(8,128)S(1)} %pad_maximum_fusion), channel_id=1, source_target_pairs={{0,3},{1,2},{2,1},{3,0},{4,7},{5,6},{6,5},{7,4},{8,11},{9,10},{10,... | collective-permute-start | bytes 221192 | tf_op jit(solution)/shard_map/ppermute | solution.py:325
  6.4 9.7 %collective-permute-start.3 = (f32[1,1,5,128,128]{4,3,2,1,0:T(8,128)S(1)}, f32[1,1,5,128,128]{4,3,2,1,0:T(8,128)S(1)}, u32[]{:S(2)}, u32[]{:S(2)}) collective-permute-start(f32[1,1,5,128,128]{4,3,2,1,0:T(8,128)S(1)} %get-tuple-element.25), channel_id=1, source_target_pairs={{0,3},{1,2},{2,1},{3,0},{4,7},{5,6},{6,5},{7,4},{8,11},{9,10},{10,... | collective-permute-start | bytes 983048 | tf_op jit(solution)/shard_map/ppermute | solution.py:325
  9.0 6.2 %collective-permute-start.4 = (f32[4,32,128]{2,1,0:T(8,128)S(1)}, f32[4,32,128]{2,1,0:T(8,128)S(1)}, u32[]{:S(2)}, u32[]{:S(2)}) collective-permute-start(f32[4,32,128]{2,1,0:T(8,128)S(1)} %maximum_select_fusion.1.refs_2_.refs_3_), channel_id=1, source_target_pairs={{4,8},{8,4},{12,16},{16,12},{20,24},{24,20},{5,9},{9,5},{13,17},{1... | collective-permute-start | bytes 196616 | tf_op jit(solution)/shard_map/ppermute | solution.py:331
  9.7 7.3 %collective-permute-start.6 = (f32[4,32,128]{2,1,0:T(8,128)S(1)}, f32[4,32,128]{2,1,0:T(8,128)S(1)}, u32[]{:S(2)}, u32[]{:S(2)}) collective-permute-start(f32[4,32,128]{2,1,0:T(8,128)S(1)} %maximum_select_fusion.2.refs_3_), channel_id=1, source_target_pairs={{0,4},{4,0},{8,12},{12,8},{16,20},{20,16},{24,28},{28,24},{1,5},{5... | collective-permute-start | bytes 196616 | tf_op jit(solution)/shard_map/ppermute | solution.py:334
  16.1 2.4 %collective-permute-start.5 = (f32[1,1,5,128,128]{4,3,2,1,0:T(8,128)S(1)}, f32[1,1,5,128,128]{4,3,2,1,0:T(8,128)S(1)}, u32[]{:S(2)}, u32[]{:S(2)}) collective-permute-start(f32[1,1,5,128,128]{4,3,2,1,0:T(8,128)S(1)} %collective-permute-done.3.refs_0_), channel_id=1, source_target_pairs={{0,1},{1,0},{2,3},{3,2},{4,5},{5,4},{6,7},{7,6},{8,9},{9,8},{10,11... | collective-permute-start | bytes 983048 | tf_op jit(solution)/shard_map/ppermute | solution.py:328
  17.1 10.1 %collective-permute-start.7 = (f32[1,1,5,128,128]{4,3,2,1,0:T(8,128)S(1)}, f32[1,1,5,128,128]{4,3,2,1,0:T(8,128)S(1)}, u32[]{:S(2)}, u32[]{:S(2)}) collective-permute-start(f32[1,1,5,128,128]{4,3,2,1,0:T(8,128)S(1)} %get-tuple-element.29), channel_id=1, source_target_pairs={{0,3},{1,2},{2,1},{3,0},{4,7},{5,6},{6,5},{7,4},{8,11},{9,10},{10,... | collective-permute-start | bytes 983048 | tf_op jit(solution)/shard_map/ppermute | solution.py:325
  19.8 7.3 %collective-permute-start.8 = (f32[3,32,128]{2,1,0:T(8,128)S(1)}, f32[3,32,128]{2,1,0:T(8,128)S(1)}, u32[]{:S(2)}, u32[]{:S(2)}) collective-permute-start(f32[3,32,128]{2,1,0:T(8,128)S(1)} %one_0.1.refs_1_), channel_id=1, source_target_pairs={{4,8},{8,4},{12,16},{16,12},{20,24},{24,20},{5,9},{9,5},{13,17},{1... | collective-permute-start | bytes 147464 | tf_op jit(solution)/shard_map/ppermute | solution.py:331
  21.1 7.7 %collective-permute-start.11 = (f32[3,32,128]{2,1,0:T(8,128)S(1)}, f32[3,32,128]{2,1,0:T(8,128)S(1)}, u32[]{:S(2)}, u32[]{:S(2)}) collective-permute-start(f32[3,32,128]{2,1,0:T(8,128)S(1)} %one_1.1.refs_2_), channel_id=1, source_target_pairs={{0,4},{4,0},{8,12},{12,8},{16,20},{20,16},{24,28},{28,24},{1,5},{5... | collective-permute-start | bytes 147464 | tf_op jit(solution)/shard_map/ppermute | solution.py:334
  27.4 4.1 %collective-permute-start.9 = (f32[3,32,128]{2,1,0:T(8,128)S(1)}, f32[3,32,128]{2,1,0:T(8,128)S(1)}, u32[]{:S(2)}, u32[]{:S(2)}) collective-permute-start(f32[3,32,128]{2,1,0:T(8,128)S(1)} %pad_maximum_fusion.5), channel_id=1, source_target_pairs={{0,3},{1,2},{2,1},{3,0},{4,7},{5,6},{6,5},{7,4},{8,11},{9,10},{10,... | collective-permute-start | bytes 147464 | tf_op jit(solution)/shard_map/ppermute | solution.py:325
  29.1 3.8 %collective-permute-start.12 = (f32[3,32,128]{2,1,0:T(8,128)S(1)}, f32[3,32,128]{2,1,0:T(8,128)S(1)}, u32[]{:S(2)}, u32[]{:S(2)}) collective-permute-start(f32[3,32,128]{2,1,0:T(8,128)S(1)} %pad_maximum_fusion.6), channel_id=1, source_target_pairs={{0,3},{1,2},{2,1},{3,0},{4,7},{5,6},{6,5},{7,4},{8,11},{9,10},{10,... | collective-permute-start | bytes 147464 | tf_op jit(solution)/shard_map/ppermute | solution.py:325
  31.5 7.3 %collective-permute-start.14 = (f32[4,32,128]{2,1,0:T(8,128)S(1)}, f32[4,32,128]{2,1,0:T(8,128)S(1)}, u32[]{:S(2)}, u32[]{:S(2)}) collective-permute-start(f32[4,32,128]{2,1,0:T(8,128)S(1)} %pad_maximum_fusion.1.refs_3_.refs_5_), channel_id=1, source_target_pairs={{4,8},{8,4},{12,16},{16,12},{20,24},{24,20},{5,9},{9,5},{13,17},{1... | collective-permute-start | bytes 196616 | tf_op jit(solution)/shard_map/ppermute | solution.py:331
  32.2 4.8 %collective-permute-start.10 = (f32[1,1,5,128,128]{4,3,2,1,0:T(8,128)S(1)}, f32[1,1,5,128,128]{4,3,2,1,0:T(8,128)S(1)}, u32[]{:S(2)}, u32[]{:S(2)}) collective-permute-start(f32[1,1,5,128,128]{4,3,2,1,0:T(8,128)S(1)} %collective-permute-done.7.refs_0_), channel_id=1, source_target_pairs={{0,1},{1,0},{2,3},{3,2},{4,5},{5,4},{6,7},{7,6},{8,9},{9,8},{10,11... | collective-permute-start | bytes 983048 | tf_op jit(solution)/shard_map/ppermute | solution.py:328
  32.9 6.9 %collective-permute-start.13 = (f32[4,32,128]{2,1,0:T(8,128)S(1)}, f32[4,32,128]{2,1,0:T(8,128)S(1)}, u32[]{:S(2)}, u32[]{:S(2)}) collective-permute-start(f32[4,32,128]{2,1,0:T(8,128)S(1)} %pad_maximum_fusion.2.refs_4_.refs_5_), channel_id=1, source_target_pairs={{0,4},{4,0},{8,12},{12,8},{16,20},{20,16},{24,28},{28,24},{1,5},{5... | collective-permute-start | bytes 196616 | tf_op jit(solution)/shard_map/ppermute | solution.py:334
  39.1 6.6 %collective-permute-start.16 = (f32[4,32,128]{2,1,0:T(8,128)S(1)}, f32[4,32,128]{2,1,0:T(8,128)S(1)}, u32[]{:S(2)}, u32[]{:S(2)}) collective-permute-start(f32[4,32,128]{2,1,0:T(8,128)S(1)} %three_0.1.refs_3_), channel_id=1, source_target_pairs={{4,8},{8,4},{12,16},{16,12},{20,24},{24,20},{5,9},{9,5},{13,17},{1... | collective-permute-start | bytes 196616 | tf_op jit(solution)/shard_map/ppermute | solution.py:331
  40.1 6.7 %collective-permute-start.15 = (f32[4,32,128]{2,1,0:T(8,128)S(1)}, f32[4,32,128]{2,1,0:T(8,128)S(1)}, u32[]{:S(2)}, u32[]{:S(2)}) collective-permute-start(f32[4,32,128]{2,1,0:T(8,128)S(1)} %three_1.1.refs_4_), channel_id=1, source_target_pairs={{0,4},{4,0},{8,12},{12,8},{16,20},{20,16},{24,28},{28,24},{1,5},{5... | collective-permute-start | bytes 196616 | tf_op jit(solution)/shard_map/ppermute | solution.py:334
  46.9 11.9 %copy-start.2 = (f32[8,8,8]{2,1,0:T(8,128)S(1)}, f32[8,8,8]{2,1,0:T(8,128)}, u32[]{:S(2)}) copy-start(f32[8,8,8]{2,1,0:T(8,128)} %rot_ref.1) | copy-start | bytes 6148
  47.4 1.3 %collective-permute-start.17 = (f32[4,24,128]{2,1,0:T(8,128)S(1)}, f32[4,24,128]{2,1,0:T(8,128)S(1)}, u32[]{:S(2)}, u32[]{:S(2)}) collective-permute-start(f32[4,24,128]{2,1,0:T(8,128)S(1)} %get-tuple-element.40), channel_id=1, source_target_pairs={{0,1},{1,0},{2,3},{3,2},{4,5},{5,4},{6,7},{7,6},{8,9},{9,8},{10,11... | collective-permute-start | bytes 147464 | tf_op jit(solution)/shard_map/ppermute | solution.py:328

commit v9 on v7

--- a/solution.py
+++ b/solution.py
@@ -222,13 +222,13 @@
         kept, sent = jnp.where(edge, border, inner), jnp.where(edge, inner, border)
         for b in range(blocks):
             rows = slice(b * VEC, (b + 1) * VEC)
-            kept_ref[blocks - 1 - b, c * VEC : (c + 1) * VEC, :] = kept[rows]
-            sent_ref[blocks - 1 - b, c * VEC : (c + 1) * VEC, :] = sent[rows]
+            kept_ref[b, c * VEC : (c + 1) * VEC, :] = kept[rows]
+            sent_ref[b, c * VEC : (c + 1) * VEC, :] = sent[rows]
     for b in range(blocks):
         rows = slice(b * VEC, (b + 1) * VEC)
         for ref in (kept_ref, sent_ref):
-            ref[blocks - 1 - b, 2 * VEC :, :] = jnp.zeros((VEC, size), jnp.float32)
-            ref[blocks - 1 - b, 2 * VEC :, 0:VEC] = gram[rows, rows]
+            ref[b, 2 * VEC :, :] = jnp.zeros((VEC, size), jnp.float32)
+            ref[b, 2 * VEC :, 0:VEC] = gram[rows, rows]
 
 
 def step(kind, u, name, h_ready, *operands):
@@ -292,7 +292,7 @@
             mixed.append(total)
     for w in range(wide):
         for c in range(cols):
-            out_ref[:, 0, w * cols + c, :] = mixed[(wide - 1 - w) * cols + c]
+            out_ref[:, 0, w * cols + c, :] = mixed[w * cols + c]
 
 
 def finish(flags, cols, node_count, parts, rotation):
@@ -386,16 +386,8 @@
     kept, sent = step("last", 1, "four_1", h_four, rims[1], acc[1], *four, flags)
 
     sent = core(sent)
-    packed = jnp.where(half == 1, jnp.concatenate([kept, sent]), jnp.concatenate([sent, kept]))
-    groups = [[(wide - 1 - i) * grp + g for i in range(wide)] for g in range(grp)]
-    packed = lax.all_to_all(
-        packed,
-        ("wide", "grp"),
-        split_axis=0,
-        concat_axis=0,
-        tiled=True,
-        axis_index_groups=groups,
-    )
+    packed = jnp.where(half == 1, jnp.concatenate([sent, kept]), jnp.concatenate([kept, sent]))
+    packed = lax.all_to_all(packed, "wide", split_axis=0, concat_axis=0, tiled=True)
     node_count = grp * wide * cols * size
     return finish(flags, cols, node_count, packed, rotation)
 

time: 60.8 us -> 63.1 us (1.038)
  blocking collectives: 9.93 us -> 12.2 us
    all_to_all x1, blocking collectives: 9.93 us -> 12.2 us  [body(): lax.all_to_all(packed, 'wide', split_axis=0, concat_axis=0, tiled=True)]
  transfers between devices with their start and end apart: 18 -> 18, of which waited for: 9 -> 9; matrix products, arithmetic and copies ran while one was open for 1% -> 1% of each run, Pallas kernels for 13% -> 12%
where the time goes in v9:
time: 63.1 us; the launch traced here: 62.8 us
  starting transfers between devices  28.4 us (45%)
  blocking collectives  12.2 us (19%)
  Pallas kernels  9.94 us (16%)
  waiting for transfers between devices  9.83 us (16%)
  local copies, waits for them, and re-layouts  1.99 us (3%)
    ppermute x4, starting transfers between devices, over_near(): return lax.ppermute(value, 'wide', near)  18.4 us
    all_to_all x1, blocking collectives, body(): lax.all_to_all(packed, 'wide', split_axis=0, concat_axis=0, tiled=True)  12.2 us
    ppermute x5, starting transfers between devices, across(): return lax.ppermute(value, 'grp', [(i, i ^ 3) for i in range(grp)])  6.05 us
    ppermute x5, waiting for transfers between devices, across(): return lax.ppermute(value, 'grp', [(i, i ^ 3) for i in range(grp)])  5.78 us
    pallas_call x8, Pallas kernels, step(): pl.pallas_call(functools.partial(step_kernel, kind, u, len(h_ready)), in_...  3.69 us
    ppermute x4, starting transfers between devices, over_far(): return lax.ppermute(value, 'wide', far)  2.66 us
    ppermute x5, waiting for transfers between devices, core(): return lax.ppermute(value, 'grp', [(i, i ^ 1) for i in range(grp)])  2.38 us
    pallas_call x3, Pallas kernels, prepare(): pl.pallas_call(functools.partial(prepare_kernel, mode), in_specs=[SMEM] +...  2.37 us
  transfers between devices with their start and end apart: 18, of which 9 were waited for; matrix products, arithmetic and copies ran while one was open for 1% of the time, Pallas kernels for 12%

profile of v9, /device:TPU:0, one launch (start us, length us, event | category | flops | bytes accessed | tf_op | source)
XLA Modules:
  0.0 62.8 jit_solution(4271503023782853758)
XLA Ops:
  0.0 0.5 collective-permute-start.1
  0.6 0.1 broadcast_in_dim.11
  0.8 0.8 %copy-done.1 = f32[64,1,2,128]{3,2,1,0:T(2,128)S(1)} copy-done((f32[64,1,2,128]{3,2,1,0:T(2,128)S(1)}, f32[64,1,2,128]{3,2,1,0:T(2,128)}, u32[]{:S(2)}) %copy-start.1) | copy-done | bytes 65560
  1.6 0.7 %copy-done.3 = s32[1,2,5]{2,1,0:T(2,128)S(1)} copy-done((s32[1,2,5]{2,1,0:T(2,128)S(1)}, s32[1,2,5]{2,1,0:T(2,128)}, u32[]{:S(2)}) %copy-start.3) | copy-done | bytes 64
  2.4 0.1 collective-permute-start
  2.5 1.1 %collective-permute-done = f32[72,128]{1,0:T(8,128)S(1)} collective-permute-done((f32[72,128]{1,0:T(8,128)S(1)}, f32[72,128]{1,0:T(8,128)S(1)}, u32[]{:S(2)}, u32[]{:S(2)}) %collective-permute-start) | collective-permute-done | bytes 36896 | tf_op jit(solution)/shard_map/ppermute | solution.py:331
  3.7 2.7 %collective-permute-start.2 = (f32[2,72,128]{2,1,0:T(8,128)S(1)}, f32[2,72,128]{2,1,0:T(8,128)S(1)}, u32[]{:S(2)}, u32[]{:S(2)}) collective-permute-start(f32[2,72,128]{2,1,0:T(8,128)S(1)} %pad_maximum_fusion), channel_id=1, source_target_pairs={{0,3},{1,2},{2,1},{3,0},{4,7},{5,6},{6,5},{7,4},{8,11},{9,10},{10,... | collective-permute-start | bytes 221192 | tf_op jit(solution)/shard_map/ppermute | solution.py:328
  6.4 0.1 collective-permute-start.3
  6.5 2.5 %collective-permute-done.2 = f32[2,72,128]{2,1,0:T(8,128)S(1)} collective-permute-done((f32[2,72,128]{2,1,0:T(8,128)S(1)}, f32[2,72,128]{2,1,0:T(8,128)S(1)}, u32[]{:S(2)}, u32[]{:S(2)}) %collective-permute-start.2) | collective-permute-done | bytes 73760 | tf_op jit(solution)/shard_map/ppermute | solution.py:328
  9.0 0.7 %collective-permute-start.4 = (f32[4,32,128]{2,1,0:T(8,128)S(1)}, f32[4,32,128]{2,1,0:T(8,128)S(1)}, u32[]{:S(2)}, u32[]{:S(2)}) collective-permute-start(f32[4,32,128]{2,1,0:T(8,128)S(1)} %maximum_select_fusion.1.refs_2_.refs_3_), channel_id=1, source_target_pairs={{4,8},{8,4},{12,16},{16,12},{20,24},{24,20},{5,9},{9,5},{13,17},{1... | collective-permute-start | bytes 196616 | tf_op jit(solution)/shard_map/ppermute | solution.py:334
  9.7 4.4 %collective-permute-start.6 = (f32[4,32,128]{2,1,0:T(8,128)S(1)}, f32[4,32,128]{2,1,0:T(8,128)S(1)}, u32[]{:S(2)}, u32[]{:S(2)}) collective-permute-start(f32[4,32,128]{2,1,0:T(8,128)S(1)} %maximum_select_fusion.2.refs_3_), channel_id=1, source_target_pairs={{0,4},{4,0},{8,12},{12,8},{16,20},{20,16},{24,28},{28,24},{1,5},{5... | collective-permute-start | bytes 196616 | tf_op jit(solution)/shard_map/ppermute | solution.py:337
  14.3 0.1 concatenate.27.codes_ref
  14.3 0.9 %prepare_chip.1.refs_0_ = bf16[2,2,256,1152]{3,2,1,0:T(8,128)(2,1)S(1)} custom-call(s32[44]{0:T(128)S(1)} %concatenate.27.codes_ref, f32[1,2,5,128,128]{4,3,2,1,0:T(8,128)S(1)} %copy-done, f32[1,2,5,128,128]{4,3,2,1,0:T(8,128)S(1)} %collective-permute-done.1.core_ref.refs_1_), custom_call_target="tpu_custom_call" | custom-call | tf_op jit(solution)/shard_map/prepare_chip/pallas_call | solution.py:114
  15.3 0.8 %collective-permute-done.3.refs_0_ = f32[1,1,5,128,128]{4,3,2,1,0:T(8,128)S(1)} collective-permute-done((f32[1,1,5,128,128]{4,3,2,1,0:T(8,128)S(1)}, f32[1,1,5,128,128]{4,3,2,1,0:T(8,128)S(1)}, u32[]{:S(2)}, u32[]{:S(2)}) %collective-permute-start.3) | collective-permute-done | bytes 327712 | tf_op jit(solution)/shard_map/ppermute | solution.py:328
  16.1 0.5 collective-permute-start.5
  16.5 0.5 collective-permute-done.6.refs_4_
  17.1 1.4 %collective-permute-start.7 = (f32[1,1,5,128,128]{4,3,2,1,0:T(8,128)S(1)}, f32[1,1,5,128,128]{4,3,2,1,0:T(8,128)S(1)}, u32[]{:S(2)}, u32[]{:S(2)}) collective-permute-start(f32[1,1,5,128,128]{4,3,2,1,0:T(8,128)S(1)} %get-tuple-element.27), channel_id=1, source_target_pairs={{0,3},{1,2},{2,1},{3,0},{4,7},{5,6},{6,5},{7,4},{8,11},{9,10},{10,... | collective-permute-start | bytes 983048 | tf_op jit(solution)/shard_map/ppermute | solution.py:328
  18.5 0.7 %prepare_border.1.refs_1_ = bf16[1,2,256,1152]{3,2,1,0:T(8,128)(2,1)S(1)} custom-call(s32[44]{0:T(128)S(1)} %concatenate.27.codes_ref, f32[1,1,5,128,128]{4,3,2,1,0:T(8,128)S(1)} %collective-permute-done.3.refs_0_, f32[1,1,5,128,128]{4,3,2,1,0:T(8,128)S(1)} %collective-permute-done.5.refs_1_), custom_call_target="tpu_custom_call" | custom-call | tf_op jit(solution)/shard_map/prepare_border/pallas_call | solution.py:114
  19.2 0.6 one_0.1.refs_1_
  19.8 0.7 %collective-permute-start.8 = (f32[3,32,128]{2,1,0:T(8,128)S(1)}, f32[3,32,128]{2,1,0:T(8,128)S(1)}, u32[]{:S(2)}, u32[]{:S(2)}) collective-permute-start(f32[3,32,128]{2,1,0:T(8,128)S(1)} %one_0.1.refs_1_), channel_id=1, source_target_pairs={{4,8},{8,4},{12,16},{16,12},{20,24},{24,20},{5,9},{9,5},{13,17},{1... | collective-permute-start | bytes 147464 | tf_op jit(solution)/shard_map/ppermute | solution.py:334
  20.5 0.6 one_1.1.refs_2_
  21.1 5.3 %collective-permute-start.11 = (f32[3,32,128]{2,1,0:T(8,128)S(1)}, f32[3,32,128]{2,1,0:T(8,128)S(1)}, u32[]{:S(2)}, u32[]{:S(2)}) collective-permute-start(f32[3,32,128]{2,1,0:T(8,128)S(1)} %one_1.1.refs_2_), channel_id=1, source_target_pairs={{0,4},{4,0},{8,12},{12,8},{16,20},{20,16},{24,28},{28,24},{1,5},{5... | collective-permute-start | bytes 147464 | tf_op jit(solution)/shard_map/ppermute | solution.py:337
  26.4 0.4 two_inner_1.1.refs_2_
  26.8 0.4 two_inner_0.1.refs_2_
  27.2 0.2 two_0.1
  27.4 1.4 %collective-permute-start.9 = (f32[3,32,128]{2,1,0:T(8,128)S(1)}, f32[3,32,128]{2,1,0:T(8,128)S(1)}, u32[]{:S(2)}, u32[]{:S(2)}) collective-permute-start(f32[3,32,128]{2,1,0:T(8,128)S(1)} %pad_maximum_fusion.5), channel_id=1, source_target_pairs={{0,3},{1,2},{2,1},{3,0},{4,7},{5,6},{6,5},{7,4},{8,11},{9,10},{10,... | collective-permute-start | bytes 147464 | tf_op jit(solution)/shard_map/ppermute | solution.py:328
  28.9 0.2 two_1.1
  29.1 0.4 collective-permute-start.12
  29.6 1.9 %collective-permute-done.9 = f32[3,32,128]{2,1,0:T(8,128)S(1)} collective-permute-done((f32[3,32,128]{2,1,0:T(8,128)S(1)}, f32[3,32,128]{2,1,0:T(8,128)S(1)}, u32[]{:S(2)}, u32[]{:S(2)}) %collective-permute-start.9) | collective-permute-done | bytes 49184 | tf_op jit(solution)/shard_map/ppermute | solution.py:328
  31.5 0.7 %collective-permute-start.14 = (f32[4,32,128]{2,1,0:T(8,128)S(1)}, f32[4,32,128]{2,1,0:T(8,128)S(1)}, u32[]{:S(2)}, u32[]{:S(2)}) collective-permute-start(f32[4,32,128]{2,1,0:T(8,128)S(1)} %pad_maximum_fusion.1.refs_3_.refs_5_), channel_id=1, source_target_pairs={{4,8},{8,4},{12,16},{16,12},{20,24},{24,20},{5,9},{9,5},{13,17},{1... | collective-permute-start | bytes 196616 | tf_op jit(solution)/shard_map/ppermute | solution.py:334
  32.2 0.2 collective-permute-start.10
  32.4 0.5 collective-permute-done.12
  32.9 4.0 %collective-permute-start.13 = (f32[4,32,128]{2,1,0:T(8,128)S(1)}, f32[4,32,128]{2,1,0:T(8,128)S(1)}, u32[]{:S(2)}, u32[]{:S(2)}) collective-permute-start(f32[4,32,128]{2,1,0:T(8,128)S(1)} %pad_maximum_fusion.2.refs_4_.refs_5_), channel_id=1, source_target_pairs={{0,4},{4,0},{8,12},{12,8},{16,20},{20,16},{24,28},{28,24},{1,5},{5... | collective-permute-start | bytes 196616 | tf_op jit(solution)/shard_map/ppermute | solution.py:337
  37.0 0.7 %prepare_inner.1.refs_2_ = bf16[1,2,256,1152]{3,2,1,0:T(8,128)(2,1)S(1)} custom-call(s32[44]{0:T(128)S(1)} %concatenate.27.codes_ref, f32[1,1,5,128,128]{4,3,2,1,0:T(8,128)S(1)} %collective-permute-done.7.refs_0_, f32[1,1,5,128,128]{4,3,2,1,0:T(8,128)S(1)} %collective-permute-done.10.refs_1_), custom_call_target="tpu_custom_call" | custom-call | tf_op jit(solution)/shard_map/prepare_inner/pallas_call | solution.py:114
  37.7 0.5 three_inner_0.1.refs_4_
  38.3 0.3 three_0.1.refs_3_
  38.6 0.7 %collective-permute-start.16 = (f32[4,32,128]{2,1,0:T(8,128)S(1)}, f32[4,32,128]{2,1,0:T(8,128)S(1)}, u32[]{:S(2)}, u32[]{:S(2)}) collective-permute-start(f32[4,32,128]{2,1,0:T(8,128)S(1)} %three_0.1.refs_3_), channel_id=1, source_target_pairs={{4,8},{8,4},{12,16},{16,12},{20,24},{24,20},{5,9},{9,5},{13,17},{1... | collective-permute-start | bytes 196616 | tf_op jit(solution)/shard_map/ppermute | solution.py:334
  39.3 0.4 collective-permute-done.13.refs_5_
  39.7 0.7 %three_1.1.refs_4_ = f32[4,32,128]{2,1,0:T(8,128)S(1)} custom-call(bf16[2,2,256,1152]{3,2,1,0:T(8,128)(2,1)S(1)} %prepare_chip.1.refs_0_, bf16[1,2,256,1152]{3,2,1,0:T(8,128)(2,1)S(1)} %prepare_border.1.refs_1_, bf16[1,2,256,1152]{3,2,1,0:T(8,128)(2,1)S(1)} %prepare_inner.1.refs_2_, f32[4,32,128]{2,1,0:T(8,128)S(1)} %pad_maximum_fusion.1.refs_3_.refs_5_, ...), custom_call_target="tpu_custom_call" | custom-call | flops 150994944 | bytes 2359296 | tf_op jit(solution)/shard_map/three_1/pallas_call | solution.py:244
  40.4 4.6 %collective-permute-start.15 = (f32[4,32,128]{2,1,0:T(8,128)S(1)}, f32[4,32,128]{2,1,0:T(8,128)S(1)}, u32[]{:S(2)}, u32[]{:S(2)}) collective-permute-start(f32[4,32,128]{2,1,0:T(8,128)S(1)} %three_1.1.refs_4_), channel_id=1, source_target_pairs={{0,4},{4,0},{8,12},{12,8},{16,20},{20,16},{24,28},{28,24},{1,5},{5... | collective-permute-start | bytes 196616 | tf_op jit(solution)/shard_map/ppermute | solution.py:337
  45.0 0.5 four_inner_0.1.refs_4_
  45.5 0.5 four_inner_1.1.refs_4_
  46.1 0.5 four_0.1
  46.6 0.7 %collective-permute-done.15.refs_3_ = f32[4,32,128]{2,1,0:T(8,128)S(1)} collective-permute-done((f32[4,32,128]{2,1,0:T(8,128)S(1)}, f32[4,32,128]{2,1,0:T(8,128)S(1)}, u32[]{:S(2)}, u32[]{:S(2)}) %collective-permute-start.15) | collective-permute-done | bytes 65568 | tf_op jit(solution)/shard_map/ppermute | solution.py:337
  47.3 0.5 four_1.1
  47.9 1.2 %collective-permute-done.17 = f32[4,24,128]{2,1,0:T(8,128)S(1)} collective-permute-done((f32[4,24,128]{2,1,0:T(8,128)S(1)}, f32[4,24,128]{2,1,0:T(8,128)S(1)}, u32[]{:S(2)}, u32[]{:S(2)}) %collective-permute-start.17) | collective-permute-done | bytes 49184 | tf_op jit(solution)/shard_map/ppermute | solution.py:331
  49.1 12.2 %all_to_all.5.parts_ref = f32[8,24,128]{2,1,0:T(8,128)S(1)} all-to-all(f32[8,24,128]{2,1,0:T(8,128)S(1)} %maximum_select_fusion), channel_id=1, replica_groups=mesh['wide'=8,'grp'=4] {'wide'}, dimensions={0} | all-to-all | bytes 196608 | tf_op jit(solution)/shard_map/all_to_all | solution.py:390
  61.3 1.5 %finish.1 = f32[8,1,16,128]{3,2,1,0:T(8,128)} custom-call(s32[32,128]{1,0:T(8,128)S(1)} %broadcast_in_dim.12.flags_ref.refs_7_, f32[8,24,128]{2,1,0:T(8,128)S(1)} %all_to_all.5.parts_ref, f32[8,8,8]{2,1,0:T(8,128)S(1)} %copy-done.2), custom_call_target="tpu_custom_call" | custom-call | tf_op jit(solution)/shard_map/finish/pallas_call | solution.py:300
  (46 shorter events, 0.7 us)
Async XLA Ops:
  0.0 3.7 %copy-start = (f32[1,2,5,128,128]{4,3,2,1,0:T(8,128)S(1)}, f32[1,2,5,128,128]{4,3,2,1,0:T(8,128)}, u32[]{:S(2)}) copy-start(f32[1,2,5,128,128]{4,3,2,1,0:T(8,128)} %refs_0_.1) | copy-start | bytes 1966084
  0.0 3.6 %collective-permute-start.1 = (f32[1,2,5,128,128]{4,3,2,1,0:T(8,128)}, f32[1,2,5,128,128]{4,3,2,1,0:T(8,128)S(1)}, u32[]{:S(2)}, u32[]{:S(2)}) collective-permute-start(f32[1,2,5,128,128]{4,3,2,1,0:T(8,128)} %refs_0_.1), channel_id=1, source_target_pairs={{0,1},{1,0},{2,3},{3,2},{4,5},{5,4},{6,7},{7,6},{8,9},{9,8},{10,11... | collective-permute-start | bytes 1966088 | tf_op jit(solution)/shard_map/ppermute | solution.py:331
  0.8 0.8 %copy-start.1 = (f32[64,1,2,128]{3,2,1,0:T(2,128)S(1)}, f32[64,1,2,128]{3,2,1,0:T(2,128)}, u32[]{:S(2)}) copy-start(f32[64,1,2,128]{3,2,1,0:T(2,128)} %slab_ref.1) | copy-start | bytes 196612
  1.6 0.7 %copy-start.3 = (s32[1,2,5]{2,1,0:T(2,128)S(1)}, s32[1,2,5]{2,1,0:T(2,128)}, u32[]{:S(2)}) copy-start(s32[1,2,5]{2,1,0:T(2,128)} %codes_ref.1) | copy-start | bytes 124
  2.4 1.3 %collective-permute-start = (f32[72,128]{1,0:T(8,128)S(1)}, f32[72,128]{1,0:T(8,128)S(1)}, u32[]{:S(2)}, u32[]{:S(2)}) collective-permute-start(f32[72,128]{1,0:T(8,128)S(1)} %get-tuple-element.46), channel_id=1, source_target_pairs={{0,1},{1,0},{2,3},{3,2},{4,5},{5,4},{6,7},{7,6},{8,9},{9,8},{10,11... | collective-permute-start | bytes 110600 | tf_op jit(solution)/shard_map/ppermute | solution.py:331
  3.7 5.3 %collective-permute-start.2 = (f32[2,72,128]{2,1,0:T(8,128)S(1)}, f32[2,72,128]{2,1,0:T(8,128)S(1)}, u32[]{:S(2)}, u32[]{:S(2)}) collective-permute-start(f32[2,72,128]{2,1,0:T(8,128)S(1)} %pad_maximum_fusion), channel_id=1, source_target_pairs={{0,3},{1,2},{2,1},{3,0},{4,7},{5,6},{6,5},{7,4},{8,11},{9,10},{10,... | collective-permute-start | bytes 221192 | tf_op jit(solution)/shard_map/ppermute | solution.py:328
  6.4 9.7 %collective-permute-start.3 = (f32[1,1,5,128,128]{4,3,2,1,0:T(8,128)S(1)}, f32[1,1,5,128,128]{4,3,2,1,0:T(8,128)S(1)}, u32[]{:S(2)}, u32[]{:S(2)}) collective-permute-start(f32[1,1,5,128,128]{4,3,2,1,0:T(8,128)S(1)} %get-tuple-element.23), channel_id=1, source_target_pairs={{0,3},{1,2},{2,1},{3,0},{4,7},{5,6},{6,5},{7,4},{8,11},{9,10},{10,... | collective-permute-start | bytes 983048 | tf_op jit(solution)/shard_map/ppermute | solution.py:328
  9.0 6.2 %collective-permute-start.4 = (f32[4,32,128]{2,1,0:T(8,128)S(1)}, f32[4,32,128]{2,1,0:T(8,128)S(1)}, u32[]{:S(2)}, u32[]{:S(2)}) collective-permute-start(f32[4,32,128]{2,1,0:T(8,128)S(1)} %maximum_select_fusion.1.refs_2_.refs_3_), channel_id=1, source_target_pairs={{4,8},{8,4},{12,16},{16,12},{20,24},{24,20},{5,9},{9,5},{13,17},{1... | collective-permute-start | bytes 196616 | tf_op jit(solution)/shard_map/ppermute | solution.py:334
  9.7 7.3 %collective-permute-start.6 = (f32[4,32,128]{2,1,0:T(8,128)S(1)}, f32[4,32,128]{2,1,0:T(8,128)S(1)}, u32[]{:S(2)}, u32[]{:S(2)}) collective-permute-start(f32[4,32,128]{2,1,0:T(8,128)S(1)} %maximum_select_fusion.2.refs_3_), channel_id=1, source_target_pairs={{0,4},{4,0},{8,12},{12,8},{16,20},{20,16},{24,28},{28,24},{1,5},{5... | collective-permute-start | bytes 196616 | tf_op jit(solution)/shard_map/ppermute | solution.py:337
  16.1 2.4 %collective-permute-start.5 = (f32[1,1,5,128,128]{4,3,2,1,0:T(8,128)S(1)}, f32[1,1,5,128,128]{4,3,2,1,0:T(8,128)S(1)}, u32[]{:S(2)}, u32[]{:S(2)}) collective-permute-start(f32[1,1,5,128,128]{4,3,2,1,0:T(8,128)S(1)} %collective-permute-done.3.refs_0_), channel_id=1, source_target_pairs={{0,1},{1,0},{2,3},{3,2},{4,5},{5,4},{6,7},{7,6},{8,9},{9,8},{10,11... | collective-permute-start | bytes 983048 | tf_op jit(solution)/shard_map/ppermute | solution.py:331
  17.1 10.1 %collective-permute-start.7 = (f32[1,1,5,128,128]{4,3,2,1,0:T(8,128)S(1)}, f32[1,1,5,128,128]{4,3,2,1,0:T(8,128)S(1)}, u32[]{:S(2)}, u32[]{:S(2)}) collective-permute-start(f32[1,1,5,128,128]{4,3,2,1,0:T(8,128)S(1)} %get-tuple-element.27), channel_id=1, source_target_pairs={{0,3},{1,2},{2,1},{3,0},{4,7},{5,6},{6,5},{7,4},{8,11},{9,10},{10,... | collective-permute-start | bytes 983048 | tf_op jit(solution)/shard_map/ppermute | solution.py:328
  19.8 7.3 %collective-permute-start.8 = (f32[3,32,128]{2,1,0:T(8,128)S(1)}, f32[3,32,128]{2,1,0:T(8,128)S(1)}, u32[]{:S(2)}, u32[]{:S(2)}) collective-permute-start(f32[3,32,128]{2,1,0:T(8,128)S(1)} %one_0.1.refs_1_), channel_id=1, source_target_pairs={{4,8},{8,4},{12,16},{16,12},{20,24},{24,20},{5,9},{9,5},{13,17},{1... | collective-permute-start | bytes 147464 | tf_op jit(solution)/shard_map/ppermute | solution.py:334
  21.1 7.7 %collective-permute-start.11 = (f32[3,32,128]{2,1,0:T(8,128)S(1)}, f32[3,32,128]{2,1,0:T(8,128)S(1)}, u32[]{:S(2)}, u32[]{:S(2)}) collective-permute-start(f32[3,32,128]{2,1,0:T(8,128)S(1)} %one_1.1.refs_2_), channel_id=1, source_target_pairs={{0,4},{4,0},{8,12},{12,8},{16,20},{20,16},{24,28},{28,24},{1,5},{5... | collective-permute-start | bytes 147464 | tf_op jit(solution)/shard_map/ppermute | solution.py:337
  27.4 4.1 %collective-permute-start.9 = (f32[3,32,128]{2,1,0:T(8,128)S(1)}, f32[3,32,128]{2,1,0:T(8,128)S(1)}, u32[]{:S(2)}, u32[]{:S(2)}) collective-permute-start(f32[3,32,128]{2,1,0:T(8,128)S(1)} %pad_maximum_fusion.5), channel_id=1, source_target_pairs={{0,3},{1,2},{2,1},{3,0},{4,7},{5,6},{6,5},{7,4},{8,11},{9,10},{10,... | collective-permute-start | bytes 147464 | tf_op jit(solution)/shard_map/ppermute | solution.py:328
  29.1 3.8 %collective-permute-start.12 = (f32[3,32,128]{2,1,0:T(8,128)S(1)}, f32[3,32,128]{2,1,0:T(8,128)S(1)}, u32[]{:S(2)}, u32[]{:S(2)}) collective-permute-start(f32[3,32,128]{2,1,0:T(8,128)S(1)} %pad_maximum_fusion.6), channel_id=1, source_target_pairs={{0,3},{1,2},{2,1},{3,0},{4,7},{5,6},{6,5},{7,4},{8,11},{9,10},{10,... | collective-permute-start | bytes 147464 | tf_op jit(solution)/shard_map/ppermute | solution.py:328
  31.5 6.8 %collective-permute-start.14 = (f32[4,32,128]{2,1,0:T(8,128)S(1)}, f32[4,32,128]{2,1,0:T(8,128)S(1)}, u32[]{:S(2)}, u32[]{:S(2)}) collective-permute-start(f32[4,32,128]{2,1,0:T(8,128)S(1)} %pad_maximum_fusion.1.refs_3_.refs_5_), channel_id=1, source_target_pairs={{4,8},{8,4},{12,16},{16,12},{20,24},{24,20},{5,9},{9,5},{13,17},{1... | collective-permute-start | bytes 196616 | tf_op jit(solution)/shard_map/ppermute | solution.py:334
  32.2 4.8 %collective-permute-start.10 = (f32[1,1,5,128,128]{4,3,2,1,0:T(8,128)S(1)}, f32[1,1,5,128,128]{4,3,2,1,0:T(8,128)S(1)}, u32[]{:S(2)}, u32[]{:S(2)}) collective-permute-start(f32[1,1,5,128,128]{4,3,2,1,0:T(8,128)S(1)} %collective-permute-done.7.refs_0_), channel_id=1, source_target_pairs={{0,1},{1,0},{2,3},{3,2},{4,5},{5,4},{6,7},{7,6},{8,9},{9,8},{10,11... | collective-permute-start | bytes 983048 | tf_op jit(solution)/shard_map/ppermute | solution.py:331
  32.9 6.8 %collective-permute-start.13 = (f32[4,32,128]{2,1,0:T(8,128)S(1)}, f32[4,32,128]{2,1,0:T(8,128)S(1)}, u32[]{:S(2)}, u32[]{:S(2)}) collective-permute-start(f32[4,32,128]{2,1,0:T(8,128)S(1)} %pad_maximum_fusion.2.refs_4_.refs_5_), channel_id=1, source_target_pairs={{0,4},{4,0},{8,12},{12,8},{16,20},{20,16},{24,28},{28,24},{1,5},{5... | collective-permute-start | bytes 196616 | tf_op jit(solution)/shard_map/ppermute | solution.py:337
  38.6 7.5 %collective-permute-start.16 = (f32[4,32,128]{2,1,0:T(8,128)S(1)}, f32[4,32,128]{2,1,0:T(8,128)S(1)}, u32[]{:S(2)}, u32[]{:S(2)}) collective-permute-start(f32[4,32,128]{2,1,0:T(8,128)S(1)} %three_0.1.refs_3_), channel_id=1, source_target_pairs={{4,8},{8,4},{12,16},{16,12},{20,24},{24,20},{5,9},{9,5},{13,17},{1... | collective-permute-start | bytes 196616 | tf_op jit(solution)/shard_map/ppermute | solution.py:334
  40.4 6.8 %collective-permute-start.15 = (f32[4,32,128]{2,1,0:T(8,128)S(1)}, f32[4,32,128]{2,1,0:T(8,128)S(1)}, u32[]{:S(2)}, u32[]{:S(2)}) collective-permute-start(f32[4,32,128]{2,1,0:T(8,128)S(1)} %three_1.1.refs_4_), channel_id=1, source_target_pairs={{0,4},{4,0},{8,12},{12,8},{16,20},{20,16},{24,28},{28,24},{1,5},{5... | collective-permute-start | bytes 196616 | tf_op jit(solution)/shard_map/ppermute | solution.py:337
  47.2 14.1 %copy-start.2 = (f32[8,8,8]{2,1,0:T(8,128)S(1)}, f32[8,8,8]{2,1,0:T(8,128)}, u32[]{:S(2)}) copy-start(f32[8,8,8]{2,1,0:T(8,128)} %rot_ref.1) | copy-start | bytes 6148
  47.8 1.3 %collective-permute-start.17 = (f32[4,24,128]{2,1,0:T(8,128)S(1)}, f32[4,24,128]{2,1,0:T(8,128)S(1)}, u32[]{:S(2)}, u32[]{:S(2)}) collective-permute-start(f32[4,24,128]{2,1,0:T(8,128)S(1)} %get-tuple-element.35), channel_id=1, source_target_pairs={{0,1},{1,0},{2,3},{3,2},{4,5},{5,4},{6,7},{7,6},{8,9},{9,8},{10,11... | collective-permute-start | bytes 147464 | tf_op jit(solution)/shard_map/ppermute | solution.py:331

commit v10 on v7

--- a/solution.py
+++ b/solution.py
@@ -365,14 +365,12 @@
     one.append(step("first", 1, "one_1", h_three, *zero, rim))
     rims = over_far(one[0]), over_near(one[1])
     acc = [inner(u, f"two_inner_{u}", h_two, one, zero[u]) for u in range(cols)]
-    two, sent, before = [], (), []
-    for u in range(cols):
-        rim = after(rims[u], (sent, inside))
-        two.append(step("next", u, f"two_{u}", h_two, rim, acc[u]))
-        sent = jnp.concatenate([two[u], one[u][:1]])
-        other = across(sent)
-        two[u] = jnp.concatenate([two[u], other[1:2], other[0:1]])
-        before.append(jnp.concatenate([one[u], other[2:]]))
+    two = [step("next", 0, "two_0", h_two, rims[0], after(acc[0], inside))]
+    rim = after(rims[1], (two[0], inside))
+    two.append(step("next", 1, "two_1", h_two, rim, acc[1]))
+    other = across(two[0]), across(jnp.concatenate([two[1], one[0][:1], one[1][:1]]))
+    two = [jnp.concatenate([two[u], other[u][1:2], other[u][0:1]]) for u in range(cols)]
+    before = [jnp.concatenate([one[u], other[1][2 + u : 3 + u]]) for u in range(cols)]
     inside_core = core(after(inside, two[0]))
     h_four = h_three + [prepare("inner", codes, inside, inside_core)]
     rims = over_far(two[0]), over_near(two[1])

time: 60.8 us -> 60.8 us (level)
  starting transfers between devices: 28.4 us -> 27.6 us
  waiting for transfers between devices: 9.83 us -> 10.6 us
    ppermute x5, waiting for transfers between devices: 5.78 us -> 6.56 us  [across(): return lax.ppermute(value, 'grp', [(i, i ^ 3) for i in range(grp)])]
    ppermute x4, starting transfers between devices: 18.4 us -> 17.7 us  [over_near(): return lax.ppermute(value, 'wide', near)]
where the time goes in v10:
time: 60.8 us; the launch traced here: 60.5 us
  starting transfers between devices  27.6 us (45%)
  waiting for transfers between devices  10.6 us (17%)
  blocking collectives  9.94 us (16%)
  Pallas kernels  9.93 us (16%)
  local copies, waits for them, and re-layouts  1.98 us (3%)
    ppermute x4, starting transfers between devices, over_near(): return lax.ppermute(value, 'wide', near)  17.7 us
    all_to_all x1, blocking collectives, body(): lax.all_to_all(packed, ('wide', 'grp'), split_axis=0, concat_axis=0, tile...  9.94 us
    ppermute x5, waiting for transfers between devices, across(): return lax.ppermute(value, 'grp', [(i, i ^ 3) for i in range(grp)])  6.56 us
    ppermute x5, starting transfers between devices, across(): return lax.ppermute(value, 'grp', [(i, i ^ 3) for i in range(grp)])  6.06 us
    pallas_call x8, Pallas kernels, step(): pl.pallas_call(functools.partial(step_kernel, kind, u, len(h_ready)), in_...  3.69 us
    ppermute x4, starting transfers between devices, over_far(): return lax.ppermute(value, 'wide', far)  2.66 us
    ppermute x5, waiting for transfers between devices, core(): return lax.ppermute(value, 'grp', [(i, i ^ 1) for i in range(grp)])  2.38 us
    pallas_call x3, Pallas kernels, prepare(): pl.pallas_call(functools.partial(prepare_kernel, mode), in_specs=[SMEM] +...  2.37 us
  transfers between devices with their start and end apart: 18, of which 9 were waited for; matrix products, arithmetic and copies ran while one was open for 1% of the time, Pallas kernels for 13%

profile of v10, /device:TPU:0, one launch (start us, length us, event | category | flops | bytes accessed | tf_op | source)
XLA Modules:
  0.0 60.5 jit_solution(12250600820429513752)
XLA Ops:
  0.0 0.5 collective-permute-start.1
  0.6 0.1 broadcast_in_dim.11
  0.8 0.8 %copy-done.1 = f32[64,1,2,128]{3,2,1,0:T(2,128)S(1)} copy-done((f32[64,1,2,128]{3,2,1,0:T(2,128)S(1)}, f32[64,1,2,128]{3,2,1,0:T(2,128)}, u32[]{:S(2)}) %copy-start.1) | copy-done | bytes 65560
  1.6 0.7 %copy-done.3 = s32[1,2,5]{2,1,0:T(2,128)S(1)} copy-done((s32[1,2,5]{2,1,0:T(2,128)S(1)}, s32[1,2,5]{2,1,0:T(2,128)}, u32[]{:S(2)}) %copy-start.3) | copy-done | bytes 64
  2.4 0.1 collective-permute-start
  2.5 1.1 %collective-permute-done = f32[72,128]{1,0:T(8,128)S(1)} collective-permute-done((f32[72,128]{1,0:T(8,128)S(1)}, f32[72,128]{1,0:T(8,128)S(1)}, u32[]{:S(2)}, u32[]{:S(2)}) %collective-permute-start) | collective-permute-done | bytes 36896 | tf_op jit(solution)/shard_map/ppermute | solution.py:331
  3.7 2.7 %collective-permute-start.2 = (f32[2,72,128]{2,1,0:T(8,128)S(1)}, f32[2,72,128]{2,1,0:T(8,128)S(1)}, u32[]{:S(2)}, u32[]{:S(2)}) collective-permute-start(f32[2,72,128]{2,1,0:T(8,128)S(1)} %pad_maximum_fusion.2), channel_id=1, source_target_pairs={{0,3},{1,2},{2,1},{3,0},{4,7},{5,6},{6,5},{7,4},{8,11},{9,10},{10,... | collective-permute-start | bytes 221192 | tf_op jit(solution)/shard_map/ppermute | solution.py:328
  6.4 0.1 collective-permute-start.3
  6.5 2.5 %collective-permute-done.2 = f32[2,72,128]{2,1,0:T(8,128)S(1)} collective-permute-done((f32[2,72,128]{2,1,0:T(8,128)S(1)}, f32[2,72,128]{2,1,0:T(8,128)S(1)}, u32[]{:S(2)}, u32[]{:S(2)}) %collective-permute-start.2) | collective-permute-done | bytes 73760 | tf_op jit(solution)/shard_map/ppermute | solution.py:328
  9.0 0.7 %collective-permute-start.4 = (f32[4,32,128]{2,1,0:T(8,128)S(1)}, f32[4,32,128]{2,1,0:T(8,128)S(1)}, u32[]{:S(2)}, u32[]{:S(2)}) collective-permute-start(f32[4,32,128]{2,1,0:T(8,128)S(1)} %maximum_select_fusion.1.refs_2_.refs_3_), channel_id=1, source_target_pairs={{4,8},{8,4},{12,16},{16,12},{20,24},{24,20},{5,9},{9,5},{13,17},{1... | collective-permute-start | bytes 196616 | tf_op jit(solution)/shard_map/ppermute | solution.py:334
  9.7 4.4 %collective-permute-start.6 = (f32[4,32,128]{2,1,0:T(8,128)S(1)}, f32[4,32,128]{2,1,0:T(8,128)S(1)}, u32[]{:S(2)}, u32[]{:S(2)}) collective-permute-start(f32[4,32,128]{2,1,0:T(8,128)S(1)} %maximum_select_fusion.2.refs_3_), channel_id=1, source_target_pairs={{0,4},{4,0},{8,12},{12,8},{16,20},{20,16},{24,28},{28,24},{1,5},{5... | collective-permute-start | bytes 196616 | tf_op jit(solution)/shard_map/ppermute | solution.py:337
  14.3 0.1 concatenate.24.codes_ref
  14.3 0.9 %prepare_chip.1.refs_0_ = bf16[2,2,256,1152]{3,2,1,0:T(8,128)(2,1)S(1)} custom-call(s32[44]{0:T(128)S(1)} %concatenate.24.codes_ref, f32[1,2,5,128,128]{4,3,2,1,0:T(8,128)S(1)} %copy-done, f32[1,2,5,128,128]{4,3,2,1,0:T(8,128)S(1)} %collective-permute-done.1.core_ref.refs_1_), custom_call_target="tpu_custom_call" | custom-call | tf_op jit(solution)/shard_map/prepare_chip/pallas_call | solution.py:114
  15.3 0.8 %collective-permute-done.3.refs_0_ = f32[1,1,5,128,128]{4,3,2,1,0:T(8,128)S(1)} collective-permute-done((f32[1,1,5,128,128]{4,3,2,1,0:T(8,128)S(1)}, f32[1,1,5,128,128]{4,3,2,1,0:T(8,128)S(1)}, u32[]{:S(2)}, u32[]{:S(2)}) %collective-permute-start.3) | collective-permute-done | bytes 327712 | tf_op jit(solution)/shard_map/ppermute | solution.py:328
  16.1 0.5 collective-permute-start.5
  16.5 0.5 collective-permute-done.6.refs_4_
  17.1 1.4 %collective-permute-start.7 = (f32[1,1,5,128,128]{4,3,2,1,0:T(8,128)S(1)}, f32[1,1,5,128,128]{4,3,2,1,0:T(8,128)S(1)}, u32[]{:S(2)}, u32[]{:S(2)}) collective-permute-start(f32[1,1,5,128,128]{4,3,2,1,0:T(8,128)S(1)} %get-tuple-element.27), channel_id=1, source_target_pairs={{0,3},{1,2},{2,1},{3,0},{4,7},{5,6},{6,5},{7,4},{8,11},{9,10},{10,... | collective-permute-start | bytes 983048 | tf_op jit(solution)/shard_map/ppermute | solution.py:328
  18.5 0.7 %prepare_border.1.refs_1_ = bf16[1,2,256,1152]{3,2,1,0:T(8,128)(2,1)S(1)} custom-call(s32[44]{0:T(128)S(1)} %concatenate.24.codes_ref, f32[1,1,5,128,128]{4,3,2,1,0:T(8,128)S(1)} %collective-permute-done.3.refs_0_, f32[1,1,5,128,128]{4,3,2,1,0:T(8,128)S(1)} %collective-permute-done.5.refs_1_), custom_call_target="tpu_custom_call" | custom-call | tf_op jit(solution)/shard_map/prepare_border/pallas_call | solution.py:114
  19.2 0.6 one_0.1.refs_1_
  19.8 0.7 %collective-permute-start.8 = (f32[3,32,128]{2,1,0:T(8,128)S(1)}, f32[3,32,128]{2,1,0:T(8,128)S(1)}, u32[]{:S(2)}, u32[]{:S(2)}) collective-permute-start(f32[3,32,128]{2,1,0:T(8,128)S(1)} %one_0.1.refs_1_), channel_id=1, source_target_pairs={{4,8},{8,4},{12,16},{16,12},{20,24},{24,20},{5,9},{9,5},{13,17},{1... | collective-permute-start | bytes 147464 | tf_op jit(solution)/shard_map/ppermute | solution.py:334
  20.5 0.6 one_1.1.refs_2_
  21.1 5.3 %collective-permute-start.11 = (f32[3,32,128]{2,1,0:T(8,128)S(1)}, f32[3,32,128]{2,1,0:T(8,128)S(1)}, u32[]{:S(2)}, u32[]{:S(2)}) collective-permute-start(f32[3,32,128]{2,1,0:T(8,128)S(1)} %one_1.1.refs_2_), channel_id=1, source_target_pairs={{0,4},{4,0},{8,12},{12,8},{16,20},{20,16},{24,28},{28,24},{1,5},{5... | collective-permute-start | bytes 147464 | tf_op jit(solution)/shard_map/ppermute | solution.py:337
  26.4 0.4 two_inner_0.1.refs_2_
  26.8 0.3 two_inner_1.1.refs_2_
  27.2 0.2 two_0.1
  27.4 1.8 %collective-permute-start.9 = (f32[2,32,128]{2,1,0:T(8,128)S(1)}, f32[2,32,128]{2,1,0:T(8,128)S(1)}, u32[]{:S(2)}, u32[]{:S(2)}) collective-permute-start(f32[2,32,128]{2,1,0:T(8,128)S(1)} %two_0.1), channel_id=1, source_target_pairs={{0,3},{1,2},{2,1},{3,0},{4,7},{5,6},{6,5},{7,4},{8,11},{9,10},{10,... | collective-permute-start | bytes 98312 | tf_op jit(solution)/shard_map/ppermute | solution.py:328
  29.2 0.2 two_1.1
  29.5 0.1 collective-permute-start.12
  29.5 1.4 %collective-permute-done.9 = f32[2,32,128]{2,1,0:T(8,128)S(1)} collective-permute-done((f32[2,32,128]{2,1,0:T(8,128)S(1)}, f32[2,32,128]{2,1,0:T(8,128)S(1)}, u32[]{:S(2)}, u32[]{:S(2)}) %collective-permute-start.9) | collective-permute-done | bytes 32800 | tf_op jit(solution)/shard_map/ppermute | solution.py:328
  30.9 0.7 %collective-permute-start.14 = (f32[4,32,128]{2,1,0:T(8,128)S(1)}, f32[4,32,128]{2,1,0:T(8,128)S(1)}, u32[]{:S(2)}, u32[]{:S(2)}) collective-permute-start(f32[4,32,128]{2,1,0:T(8,128)S(1)} %pad_maximum_fusion.3.refs_3_.refs_5_), channel_id=1, source_target_pairs={{4,8},{8,4},{12,16},{16,12},{20,24},{24,20},{5,9},{9,5},{13,17},{1... | collective-permute-start | bytes 196616 | tf_op jit(solution)/shard_map/ppermute | solution.py:334
  31.6 0.1 collective-permute-start.10
  31.7 1.9 %collective-permute-done.12 = f32[4,32,128]{2,1,0:T(8,128)S(1)} collective-permute-done((f32[4,32,128]{2,1,0:T(8,128)S(1)}, f32[4,32,128]{2,1,0:T(8,128)S(1)}, u32[]{:S(2)}, u32[]{:S(2)}) %collective-permute-start.12) | collective-permute-done | bytes 65568 | tf_op jit(solution)/shard_map/ppermute | solution.py:328
  33.6 3.3 %collective-permute-start.13 = (f32[4,32,128]{2,1,0:T(8,128)S(1)}, f32[4,32,128]{2,1,0:T(8,128)S(1)}, u32[]{:S(2)}, u32[]{:S(2)}) collective-permute-start(f32[4,32,128]{2,1,0:T(8,128)S(1)} %fusion.refs_4_.refs_5_), channel_id=1, source_target_pairs={{0,4},{4,0},{8,12},{12,8},{16,20},{20,16},{24,28},{28,24},{1,5},{5... | collective-permute-start | bytes 196616 | tf_op jit(solution)/shard_map/ppermute | solution.py:337
  37.0 0.7 %prepare_inner.1.refs_2_ = bf16[1,2,256,1152]{3,2,1,0:T(8,128)(2,1)S(1)} custom-call(s32[44]{0:T(128)S(1)} %concatenate.24.codes_ref, f32[1,1,5,128,128]{4,3,2,1,0:T(8,128)S(1)} %collective-permute-done.7.refs_0_, f32[1,1,5,128,128]{4,3,2,1,0:T(8,128)S(1)} %collective-permute-done.10.refs_1_), custom_call_target="tpu_custom_call" | custom-call | tf_op jit(solution)/shard_map/prepare_inner/pallas_call | solution.py:114
  37.7 0.5 three_inner_0.1.refs_4_
  38.3 0.3 three_0.1.refs_3_
  38.6 0.7 %collective-permute-start.16 = (f32[4,32,128]{2,1,0:T(8,128)S(1)}, f32[4,32,128]{2,1,0:T(8,128)S(1)}, u32[]{:S(2)}, u32[]{:S(2)}) collective-permute-start(f32[4,32,128]{2,1,0:T(8,128)S(1)} %three_0.1.refs_3_), channel_id=1, source_target_pairs={{4,8},{8,4},{12,16},{16,12},{20,24},{24,20},{5,9},{9,5},{13,17},{1... | collective-permute-start | bytes 196616 | tf_op jit(solution)/shard_map/ppermute | solution.py:334
  39.2 0.4 collective-permute-done.13.refs_5_
  39.7 0.7 %three_1.1.refs_4_ = f32[4,32,128]{2,1,0:T(8,128)S(1)} custom-call(bf16[2,2,256,1152]{3,2,1,0:T(8,128)(2,1)S(1)} %prepare_chip.1.refs_0_, bf16[1,2,256,1152]{3,2,1,0:T(8,128)(2,1)S(1)} %prepare_border.1.refs_1_, bf16[1,2,256,1152]{3,2,1,0:T(8,128)(2,1)S(1)} %prepare_inner.1.refs_2_, f32[4,32,128]{2,1,0:T(8,128)S(1)} %pad_maximum_fusion.3.refs_3_.refs_5_, ...), custom_call_target="tpu_custom_call" | custom-call | flops 150994944 | bytes 2359296 | tf_op jit(solution)/shard_map/three_1/pallas_call | solution.py:244
  40.4 4.6 %collective-permute-start.15 = (f32[4,32,128]{2,1,0:T(8,128)S(1)}, f32[4,32,128]{2,1,0:T(8,128)S(1)}, u32[]{:S(2)}, u32[]{:S(2)}) collective-permute-start(f32[4,32,128]{2,1,0:T(8,128)S(1)} %three_1.1.refs_4_), channel_id=1, source_target_pairs={{0,4},{4,0},{8,12},{12,8},{16,20},{20,16},{24,28},{28,24},{1,5},{5... | collective-permute-start | bytes 196616 | tf_op jit(solution)/shard_map/ppermute | solution.py:337
  45.0 0.5 four_inner_0.1.refs_4_
  45.5 0.5 four_inner_1.1.refs_4_
  46.1 0.5 four_0.1
  46.5 0.7 %collective-permute-done.15.refs_3_ = f32[4,32,128]{2,1,0:T(8,128)S(1)} collective-permute-done((f32[4,32,128]{2,1,0:T(8,128)S(1)}, f32[4,32,128]{2,1,0:T(8,128)S(1)}, u32[]{:S(2)}, u32[]{:S(2)}) %collective-permute-start.15) | collective-permute-done | bytes 65568 | tf_op jit(solution)/shard_map/ppermute | solution.py:337
  47.2 0.5 four_1.1
  47.9 1.2 %collective-permute-done.17 = f32[4,24,128]{2,1,0:T(8,128)S(1)} collective-permute-done((f32[4,24,128]{2,1,0:T(8,128)S(1)}, f32[4,24,128]{2,1,0:T(8,128)S(1)}, u32[]{:S(2)}, u32[]{:S(2)}) %collective-permute-start.17) | collective-permute-done | bytes 49184 | tf_op jit(solution)/shard_map/ppermute | solution.py:331
  49.1 9.9 %all_to_all.5.parts_ref = f32[8,24,128]{2,1,0:T(8,128)S(1)} all-to-all(f32[8,24,128]{2,1,0:T(8,128)S(1)} %maximum_select_fusion), channel_id=1, replica_groups={{28,24,20,16,12,8,4,0},{29,25,21,17,13,9,5,1},{30,26,22,18,14,10,6,2},{..., dimensions={0} | all-to-all | bytes 196608 | tf_op jit(solution)/shard_map/all_to_all | solution.py:389
  59.0 1.5 %finish.1 = f32[8,1,16,128]{3,2,1,0:T(8,128)} custom-call(s32[32,128]{1,0:T(8,128)S(1)} %broadcast_in_dim.12.flags_ref.refs_7_, f32[8,24,128]{2,1,0:T(8,128)S(1)} %all_to_all.5.parts_ref, f32[8,8,8]{2,1,0:T(8,128)S(1)} %copy-done.2), custom_call_target="tpu_custom_call" | custom-call | tf_op jit(solution)/shard_map/finish/pallas_call | solution.py:300
  (45 shorter events, 0.7 us)
Async XLA Ops:
  0.0 3.7 %copy-start = (f32[1,2,5,128,128]{4,3,2,1,0:T(8,128)S(1)}, f32[1,2,5,128,128]{4,3,2,1,0:T(8,128)}, u32[]{:S(2)}) copy-start(f32[1,2,5,128,128]{4,3,2,1,0:T(8,128)} %refs_0_.1) | copy-start | bytes 1966084
  0.0 3.6 %collective-permute-start.1 = (f32[1,2,5,128,128]{4,3,2,1,0:T(8,128)}, f32[1,2,5,128,128]{4,3,2,1,0:T(8,128)S(1)}, u32[]{:S(2)}, u32[]{:S(2)}) collective-permute-start(f32[1,2,5,128,128]{4,3,2,1,0:T(8,128)} %refs_0_.1), channel_id=1, source_target_pairs={{0,1},{1,0},{2,3},{3,2},{4,5},{5,4},{6,7},{7,6},{8,9},{9,8},{10,11... | collective-permute-start | bytes 1966088 | tf_op jit(solution)/shard_map/ppermute | solution.py:331
  0.8 0.8 %copy-start.1 = (f32[64,1,2,128]{3,2,1,0:T(2,128)S(1)}, f32[64,1,2,128]{3,2,1,0:T(2,128)}, u32[]{:S(2)}) copy-start(f32[64,1,2,128]{3,2,1,0:T(2,128)} %slab_ref.1) | copy-start | bytes 196612
  1.6 0.7 %copy-start.3 = (s32[1,2,5]{2,1,0:T(2,128)S(1)}, s32[1,2,5]{2,1,0:T(2,128)}, u32[]{:S(2)}) copy-start(s32[1,2,5]{2,1,0:T(2,128)} %codes_ref.1) | copy-start | bytes 124
  2.4 1.3 %collective-permute-start = (f32[72,128]{1,0:T(8,128)S(1)}, f32[72,128]{1,0:T(8,128)S(1)}, u32[]{:S(2)}, u32[]{:S(2)}) collective-permute-start(f32[72,128]{1,0:T(8,128)S(1)} %get-tuple-element.46), channel_id=1, source_target_pairs={{0,1},{1,0},{2,3},{3,2},{4,5},{5,4},{6,7},{7,6},{8,9},{9,8},{10,11... | collective-permute-start | bytes 110600 | tf_op jit(solution)/shard_map/ppermute | solution.py:331
  3.7 5.3 %collective-permute-start.2 = (f32[2,72,128]{2,1,0:T(8,128)S(1)}, f32[2,72,128]{2,1,0:T(8,128)S(1)}, u32[]{:S(2)}, u32[]{:S(2)}) collective-permute-start(f32[2,72,128]{2,1,0:T(8,128)S(1)} %pad_maximum_fusion.2), channel_id=1, source_target_pairs={{0,3},{1,2},{2,1},{3,0},{4,7},{5,6},{6,5},{7,4},{8,11},{9,10},{10,... | collective-permute-start | bytes 221192 | tf_op jit(solution)/shard_map/ppermute | solution.py:328
  6.4 9.7 %collective-permute-start.3 = (f32[1,1,5,128,128]{4,3,2,1,0:T(8,128)S(1)}, f32[1,1,5,128,128]{4,3,2,1,0:T(8,128)S(1)}, u32[]{:S(2)}, u32[]{:S(2)}) collective-permute-start(f32[1,1,5,128,128]{4,3,2,1,0:T(8,128)S(1)} %get-tuple-element.23), channel_id=1, source_target_pairs={{0,3},{1,2},{2,1},{3,0},{4,7},{5,6},{6,5},{7,4},{8,11},{9,10},{10,... | collective-permute-start | bytes 983048 | tf_op jit(solution)/shard_map/ppermute | solution.py:328
  9.0 6.2 %collective-permute-start.4 = (f32[4,32,128]{2,1,0:T(8,128)S(1)}, f32[4,32,128]{2,1,0:T(8,128)S(1)}, u32[]{:S(2)}, u32[]{:S(2)}) collective-permute-start(f32[4,32,128]{2,1,0:T(8,128)S(1)} %maximum_select_fusion.1.refs_2_.refs_3_), channel_id=1, source_target_pairs={{4,8},{8,4},{12,16},{16,12},{20,24},{24,20},{5,9},{9,5},{13,17},{1... | collective-permute-start | bytes 196616 | tf_op jit(solution)/shard_map/ppermute | solution.py:334
  9.7 7.3 %collective-permute-start.6 = (f32[4,32,128]{2,1,0:T(8,128)S(1)}, f32[4,32,128]{2,1,0:T(8,128)S(1)}, u32[]{:S(2)}, u32[]{:S(2)}) collective-permute-start(f32[4,32,128]{2,1,0:T(8,128)S(1)} %maximum_select_fusion.2.refs_3_), channel_id=1, source_target_pairs={{0,4},{4,0},{8,12},{12,8},{16,20},{20,16},{24,28},{28,24},{1,5},{5... | collective-permute-start | bytes 196616 | tf_op jit(solution)/shard_map/ppermute | solution.py:337
  16.1 2.4 %collective-permute-start.5 = (f32[1,1,5,128,128]{4,3,2,1,0:T(8,128)S(1)}, f32[1,1,5,128,128]{4,3,2,1,0:T(8,128)S(1)}, u32[]{:S(2)}, u32[]{:S(2)}) collective-permute-start(f32[1,1,5,128,128]{4,3,2,1,0:T(8,128)S(1)} %collective-permute-done.3.refs_0_), channel_id=1, source_target_pairs={{0,1},{1,0},{2,3},{3,2},{4,5},{5,4},{6,7},{7,6},{8,9},{9,8},{10,11... | collective-permute-start | bytes 983048 | tf_op jit(solution)/shard_map/ppermute | solution.py:331
  17.1 9.7 %collective-permute-start.7 = (f32[1,1,5,128,128]{4,3,2,1,0:T(8,128)S(1)}, f32[1,1,5,128,128]{4,3,2,1,0:T(8,128)S(1)}, u32[]{:S(2)}, u32[]{:S(2)}) collective-permute-start(f32[1,1,5,128,128]{4,3,2,1,0:T(8,128)S(1)} %get-tuple-element.27), channel_id=1, source_target_pairs={{0,3},{1,2},{2,1},{3,0},{4,7},{5,6},{6,5},{7,4},{8,11},{9,10},{10,... | collective-permute-start | bytes 983048 | tf_op jit(solution)/shard_map/ppermute | solution.py:328
  19.8 7.3 %collective-permute-start.8 = (f32[3,32,128]{2,1,0:T(8,128)S(1)}, f32[3,32,128]{2,1,0:T(8,128)S(1)}, u32[]{:S(2)}, u32[]{:S(2)}) collective-permute-start(f32[3,32,128]{2,1,0:T(8,128)S(1)} %one_0.1.refs_1_), channel_id=1, source_target_pairs={{4,8},{8,4},{12,16},{16,12},{20,24},{24,20},{5,9},{9,5},{13,17},{1... | collective-permute-start | bytes 147464 | tf_op jit(solution)/shard_map/ppermute | solution.py:334
  21.1 8.1 %collective-permute-start.11 = (f32[3,32,128]{2,1,0:T(8,128)S(1)}, f32[3,32,128]{2,1,0:T(8,128)S(1)}, u32[]{:S(2)}, u32[]{:S(2)}) collective-permute-start(f32[3,32,128]{2,1,0:T(8,128)S(1)} %one_1.1.refs_2_), channel_id=1, source_target_pairs={{0,4},{4,0},{8,12},{12,8},{16,20},{20,16},{24,28},{28,24},{1,5},{5... | collective-permute-start | bytes 147464 | tf_op jit(solution)/shard_map/ppermute | solution.py:337
  27.4 3.5 %collective-permute-start.9 = (f32[2,32,128]{2,1,0:T(8,128)S(1)}, f32[2,32,128]{2,1,0:T(8,128)S(1)}, u32[]{:S(2)}, u32[]{:S(2)}) collective-permute-start(f32[2,32,128]{2,1,0:T(8,128)S(1)} %two_0.1), channel_id=1, source_target_pairs={{0,3},{1,2},{2,1},{3,0},{4,7},{5,6},{6,5},{7,4},{8,11},{9,10},{10,... | collective-permute-start | bytes 98312 | tf_op jit(solution)/shard_map/ppermute | solution.py:328
  29.5 4.1 %collective-permute-start.12 = (f32[4,32,128]{2,1,0:T(8,128)S(1)}, f32[4,32,128]{2,1,0:T(8,128)S(1)}, u32[]{:S(2)}, u32[]{:S(2)}) collective-permute-start(f32[4,32,128]{2,1,0:T(8,128)S(1)} %fusion.1), channel_id=1, source_target_pairs={{0,3},{1,2},{2,1},{3,0},{4,7},{5,6},{6,5},{7,4},{8,11},{9,10},{10,... | collective-permute-start | bytes 196616 | tf_op jit(solution)/shard_map/ppermute | solution.py:328
  30.9 7.3 %collective-permute-start.14 = (f32[4,32,128]{2,1,0:T(8,128)S(1)}, f32[4,32,128]{2,1,0:T(8,128)S(1)}, u32[]{:S(2)}, u32[]{:S(2)}) collective-permute-start(f32[4,32,128]{2,1,0:T(8,128)S(1)} %pad_maximum_fusion.3.refs_3_.refs_5_), channel_id=1, source_target_pairs={{4,8},{8,4},{12,16},{16,12},{20,24},{24,20},{5,9},{9,5},{13,17},{1... | collective-permute-start | bytes 196616 | tf_op jit(solution)/shard_map/ppermute | solution.py:334
  31.6 5.4 %collective-permute-start.10 = (f32[1,1,5,128,128]{4,3,2,1,0:T(8,128)S(1)}, f32[1,1,5,128,128]{4,3,2,1,0:T(8,128)S(1)}, u32[]{:S(2)}, u32[]{:S(2)}) collective-permute-start(f32[1,1,5,128,128]{4,3,2,1,0:T(8,128)S(1)} %collective-permute-done.7.refs_0_), channel_id=1, source_target_pairs={{0,1},{1,0},{2,3},{3,2},{4,5},{5,4},{6,7},{7,6},{8,9},{9,8},{10,11... | collective-permute-start | bytes 983048 | tf_op jit(solution)/shard_map/ppermute | solution.py:331
  33.6 6.1 %collective-permute-start.13 = (f32[4,32,128]{2,1,0:T(8,128)S(1)}, f32[4,32,128]{2,1,0:T(8,128)S(1)}, u32[]{:S(2)}, u32[]{:S(2)}) collective-permute-start(f32[4,32,128]{2,1,0:T(8,128)S(1)} %fusion.refs_4_.refs_5_), channel_id=1, source_target_pairs={{0,4},{4,0},{8,12},{12,8},{16,20},{20,16},{24,28},{28,24},{1,5},{5... | collective-permute-start | bytes 196616 | tf_op jit(solution)/shard_map/ppermute | solution.py:337
  38.6 7.5 %collective-permute-start.16 = (f32[4,32,128]{2,1,0:T(8,128)S(1)}, f32[4,32,128]{2,1,0:T(8,128)S(1)}, u32[]{:S(2)}, u32[]{:S(2)}) collective-permute-start(f32[4,32,128]{2,1,0:T(8,128)S(1)} %three_0.1.refs_3_), channel_id=1, source_target_pairs={{4,8},{8,4},{12,16},{16,12},{20,24},{24,20},{5,9},{9,5},{13,17},{1... | collective-permute-start | bytes 196616 | tf_op jit(solution)/shard_map/ppermute | solution.py:334
  40.4 6.8 %collective-permute-start.15 = (f32[4,32,128]{2,1,0:T(8,128)S(1)}, f32[4,32,128]{2,1,0:T(8,128)S(1)}, u32[]{:S(2)}, u32[]{:S(2)}) collective-permute-start(f32[4,32,128]{2,1,0:T(8,128)S(1)} %three_1.1.refs_4_), channel_id=1, source_target_pairs={{0,4},{4,0},{8,12},{12,8},{16,20},{20,16},{24,28},{28,24},{1,5},{5... | collective-permute-start | bytes 196616 | tf_op jit(solution)/shard_map/ppermute | solution.py:337
  47.2 11.8 %copy-start.2 = (f32[8,8,8]{2,1,0:T(8,128)S(1)}, f32[8,8,8]{2,1,0:T(8,128)}, u32[]{:S(2)}) copy-start(f32[8,8,8]{2,1,0:T(8,128)} %rot_ref.1) | copy-start | bytes 6148
  47.8 1.3 %collective-permute-start.17 = (f32[4,24,128]{2,1,0:T(8,128)S(1)}, f32[4,24,128]{2,1,0:T(8,128)S(1)}, u32[]{:S(2)}, u32[]{:S(2)}) collective-permute-start(f32[4,24,128]{2,1,0:T(8,128)S(1)} %get-tuple-element.36), channel_id=1, source_target_pairs={{0,1},{1,0},{2,3},{3,2},{4,5},{5,4},{6,7},{7,6},{8,9},{9,8},{10,11... | collective-permute-start | bytes 147464 | tf_op jit(solution)/shard_map/ppermute | solution.py:331

commit v11 on v7

--- a/solution.py
+++ b/solution.py
@@ -285,11 +285,10 @@
     mixed = []
     for w in range(wide):
         for c in range(cols):
-            block = parts_ref[w, c * VEC : (c + 1) * VEC, :]
-            total = columns[0] * block[0:1, :]
-            for d in range(1, VEC):
-                total = total + columns[d] * block[d : d + 1, :]
-            mixed.append(total)
+            terms = [columns[d] * parts_ref[w, pl.ds(c * VEC + d, 1), :] for d in range(VEC)]
+            while len(terms) > 1:
+                terms = [low + high for low, high in zip(terms[::2], terms[1::2])]
+            mixed += terms
     for w in range(wide):
         for c in range(cols):
             out_ref[:, 0, w * cols + c, :] = mixed[(wide - 1 - w) * cols + c]

time: 60.8 us -> 60.8 us (level)
  no operation moved by 1% of the time
where the time goes in v11:
time: 60.8 us; the launch traced here: 60.5 us
  starting transfers between devices  28.4 us (47%)
  Pallas kernels  9.94 us (16%)
  blocking collectives  9.93 us (16%)
  waiting for transfers between devices  9.83 us (16%)
  local copies, waits for them, and re-layouts  1.99 us (3%)
    ppermute x4, starting transfers between devices, over_near(): return lax.ppermute(value, 'wide', near)  18.4 us
    all_to_all x1, blocking collectives, body(): lax.all_to_all(packed, ('wide', 'grp'), split_axis=0, concat_axis=0, tile...  9.93 us
    ppermute x5, starting transfers between devices, across(): return lax.ppermute(value, 'grp', [(i, i ^ 3) for i in range(grp)])  6.05 us
    ppermute x5, waiting for transfers between devices, across(): return lax.ppermute(value, 'grp', [(i, i ^ 3) for i in range(grp)])  5.78 us
    pallas_call x8, Pallas kernels, step(): pl.pallas_call(functools.partial(step_kernel, kind, u, len(h_ready)), in_...  3.69 us
    ppermute x4, starting transfers between devices, over_far(): return lax.ppermute(value, 'wide', far)  2.66 us
    ppermute x5, waiting for transfers between devices, core(): return lax.ppermute(value, 'grp', [(i, i ^ 1) for i in range(grp)])  2.38 us
    pallas_call x3, Pallas kernels, prepare(): pl.pallas_call(functools.partial(prepare_kernel, mode), in_specs=[SMEM] +...  2.37 us
  transfers between devices with their start and end apart: 18, of which 9 were waited for; matrix products, arithmetic and copies ran while one was open for 1% of the time, Pallas kernels for 13%

profile of v11, /device:TPU:0, one launch (start us, length us, event | category | flops | bytes accessed | tf_op | source)
XLA Modules:
  0.0 60.5 jit_solution(16032474101793406090)
XLA Ops:
  0.0 0.5 collective-permute-start.1
  0.6 0.1 broadcast_in_dim.11
  0.8 0.8 %copy-done.1 = f32[64,1,2,128]{3,2,1,0:T(2,128)S(1)} copy-done((f32[64,1,2,128]{3,2,1,0:T(2,128)S(1)}, f32[64,1,2,128]{3,2,1,0:T(2,128)}, u32[]{:S(2)}) %copy-start.1) | copy-done | bytes 65560
  1.6 0.7 %copy-done.3 = s32[1,2,5]{2,1,0:T(2,128)S(1)} copy-done((s32[1,2,5]{2,1,0:T(2,128)S(1)}, s32[1,2,5]{2,1,0:T(2,128)}, u32[]{:S(2)}) %copy-start.3) | copy-done | bytes 64
  2.4 0.1 collective-permute-start
  2.5 1.1 %collective-permute-done = f32[72,128]{1,0:T(8,128)S(1)} collective-permute-done((f32[72,128]{1,0:T(8,128)S(1)}, f32[72,128]{1,0:T(8,128)S(1)}, u32[]{:S(2)}, u32[]{:S(2)}) %collective-permute-start) | collective-permute-done | bytes 36896 | tf_op jit(solution)/shard_map/ppermute | solution.py:330
  3.7 2.7 %collective-permute-start.2 = (f32[2,72,128]{2,1,0:T(8,128)S(1)}, f32[2,72,128]{2,1,0:T(8,128)S(1)}, u32[]{:S(2)}, u32[]{:S(2)}) collective-permute-start(f32[2,72,128]{2,1,0:T(8,128)S(1)} %pad_maximum_fusion), channel_id=1, source_target_pairs={{0,3},{1,2},{2,1},{3,0},{4,7},{5,6},{6,5},{7,4},{8,11},{9,10},{10,... | collective-permute-start | bytes 221192 | tf_op jit(solution)/shard_map/ppermute | solution.py:327
  6.4 0.1 collective-permute-start.3
  6.5 2.5 %collective-permute-done.2 = f32[2,72,128]{2,1,0:T(8,128)S(1)} collective-permute-done((f32[2,72,128]{2,1,0:T(8,128)S(1)}, f32[2,72,128]{2,1,0:T(8,128)S(1)}, u32[]{:S(2)}, u32[]{:S(2)}) %collective-permute-start.2) | collective-permute-done | bytes 73760 | tf_op jit(solution)/shard_map/ppermute | solution.py:327
  9.0 0.7 %collective-permute-start.4 = (f32[4,32,128]{2,1,0:T(8,128)S(1)}, f32[4,32,128]{2,1,0:T(8,128)S(1)}, u32[]{:S(2)}, u32[]{:S(2)}) collective-permute-start(f32[4,32,128]{2,1,0:T(8,128)S(1)} %maximum_select_fusion.1.refs_2_.refs_3_), channel_id=1, source_target_pairs={{4,8},{8,4},{12,16},{16,12},{20,24},{24,20},{5,9},{9,5},{13,17},{1... | collective-permute-start | bytes 196616 | tf_op jit(solution)/shard_map/ppermute | solution.py:333
  9.7 4.4 %collective-permute-start.6 = (f32[4,32,128]{2,1,0:T(8,128)S(1)}, f32[4,32,128]{2,1,0:T(8,128)S(1)}, u32[]{:S(2)}, u32[]{:S(2)}) collective-permute-start(f32[4,32,128]{2,1,0:T(8,128)S(1)} %maximum_select_fusion.2.refs_3_), channel_id=1, source_target_pairs={{0,4},{4,0},{8,12},{12,8},{16,20},{20,16},{24,28},{28,24},{1,5},{5... | collective-permute-start | bytes 196616 | tf_op jit(solution)/shard_map/ppermute | solution.py:336
  14.3 0.1 concatenate.27.codes_ref
  14.3 0.9 %prepare_chip.1.refs_0_ = bf16[2,2,256,1152]{3,2,1,0:T(8,128)(2,1)S(1)} custom-call(s32[44]{0:T(128)S(1)} %concatenate.27.codes_ref, f32[1,2,5,128,128]{4,3,2,1,0:T(8,128)S(1)} %copy-done, f32[1,2,5,128,128]{4,3,2,1,0:T(8,128)S(1)} %collective-permute-done.1.core_ref.refs_1_), custom_call_target="tpu_custom_call" | custom-call | tf_op jit(solution)/shard_map/prepare_chip/pallas_call | solution.py:114
  15.3 0.8 %collective-permute-done.3.refs_0_ = f32[1,1,5,128,128]{4,3,2,1,0:T(8,128)S(1)} collective-permute-done((f32[1,1,5,128,128]{4,3,2,1,0:T(8,128)S(1)}, f32[1,1,5,128,128]{4,3,2,1,0:T(8,128)S(1)}, u32[]{:S(2)}, u32[]{:S(2)}) %collective-permute-start.3) | collective-permute-done | bytes 327712 | tf_op jit(solution)/shard_map/ppermute | solution.py:327
  16.1 0.5 collective-permute-start.5
  16.5 0.5 collective-permute-done.6.refs_4_
  17.1 1.4 %collective-permute-start.7 = (f32[1,1,5,128,128]{4,3,2,1,0:T(8,128)S(1)}, f32[1,1,5,128,128]{4,3,2,1,0:T(8,128)S(1)}, u32[]{:S(2)}, u32[]{:S(2)}) collective-permute-start(f32[1,1,5,128,128]{4,3,2,1,0:T(8,128)S(1)} %get-tuple-element.27), channel_id=1, source_target_pairs={{0,3},{1,2},{2,1},{3,0},{4,7},{5,6},{6,5},{7,4},{8,11},{9,10},{10,... | collective-permute-start | bytes 983048 | tf_op jit(solution)/shard_map/ppermute | solution.py:327
  18.5 0.7 %prepare_border.1.refs_1_ = bf16[1,2,256,1152]{3,2,1,0:T(8,128)(2,1)S(1)} custom-call(s32[44]{0:T(128)S(1)} %concatenate.27.codes_ref, f32[1,1,5,128,128]{4,3,2,1,0:T(8,128)S(1)} %collective-permute-done.3.refs_0_, f32[1,1,5,128,128]{4,3,2,1,0:T(8,128)S(1)} %collective-permute-done.5.refs_1_), custom_call_target="tpu_custom_call" | custom-call | tf_op jit(solution)/shard_map/prepare_border/pallas_call | solution.py:114
  19.2 0.6 one_0.1.refs_1_
  19.8 0.7 %collective-permute-start.8 = (f32[3,32,128]{2,1,0:T(8,128)S(1)}, f32[3,32,128]{2,1,0:T(8,128)S(1)}, u32[]{:S(2)}, u32[]{:S(2)}) collective-permute-start(f32[3,32,128]{2,1,0:T(8,128)S(1)} %one_0.1.refs_1_), channel_id=1, source_target_pairs={{4,8},{8,4},{12,16},{16,12},{20,24},{24,20},{5,9},{9,5},{13,17},{1... | collective-permute-start | bytes 147464 | tf_op jit(solution)/shard_map/ppermute | solution.py:333
  20.5 0.6 one_1.1.refs_2_
  21.1 5.3 %collective-permute-start.11 = (f32[3,32,128]{2,1,0:T(8,128)S(1)}, f32[3,32,128]{2,1,0:T(8,128)S(1)}, u32[]{:S(2)}, u32[]{:S(2)}) collective-permute-start(f32[3,32,128]{2,1,0:T(8,128)S(1)} %one_1.1.refs_2_), channel_id=1, source_target_pairs={{0,4},{4,0},{8,12},{12,8},{16,20},{20,16},{24,28},{28,24},{1,5},{5... | collective-permute-start | bytes 147464 | tf_op jit(solution)/shard_map/ppermute | solution.py:336
  26.4 0.4 two_inner_1.1.refs_2_
  26.8 0.4 two_inner_0.1.refs_2_
  27.2 0.2 two_0.1
  27.4 1.4 %collective-permute-start.9 = (f32[3,32,128]{2,1,0:T(8,128)S(1)}, f32[3,32,128]{2,1,0:T(8,128)S(1)}, u32[]{:S(2)}, u32[]{:S(2)}) collective-permute-start(f32[3,32,128]{2,1,0:T(8,128)S(1)} %pad_maximum_fusion.5), channel_id=1, source_target_pairs={{0,3},{1,2},{2,1},{3,0},{4,7},{5,6},{6,5},{7,4},{8,11},{9,10},{10,... | collective-permute-start | bytes 147464 | tf_op jit(solution)/shard_map/ppermute | solution.py:327
  28.9 0.2 two_1.1
  29.1 0.4 collective-permute-start.12
  29.6 1.9 %collective-permute-done.9 = f32[3,32,128]{2,1,0:T(8,128)S(1)} collective-permute-done((f32[3,32,128]{2,1,0:T(8,128)S(1)}, f32[3,32,128]{2,1,0:T(8,128)S(1)}, u32[]{:S(2)}, u32[]{:S(2)}) %collective-permute-start.9) | collective-permute-done | bytes 49184 | tf_op jit(solution)/shard_map/ppermute | solution.py:327
  31.5 0.7 %collective-permute-start.14 = (f32[4,32,128]{2,1,0:T(8,128)S(1)}, f32[4,32,128]{2,1,0:T(8,128)S(1)}, u32[]{:S(2)}, u32[]{:S(2)}) collective-permute-start(f32[4,32,128]{2,1,0:T(8,128)S(1)} %pad_maximum_fusion.1.refs_3_.refs_5_), channel_id=1, source_target_pairs={{4,8},{8,4},{12,16},{16,12},{20,24},{24,20},{5,9},{9,5},{13,17},{1... | collective-permute-start | bytes 196616 | tf_op jit(solution)/shard_map/ppermute | solution.py:333
  32.2 0.2 collective-permute-start.10
  32.4 0.5 collective-permute-done.12
  32.9 4.0 %collective-permute-start.13 = (f32[4,32,128]{2,1,0:T(8,128)S(1)}, f32[4,32,128]{2,1,0:T(8,128)S(1)}, u32[]{:S(2)}, u32[]{:S(2)}) collective-permute-start(f32[4,32,128]{2,1,0:T(8,128)S(1)} %pad_maximum_fusion.2.refs_4_.refs_5_), channel_id=1, source_target_pairs={{0,4},{4,0},{8,12},{12,8},{16,20},{20,16},{24,28},{28,24},{1,5},{5... | collective-permute-start | bytes 196616 | tf_op jit(solution)/shard_map/ppermute | solution.py:336
  37.0 0.7 %prepare_inner.1.refs_2_ = bf16[1,2,256,1152]{3,2,1,0:T(8,128)(2,1)S(1)} custom-call(s32[44]{0:T(128)S(1)} %concatenate.27.codes_ref, f32[1,1,5,128,128]{4,3,2,1,0:T(8,128)S(1)} %collective-permute-done.7.refs_0_, f32[1,1,5,128,128]{4,3,2,1,0:T(8,128)S(1)} %collective-permute-done.10.refs_1_), custom_call_target="tpu_custom_call" | custom-call | tf_op jit(solution)/shard_map/prepare_inner/pallas_call | solution.py:114
  37.7 0.5 three_inner_0.1.refs_4_
  38.3 0.3 three_0.1.refs_3_
  38.6 0.7 %collective-permute-start.16 = (f32[4,32,128]{2,1,0:T(8,128)S(1)}, f32[4,32,128]{2,1,0:T(8,128)S(1)}, u32[]{:S(2)}, u32[]{:S(2)}) collective-permute-start(f32[4,32,128]{2,1,0:T(8,128)S(1)} %three_0.1.refs_3_), channel_id=1, source_target_pairs={{4,8},{8,4},{12,16},{16,12},{20,24},{24,20},{5,9},{9,5},{13,17},{1... | collective-permute-start | bytes 196616 | tf_op jit(solution)/shard_map/ppermute | solution.py:333
  39.3 0.4 collective-permute-done.13.refs_5_
  39.7 0.7 %three_1.1.refs_4_ = f32[4,32,128]{2,1,0:T(8,128)S(1)} custom-call(bf16[2,2,256,1152]{3,2,1,0:T(8,128)(2,1)S(1)} %prepare_chip.1.refs_0_, bf16[1,2,256,1152]{3,2,1,0:T(8,128)(2,1)S(1)} %prepare_border.1.refs_1_, bf16[1,2,256,1152]{3,2,1,0:T(8,128)(2,1)S(1)} %prepare_inner.1.refs_2_, f32[4,32,128]{2,1,0:T(8,128)S(1)} %pad_maximum_fusion.1.refs_3_.refs_5_, ...), custom_call_target="tpu_custom_call" | custom-call | flops 150994944 | bytes 2359296 | tf_op jit(solution)/shard_map/three_1/pallas_call | solution.py:244
  40.4 4.6 %collective-permute-start.15 = (f32[4,32,128]{2,1,0:T(8,128)S(1)}, f32[4,32,128]{2,1,0:T(8,128)S(1)}, u32[]{:S(2)}, u32[]{:S(2)}) collective-permute-start(f32[4,32,128]{2,1,0:T(8,128)S(1)} %three_1.1.refs_4_), channel_id=1, source_target_pairs={{0,4},{4,0},{8,12},{12,8},{16,20},{20,16},{24,28},{28,24},{1,5},{5... | collective-permute-start | bytes 196616 | tf_op jit(solution)/shard_map/ppermute | solution.py:336
  45.0 0.5 four_inner_0.1.refs_4_
  45.5 0.5 four_inner_1.1.refs_4_
  46.1 0.5 four_0.1
  46.6 0.7 %collective-permute-done.15.refs_3_ = f32[4,32,128]{2,1,0:T(8,128)S(1)} collective-permute-done((f32[4,32,128]{2,1,0:T(8,128)S(1)}, f32[4,32,128]{2,1,0:T(8,128)S(1)}, u32[]{:S(2)}, u32[]{:S(2)}) %collective-permute-start.15) | collective-permute-done | bytes 65568 | tf_op jit(solution)/shard_map/ppermute | solution.py:336
  47.3 0.5 four_1.1
  47.9 1.2 %collective-permute-done.17 = f32[4,24,128]{2,1,0:T(8,128)S(1)} collective-permute-done((f32[4,24,128]{2,1,0:T(8,128)S(1)}, f32[4,24,128]{2,1,0:T(8,128)S(1)}, u32[]{:S(2)}, u32[]{:S(2)}) %collective-permute-start.17) | collective-permute-done | bytes 49184 | tf_op jit(solution)/shard_map/ppermute | solution.py:330
  49.1 9.9 %all_to_all.5.parts_ref = f32[8,24,128]{2,1,0:T(8,128)S(1)} all-to-all(f32[8,24,128]{2,1,0:T(8,128)S(1)} %maximum_select_fusion), channel_id=1, replica_groups={{28,24,20,16,12,8,4,0},{29,25,21,17,13,9,5,1},{30,26,22,18,14,10,6,2},{..., dimensions={0} | all-to-all | bytes 196608 | tf_op jit(solution)/shard_map/all_to_all | solution.py:390
  59.0 1.5 %finish.1 = f32[8,1,16,128]{3,2,1,0:T(8,128)} custom-call(s32[32,128]{1,0:T(8,128)S(1)} %broadcast_in_dim.12.flags_ref.refs_7_, f32[8,24,128]{2,1,0:T(8,128)S(1)} %all_to_all.5.parts_ref, f32[8,8,8]{2,1,0:T(8,128)S(1)} %copy-done.2), custom_call_target="tpu_custom_call" | custom-call | tf_op jit(solution)/shard_map/finish/pallas_call | solution.py:299
  (46 shorter events, 0.7 us)
Async XLA Ops:
  0.0 3.7 %copy-start = (f32[1,2,5,128,128]{4,3,2,1,0:T(8,128)S(1)}, f32[1,2,5,128,128]{4,3,2,1,0:T(8,128)}, u32[]{:S(2)}) copy-start(f32[1,2,5,128,128]{4,3,2,1,0:T(8,128)} %refs_0_.1) | copy-start | bytes 1966084
  0.0 3.6 %collective-permute-start.1 = (f32[1,2,5,128,128]{4,3,2,1,0:T(8,128)}, f32[1,2,5,128,128]{4,3,2,1,0:T(8,128)S(1)}, u32[]{:S(2)}, u32[]{:S(2)}) collective-permute-start(f32[1,2,5,128,128]{4,3,2,1,0:T(8,128)} %refs_0_.1), channel_id=1, source_target_pairs={{0,1},{1,0},{2,3},{3,2},{4,5},{5,4},{6,7},{7,6},{8,9},{9,8},{10,11... | collective-permute-start | bytes 1966088 | tf_op jit(solution)/shard_map/ppermute | solution.py:330
  0.8 0.8 %copy-start.1 = (f32[64,1,2,128]{3,2,1,0:T(2,128)S(1)}, f32[64,1,2,128]{3,2,1,0:T(2,128)}, u32[]{:S(2)}) copy-start(f32[64,1,2,128]{3,2,1,0:T(2,128)} %slab_ref.1) | copy-start | bytes 196612
  1.6 0.7 %copy-start.3 = (s32[1,2,5]{2,1,0:T(2,128)S(1)}, s32[1,2,5]{2,1,0:T(2,128)}, u32[]{:S(2)}) copy-start(s32[1,2,5]{2,1,0:T(2,128)} %codes_ref.1) | copy-start | bytes 124
  2.4 1.3 %collective-permute-start = (f32[72,128]{1,0:T(8,128)S(1)}, f32[72,128]{1,0:T(8,128)S(1)}, u32[]{:S(2)}, u32[]{:S(2)}) collective-permute-start(f32[72,128]{1,0:T(8,128)S(1)} %get-tuple-element.46), channel_id=1, source_target_pairs={{0,1},{1,0},{2,3},{3,2},{4,5},{5,4},{6,7},{7,6},{8,9},{9,8},{10,11... | collective-permute-start | bytes 110600 | tf_op jit(solution)/shard_map/ppermute | solution.py:330
  3.7 5.3 %collective-permute-start.2 = (f32[2,72,128]{2,1,0:T(8,128)S(1)}, f32[2,72,128]{2,1,0:T(8,128)S(1)}, u32[]{:S(2)}, u32[]{:S(2)}) collective-permute-start(f32[2,72,128]{2,1,0:T(8,128)S(1)} %pad_maximum_fusion), channel_id=1, source_target_pairs={{0,3},{1,2},{2,1},{3,0},{4,7},{5,6},{6,5},{7,4},{8,11},{9,10},{10,... | collective-permute-start | bytes 221192 | tf_op jit(solution)/shard_map/ppermute | solution.py:327
  6.4 9.7 %collective-permute-start.3 = (f32[1,1,5,128,128]{4,3,2,1,0:T(8,128)S(1)}, f32[1,1,5,128,128]{4,3,2,1,0:T(8,128)S(1)}, u32[]{:S(2)}, u32[]{:S(2)}) collective-permute-start(f32[1,1,5,128,128]{4,3,2,1,0:T(8,128)S(1)} %get-tuple-element.23), channel_id=1, source_target_pairs={{0,3},{1,2},{2,1},{3,0},{4,7},{5,6},{6,5},{7,4},{8,11},{9,10},{10,... | collective-permute-start | bytes 983048 | tf_op jit(solution)/shard_map/ppermute | solution.py:327
  9.0 6.2 %collective-permute-start.4 = (f32[4,32,128]{2,1,0:T(8,128)S(1)}, f32[4,32,128]{2,1,0:T(8,128)S(1)}, u32[]{:S(2)}, u32[]{:S(2)}) collective-permute-start(f32[4,32,128]{2,1,0:T(8,128)S(1)} %maximum_select_fusion.1.refs_2_.refs_3_), channel_id=1, source_target_pairs={{4,8},{8,4},{12,16},{16,12},{20,24},{24,20},{5,9},{9,5},{13,17},{1... | collective-permute-start | bytes 196616 | tf_op jit(solution)/shard_map/ppermute | solution.py:333
  9.7 7.3 %collective-permute-start.6 = (f32[4,32,128]{2,1,0:T(8,128)S(1)}, f32[4,32,128]{2,1,0:T(8,128)S(1)}, u32[]{:S(2)}, u32[]{:S(2)}) collective-permute-start(f32[4,32,128]{2,1,0:T(8,128)S(1)} %maximum_select_fusion.2.refs_3_), channel_id=1, source_target_pairs={{0,4},{4,0},{8,12},{12,8},{16,20},{20,16},{24,28},{28,24},{1,5},{5... | collective-permute-start | bytes 196616 | tf_op jit(solution)/shard_map/ppermute | solution.py:336
  16.1 2.4 %collective-permute-start.5 = (f32[1,1,5,128,128]{4,3,2,1,0:T(8,128)S(1)}, f32[1,1,5,128,128]{4,3,2,1,0:T(8,128)S(1)}, u32[]{:S(2)}, u32[]{:S(2)}) collective-permute-start(f32[1,1,5,128,128]{4,3,2,1,0:T(8,128)S(1)} %collective-permute-done.3.refs_0_), channel_id=1, source_target_pairs={{0,1},{1,0},{2,3},{3,2},{4,5},{5,4},{6,7},{7,6},{8,9},{9,8},{10,11... | collective-permute-start | bytes 983048 | tf_op jit(solution)/shard_map/ppermute | solution.py:330
  17.1 10.1 %collective-permute-start.7 = (f32[1,1,5,128,128]{4,3,2,1,0:T(8,128)S(1)}, f32[1,1,5,128,128]{4,3,2,1,0:T(8,128)S(1)}, u32[]{:S(2)}, u32[]{:S(2)}) collective-permute-start(f32[1,1,5,128,128]{4,3,2,1,0:T(8,128)S(1)} %get-tuple-element.27), channel_id=1, source_target_pairs={{0,3},{1,2},{2,1},{3,0},{4,7},{5,6},{6,5},{7,4},{8,11},{9,10},{10,... | collective-permute-start | bytes 983048 | tf_op jit(solution)/shard_map/ppermute | solution.py:327
  19.8 7.3 %collective-permute-start.8 = (f32[3,32,128]{2,1,0:T(8,128)S(1)}, f32[3,32,128]{2,1,0:T(8,128)S(1)}, u32[]{:S(2)}, u32[]{:S(2)}) collective-permute-start(f32[3,32,128]{2,1,0:T(8,128)S(1)} %one_0.1.refs_1_), channel_id=1, source_target_pairs={{4,8},{8,4},{12,16},{16,12},{20,24},{24,20},{5,9},{9,5},{13,17},{1... | collective-permute-start | bytes 147464 | tf_op jit(solution)/shard_map/ppermute | solution.py:333
  21.1 7.7 %collective-permute-start.11 = (f32[3,32,128]{2,1,0:T(8,128)S(1)}, f32[3,32,128]{2,1,0:T(8,128)S(1)}, u32[]{:S(2)}, u32[]{:S(2)}) collective-permute-start(f32[3,32,128]{2,1,0:T(8,128)S(1)} %one_1.1.refs_2_), channel_id=1, source_target_pairs={{0,4},{4,0},{8,12},{12,8},{16,20},{20,16},{24,28},{28,24},{1,5},{5... | collective-permute-start | bytes 147464 | tf_op jit(solution)/shard_map/ppermute | solution.py:336
  27.4 4.1 %collective-permute-start.9 = (f32[3,32,128]{2,1,0:T(8,128)S(1)}, f32[3,32,128]{2,1,0:T(8,128)S(1)}, u32[]{:S(2)}, u32[]{:S(2)}) collective-permute-start(f32[3,32,128]{2,1,0:T(8,128)S(1)} %pad_maximum_fusion.5), channel_id=1, source_target_pairs={{0,3},{1,2},{2,1},{3,0},{4,7},{5,6},{6,5},{7,4},{8,11},{9,10},{10,... | collective-permute-start | bytes 147464 | tf_op jit(solution)/shard_map/ppermute | solution.py:327
  29.1 3.8 %collective-permute-start.12 = (f32[3,32,128]{2,1,0:T(8,128)S(1)}, f32[3,32,128]{2,1,0:T(8,128)S(1)}, u32[]{:S(2)}, u32[]{:S(2)}) collective-permute-start(f32[3,32,128]{2,1,0:T(8,128)S(1)} %pad_maximum_fusion.6), channel_id=1, source_target_pairs={{0,3},{1,2},{2,1},{3,0},{4,7},{5,6},{6,5},{7,4},{8,11},{9,10},{10,... | collective-permute-start | bytes 147464 | tf_op jit(solution)/shard_map/ppermute | solution.py:327
  31.5 6.8 %collective-permute-start.14 = (f32[4,32,128]{2,1,0:T(8,128)S(1)}, f32[4,32,128]{2,1,0:T(8,128)S(1)}, u32[]{:S(2)}, u32[]{:S(2)}) collective-permute-start(f32[4,32,128]{2,1,0:T(8,128)S(1)} %pad_maximum_fusion.1.refs_3_.refs_5_), channel_id=1, source_target_pairs={{4,8},{8,4},{12,16},{16,12},{20,24},{24,20},{5,9},{9,5},{13,17},{1... | collective-permute-start | bytes 196616 | tf_op jit(solution)/shard_map/ppermute | solution.py:333
  32.2 4.8 %collective-permute-start.10 = (f32[1,1,5,128,128]{4,3,2,1,0:T(8,128)S(1)}, f32[1,1,5,128,128]{4,3,2,1,0:T(8,128)S(1)}, u32[]{:S(2)}, u32[]{:S(2)}) collective-permute-start(f32[1,1,5,128,128]{4,3,2,1,0:T(8,128)S(1)} %collective-permute-done.7.refs_0_), channel_id=1, source_target_pairs={{0,1},{1,0},{2,3},{3,2},{4,5},{5,4},{6,7},{7,6},{8,9},{9,8},{10,11... | collective-permute-start | bytes 983048 | tf_op jit(solution)/shard_map/ppermute | solution.py:330
  32.9 6.8 %collective-permute-start.13 = (f32[4,32,128]{2,1,0:T(8,128)S(1)}, f32[4,32,128]{2,1,0:T(8,128)S(1)}, u32[]{:S(2)}, u32[]{:S(2)}) collective-permute-start(f32[4,32,128]{2,1,0:T(8,128)S(1)} %pad_maximum_fusion.2.refs_4_.refs_5_), channel_id=1, source_target_pairs={{0,4},{4,0},{8,12},{12,8},{16,20},{20,16},{24,28},{28,24},{1,5},{5... | collective-permute-start | bytes 196616 | tf_op jit(solution)/shard_map/ppermute | solution.py:336
  38.6 7.5 %collective-permute-start.16 = (f32[4,32,128]{2,1,0:T(8,128)S(1)}, f32[4,32,128]{2,1,0:T(8,128)S(1)}, u32[]{:S(2)}, u32[]{:S(2)}) collective-permute-start(f32[4,32,128]{2,1,0:T(8,128)S(1)} %three_0.1.refs_3_), channel_id=1, source_target_pairs={{4,8},{8,4},{12,16},{16,12},{20,24},{24,20},{5,9},{9,5},{13,17},{1... | collective-permute-start | bytes 196616 | tf_op jit(solution)/shard_map/ppermute | solution.py:333
  40.4 6.8 %collective-permute-start.15 = (f32[4,32,128]{2,1,0:T(8,128)S(1)}, f32[4,32,128]{2,1,0:T(8,128)S(1)}, u32[]{:S(2)}, u32[]{:S(2)}) collective-permute-start(f32[4,32,128]{2,1,0:T(8,128)S(1)} %three_1.1.refs_4_), channel_id=1, source_target_pairs={{0,4},{4,0},{8,12},{12,8},{16,20},{20,16},{24,28},{28,24},{1,5},{5... | collective-permute-start | bytes 196616 | tf_op jit(solution)/shard_map/ppermute | solution.py:336
  47.2 11.8 %copy-start.2 = (f32[8,8,8]{2,1,0:T(8,128)S(1)}, f32[8,8,8]{2,1,0:T(8,128)}, u32[]{:S(2)}) copy-start(f32[8,8,8]{2,1,0:T(8,128)} %rot_ref.1) | copy-start | bytes 6148
  47.8 1.3 %collective-permute-start.17 = (f32[4,24,128]{2,1,0:T(8,128)S(1)}, f32[4,24,128]{2,1,0:T(8,128)S(1)}, u32[]{:S(2)}, u32[]{:S(2)}) collective-permute-start(f32[4,24,128]{2,1,0:T(8,128)S(1)} %get-tuple-element.36), channel_id=1, source_target_pairs={{0,1},{1,0},{2,3},{3,2},{4,5},{5,4},{6,7},{7,6},{8,9},{9,8},{10,11... | collective-permute-start | bytes 147464 | tf_op jit(solution)/shard_map/ppermute | solution.py:330

commit v12 on v10

--- a/solution.py
+++ b/solution.py
@@ -285,11 +285,10 @@
     mixed = []
     for w in range(wide):
         for c in range(cols):
-            block = parts_ref[w, c * VEC : (c + 1) * VEC, :]
-            total = columns[0] * block[0:1, :]
-            for d in range(1, VEC):
-                total = total + columns[d] * block[d : d + 1, :]
-            mixed.append(total)
+            terms = [columns[d] * parts_ref[w, pl.ds(c * VEC + d, 1), :] for d in range(VEC)]
+            while len(terms) > 1:
+                terms = [low + high for low, high in zip(terms[::2], terms[1::2])]
+            mixed += terms
     for w in range(wide):
         for c in range(cols):
             out_ref[:, 0, w * cols + c, :] = mixed[(wide - 1 - w) * cols + c]

time: 60.8 us -> 60.8 us (level)
  no operation moved by 1% of the time
where the time goes in v12:
time: 60.8 us; the launch traced here: 60.5 us
  starting transfers between devices  27.6 us (45%)
  waiting for transfers between devices  10.6 us (17%)
  blocking collectives  9.94 us (16%)
  Pallas kernels  9.93 us (16%)
  local copies, waits for them, and re-layouts  1.98 us (3%)
    ppermute x4, starting transfers between devices, over_near(): return lax.ppermute(value, 'wide', near)  17.7 us
    all_to_all x1, blocking collectives, body(): lax.all_to_all(packed, ('wide', 'grp'), split_axis=0, concat_axis=0, tile...  9.94 us
    ppermute x5, waiting for transfers between devices, across(): return lax.ppermute(value, 'grp', [(i, i ^ 3) for i in range(grp)])  6.56 us
    ppermute x5, starting transfers between devices, across(): return lax.ppermute(value, 'grp', [(i, i ^ 3) for i in range(grp)])  6.06 us
    pallas_call x8, Pallas kernels, step(): pl.pallas_call(functools.partial(step_kernel, kind, u, len(h_ready)), in_...  3.69 us
    ppermute x4, starting transfers between devices, over_far(): return lax.ppermute(value, 'wide', far)  2.66 us
    ppermute x5, waiting for transfers between devices, core(): return lax.ppermute(value, 'grp', [(i, i ^ 1) for i in range(grp)])  2.38 us
    pallas_call x3, Pallas kernels, prepare(): pl.pallas_call(functools.partial(prepare_kernel, mode), in_specs=[SMEM] +...  2.37 us
  transfers between devices with their start and end apart: 18, of which 9 were waited for; matrix products, arithmetic and copies ran while one was open for 1% of the time, Pallas kernels for 13%

profile of v12, /device:TPU:0, one launch (start us, length us, event | category | flops | bytes accessed | tf_op | source)
XLA Modules:
  0.0 60.5 jit_solution(15098511388736091793)
XLA Ops:
  0.0 0.5 collective-permute-start.1
  0.6 0.1 broadcast_in_dim.11
  0.8 0.8 %copy-done.1 = f32[64,1,2,128]{3,2,1,0:T(2,128)S(1)} copy-done((f32[64,1,2,128]{3,2,1,0:T(2,128)S(1)}, f32[64,1,2,128]{3,2,1,0:T(2,128)}, u32[]{:S(2)}) %copy-start.1) | copy-done | bytes 65560
  1.6 0.7 %copy-done.3 = s32[1,2,5]{2,1,0:T(2,128)S(1)} copy-done((s32[1,2,5]{2,1,0:T(2,128)S(1)}, s32[1,2,5]{2,1,0:T(2,128)}, u32[]{:S(2)}) %copy-start.3) | copy-done | bytes 64
  2.4 0.1 collective-permute-start
  2.5 1.1 %collective-permute-done = f32[72,128]{1,0:T(8,128)S(1)} collective-permute-done((f32[72,128]{1,0:T(8,128)S(1)}, f32[72,128]{1,0:T(8,128)S(1)}, u32[]{:S(2)}, u32[]{:S(2)}) %collective-permute-start) | collective-permute-done | bytes 36896 | tf_op jit(solution)/shard_map/ppermute | solution.py:330
  3.7 2.7 %collective-permute-start.2 = (f32[2,72,128]{2,1,0:T(8,128)S(1)}, f32[2,72,128]{2,1,0:T(8,128)S(1)}, u32[]{:S(2)}, u32[]{:S(2)}) collective-permute-start(f32[2,72,128]{2,1,0:T(8,128)S(1)} %pad_maximum_fusion.2), channel_id=1, source_target_pairs={{0,3},{1,2},{2,1},{3,0},{4,7},{5,6},{6,5},{7,4},{8,11},{9,10},{10,... | collective-permute-start | bytes 221192 | tf_op jit(solution)/shard_map/ppermute | solution.py:327
  6.4 0.1 collective-permute-start.3
  6.5 2.5 %collective-permute-done.2 = f32[2,72,128]{2,1,0:T(8,128)S(1)} collective-permute-done((f32[2,72,128]{2,1,0:T(8,128)S(1)}, f32[2,72,128]{2,1,0:T(8,128)S(1)}, u32[]{:S(2)}, u32[]{:S(2)}) %collective-permute-start.2) | collective-permute-done | bytes 73760 | tf_op jit(solution)/shard_map/ppermute | solution.py:327
  9.0 0.7 %collective-permute-start.4 = (f32[4,32,128]{2,1,0:T(8,128)S(1)}, f32[4,32,128]{2,1,0:T(8,128)S(1)}, u32[]{:S(2)}, u32[]{:S(2)}) collective-permute-start(f32[4,32,128]{2,1,0:T(8,128)S(1)} %maximum_select_fusion.1.refs_2_.refs_3_), channel_id=1, source_target_pairs={{4,8},{8,4},{12,16},{16,12},{20,24},{24,20},{5,9},{9,5},{13,17},{1... | collective-permute-start | bytes 196616 | tf_op jit(solution)/shard_map/ppermute | solution.py:333
  9.7 4.4 %collective-permute-start.6 = (f32[4,32,128]{2,1,0:T(8,128)S(1)}, f32[4,32,128]{2,1,0:T(8,128)S(1)}, u32[]{:S(2)}, u32[]{:S(2)}) collective-permute-start(f32[4,32,128]{2,1,0:T(8,128)S(1)} %maximum_select_fusion.2.refs_3_), channel_id=1, source_target_pairs={{0,4},{4,0},{8,12},{12,8},{16,20},{20,16},{24,28},{28,24},{1,5},{5... | collective-permute-start | bytes 196616 | tf_op jit(solution)/shard_map/ppermute | solution.py:336
  14.3 0.1 concatenate.24.codes_ref
  14.3 0.9 %prepare_chip.1.refs_0_ = bf16[2,2,256,1152]{3,2,1,0:T(8,128)(2,1)S(1)} custom-call(s32[44]{0:T(128)S(1)} %concatenate.24.codes_ref, f32[1,2,5,128,128]{4,3,2,1,0:T(8,128)S(1)} %copy-done, f32[1,2,5,128,128]{4,3,2,1,0:T(8,128)S(1)} %collective-permute-done.1.core_ref.refs_1_), custom_call_target="tpu_custom_call" | custom-call | tf_op jit(solution)/shard_map/prepare_chip/pallas_call | solution.py:114
  15.3 0.8 %collective-permute-done.3.refs_0_ = f32[1,1,5,128,128]{4,3,2,1,0:T(8,128)S(1)} collective-permute-done((f32[1,1,5,128,128]{4,3,2,1,0:T(8,128)S(1)}, f32[1,1,5,128,128]{4,3,2,1,0:T(8,128)S(1)}, u32[]{:S(2)}, u32[]{:S(2)}) %collective-permute-start.3) | collective-permute-done | bytes 327712 | tf_op jit(solution)/shard_map/ppermute | solution.py:327
  16.1 0.5 collective-permute-start.5
  16.5 0.5 collective-permute-done.6.refs_4_
  17.1 1.4 %collective-permute-start.7 = (f32[1,1,5,128,128]{4,3,2,1,0:T(8,128)S(1)}, f32[1,1,5,128,128]{4,3,2,1,0:T(8,128)S(1)}, u32[]{:S(2)}, u32[]{:S(2)}) collective-permute-start(f32[1,1,5,128,128]{4,3,2,1,0:T(8,128)S(1)} %get-tuple-element.27), channel_id=1, source_target_pairs={{0,3},{1,2},{2,1},{3,0},{4,7},{5,6},{6,5},{7,4},{8,11},{9,10},{10,... | collective-permute-start | bytes 983048 | tf_op jit(solution)/shard_map/ppermute | solution.py:327
  18.5 0.7 %prepare_border.1.refs_1_ = bf16[1,2,256,1152]{3,2,1,0:T(8,128)(2,1)S(1)} custom-call(s32[44]{0:T(128)S(1)} %concatenate.24.codes_ref, f32[1,1,5,128,128]{4,3,2,1,0:T(8,128)S(1)} %collective-permute-done.3.refs_0_, f32[1,1,5,128,128]{4,3,2,1,0:T(8,128)S(1)} %collective-permute-done.5.refs_1_), custom_call_target="tpu_custom_call" | custom-call | tf_op jit(solution)/shard_map/prepare_border/pallas_call | solution.py:114
  19.2 0.6 one_0.1.refs_1_
  19.8 0.7 %collective-permute-start.8 = (f32[3,32,128]{2,1,0:T(8,128)S(1)}, f32[3,32,128]{2,1,0:T(8,128)S(1)}, u32[]{:S(2)}, u32[]{:S(2)}) collective-permute-start(f32[3,32,128]{2,1,0:T(8,128)S(1)} %one_0.1.refs_1_), channel_id=1, source_target_pairs={{4,8},{8,4},{12,16},{16,12},{20,24},{24,20},{5,9},{9,5},{13,17},{1... | collective-permute-start | bytes 147464 | tf_op jit(solution)/shard_map/ppermute | solution.py:333
  20.5 0.6 one_1.1.refs_2_
  21.1 5.3 %collective-permute-start.11 = (f32[3,32,128]{2,1,0:T(8,128)S(1)}, f32[3,32,128]{2,1,0:T(8,128)S(1)}, u32[]{:S(2)}, u32[]{:S(2)}) collective-permute-start(f32[3,32,128]{2,1,0:T(8,128)S(1)} %one_1.1.refs_2_), channel_id=1, source_target_pairs={{0,4},{4,0},{8,12},{12,8},{16,20},{20,16},{24,28},{28,24},{1,5},{5... | collective-permute-start | bytes 147464 | tf_op jit(solution)/shard_map/ppermute | solution.py:336
  26.4 0.4 two_inner_0.1.refs_2_
  26.8 0.3 two_inner_1.1.refs_2_
  27.2 0.2 two_0.1
  27.4 1.8 %collective-permute-start.9 = (f32[2,32,128]{2,1,0:T(8,128)S(1)}, f32[2,32,128]{2,1,0:T(8,128)S(1)}, u32[]{:S(2)}, u32[]{:S(2)}) collective-permute-start(f32[2,32,128]{2,1,0:T(8,128)S(1)} %two_0.1), channel_id=1, source_target_pairs={{0,3},{1,2},{2,1},{3,0},{4,7},{5,6},{6,5},{7,4},{8,11},{9,10},{10,... | collective-permute-start | bytes 98312 | tf_op jit(solution)/shard_map/ppermute | solution.py:327
  29.2 0.2 two_1.1
  29.5 0.1 collective-permute-start.12
  29.5 1.4 %collective-permute-done.9 = f32[2,32,128]{2,1,0:T(8,128)S(1)} collective-permute-done((f32[2,32,128]{2,1,0:T(8,128)S(1)}, f32[2,32,128]{2,1,0:T(8,128)S(1)}, u32[]{:S(2)}, u32[]{:S(2)}) %collective-permute-start.9) | collective-permute-done | bytes 32800 | tf_op jit(solution)/shard_map/ppermute | solution.py:327
  30.9 0.7 %collective-permute-start.14 = (f32[4,32,128]{2,1,0:T(8,128)S(1)}, f32[4,32,128]{2,1,0:T(8,128)S(1)}, u32[]{:S(2)}, u32[]{:S(2)}) collective-permute-start(f32[4,32,128]{2,1,0:T(8,128)S(1)} %pad_maximum_fusion.3.refs_3_.refs_5_), channel_id=1, source_target_pairs={{4,8},{8,4},{12,16},{16,12},{20,24},{24,20},{5,9},{9,5},{13,17},{1... | collective-permute-start | bytes 196616 | tf_op jit(solution)/shard_map/ppermute | solution.py:333
  31.6 0.1 collective-permute-start.10
  31.7 1.9 %collective-permute-done.12 = f32[4,32,128]{2,1,0:T(8,128)S(1)} collective-permute-done((f32[4,32,128]{2,1,0:T(8,128)S(1)}, f32[4,32,128]{2,1,0:T(8,128)S(1)}, u32[]{:S(2)}, u32[]{:S(2)}) %collective-permute-start.12) | collective-permute-done | bytes 65568 | tf_op jit(solution)/shard_map/ppermute | solution.py:327
  33.6 3.3 %collective-permute-start.13 = (f32[4,32,128]{2,1,0:T(8,128)S(1)}, f32[4,32,128]{2,1,0:T(8,128)S(1)}, u32[]{:S(2)}, u32[]{:S(2)}) collective-permute-start(f32[4,32,128]{2,1,0:T(8,128)S(1)} %fusion.refs_4_.refs_5_), channel_id=1, source_target_pairs={{0,4},{4,0},{8,12},{12,8},{16,20},{20,16},{24,28},{28,24},{1,5},{5... | collective-permute-start | bytes 196616 | tf_op jit(solution)/shard_map/ppermute | solution.py:336
  37.0 0.7 %prepare_inner.1.refs_2_ = bf16[1,2,256,1152]{3,2,1,0:T(8,128)(2,1)S(1)} custom-call(s32[44]{0:T(128)S(1)} %concatenate.24.codes_ref, f32[1,1,5,128,128]{4,3,2,1,0:T(8,128)S(1)} %collective-permute-done.7.refs_0_, f32[1,1,5,128,128]{4,3,2,1,0:T(8,128)S(1)} %collective-permute-done.10.refs_1_), custom_call_target="tpu_custom_call" | custom-call | tf_op jit(solution)/shard_map/prepare_inner/pallas_call | solution.py:114
  37.7 0.5 three_inner_0.1.refs_4_
  38.3 0.3 three_0.1.refs_3_
  38.6 0.7 %collective-permute-start.16 = (f32[4,32,128]{2,1,0:T(8,128)S(1)}, f32[4,32,128]{2,1,0:T(8,128)S(1)}, u32[]{:S(2)}, u32[]{:S(2)}) collective-permute-start(f32[4,32,128]{2,1,0:T(8,128)S(1)} %three_0.1.refs_3_), channel_id=1, source_target_pairs={{4,8},{8,4},{12,16},{16,12},{20,24},{24,20},{5,9},{9,5},{13,17},{1... | collective-permute-start | bytes 196616 | tf_op jit(solution)/shard_map/ppermute | solution.py:333
  39.2 0.4 collective-permute-done.13.refs_5_
  39.7 0.7 %three_1.1.refs_4_ = f32[4,32,128]{2,1,0:T(8,128)S(1)} custom-call(bf16[2,2,256,1152]{3,2,1,0:T(8,128)(2,1)S(1)} %prepare_chip.1.refs_0_, bf16[1,2,256,1152]{3,2,1,0:T(8,128)(2,1)S(1)} %prepare_border.1.refs_1_, bf16[1,2,256,1152]{3,2,1,0:T(8,128)(2,1)S(1)} %prepare_inner.1.refs_2_, f32[4,32,128]{2,1,0:T(8,128)S(1)} %pad_maximum_fusion.3.refs_3_.refs_5_, ...), custom_call_target="tpu_custom_call" | custom-call | flops 150994944 | bytes 2359296 | tf_op jit(solution)/shard_map/three_1/pallas_call | solution.py:244
  40.4 4.6 %collective-permute-start.15 = (f32[4,32,128]{2,1,0:T(8,128)S(1)}, f32[4,32,128]{2,1,0:T(8,128)S(1)}, u32[]{:S(2)}, u32[]{:S(2)}) collective-permute-start(f32[4,32,128]{2,1,0:T(8,128)S(1)} %three_1.1.refs_4_), channel_id=1, source_target_pairs={{0,4},{4,0},{8,12},{12,8},{16,20},{20,16},{24,28},{28,24},{1,5},{5... | collective-permute-start | bytes 196616 | tf_op jit(solution)/shard_map/ppermute | solution.py:336
  45.0 0.5 four_inner_0.1.refs_4_
  45.5 0.5 four_inner_1.1.refs_4_
  46.1 0.5 four_0.1
  46.5 0.7 %collective-permute-done.15.refs_3_ = f32[4,32,128]{2,1,0:T(8,128)S(1)} collective-permute-done((f32[4,32,128]{2,1,0:T(8,128)S(1)}, f32[4,32,128]{2,1,0:T(8,128)S(1)}, u32[]{:S(2)}, u32[]{:S(2)}) %collective-permute-start.15) | collective-permute-done | bytes 65568 | tf_op jit(solution)/shard_map/ppermute | solution.py:336
  47.2 0.5 four_1.1
  47.9 1.2 %collective-permute-done.17 = f32[4,24,128]{2,1,0:T(8,128)S(1)} collective-permute-done((f32[4,24,128]{2,1,0:T(8,128)S(1)}, f32[4,24,128]{2,1,0:T(8,128)S(1)}, u32[]{:S(2)}, u32[]{:S(2)}) %collective-permute-start.17) | collective-permute-done | bytes 49184 | tf_op jit(solution)/shard_map/ppermute | solution.py:330
  49.1 9.9 %all_to_all.5.parts_ref = f32[8,24,128]{2,1,0:T(8,128)S(1)} all-to-all(f32[8,24,128]{2,1,0:T(8,128)S(1)} %maximum_select_fusion), channel_id=1, replica_groups={{28,24,20,16,12,8,4,0},{29,25,21,17,13,9,5,1},{30,26,22,18,14,10,6,2},{..., dimensions={0} | all-to-all | bytes 196608 | tf_op jit(solution)/shard_map/all_to_all | solution.py:388
  59.0 1.5 %finish.1 = f32[8,1,16,128]{3,2,1,0:T(8,128)} custom-call(s32[32,128]{1,0:T(8,128)S(1)} %broadcast_in_dim.12.flags_ref.refs_7_, f32[8,24,128]{2,1,0:T(8,128)S(1)} %all_to_all.5.parts_ref, f32[8,8,8]{2,1,0:T(8,128)S(1)} %copy-done.2), custom_call_target="tpu_custom_call" | custom-call | tf_op jit(solution)/shard_map/finish/pallas_call | solution.py:299
  (45 shorter events, 0.7 us)
Async XLA Ops:
  0.0 3.7 %copy-start = (f32[1,2,5,128,128]{4,3,2,1,0:T(8,128)S(1)}, f32[1,2,5,128,128]{4,3,2,1,0:T(8,128)}, u32[]{:S(2)}) copy-start(f32[1,2,5,128,128]{4,3,2,1,0:T(8,128)} %refs_0_.1) | copy-start | bytes 1966084
  0.0 3.6 %collective-permute-start.1 = (f32[1,2,5,128,128]{4,3,2,1,0:T(8,128)}, f32[1,2,5,128,128]{4,3,2,1,0:T(8,128)S(1)}, u32[]{:S(2)}, u32[]{:S(2)}) collective-permute-start(f32[1,2,5,128,128]{4,3,2,1,0:T(8,128)} %refs_0_.1), channel_id=1, source_target_pairs={{0,1},{1,0},{2,3},{3,2},{4,5},{5,4},{6,7},{7,6},{8,9},{9,8},{10,11... | collective-permute-start | bytes 1966088 | tf_op jit(solution)/shard_map/ppermute | solution.py:330
  0.8 0.8 %copy-start.1 = (f32[64,1,2,128]{3,2,1,0:T(2,128)S(1)}, f32[64,1,2,128]{3,2,1,0:T(2,128)}, u32[]{:S(2)}) copy-start(f32[64,1,2,128]{3,2,1,0:T(2,128)} %slab_ref.1) | copy-start | bytes 196612
  1.6 0.7 %copy-start.3 = (s32[1,2,5]{2,1,0:T(2,128)S(1)}, s32[1,2,5]{2,1,0:T(2,128)}, u32[]{:S(2)}) copy-start(s32[1,2,5]{2,1,0:T(2,128)} %codes_ref.1) | copy-start | bytes 124
  2.4 1.3 %collective-permute-start = (f32[72,128]{1,0:T(8,128)S(1)}, f32[72,128]{1,0:T(8,128)S(1)}, u32[]{:S(2)}, u32[]{:S(2)}) collective-permute-start(f32[72,128]{1,0:T(8,128)S(1)} %get-tuple-element.46), channel_id=1, source_target_pairs={{0,1},{1,0},{2,3},{3,2},{4,5},{5,4},{6,7},{7,6},{8,9},{9,8},{10,11... | collective-permute-start | bytes 110600 | tf_op jit(solution)/shard_map/ppermute | solution.py:330
  3.7 5.3 %collective-permute-start.2 = (f32[2,72,128]{2,1,0:T(8,128)S(1)}, f32[2,72,128]{2,1,0:T(8,128)S(1)}, u32[]{:S(2)}, u32[]{:S(2)}) collective-permute-start(f32[2,72,128]{2,1,0:T(8,128)S(1)} %pad_maximum_fusion.2), channel_id=1, source_target_pairs={{0,3},{1,2},{2,1},{3,0},{4,7},{5,6},{6,5},{7,4},{8,11},{9,10},{10,... | collective-permute-start | bytes 221192 | tf_op jit(solution)/shard_map/ppermute | solution.py:327
  6.4 9.7 %collective-permute-start.3 = (f32[1,1,5,128,128]{4,3,2,1,0:T(8,128)S(1)}, f32[1,1,5,128,128]{4,3,2,1,0:T(8,128)S(1)}, u32[]{:S(2)}, u32[]{:S(2)}) collective-permute-start(f32[1,1,5,128,128]{4,3,2,1,0:T(8,128)S(1)} %get-tuple-element.23), channel_id=1, source_target_pairs={{0,3},{1,2},{2,1},{3,0},{4,7},{5,6},{6,5},{7,4},{8,11},{9,10},{10,... | collective-permute-start | bytes 983048 | tf_op jit(solution)/shard_map/ppermute | solution.py:327
  9.0 6.2 %collective-permute-start.4 = (f32[4,32,128]{2,1,0:T(8,128)S(1)}, f32[4,32,128]{2,1,0:T(8,128)S(1)}, u32[]{:S(2)}, u32[]{:S(2)}) collective-permute-start(f32[4,32,128]{2,1,0:T(8,128)S(1)} %maximum_select_fusion.1.refs_2_.refs_3_), channel_id=1, source_target_pairs={{4,8},{8,4},{12,16},{16,12},{20,24},{24,20},{5,9},{9,5},{13,17},{1... | collective-permute-start | bytes 196616 | tf_op jit(solution)/shard_map/ppermute | solution.py:333
  9.7 7.3 %collective-permute-start.6 = (f32[4,32,128]{2,1,0:T(8,128)S(1)}, f32[4,32,128]{2,1,0:T(8,128)S(1)}, u32[]{:S(2)}, u32[]{:S(2)}) collective-permute-start(f32[4,32,128]{2,1,0:T(8,128)S(1)} %maximum_select_fusion.2.refs_3_), channel_id=1, source_target_pairs={{0,4},{4,0},{8,12},{12,8},{16,20},{20,16},{24,28},{28,24},{1,5},{5... | collective-permute-start | bytes 196616 | tf_op jit(solution)/shard_map/ppermute | solution.py:336
  16.1 2.4 %collective-permute-start.5 = (f32[1,1,5,128,128]{4,3,2,1,0:T(8,128)S(1)}, f32[1,1,5,128,128]{4,3,2,1,0:T(8,128)S(1)}, u32[]{:S(2)}, u32[]{:S(2)}) collective-permute-start(f32[1,1,5,128,128]{4,3,2,1,0:T(8,128)S(1)} %collective-permute-done.3.refs_0_), channel_id=1, source_target_pairs={{0,1},{1,0},{2,3},{3,2},{4,5},{5,4},{6,7},{7,6},{8,9},{9,8},{10,11... | collective-permute-start | bytes 983048 | tf_op jit(solution)/shard_map/ppermute | solution.py:330
  17.1 9.7 %collective-permute-start.7 = (f32[1,1,5,128,128]{4,3,2,1,0:T(8,128)S(1)}, f32[1,1,5,128,128]{4,3,2,1,0:T(8,128)S(1)}, u32[]{:S(2)}, u32[]{:S(2)}) collective-permute-start(f32[1,1,5,128,128]{4,3,2,1,0:T(8,128)S(1)} %get-tuple-element.27), channel_id=1, source_target_pairs={{0,3},{1,2},{2,1},{3,0},{4,7},{5,6},{6,5},{7,4},{8,11},{9,10},{10,... | collective-permute-start | bytes 983048 | tf_op jit(solution)/shard_map/ppermute | solution.py:327
  19.8 7.3 %collective-permute-start.8 = (f32[3,32,128]{2,1,0:T(8,128)S(1)}, f32[3,32,128]{2,1,0:T(8,128)S(1)}, u32[]{:S(2)}, u32[]{:S(2)}) collective-permute-start(f32[3,32,128]{2,1,0:T(8,128)S(1)} %one_0.1.refs_1_), channel_id=1, source_target_pairs={{4,8},{8,4},{12,16},{16,12},{20,24},{24,20},{5,9},{9,5},{13,17},{1... | collective-permute-start | bytes 147464 | tf_op jit(solution)/shard_map/ppermute | solution.py:333
  21.1 8.1 %collective-permute-start.11 = (f32[3,32,128]{2,1,0:T(8,128)S(1)}, f32[3,32,128]{2,1,0:T(8,128)S(1)}, u32[]{:S(2)}, u32[]{:S(2)}) collective-permute-start(f32[3,32,128]{2,1,0:T(8,128)S(1)} %one_1.1.refs_2_), channel_id=1, source_target_pairs={{0,4},{4,0},{8,12},{12,8},{16,20},{20,16},{24,28},{28,24},{1,5},{5... | collective-permute-start | bytes 147464 | tf_op jit(solution)/shard_map/ppermute | solution.py:336
  27.4 3.5 %collective-permute-start.9 = (f32[2,32,128]{2,1,0:T(8,128)S(1)}, f32[2,32,128]{2,1,0:T(8,128)S(1)}, u32[]{:S(2)}, u32[]{:S(2)}) collective-permute-start(f32[2,32,128]{2,1,0:T(8,128)S(1)} %two_0.1), channel_id=1, source_target_pairs={{0,3},{1,2},{2,1},{3,0},{4,7},{5,6},{6,5},{7,4},{8,11},{9,10},{10,... | collective-permute-start | bytes 98312 | tf_op jit(solution)/shard_map/ppermute | solution.py:327
  29.5 4.1 %collective-permute-start.12 = (f32[4,32,128]{2,1,0:T(8,128)S(1)}, f32[4,32,128]{2,1,0:T(8,128)S(1)}, u32[]{:S(2)}, u32[]{:S(2)}) collective-permute-start(f32[4,32,128]{2,1,0:T(8,128)S(1)} %fusion.1), channel_id=1, source_target_pairs={{0,3},{1,2},{2,1},{3,0},{4,7},{5,6},{6,5},{7,4},{8,11},{9,10},{10,... | collective-permute-start | bytes 196616 | tf_op jit(solution)/shard_map/ppermute | solution.py:327
  30.9 7.3 %collective-permute-start.14 = (f32[4,32,128]{2,1,0:T(8,128)S(1)}, f32[4,32,128]{2,1,0:T(8,128)S(1)}, u32[]{:S(2)}, u32[]{:S(2)}) collective-permute-start(f32[4,32,128]{2,1,0:T(8,128)S(1)} %pad_maximum_fusion.3.refs_3_.refs_5_), channel_id=1, source_target_pairs={{4,8},{8,4},{12,16},{16,12},{20,24},{24,20},{5,9},{9,5},{13,17},{1... | collective-permute-start | bytes 196616 | tf_op jit(solution)/shard_map/ppermute | solution.py:333
  31.6 5.4 %collective-permute-start.10 = (f32[1,1,5,128,128]{4,3,2,1,0:T(8,128)S(1)}, f32[1,1,5,128,128]{4,3,2,1,0:T(8,128)S(1)}, u32[]{:S(2)}, u32[]{:S(2)}) collective-permute-start(f32[1,1,5,128,128]{4,3,2,1,0:T(8,128)S(1)} %collective-permute-done.7.refs_0_), channel_id=1, source_target_pairs={{0,1},{1,0},{2,3},{3,2},{4,5},{5,4},{6,7},{7,6},{8,9},{9,8},{10,11... | collective-permute-start | bytes 983048 | tf_op jit(solution)/shard_map/ppermute | solution.py:330
  33.6 6.1 %collective-permute-start.13 = (f32[4,32,128]{2,1,0:T(8,128)S(1)}, f32[4,32,128]{2,1,0:T(8,128)S(1)}, u32[]{:S(2)}, u32[]{:S(2)}) collective-permute-start(f32[4,32,128]{2,1,0:T(8,128)S(1)} %fusion.refs_4_.refs_5_), channel_id=1, source_target_pairs={{0,4},{4,0},{8,12},{12,8},{16,20},{20,16},{24,28},{28,24},{1,5},{5... | collective-permute-start | bytes 196616 | tf_op jit(solution)/shard_map/ppermute | solution.py:336
  38.6 7.5 %collective-permute-start.16 = (f32[4,32,128]{2,1,0:T(8,128)S(1)}, f32[4,32,128]{2,1,0:T(8,128)S(1)}, u32[]{:S(2)}, u32[]{:S(2)}) collective-permute-start(f32[4,32,128]{2,1,0:T(8,128)S(1)} %three_0.1.refs_3_), channel_id=1, source_target_pairs={{4,8},{8,4},{12,16},{16,12},{20,24},{24,20},{5,9},{9,5},{13,17},{1... | collective-permute-start | bytes 196616 | tf_op jit(solution)/shard_map/ppermute | solution.py:333
  40.4 6.8 %collective-permute-start.15 = (f32[4,32,128]{2,1,0:T(8,128)S(1)}, f32[4,32,128]{2,1,0:T(8,128)S(1)}, u32[]{:S(2)}, u32[]{:S(2)}) collective-permute-start(f32[4,32,128]{2,1,0:T(8,128)S(1)} %three_1.1.refs_4_), channel_id=1, source_target_pairs={{0,4},{4,0},{8,12},{12,8},{16,20},{20,16},{24,28},{28,24},{1,5},{5... | collective-permute-start | bytes 196616 | tf_op jit(solution)/shard_map/ppermute | solution.py:336
  47.2 11.8 %copy-start.2 = (f32[8,8,8]{2,1,0:T(8,128)S(1)}, f32[8,8,8]{2,1,0:T(8,128)}, u32[]{:S(2)}) copy-start(f32[8,8,8]{2,1,0:T(8,128)} %rot_ref.1) | copy-start | bytes 6148
  47.8 1.3 %collective-permute-start.17 = (f32[4,24,128]{2,1,0:T(8,128)S(1)}, f32[4,24,128]{2,1,0:T(8,128)S(1)}, u32[]{:S(2)}, u32[]{:S(2)}) collective-permute-start(f32[4,24,128]{2,1,0:T(8,128)S(1)} %get-tuple-element.36), channel_id=1, source_target_pairs={{0,1},{1,0},{2,3},{3,2},{4,5},{5,4},{6,7},{7,6},{8,9},{9,8},{10,11... | collective-permute-start | bytes 147464 | tf_op jit(solution)/shard_map/ppermute | solution.py:330
